TPU v7x, 32 devices: a whole 2x2x4 slice. The times are simulated.
32 devices in a mesh: ctx: 8 (over z, x), head: 4 (over y, core).
Axes of the slice: x: 2, y: 2, z: 4, core: 2. Of those that a mesh axis runs over, the one named last changes fastest.
Arguments:
- queries: bfloat16 [8192, 4096], P('ctx', 'head'), may hold values from -30 to 30
- keys: bfloat16 [8192, 4096], P('ctx', 'head'), may hold values from -30 to 30
- values: bfloat16 [8192, 4096], P('ctx', 'head'), may hold values from -14 to 14
- selection: int32 [32, 8], P('ctx'), may hold values from 0 to 31, as said below
- norm_gain: bfloat16 [4096], P('head'), may hold values from 0.099609375 to 1.8984375
Outputs:
- normed: bfloat16 [8192, 4096], P('ctx', 'head')
Inputs may be any that keep to these rules, and one draw needn't show every extreme that they name: `selection`: row c lists span c's blocks: the first entry is c; every other entry is a distinct block earlier than c, or c again where no block is selected. Block b belongs to the device holding span b, which is b // 4. Among the entries after the first in the 4 rows of one device, at most 2 that differ from their row's span name blocks of any one device.
All inputs are finite; a program needn't handle non-finite values.
Results may differ from a plain program's by a relative error of at most 0.0052.
Values may be sent and summed in bfloat16 or wider, within the bound.
No kernel may reach another device: no remote copies, remote signals or barrier semaphores. Data moves between devices by JAX's collectives and lax.ppermute only.
A program may use at most 192 MiB of HBM per device.

v0:
```python
from functools import partial
import math

import jax
import jax.numpy as jnp
from jax import lax
from jax.sharding import PartitionSpec as P

HEADS = 32
HD = 128
CAP = 2


def partial_state(query_rows, key_block, value_block, causal):
    scores = jnp.einsum(
        "sqhd,skhd->shqk", query_rows, key_block, preferred_element_type=jnp.float32
    ) * query_rows.shape[3] ** (-0.5)
    if causal:
        query_pos = lax.broadcasted_iota(jnp.int32, scores.shape, 2)
        key_pos = lax.broadcasted_iota(jnp.int32, scores.shape, 3)
        scores = jnp.where(key_pos <= query_pos, scores, -1e30)
    row_peak = jnp.max(scores, axis=3)
    exponentials = jnp.exp(scores - row_peak[..., None])
    row_sum = jnp.sum(exponentials, axis=3)
    weights = exponentials.astype(jnp.bfloat16)
    blended = jnp.einsum(
        "shqk,skhd->sqhd", weights, value_block, preferred_element_type=jnp.float32
    )
    blended = blended / jnp.transpose(row_sum, (0, 2, 1))[..., None]
    return (blended, row_peak + jnp.log(row_sum))


def slot_plan(selected, first_span, per_dev, capacity):
    own_span = first_span + lax.broadcasted_iota(jnp.int32, selected.shape, 0)
    is_live = (selected != own_span).reshape(-1)
    owner_dev = (selected // per_dev).reshape(-1)
    pair_count = owner_dev.shape[0]
    is_later = lax.broadcasted_iota(jnp.int32, (pair_count, pair_count), 0) > lax.broadcasted_iota(
        jnp.int32, (pair_count, pair_count), 1
    )
    earlier = is_later & (owner_dev[:, None] == owner_dev[None, :]) & is_live[None, :]
    slot_rank = jnp.sum(earlier.astype(jnp.int32), axis=1)
    slot_index = jnp.where(is_live, owner_dev * capacity + slot_rank, 0)
    return (slot_index, is_live, (selected % per_dev).reshape(-1))


def shards(queries, keys, values, selection, norm_gain):
    n_ctx = lax.axis_size("ctx")
    device = lax.axis_index("ctx")
    rows, width = queries.shape
    per_dev, topk_count = selection.shape
    block_rows = rows // per_dev
    heads_dev = width // HD
    slot_count = n_ctx * CAP
    group_size = math.gcd(slot_count, 4)
    query_blocks = queries.reshape(per_dev, block_rows, heads_dev, HD)
    key_blocks = keys.reshape(per_dev, block_rows, heads_dev, HD)
    value_blocks = values.reshape(per_dev, block_rows, heads_dev, HD)
    slot_index, is_live, local_block = slot_plan(selection[:, 1:], device * per_dev, per_dev, CAP)
    pair_count = slot_index.shape[0]
    pair_span = lax.broadcasted_iota(jnp.int32, (pair_count,), 0) // (topk_count - 1)
    slot_ids = lax.broadcasted_iota(jnp.int32, (slot_count, pair_count), 0)
    placed = (slot_ids == slot_index[None, :]) & is_live[None, :]
    slot_span = jnp.sum(jnp.where(placed, pair_span[None, :], 0), axis=1)
    everyone = lax.all_gather(selection, "ctx", axis=0, tiled=True)
    requests = everyone[:, 1:].reshape(n_ctx, per_dev, topk_count - 1)
    first_spans = lax.broadcasted_iota(jnp.int32, (n_ctx,), 0) * per_dev
    all_slots, all_live, all_local = jax.vmap(partial(slot_plan, per_dev=per_dev, capacity=CAP))(
        requests, first_spans
    )
    owner_devs = requests.reshape(n_ctx, -1) // per_dev
    served = all_live & (owner_devs == device)
    capacity_ids = lax.broadcasted_iota(jnp.int32, (1, CAP, 1), 1)
    matched = served[:, None, :] & (all_slots[:, None, :] == device * CAP + capacity_ids)
    send_block = jnp.sum(jnp.where(matched, all_local[:, None, :], 0), axis=2)
    key_out = key_blocks[send_block].reshape(n_ctx, CAP, block_rows, width)
    value_out = value_blocks[send_block].reshape(n_ctx, CAP, block_rows, width)
    key_in, value_in = (
        lax.all_to_all(key_out, "ctx", split_axis=0, concat_axis=0, tiled=True),
        lax.all_to_all(value_out, "ctx", split_axis=0, concat_axis=0, tiled=True),
    )

    def one_group(packed):
        group_keys, group_values, group_span = packed
        blended, log_sums = partial_state(query_blocks[group_span], group_keys, group_values, False)
        return (blended.astype(jnp.bfloat16), log_sums)

    slot_out, slot_lse = lax.map(
        one_group,
        (
            key_in.reshape(-1, group_size, block_rows, heads_dev, HD),
            value_in.reshape(-1, group_size, block_rows, heads_dev, HD),
            slot_span.reshape(-1, group_size),
        ),
    )
    slot_out = slot_out.reshape(slot_count, block_rows, heads_dev, HD)
    slot_lse = slot_lse.reshape(slot_count, heads_dev, block_rows)
    own_out, own_lse = partial_state(query_blocks, key_blocks, value_blocks, True)
    live_pairs = is_live.reshape(per_dev, topk_count - 1)
    pair_out = (
        slot_out[slot_index]
        .reshape(per_dev, topk_count - 1, block_rows, heads_dev, HD)
        .astype(jnp.float32)
    )
    pair_lse = jnp.where(
        live_pairs[:, :, None, None],
        slot_lse[slot_index].reshape(per_dev, topk_count - 1, heads_dev, block_rows),
        -1e30,
    )
    highest = jnp.maximum(own_lse, jnp.max(pair_lse, axis=1))
    own_weight = jnp.exp(own_lse - highest)
    pair_weight = jnp.where(live_pairs[:, :, None, None], jnp.exp(pair_lse - highest[:, None]), 0.0)
    numerator = jnp.transpose(own_weight, (0, 2, 1))[..., None] * own_out
    numerator = numerator + jnp.sum(
        jnp.transpose(pair_weight, (0, 1, 3, 2))[..., None] * pair_out, axis=1
    )
    denominator = own_weight + jnp.sum(pair_weight, axis=1)
    attended = (numerator / jnp.transpose(denominator, (0, 2, 1))[..., None]).reshape(rows, width)
    squares = jnp.sum(attended * attended, axis=1)
    summed = lax.psum(squares, "head")
    factor = lax.rsqrt(summed / (HEADS * HD) + 1e-06)
    return (attended * factor[:, None] * norm_gain.astype(jnp.float32)[None, :]).astype(
        jnp.bfloat16
    )


def solution(mesh):
    placed = (P("ctx", "head"), P("ctx", "head"), P("ctx", "head"), P("ctx", None), P("head"))
    return jax.shard_map(
        shards, mesh=mesh, in_specs=placed, out_specs=P("ctx", "head"), check_vma=False
    )
```

profile of v0, /device:TPU:24, one launch (start us, length us, event | category | flops | bytes accessed | tf_op | source)
XLA Modules:
  0.0 513.8 jit_solution(3790360250614226764)
XLA Ops:
  0.0 22.5 %all-gather = s32[8,4,8]{2,1,0:T(4,128)S(1)} all-gather(s32[1,4,8]{2,1,0:T(4,128)} %bitcast.130), channel_id=1, replica_groups=mesh['ctx'=8,'head'=4] {'ctx'}, dimensions={0}, use_global_device_ids=true | all-gather | bytes 1152 | tf_op jit(solution)/shard_map/all_gather | solution.py:65
  23.1 0.6 convert_reduce_fusion
  23.9 0.2 select_reduce_fusion.2
  24.3 2.2 copy.73
  26.6 4.7 gather_fusion.1
  31.3 12.6 %copy.61 = bf16[16,256,8,128]{1,3,2,0:T(8,128)(2,1)} copy(bf16[16,256,8,128]{3,2,1,0:T(8,128)(2,1)} %gather_fusion.1) | data formatting | bytes 16777216 | tf_op jit(solution)/shard_map/gather | solution.py:77
  43.8 9.1 %all-to-all-start = ((bf16[8,2,256,1024]{2,3,1,0:T(8,128)(2,1)}), bf16[8,2,256,1024]{2,3,1,0:T(8,128)(2,1)}, u32[]{:S(2)}, u32[]{:S(2)}) async-start(bf16[8,2,256,1024]{2,3,1,0:T(8,128)(2,1)} %bitcast.119), calls=%async_computation | async-start | bytes 16777216 | tf_op jit(solution)/shard_map/all_to_all | solution.py:80
  53.0 2.2 copy.72
  55.2 4.7 gather_fusion.2
  59.9 12.9 %copy.69 = bf16[16,256,8,128]{1,3,2,0:T(8,128)(2,1)} copy(bf16[16,256,8,128]{3,2,1,0:T(8,128)(2,1)} %gather_fusion.2) | data formatting | bytes 16777216 | tf_op jit(solution)/shard_map/reshape | solution.py:76
  72.8 157.5 %all-to-all-done = bf16[8,2,256,1024]{2,3,1,0:T(8,128)(2,1)} async-done(((bf16[8,2,256,1024]{2,3,1,0:T(8,128)(2,1)}), bf16[8,2,256,1024]{2,3,1,0:T(8,128)(2,1)}, u32[]{:S(2)}, u32[]{:S(2)}) %all-to-all-start) | async-done | bytes 8388640 | tf_op jit(solution)/shard_map/all_to_all | solution.py:80
  230.3 6.5 %all-to-all-start.1 = ((bf16[8,2,256,1024]{2,3,1,0:T(8,128)(2,1)}), bf16[8,2,256,1024]{2,3,1,0:T(8,128)(2,1)}, u32[]{:S(2)}, u32[]{:S(2)}) async-start(bf16[8,2,256,1024]{2,3,1,0:T(8,128)(2,1)} %bitcast.118), calls=%async_computation.1 | async-start | bytes 16777216 | tf_op jit(solution)/shard_map/all_to_all | solution.py:79
  237.2 0.2 convert_reduce_fusion.1
  237.5 0.1 select_reduce_fusion.1
  237.7 2.2 copy.71
  240.0 2.8 fusion.25
  242.8 3.4 copy-done.5
  246.2 1.4 fusion.24
  247.6 170.2 %all-to-all-done.1 = bf16[8,2,256,1024]{2,3,1,0:T(8,128)(2,1)} async-done(((bf16[8,2,256,1024]{2,3,1,0:T(8,128)(2,1)}), bf16[8,2,256,1024]{2,3,1,0:T(8,128)(2,1)}, u32[]{:S(2)}, u32[]{:S(2)}) %all-to-all-start.1) | async-done | bytes 8388640 | tf_op jit(solution)/shard_map/all_to_all | solution.py:79
  417.8 53.9 %while.12 = (s32[]{:T(128)}, bf16[4,4,256,8,128]{2,4,3,1,0:T(8,128)(2,1)}, f32[4,4,8,256]{3,2,1,0:T(8,128)S(1)}, bf16[4,4,256,8,128]{2,4,3,1,0:T(8,128)(2,1)}, s...) while((s32[]{:T(128)}, ...), condition=%wide.region_9.10_spmd, body=%wide.region_6.9_spmd.sunk | while | flops 1092609024 | bytes 54793940 | solution.py:88
  417.8 1.3 copy-done
  419.1 2.5 gather_fusion
  421.7 3.0 multiply_reduce_fusion.3
  424.7 1.6 fusion.64
  426.3 5.0 bitcast_dynamic-update-slice_fusion.4
  431.2 1.3 copy-done
  432.5 2.5 gather_fusion
  435.1 3.0 multiply_reduce_fusion.3
  438.1 1.6 fusion.64
  439.7 5.0 bitcast_dynamic-update-slice_fusion.4
  444.7 1.3 copy-done
  446.0 2.5 gather_fusion
  448.5 3.0 multiply_reduce_fusion.3
  451.5 1.6 fusion.64
  453.1 5.0 bitcast_dynamic-update-slice_fusion.4
  458.2 1.3 copy-done
  459.5 2.5 gather_fusion
  462.0 3.0 multiply_reduce_fusion.3
  465.0 1.6 fusion.64
  466.6 5.1 bitcast_dynamic-update-slice_fusion.4
  471.7 10.0 %gather_fusion.4 = bf16[28,256,8,128]{1,3,2,0:T(8,128)(2,1)} fusion(bf16[16,256,8,128]{1,3,2,0:T(8,128)(2,1)} %bitcast.24, s32[1024]{0:T(1024)S(1)} %pad_clamp_fusion.1), kind=kCustom, calls=%fused_computation.4 | custom fusion | bytes 29360240 | tf_op jit(solution)/shard_map/gather | solution.py:101
  481.7 0.6 gather_fusion.3
  482.4 0.1 fusion.44
  482.6 11.1 %fusion.22 = f32[4,256,8,128]{1,3,2,0:T(8,128)S(1)} fusion(bf16[4,7,256,8,128]{2,4,3,1,0:T(8,128)(2,1)} %bitcast.113, f32[4,7,256,8]{2,3,1,0:T(8,128)S(1)} %get-tuple-element.97), kind=kLoop, calls=%fused_computation.31 | loop fusion | flops 20971520 | bytes 19103744 | tf_op jit(solution)/shard_map/reduce_sum | solution.py:114
  493.7 3.7 multiply_reduce_fusion.1
  497.5 5.2 %copy.66 = f32[4,256,8,128]{3,2,1,0:T(8,128)} copy(f32[4,256,8,128]{1,3,2,0:T(8,128)} %get-tuple-element.101) | data formatting | bytes 8388608 | tf_op jit(solution)/shard_map/div | solution.py:118
  502.7 6.9 %psum.7 = f32[1024]{0:T(1024)S(1)} all-reduce(f32[1024]{0:T(1024)S(1)} %bitcast.131), channel_id=1, replica_groups=mesh['ctx'=8,'head'=4] {'head'}, use_global_device_ids=true, to_apply=%region_14.15 | all-reduce | flops 1024 | bytes 8192 | tf_op jit(solution)/shard_map/psum | solution.py:120
  509.6 4.3 fusion.29
  (76 shorter events, 2.0 us)
Async XLA Ops:
  26.6 4.7 copy-start.2
  43.8 186.4 %all-to-all-start = ((bf16[8,2,256,1024]{2,3,1,0:T(8,128)(2,1)}), bf16[8,2,256,1024]{2,3,1,0:T(8,128)(2,1)}, u32[]{:S(2)}, u32[]{:S(2)}) async-start(bf16[8,2,256,1024]{2,3,1,0:T(8,128)(2,1)} %bitcast.119), calls=%async_computation | async-start | bytes 16777216 | tf_op jit(solution)/shard_map/all_to_all | solution.py:80
  55.2 4.7 copy-start.4
  230.3 6.5 %copy-start.7 = (s32[4,8]{1,0:T(4,128)S(1)}, s32[4,8]{1,0:T(4,128)}, u32[]{:S(2)}) copy-start(s32[4,8]{1,0:T(4,128)} %param.10) | copy-start | bytes 388
  230.3 9.7 %copy-start.8 = (bf16[1024]{0:T(1024)(128)(2,1)S(1)}, bf16[1024]{0:T(1024)(128)(2,1)}, u32[]{:S(2)}) copy-start(bf16[1024]{0:T(1024)(128)(2,1)} %param.11) | copy-start | bytes 6148
  230.3 187.5 %all-to-all-start.1 = ((bf16[8,2,256,1024]{2,3,1,0:T(8,128)(2,1)}), bf16[8,2,256,1024]{2,3,1,0:T(8,128)(2,1)}, u32[]{:S(2)}, u32[]{:S(2)}) async-start(bf16[8,2,256,1024]{2,3,1,0:T(8,128)(2,1)} %bitcast.118), calls=%async_computation.1 | async-start | bytes 16777216 | tf_op jit(solution)/shard_map/all_to_all | solution.py:79
  242.8 3.4 copy-start.5
  417.8 1.3 copy-start
  426.2 5.0 copy-start.1
  431.2 1.3 copy-start
  439.7 5.0 copy-start.1
  444.7 1.3 copy-start
  453.1 5.0 copy-start.1
  458.1 1.3 copy-start
  466.6 5.1 copy-start.1
  482.6 11.2 %copy-start.3 = (bf16[128,8,8,128]{3,2,1,0:T(8,128)(2,1)S(1)}, bf16[128,8,8,128]{3,2,1,0:T(8,128)(2,1)}, u32[]{:S(2)}) copy-start(bf16[128,8,8,128]{3,2,1,0:T(8,128)(2,1)} %copy-done.2) | copy-start | bytes 6291460
  482.6 11.2 %copy-start.6 = (f32[4,8,256,256]{2,3,1,0:T(8,128)S(1)}, f32[4,8,256,256]{2,3,1,0:T(8,128)}, u32[]{:S(2)}) copy-start(f32[4,8,256,256]{2,3,1,0:T(8,128)} %copy-done.5) | copy-start | bytes 25165828
where the time goes:
time: 516 us; the launch traced here: 514 us
  waiting for transfers between devices  328 us (64%)
  local copies, waits for them, and re-layouts  77.4 us (15%)
  matrix products  38.5 us (7%)
  blocking collectives  29.3 us (6%)
  other arithmetic  24.8 us (5%)
  starting transfers between devices  15.7 us (3%)
    all_to_all x1, waiting for transfers between devices, shards(): lax.all_to_all(key_out, 'ctx', split_axis=0, concat_axis=0, tiled=True)  170 us
    all_to_all x1, waiting for transfers between devices, shards(): lax.all_to_all(value_out, 'ctx', split_axis=0, concat_axis=0, tiled=True)  157 us
    dot_general x5, matrix products, partial_state(): jnp.einsum('shqk,skhd->sqhd', weights, value_block, preferred_element_typ...  23.7 us
    all_gather x1, blocking collectives, shards(): everyone = lax.all_gather(selection, 'ctx', axis=0, tiled=True)  22.5 us
    gather x2, local copies, waits for them, and re-layouts, shards(): value_out = value_blocks[send_block].reshape(n_ctx, CAP, block_rows, width)  17.3 us
    dot_general x5, matrix products, partial_state(): jnp.einsum('sqhd,skhd->shqk', query_rows, key_block, preferred_element_ty...  14.8 us
    reshape x1, local copies, waits for them, and re-layouts, shards(): key_out = key_blocks[send_block].reshape(n_ctx, CAP, block_rows, width)  12.9 us
    reduce_sum x1, other arithmetic, shards(): jnp.sum(jnp.transpose(pair_weight, (0, 1, 3, 2))[..., None] * pair_out, a...  11.1 us
  transfers between devices with their start and end apart: 2, of which 2 were waited for; matrix products, arithmetic and copies ran while one was open for 5% of the time, Pallas kernels for 0%

commit v1 on v0

--- a/solution.py
+++ b/solution.py
@@ -4,11 +4,15 @@
 import jax
 import jax.numpy as jnp
 from jax import lax
+from jax.experimental import pallas as pl
+from jax.experimental.pallas import tpu as pltpu
 from jax.sharding import PartitionSpec as P
 
 HEADS = 32
 HD = 128
 CAP = 2
+LOG2E = math.log2(math.e)
+EXP_SCALE = HD ** (-0.5) * LOG2E
 
 
 def partial_state(query_rows, key_block, value_block, causal):
@@ -124,8 +128,280 @@
     )
 
 
+def attention_kernel(set_sizes, causal, per_dev, block_rows, *refs):
+    n_q, n_kv = set_sizes
+    lists = refs[0]
+    q_refs = refs[1 : 1 + n_q]
+    kv_refs = refs[1 + n_q : 1 + n_q + n_kv]
+    out_ref, lse_ref, k_scr, vt_scr, q_scr, acc_ref, top_ref, sum_ref = refs[1 + n_q + n_kv :]
+    spans = n_q * per_dev
+    last = lists.shape[1] - 1
+    for piece, ref in enumerate(q_refs):
+        for b in range(per_dev):
+            q_scr[piece * per_dev + b] = ref[b * block_rows : (b + 1) * block_rows, :]
+    for piece, ref in enumerate(kv_refs):
+        for b in range(per_dev):
+            k_scr[piece * per_dev + b] = ref[0, b * block_rows : (b + 1) * block_rows, :]
+            vt_scr[piece * per_dev + b] = ref[1, b * block_rows : (b + 1) * block_rows, :].T
+
+    def absorb(q, blocks, mask=False):
+        scores = [
+            lax.dot_general(
+                k_scr[b], q, (((1,), (1,)), ((), ())), preferred_element_type=jnp.float32
+            )
+            for b in blocks
+        ]
+        if mask:
+            key_pos = lax.broadcasted_iota(jnp.int32, scores[0].shape, 0)
+            query_pos = lax.broadcasted_iota(jnp.int32, scores[0].shape, 1)
+            scores = [jnp.where(key_pos <= query_pos, s, -1e30) for s in scores]
+        old = top_ref[...]
+        top = old
+        for s in scores:
+            top = jnp.maximum(top, jnp.max(s, axis=0, keepdims=True))
+        decay = jnp.exp2((old - top) * EXP_SCALE)
+        total = sum_ref[...] * decay
+        acc = acc_ref[...] * decay
+        for s, b in zip(scores, blocks):
+            p = jnp.exp2((s - top) * EXP_SCALE)
+            total = total + jnp.sum(p, axis=0, keepdims=True)
+            acc = acc + jnp.dot(
+                vt_scr[b], p.astype(jnp.bfloat16), preferred_element_type=jnp.float32
+            )
+        top_ref[...] = top
+        sum_ref[...] = total
+        acc_ref[...] = acc
+
+    def one_span(span, carry):
+        count = lists[span, last]
+        live = count >= 0 if causal else count > 0
+
+        @pl.when(live)
+        def _():
+            top_ref[...] = jnp.full_like(top_ref, -1e30)
+            sum_ref[...] = jnp.zeros_like(sum_ref)
+            acc_ref[...] = jnp.zeros_like(acc_ref)
+            q = q_scr[span]
+            if causal:
+                absorb(q, [span], mask=True)
+
+            def pair(i, carry):
+                absorb(q, [lists[span, 2 * i], lists[span, 2 * i + 1]])
+                return carry
+
+            lax.fori_loop(0, count // 2, pair, 0)
+
+            @pl.when(count % 2 == 1)
+            def _():
+                absorb(q, [lists[span, count - 1]])
+
+            total = sum_ref[...]
+            out_ref[span] = (acc_ref[...] / total).astype(out_ref.dtype)
+            lse_ref[pl.ds(span, 1), :] = top_ref[...] * EXP_SCALE + jnp.log(total) * LOG2E
+
+        if not causal:
+
+            @pl.when(jnp.logical_not(live))
+            def _():
+                out_ref[span] = jnp.zeros(out_ref.shape[1:], out_ref.dtype)
+                lse_ref[pl.ds(span, 1), :] = jnp.full((1, block_rows), -1e30, jnp.float32)
+
+        return carry
+
+    lax.fori_loop(0, spans, one_span, 0)
+
+
+def attention_call(lists, q_pieces, kv_pieces, causal, per_dev, block_rows):
+    n_q, n_kv = len(q_pieces), len(kv_pieces)
+    spans = n_q * per_dev
+    vmem = pl.BlockSpec(memory_space=pltpu.VMEM)
+    return pl.pallas_call(
+        partial(attention_kernel, (n_q, n_kv), causal, per_dev, block_rows),
+        out_shape=(
+            jax.ShapeDtypeStruct(
+                (spans, HD, block_rows), jnp.float32 if causal else jnp.bfloat16
+            ),
+            jax.ShapeDtypeStruct((spans, block_rows), jnp.float32),
+        ),
+        in_specs=[pl.BlockSpec(memory_space=pltpu.SMEM)] + [vmem] * (n_q + n_kv),
+        out_specs=(vmem, vmem),
+        scratch_shapes=[
+            pltpu.VMEM((n_kv * per_dev, block_rows, HD), jnp.bfloat16),
+            pltpu.VMEM((n_kv * per_dev, HD, block_rows), jnp.bfloat16),
+            pltpu.VMEM((spans, block_rows, HD), jnp.bfloat16),
+            pltpu.VMEM((HD, block_rows), jnp.float32),
+            pltpu.VMEM((1, block_rows), jnp.float32),
+            pltpu.VMEM((1, block_rows), jnp.float32),
+        ],
+        compiler_params=pltpu.CompilerParams(vmem_limit_bytes=32 * 1024 * 1024),
+        cost_estimate=pl.CostEstimate(
+            flops=32 * 4 * block_rows * block_rows * HD,
+            bytes_accessed=4 * 1024 * 1024,
+            transcendentals=32 * block_rows * block_rows,
+        ),
+        name="own_attention" if causal else "served_attention",
+    )(lists, *q_pieces, *kv_pieces)
+
+
+def merge_kernel(per_dev, valid, *refs):
+    outs, lses = refs[0:3], refs[3:6]
+    keep_ref, send_ref, squares_ref = refs[6:]
+    for span in range(2 * per_dev):
+        rows = slice(span, span + 1)
+        lse = [lses[0][rows, :]]
+        for i in (1, 2):
+            lse.append(jnp.where(valid[i - 1] > 0, lses[i][rows, :], -1e30))
+        top = jnp.maximum(jnp.maximum(lse[0], lse[1]), lse[2])
+        weight = [jnp.exp2(v - top) for v in lse]
+        mixed = weight[0] * outs[0][span]
+        for i in (1, 2):
+            mixed = mixed + weight[i] * outs[i][span].astype(jnp.float32)
+        mixed = mixed / (weight[0] + weight[1] + weight[2])
+        squares_ref[rows, :] = jnp.sum(mixed * mixed, axis=0, keepdims=True)
+        target = keep_ref if span < per_dev else send_ref
+        block_rows = mixed.shape[1]
+        start = (span % per_dev) * block_rows
+        target[start : start + block_rows, :] = mixed.T.astype(target.dtype)
+
+
+def merge_call(valid, own, near, far, per_dev, block_rows):
+    vmem = pl.BlockSpec(memory_space=pltpu.VMEM)
+    half = jax.ShapeDtypeStruct((per_dev * block_rows, HD), jnp.bfloat16)
+
+    def kernel(valid_ref, *refs):
+        merge_kernel(per_dev, (valid_ref[0], valid_ref[1]), *refs)
+
+    return pl.pallas_call(
+        kernel,
+        out_shape=(half, half, jax.ShapeDtypeStruct((2 * per_dev, block_rows), jnp.float32)),
+        in_specs=[pl.BlockSpec(memory_space=pltpu.SMEM)] + [vmem] * 6,
+        out_specs=(vmem, vmem, vmem),
+        compiler_params=pltpu.CompilerParams(vmem_limit_bytes=32 * 1024 * 1024),
+        name="merge",
+    )(valid, own[0], near[0], far[0], own[1], near[1], far[1])
+
+
+def finish_kernel(per_dev, half, place_ref, *refs):
+    pieces = refs[: 2 * half]
+    squares_ref, gain_ref, out_ref = refs[2 * half :]
+    block_rows = squares_ref.shape[1]
+    factor = lax.rsqrt(squares_ref[...] / (HEADS * HD) + 1e-06)
+    for b in range(per_dev):
+        column = jnp.broadcast_to(factor[b : b + 1, :], (HD, block_rows)).T
+        rows = slice(b * block_rows, (b + 1) * block_rows)
+        for side in range(2):
+            for c in range(half):
+                start = pl.multiple_of((place_ref[side] * half + c) * HD, HD)
+                piece = pieces[side * half + c][rows, :].astype(jnp.float32)
+                gain = gain_ref[:, pl.ds(start, HD)].astype(jnp.float32)
+                out_ref[rows, pl.ds(start, HD)] = (piece * column * gain).astype(out_ref.dtype)
+
+
+def finish_call(place, kept, returned, squares, gain, per_dev):
+    vmem = pl.BlockSpec(memory_space=pltpu.VMEM)
+    rows = kept[0].shape[0]
+    width = gain.shape[0]
+    return pl.pallas_call(
+        partial(finish_kernel, per_dev, len(kept)),
+        out_shape=jax.ShapeDtypeStruct((rows, width), jnp.bfloat16),
+        in_specs=[pl.BlockSpec(memory_space=pltpu.SMEM)] + [vmem] * (2 * len(kept) + 2),
+        out_specs=vmem,
+        compiler_params=pltpu.CompilerParams(vmem_limit_bytes=32 * 1024 * 1024),
+        name="finish",
+    )(place, *kept, *returned, squares, gain.reshape(1, width))
+
+
+def slot_lists(rows, span_ids, level, x, per_dev, allowed_level, include_self):
+    owner = rows // per_dev
+    block_level, block_x = owner // 2, owner % 2
+    live = (rows != span_ids[:, None]) & allowed_level(block_level)
+    slot = jnp.where(block_level == level, 0, 2 * per_dev)
+    slot = slot + jnp.where(block_x == x, 0, per_dev) + rows % per_dev
+    count = rows.shape[1]
+    t = jnp.arange(count)
+    rank = jnp.sum((t[None, :, None] > t[None, None, :]) & live[:, None, :], axis=2)
+    hit = live[:, :, None] & (rank[:, :, None] == t[None, None, :])
+    packed = jnp.sum(jnp.where(hit, slot[:, :, None], 0), axis=1)
+    total = jnp.sum(live.astype(jnp.int32), axis=1, keepdims=True)
+    return jnp.concatenate([packed, total], axis=1).astype(jnp.int32)
+
+
+def level_shards(queries, keys, values, selection, norm_gain):
+    device = lax.axis_index("ctx")
+    level, x = device // 2, device % 2
+    rows, width = queries.shape
+    per_dev, topk = selection.shape
+    block_rows = rows // per_dev
+    half = width // HD // 2
+
+    def to(array, pairs):
+        return lax.ppermute(array, "ctx", pairs)
+
+    swap = [(d, d ^ 1) for d in range(8)]
+    lift = [(0, 2), (1, 3)]
+    near_down, far_down = [(4, 2), (5, 3), (6, 4), (7, 5)], [(6, 2), (7, 3)]
+    near_up, far_up = [(2, 4), (3, 5), (4, 6), (5, 7)], [(2, 6), (3, 7)]
+
+    everyone = lax.all_gather(selection, "ctx", axis=0, tiled=True)
+
+    def level_rows(at):
+        at = jnp.clip(at, 0, 3)
+        first = jnp.stack([(at * 2 + x) * per_dev, (at * 2 + 1 - x) * per_dev])
+        ids = (first[:, None] + jnp.arange(per_dev)[None, :]).reshape(-1)
+        return everyone[ids, 1:], ids
+
+    own_rows, own_ids = level_rows(level)
+    own_lists = slot_lists(
+        own_rows, own_ids, level, x, per_dev,
+        lambda b: (b == level) | ((level == 1) & (b == 0)), True,
+    )
+    near_rows, near_ids = level_rows(level + 1)
+    near_lists = slot_lists(
+        near_rows, near_ids, level, x, per_dev,
+        lambda b: ((level == 2) & (b == 2)) | ((level == 1) & (b <= 1)), False,
+    )
+    far_rows, far_ids = level_rows(level + 2)
+    far_lists = slot_lists(
+        far_rows, far_ids, level, x, per_dev, lambda b: (level == 1) & (b <= 1), False
+    )
+    served_lists = jnp.concatenate([near_lists, far_lists], axis=0)
+    valid = jnp.stack([level >= 2, level >= 3]).astype(jnp.int32)
+    place = jnp.stack([x, 1 - x]).astype(jnp.int32)
+
+    def columns(array, head):
+        return lax.dynamic_slice(array, (0, head * HD), (rows, HD))
+
+    kept, returned, squares = [], [], []
+    for c in range(half):
+        here, there = x * half + c, (1 - x) * half + c
+        kv_keep = jnp.stack([columns(keys, here), columns(values, here)])
+        kv_swap = to(jnp.stack([columns(keys, there), columns(values, there)]), swap)
+        q_keep = columns(queries, here)
+        q_swap = to(columns(queries, there), swap)
+        low = [to(kv_keep, lift), to(kv_swap, lift)]
+        near_q = [to(q_keep, near_down), to(q_swap, near_down)]
+        far_q = [to(q_keep, far_down), to(q_swap, far_down)]
+        kv = [kv_keep, kv_swap] + low
+        served, served_lse = attention_call(
+            served_lists, near_q + far_q, kv, False, per_dev, block_rows
+        )
+        spans = 2 * per_dev
+        near = (to(served[:spans], near_up), to(served_lse[:spans], near_up))
+        far = (to(served[spans:], far_up), to(served_lse[spans:], far_up))
+        own = attention_call(own_lists, [q_keep, q_swap], kv, True, per_dev, block_rows)
+        keep, send, square = merge_call(valid, own, near, far, per_dev, block_rows)
+        kept.append(keep)
+        returned.append(to(send, swap))
+        squares.append(square)
+    square = sum(squares[1:], squares[0])
+    square = square[:per_dev] + to(square[per_dev:], swap)
+    square = lax.psum(square, "head")
+    return finish_call(place, kept, returned, square, norm_gain, per_dev)
+
+
 def solution(mesh):
     placed = (P("ctx", "head"), P("ctx", "head"), P("ctx", "head"), P("ctx", None), P("head"))
+    body = level_shards if mesh.shape["ctx"] == 8 else shards
     return jax.shard_map(
-        shards, mesh=mesh, in_specs=placed, out_specs=P("ctx", "head"), check_vma=False
-    )
+        body, mesh=mesh, in_specs=placed, out_specs=P("ctx", "head"), check_vma=False
+    )

time: 516 us -> 325 us (0.63)
  the two profiles are of different devices: /device:TPU:24 before, /device:TPU:8 now
where the time goes in v1:
time: 325 us; the launch traced here: 324 us
  Pallas kernels  92.5 us (28%)
  starting transfers between devices  85.3 us (26%)
  local copies, waits for them, and re-layouts  54.3 us (17%)
  blocking collectives  48.4 us (15%)
  waiting for transfers between devices  33.1 us (10%)
  other arithmetic  9.34 us (3%)
    pallas_call x8, Pallas kernels, attention_call(): pl.pallas_call(partial(attention_kernel, (n_q, n_kv), causal, per_dev, bl...  85.5 us
    ppermute x53, starting transfers between devices, to(): return lax.ppermute(array, 'ctx', pairs)  85.3 us
    gather x96, local copies, waits for them, and re-layouts  47.1 us
    all_gather x1, blocking collectives, level_shards(): everyone = lax.all_gather(selection, 'ctx', axis=0, tiled=True)  42.4 us
    ppermute x53, waiting for transfers between devices, to(): return lax.ppermute(array, 'ctx', pairs)  33.1 us
  transfers between devices with their start and end apart: 53, of which 10 were waited for; matrix products, arithmetic and copies ran while one was open for 19% of the time, Pallas kernels for 27%

profile of v1, /device:TPU:8, one launch (start us, length us, event | category | flops | bytes accessed | tf_op | source)
XLA Modules:
  0.0 324.0 jit_solution(13988428787996429349)
XLA Ops:
  0.0 2.7 constant_dynamic-slice_fusion.3
  2.7 1.4 collective-permute-start.40
  5.5 2.2 dynamic-slice_bitcast_fusion
  8.6 1.5 collective-permute-start.37
  10.6 1.5 collective-permute-start.24
  13.1 42.4 %all-gather = s32[8,4,8]{2,1,0:T(4,128)S(1)} all-gather(s32[1,4,8]{2,1,0:T(4,128)S(1)} %bitcast.66), channel_id=1, replica_groups=mesh['ctx'=8,'head'=4] {'ctx'}, dimensions={0}, use_global_device_ids=true | all-gather | bytes 1152 | tf_op jit(solution)/shard_map/all_gather | solution.py:345
  55.5 15.7 %while.4 = (s32[]{:T(128)}, s32[32,8]{0,1:T(8,128)S(1)}, s32[8,2]{0,1:T(2,128)S(1)}, s32[8,7]{0,1:T(8,128)S(1)}, s32[]{:T(128)}, /*index=5*/s32[]{:T(128)}) while((s32[]{:T(128)}, s32[32,8]{0,1:T(8,128)S(1)}, s32[8,2]{0,1:T(2,128)S(1)}, s32[8,7]{0,1:T(8,128)S(1)}, s32[]{:T(128)}, /*index=5*/s32[]{:T(128)}) %tuple.110), condition=%wide.while_cond.1, body=%wide.while_body.1.sunk | while | flops 2 | bytes 225 | solution.py:351
  71.2 15.8 %while.5 = (s32[]{:T(128)}, s32[32,8]{0,1:T(8,128)S(1)}, s32[8,2]{0,1:T(2,128)S(1)}, s32[8,7]{0,1:T(8,128)S(1)}, s32[]{:T(128)}, /*index=5*/s32[]{:T(128)}) while((s32[]{:T(128)}, s32[32,8]{0,1:T(8,128)S(1)}, s32[8,2]{0,1:T(2,128)S(1)}, s32[8,7]{0,1:T(8,128)S(1)}, s32[]{:T(128)}, /*index=5*/s32[]{:T(128)}) %tuple.113), condition=%wide.while_cond.2, body=%wide.while_body.2.sunk | while | flops 2 | bytes 225 | solution.py:351
  87.1 15.8 %while.3 = (s32[]{:T(128)}, s32[32,8]{0,1:T(8,128)S(1)}, s32[8,2]{0,1:T(2,128)S(1)}, s32[8,7]{0,1:T(8,128)S(1)}, s32[]{:T(128)}, /*index=5*/s32[]{:T(128)}) while((s32[]{:T(128)}, s32[32,8]{0,1:T(8,128)S(1)}, s32[8,2]{0,1:T(2,128)S(1)}, s32[8,7]{0,1:T(8,128)S(1)}, s32[]{:T(128)}, /*index=5*/s32[]{:T(128)}) %tuple.114), condition=%wide.while_cond, body=%wide.while_body.sunk | while | flops 2 | bytes 225 | solution.py:351
  106.9 1.3 collective-permute-start.28
  110.3 1.6 collective-permute-start.12
  113.3 3.1 collective-permute-done.28.refs_1_
  116.4 1.7 collective-permute-start.25
  118.2 1.5 collective-permute-done.30.refs_3_
  123.3 1.3 collective-permute-start.39
  124.7 1.9 pad_maximum_fusion.1
  126.6 5.0 %collective-permute-done.16.refs_1_ = bf16[1024,128]{1,0:T(8,128)(2,1)} collective-permute-done((bf16[1024,128]{1,0:T(8,128)(2,1)S(1)}, bf16[1024,128]{1,0:T(8,128)(2,1)}, u32[]{:S(2)}, u32[]{:S(2)}) %collective-permute-start.16) | collective-permute-done | bytes 262176 | tf_op jit(solution)/shard_map/ppermute | solution.py:338
  138.2 3.9 %collective-permute-done.43.refs_4_ = bf16[1024,128]{1,0:T(8,128)(2,1)} collective-permute-done((bf16[1024,128]{1,0:T(8,128)(2,1)}, bf16[1024,128]{1,0:T(8,128)(2,1)}, u32[]{:S(2)}, u32[]{:S(2)}) %collective-permute-start.43) | collective-permute-done | bytes 262176 | tf_op jit(solution)/shard_map/ppermute | solution.py:338
  143.4 1.3 collective-permute-start.31
  144.7 12.4 %served_attention.7 = (bf16[16,128,256]{2,1,0:T(8,128)(2,1)S(1)}, f32[16,256]{1,0:T(8,128)S(1)}) custom-call(s32[16,8]{1,0:T(8,128)S(1)} %add_add_fusion.refs_0_, bf16[1024,128]{1,0:T(8,128)(2,1)} %collective-permute-done.40.refs_1_, bf16[1024,128]{1,0:T(8,128)(2,1)} %collective-permute-done.41.refs_2_, bf16[1024,128]{1,0:T(8,128)(2,1)} %collective-permute-done.42.refs_3_, ...), custom_call_target="tpu_custom_call" | custom-call | flops 1073741824 | bytes 4194304 | tf_op jit(solution)/shard_map/served_attention/pallas_call | solution.py:218
  159.7 1.7 collective-permute-start.1
  163.8 12.0 %served_attention.6 = (bf16[16,128,256]{2,1,0:T(8,128)(2,1)S(1)}, f32[16,256]{1,0:T(8,128)S(1)}) custom-call(s32[16,8]{1,0:T(8,128)S(1)} %add_add_fusion.refs_0_, bf16[1024,128]{1,0:T(8,128)(2,1)} %collective-permute-done.28.refs_1_, bf16[1024,128]{1,0:T(8,128)(2,1)S(1)} %collective-permute-done.29.refs_2_, bf16[1024,128]{1,0:T(8,128)(2,1)S(1)} %copy-done.1, ...), custom_call_target="tpu_custom_call" | custom-call | flops 1073741824 | bytes 4194304 | tf_op jit(solution)/shard_map/served_attention/pallas_call | solution.py:218
  179.8 10.2 %collective-permute-done.17.refs_2_ = bf16[1024,128]{1,0:T(8,128)(2,1)S(1)} collective-permute-done((bf16[1024,128]{1,0:T(8,128)(2,1)}, bf16[1024,128]{1,0:T(8,128)(2,1)S(1)}, u32[]{:S(2)}, u32[]{:S(2)}) %collective-permute-start.17) | collective-permute-done | bytes 262176 | tf_op jit(solution)/shard_map/ppermute | solution.py:338
  195.3 11.8 %served_attention.5 = (bf16[16,128,256]{2,1,0:T(8,128)(2,1)S(1)}, f32[16,256]{1,0:T(8,128)S(1)}) custom-call(s32[16,8]{1,0:T(8,128)S(1)} %add_add_fusion.refs_0_, bf16[1024,128]{1,0:T(8,128)(2,1)} %collective-permute-done.16.refs_1_, bf16[1024,128]{1,0:T(8,128)(2,1)S(1)} %collective-permute-done.17.refs_2_, ...), custom_call_target="tpu_custom_call" | custom-call | flops 1073741824 | bytes 4194304 | tf_op jit(solution)/shard_map/served_attention/pallas_call | solution.py:218
  208.5 1.3 collective-permute-start.44
  209.9 5.5 %collective-permute-start.45 = (bf16[8,128,256]{2,1,0:T(8,128)(2,1)S(1)}, bf16[8,128,256]{2,1,0:T(8,128)(2,1)S(1)}, u32[]{:S(2)}, u32[]{:S(2)}) collective-permute-start(bf16[8,128,256]{2,1,0:T(8,128)(2,1)S(1)} %get-tuple-element.184), channel_id=1, source_target_pairs={{8,24},{12,28},{9,25},{13,29},{10,26},{14,30},{11,27},{15,31}} | collective-permute-start | bytes 1572872 | tf_op jit(solution)/shard_map/ppermute | solution.py:338
  215.4 1.8 collective-permute-start.46
  218.5 1.3 collective-permute-start.32
  219.9 3.5 %collective-permute-done.46.refs_4_ = f32[8,256]{1,0:T(8,128)S(1)} collective-permute-done((f32[8,256]{1,0:T(8,128)S(1)}, f32[8,256]{1,0:T(8,128)S(1)}, u32[]{:S(2)}, u32[]{:S(2)}) %collective-permute-start.46) | collective-permute-done | bytes 8224 | tf_op jit(solution)/shard_map/ppermute | solution.py:338
  223.4 6.1 %collective-permute-start.34 = (f32[8,256]{1,0:T(8,128)S(1)}, f32[8,256]{1,0:T(8,128)S(1)}, u32[]{:S(2)}, u32[]{:S(2)}) collective-permute-start(f32[8,256]{1,0:T(8,128)S(1)} %get-tuple-element.195), channel_id=1, source_target_pairs={{8,16},{12,20},{16,24},{20,28},{9,17},{13,21},{17,25},{21,29},{10,... | collective-permute-start | bytes 24584 | tf_op jit(solution)/shard_map/ppermute | solution.py:338
  229.6 3.2 collective-permute-start.35
  232.8 11.5 %served_attention.4 = (bf16[16,128,256]{2,1,0:T(8,128)(2,1)S(1)}, f32[16,256]{1,0:T(8,128)S(1)}) custom-call(s32[16,8]{1,0:T(8,128)S(1)} %add_add_fusion.refs_0_, bf16[1024,128]{1,0:T(8,128)(2,1)S(1)} %collective-permute-done.4.refs_1_, bf16[1024,128]{1,0:T(8,128)(2,1)S(1)} %collective-permute-done.5.refs_2_, ...), custom_call_target="tpu_custom_call" | custom-call | flops 1073741824 | bytes 4194304 | tf_op jit(solution)/shard_map/served_attention/pallas_call | solution.py:218
  247.0 2.4 collective-permute-start.33
  249.4 2.8 collective-permute-start.20
  252.2 9.8 %own_attention.7 = (f32[8,128,256]{2,1,0:T(8,128)S(1)}, f32[8,256]{1,0:T(8,128)S(1)}) custom-call(s32[8,8]{1,0:T(8,128)S(1)} %pad_add_fusion.refs_0_, bf16[1024,128]{1,0:T(8,128)(2,1)S(1)} %get-tuple-element.183.refs_1_, bf16[1024,128]{1,0:T(8,128)(2,1)} %collective-permute-done.36.refs_2_, bf16[2,1024,128]{2,1,0:T(8,128)(2,1)S(1)} %pad_maximum_fusion.6.refs_3_.refs_5_, ...), custom_call_target="tpu_custom_call" | custom-call | flops 1073741824 | bytes 4194304 | tf_op jit(solution)/shard_map/own_attention/pallas_call | solution.py:218
  262.0 1.3 collective-permute-start.21
  263.4 1.3 collective-permute-start.8
  264.7 1.3 collective-permute-start.9
  266.0 9.5 %own_attention.6 = (f32[8,128,256]{2,1,0:T(8,128)S(1)}, f32[8,256]{1,0:T(8,128)S(1)}) custom-call(s32[8,8]{1,0:T(8,128)S(1)} %pad_add_fusion.refs_0_, bf16[1024,128]{1,0:T(8,128)(2,1)S(1)} %get-tuple-element.178.refs_1_, bf16[1024,128]{1,0:T(8,128)(2,1)S(1)} %collective-permute-done.24.refs_2_, bf16[2,1024,128]{2,1,0:T(8,128)(2,1)S(1)} %pad_maximum_fusion.4.refs_3_.refs_5_, ...), custom_call_target="tpu_custom_call" | custom-call | flops 1073741824 | bytes 4194304 | tf_op jit(solution)/shard_map/own_attention/pallas_call | solution.py:218
  275.6 9.4 %own_attention.5 = (f32[8,128,256]{2,1,0:T(8,128)S(1)}, f32[8,256]{1,0:T(8,128)S(1)}) custom-call(s32[8,8]{1,0:T(8,128)S(1)} %pad_add_fusion.refs_0_, bf16[1024,128]{1,0:T(8,128)(2,1)S(1)} %get-tuple-element.180.refs_1_, bf16[1024,128]{1,0:T(8,128)(2,1)} %collective-permute-done.12.refs_2_, bf16[2,1024,128]{2,1,0:T(8,128)(2,1)S(1)} %pad_maximum_fusion.2.refs_3_.refs_5_, ...), custom_call_target="tpu_custom_call" | custom-call | flops 1073741824 | bytes 4194304 | tf_op jit(solution)/shard_map/own_attention/pallas_call | solution.py:218
  287.7 9.1 %own_attention.4 = (f32[8,128,256]{2,1,0:T(8,128)S(1)}, f32[8,256]{1,0:T(8,128)S(1)}) custom-call(s32[8,8]{1,0:T(8,128)S(1)} %pad_add_fusion.refs_0_, bf16[1024,128]{1,0:T(8,128)(2,1)S(1)} %get-tuple-element.182.refs_1_, bf16[1024,128]{1,0:T(8,128)(2,1)S(1)} %collective-permute-done.refs_2_, bf16[2,1024,128]{2,1,0:T(8,128)(2,1)S(1)} %pad_maximum_fusion.refs_3_.refs_5_, ...), custom_call_target="tpu_custom_call" | custom-call | flops 1073741824 | bytes 4194304 | tf_op jit(solution)/shard_map/own_attention/pallas_call | solution.py:218
  301.0 5.3 %collective-permute-start.52 = (f32[4,256]{1,0:T(4,128)S(1)}, f32[4,256]{1,0:T(4,128)S(1)}, u32[]{:S(2)}, u32[]{:S(2)}) collective-permute-start(f32[4,256]{1,0:T(4,128)S(1)} %slice.103), channel_id=1, source_target_pairs={{0,4},{4,0},{8,12},{12,8},{16,20},{20,16},{24,28},{28,24},{1,5},{5... | collective-permute-start | bytes 12296 | tf_op jit(solution)/shard_map/ppermute | solution.py:338
  306.4 1.9 collective-permute-start.50
  308.5 1.9 collective-permute-start.48
  310.5 6.0 %psum.7.refs_8_ = f32[4,256]{1,0:T(4,128)S(1)} all-reduce(f32[4,256]{1,0:T(4,128)S(1)} %slice_add_fusion), channel_id=1, replica_groups=mesh['ctx'=8,'head'=4] {'head'}, use_global_device_ids=true, to_apply=%region_9.10 | all-reduce | flops 1024 | bytes 8192 | tf_op jit(solution)/shard_map/psum | solution.py:398
  316.5 1.9 collective-permute-done.49.refs_5_
  318.3 2.8 collective-permute-done.48.refs_4_
  321.2 2.8 finish.1
  (253 shorter events, 96.5 us)
Async XLA Ops:
  2.7 105.8 %collective-permute-start.40 = (bf16[1024,128]{1,0:T(8,128)(2,1)S(1)}, bf16[1024,128]{1,0:T(8,128)(2,1)}, u32[]{:S(2)}, u32[]{:S(2)}) collective-permute-start(bf16[1024,128]{1,0:T(8,128)(2,1)S(1)} %get-tuple-element.183.refs_1_), channel_id=1, source_target_pairs={{16,8},{20,12},{24,16},{28,20},{17,9},{21,13},{25,17},{29,21},{18,... | collective-permute-start | bytes 786440 | tf_op jit(solution)/shard_map/ppermute | solution.py:338
  4.2 106.1 %collective-permute-start.42 = (bf16[1024,128]{1,0:T(8,128)(2,1)S(1)}, bf16[1024,128]{1,0:T(8,128)(2,1)}, u32[]{:S(2)}, u32[]{:S(2)}) collective-permute-start(bf16[1024,128]{1,0:T(8,128)(2,1)S(1)} %get-tuple-element.183.refs_1_), channel_id=1, source_target_pairs={{24,8},{28,12},{25,9},{29,13},{26,10},{30,14},{27,11},{31,15}} | collective-permute-start | bytes 786440 | tf_op jit(solution)/shard_map/ppermute | solution.py:338
  8.6 114.7 %collective-permute-start.37 = (bf16[2,1024,128]{2,1,0:T(8,128)(2,1)}, bf16[2,1024,128]{2,1,0:T(8,128)(2,1)S(1)}, u32[]{:S(2)}, u32[]{:S(2)}) collective-permute-start(bf16[2,1024,128]{2,1,0:T(8,128)(2,1)} %pad_maximum_fusion.7), channel_id=1, source_target_pairs={{0,4},{4,0},{8,12},{12,8},{16,20},{20,16},{24,28},{28,24},{1,5},{5... | collective-permute-start | bytes 1572872 | tf_op jit(solution)/shard_map/ppermute | solution.py:338
  10.1 96.9 %collective-permute-start.36 = (bf16[1024,128]{1,0:T(8,128)(2,1)}, bf16[1024,128]{1,0:T(8,128)(2,1)}, u32[]{:S(2)}, u32[]{:S(2)}) collective-permute-start(bf16[1024,128]{1,0:T(8,128)(2,1)} %get-tuple-element.176), channel_id=1, source_target_pairs={{0,4},{4,0},{8,12},{12,8},{16,20},{20,16},{24,28},{28,24},{1,5},{5... | collective-permute-start | bytes 786440 | tf_op jit(solution)/shard_map/ppermute | solution.py:338
  10.6 101.4 %collective-permute-start.24 = (bf16[1024,128]{1,0:T(8,128)(2,1)}, bf16[1024,128]{1,0:T(8,128)(2,1)S(1)}, u32[]{:S(2)}, u32[]{:S(2)}) collective-permute-start(bf16[1024,128]{1,0:T(8,128)(2,1)} %get-tuple-element.177), channel_id=1, source_target_pairs={{0,4},{4,0},{8,12},{12,8},{16,20},{20,16},{24,28},{28,24},{1,5},{5... | collective-permute-start | bytes 786440 | tf_op jit(solution)/shard_map/ppermute | solution.py:338
  108.5 11.2 %collective-permute-start.30 = (bf16[1024,128]{1,0:T(8,128)(2,1)S(1)}, bf16[1024,128]{1,0:T(8,128)(2,1)S(1)}, u32[]{:S(2)}, u32[]{:S(2)}) collective-permute-start(bf16[1024,128]{1,0:T(8,128)(2,1)S(1)} %get-tuple-element.178.refs_1_), channel_id=1, source_target_pairs={{24,8},{28,12},{25,9},{29,13},{26,10},{30,14},{27,11},{31,15}} | collective-permute-start | bytes 786440 | tf_op jit(solution)/shard_map/ppermute | solution.py:338
  110.3 11.7 %collective-permute-start.12 = (bf16[1024,128]{1,0:T(8,128)(2,1)}, bf16[1024,128]{1,0:T(8,128)(2,1)}, u32[]{:S(2)}, u32[]{:S(2)}) collective-permute-start(bf16[1024,128]{1,0:T(8,128)(2,1)} %get-tuple-element.179), channel_id=1, source_target_pairs={{0,4},{4,0},{8,12},{12,8},{16,20},{20,16},{24,28},{28,24},{1,5},{5... | collective-permute-start | bytes 786440 | tf_op jit(solution)/shard_map/ppermute | solution.py:338
  112.0 21.0 %collective-permute-start.38 = (bf16[2,1024,128]{2,1,0:T(8,128)(2,1)S(1)}, bf16[2,1024,128]{2,1,0:T(8,128)(2,1)}, u32[]{:S(2)}, u32[]{:S(2)}) collective-permute-start(bf16[2,1024,128]{2,1,0:T(8,128)(2,1)S(1)} %pad_maximum_fusion.6.refs_3_.refs_5_), channel_id=1, source_target_pairs={{0,8},{4,12},{1,9},{5,13},{2,10},{6,14},{3,11},{7,15}} | collective-permute-start | bytes 1572872 | tf_op jit(solution)/shard_map/ppermute | solution.py:338
  116.4 19.4 %collective-permute-start.25 = (bf16[2,1024,128]{2,1,0:T(8,128)(2,1)}, bf16[2,1024,128]{2,1,0:T(8,128)(2,1)}, u32[]{:S(2)}, u32[]{:S(2)}) collective-permute-start(bf16[2,1024,128]{2,1,0:T(8,128)(2,1)} %pad_maximum_fusion.5), channel_id=1, source_target_pairs={{0,4},{4,0},{8,12},{12,8},{16,20},{20,16},{24,28},{28,24},{1,5},{5... | collective-permute-start | bytes 1572872 | tf_op jit(solution)/shard_map/ppermute | solution.py:338
  120.4 11.2 %collective-permute-start.16 = (bf16[1024,128]{1,0:T(8,128)(2,1)S(1)}, bf16[1024,128]{1,0:T(8,128)(2,1)}, u32[]{:S(2)}, u32[]{:S(2)}) collective-permute-start(bf16[1024,128]{1,0:T(8,128)(2,1)S(1)} %get-tuple-element.180.refs_1_), channel_id=1, source_target_pairs={{16,8},{20,12},{24,16},{28,20},{17,9},{21,13},{25,17},{29,21},{18,... | collective-permute-start | bytes 786440 | tf_op jit(solution)/shard_map/ppermute | solution.py:338
  122.0 12.6 %collective-permute-start.41 = (bf16[1024,128]{1,0:T(8,128)(2,1)}, bf16[1024,128]{1,0:T(8,128)(2,1)}, u32[]{:S(2)}, u32[]{:S(2)}) collective-permute-start(bf16[1024,128]{1,0:T(8,128)(2,1)} %collective-permute-done.36.refs_2_), channel_id=1, source_target_pairs={{16,8},{20,12},{24,16},{28,20},{17,9},{21,13},{25,17},{29,21},{18,... | collective-permute-start | bytes 786440 | tf_op jit(solution)/shard_map/ppermute | solution.py:338
  123.3 20.1 %collective-permute-start.39 = (bf16[2,1024,128]{2,1,0:T(8,128)(2,1)S(1)}, bf16[2,1024,128]{2,1,0:T(8,128)(2,1)}, u32[]{:S(2)}, u32[]{:S(2)}) collective-permute-start(bf16[2,1024,128]{2,1,0:T(8,128)(2,1)S(1)} %collective-permute-done.37.refs_4_.refs_6_), channel_id=1, source_target_pairs={{0,8},{4,12},{1,9},{5,13},{2,10},{6,14},{3,11},{7,15}} | collective-permute-start | bytes 1572872 | tf_op jit(solution)/shard_map/ppermute | solution.py:338
  131.6 10.5 %collective-permute-start.43 = (bf16[1024,128]{1,0:T(8,128)(2,1)}, bf16[1024,128]{1,0:T(8,128)(2,1)}, u32[]{:S(2)}, u32[]{:S(2)}) collective-permute-start(bf16[1024,128]{1,0:T(8,128)(2,1)} %collective-permute-done.36.refs_2_), channel_id=1, source_target_pairs={{24,8},{28,12},{25,9},{29,13},{26,10},{30,14},{27,11},{31,15}} | collective-permute-start | bytes 786440 | tf_op jit(solution)/shard_map/ppermute | solution.py:338
  133.0 24.1 %collective-permute-start.26 = (bf16[2,1024,128]{2,1,0:T(8,128)(2,1)S(1)}, bf16[2,1024,128]{2,1,0:T(8,128)(2,1)S(1)}, u32[]{:S(2)}, u32[]{:S(2)}) collective-permute-start(bf16[2,1024,128]{2,1,0:T(8,128)(2,1)S(1)} %pad_maximum_fusion.4.refs_3_.refs_5_), channel_id=1, source_target_pairs={{0,8},{4,12},{1,9},{5,13},{2,10},{6,14},{3,11},{7,15}} | collective-permute-start | bytes 1572872 | tf_op jit(solution)/shard_map/ppermute | solution.py:338
  134.6 26.9 %collective-permute-start.13 = (bf16[2,1024,128]{2,1,0:T(8,128)(2,1)}, bf16[2,1024,128]{2,1,0:T(8,128)(2,1)S(1)}, u32[]{:S(2)}, u32[]{:S(2)}) collective-permute-start(bf16[2,1024,128]{2,1,0:T(8,128)(2,1)} %pad_maximum_fusion.3), channel_id=1, source_target_pairs={{0,4},{4,0},{8,12},{12,8},{16,20},{20,16},{24,28},{28,24},{1,5},{5... | collective-permute-start | bytes 1572872 | tf_op jit(solution)/shard_map/ppermute | solution.py:338
  135.8 26.8 %collective-permute-start.27 = (bf16[2,1024,128]{2,1,0:T(8,128)(2,1)}, bf16[2,1024,128]{2,1,0:T(8,128)(2,1)S(1)}, u32[]{:S(2)}, u32[]{:S(2)}) collective-permute-start(bf16[2,1024,128]{2,1,0:T(8,128)(2,1)} %collective-permute-done.25.refs_4_.refs_6_), channel_id=1, source_target_pairs={{0,8},{4,12},{1,9},{5,13},{2,10},{6,14},{3,11},{7,15}} | collective-permute-start | bytes 1572872 | tf_op jit(solution)/shard_map/ppermute | solution.py:338
  142.1 16.3 %collective-permute-start.29 = (bf16[1024,128]{1,0:T(8,128)(2,1)S(1)}, bf16[1024,128]{1,0:T(8,128)(2,1)S(1)}, u32[]{:S(2)}, u32[]{:S(2)}) collective-permute-start(bf16[1024,128]{1,0:T(8,128)(2,1)S(1)} %collective-permute-done.24.refs_2_), channel_id=1, source_target_pairs={{16,8},{20,12},{24,16},{28,20},{17,9},{21,13},{25,17},{29,21},{18,... | collective-permute-start | bytes 786440 | tf_op jit(solution)/shard_map/ppermute | solution.py:338
  143.4 16.3 %collective-permute-start.31 = (bf16[1024,128]{1,0:T(8,128)(2,1)S(1)}, bf16[1024,128]{1,0:T(8,128)(2,1)S(1)}, u32[]{:S(2)}, u32[]{:S(2)}) collective-permute-start(bf16[1024,128]{1,0:T(8,128)(2,1)S(1)} %collective-permute-done.24.refs_2_), channel_id=1, source_target_pairs={{24,8},{28,12},{25,9},{29,13},{26,10},{30,14},{27,11},{31,15}} | collective-permute-start | bytes 786440 | tf_op jit(solution)/shard_map/ppermute | solution.py:338
  157.1 18.7 %collective-permute-start.18 = (bf16[1024,128]{1,0:T(8,128)(2,1)S(1)}, bf16[1024,128]{1,0:T(8,128)(2,1)S(1)}, u32[]{:S(2)}, u32[]{:S(2)}) collective-permute-start(bf16[1024,128]{1,0:T(8,128)(2,1)S(1)} %get-tuple-element.180.refs_1_), channel_id=1, source_target_pairs={{24,8},{28,12},{25,9},{29,13},{26,10},{30,14},{27,11},{31,15}} | collective-permute-start | bytes 786440 | tf_op jit(solution)/shard_map/ppermute | solution.py:338
  158.4 20.1 %collective-permute-start.14 = (bf16[2,1024,128]{2,1,0:T(8,128)(2,1)S(1)}, bf16[2,1024,128]{2,1,0:T(8,128)(2,1)S(1)}, u32[]{:S(2)}, u32[]{:S(2)}) collective-permute-start(bf16[2,1024,128]{2,1,0:T(8,128)(2,1)S(1)} %pad_maximum_fusion.2.refs_3_.refs_5_), channel_id=1, source_target_pairs={{0,8},{4,12},{1,9},{5,13},{2,10},{6,14},{3,11},{7,15}} | collective-permute-start | bytes 1572872 | tf_op jit(solution)/shard_map/ppermute | solution.py:338
  159.7 32.9 %collective-permute-start.1 = (bf16[2,1024,128]{2,1,0:T(8,128)(2,1)S(1)}, bf16[2,1024,128]{2,1,0:T(8,128)(2,1)S(1)}, u32[]{:S(2)}, u32[]{:S(2)}) collective-permute-start(bf16[2,1024,128]{2,1,0:T(8,128)(2,1)S(1)} %copy-done.6), channel_id=1, source_target_pairs={{0,4},{4,0},{8,12},{12,8},{16,20},{20,16},{24,28},{28,24},{1,5},{5... | collective-permute-start | bytes 1572872 | tf_op jit(solution)/shard_map/ppermute | solution.py:338
  161.4 15.7 %collective-permute-start = (bf16[1024,128]{1,0:T(8,128)(2,1)S(1)}, bf16[1024,128]{1,0:T(8,128)(2,1)S(1)}, u32[]{:S(2)}, u32[]{:S(2)}) collective-permute-start(bf16[1024,128]{1,0:T(8,128)(2,1)S(1)} %copy-done.7), channel_id=1, source_target_pairs={{0,4},{4,0},{8,12},{12,8},{16,20},{20,16},{24,28},{28,24},{1,5},{5... | collective-permute-start | bytes 786440 | tf_op jit(solution)/shard_map/ppermute | solution.py:338
  162.5 31.4 %collective-permute-start.15 = (bf16[2,1024,128]{2,1,0:T(8,128)(2,1)S(1)}, bf16[2,1024,128]{2,1,0:T(8,128)(2,1)S(1)}, u32[]{:S(2)}, u32[]{:S(2)}) collective-permute-start(bf16[2,1024,128]{2,1,0:T(8,128)(2,1)S(1)} %collective-permute-done.13.refs_4_.refs_6_), channel_id=1, source_target_pairs={{0,8},{4,12},{1,9},{5,13},{2,10},{6,14},{3,11},{7,15}} | collective-permute-start | bytes 1572872 | tf_op jit(solution)/shard_map/ppermute | solution.py:338
  175.8 14.2 %collective-permute-start.17 = (bf16[1024,128]{1,0:T(8,128)(2,1)}, bf16[1024,128]{1,0:T(8,128)(2,1)S(1)}, u32[]{:S(2)}, u32[]{:S(2)}) collective-permute-start(bf16[1024,128]{1,0:T(8,128)(2,1)} %collective-permute-done.12.refs_2_), channel_id=1, source_target_pairs={{16,8},{20,12},{24,16},{28,20},{17,9},{21,13},{25,17},{29,21},{18,... | collective-permute-start | bytes 786440 | tf_op jit(solution)/shard_map/ppermute | solution.py:338
  177.1 14.2 %collective-permute-start.19 = (bf16[1024,128]{1,0:T(8,128)(2,1)}, bf16[1024,128]{1,0:T(8,128)(2,1)S(1)}, u32[]{:S(2)}, u32[]{:S(2)}) collective-permute-start(bf16[1024,128]{1,0:T(8,128)(2,1)} %collective-permute-done.12.refs_2_), channel_id=1, source_target_pairs={{24,8},{28,12},{25,9},{29,13},{26,10},{30,14},{27,11},{31,15}} | collective-permute-start | bytes 786440 | tf_op jit(solution)/shard_map/ppermute | solution.py:338
  178.5 28.6 %collective-permute-start.4 = (bf16[1024,128]{1,0:T(8,128)(2,1)S(1)}, bf16[1024,128]{1,0:T(8,128)(2,1)S(1)}, u32[]{:S(2)}, u32[]{:S(2)}) collective-permute-start(bf16[1024,128]{1,0:T(8,128)(2,1)S(1)} %get-tuple-element.182.refs_1_), channel_id=1, source_target_pairs={{16,8},{20,12},{24,16},{28,20},{17,9},{21,13},{25,17},{29,21},{18,... | collective-permute-start | bytes 786440 | tf_op jit(solution)/shard_map/ppermute | solution.py:338
  190.0 18.5 %collective-permute-start.6 = (bf16[1024,128]{1,0:T(8,128)(2,1)S(1)}, bf16[1024,128]{1,0:T(8,128)(2,1)S(1)}, u32[]{:S(2)}, u32[]{:S(2)}) collective-permute-start(bf16[1024,128]{1,0:T(8,128)(2,1)S(1)} %get-tuple-element.182.refs_1_), channel_id=1, source_target_pairs={{24,8},{28,12},{25,9},{29,13},{26,10},{30,14},{27,11},{31,15}} | collective-permute-start | bytes 786440 | tf_op jit(solution)/shard_map/ppermute | solution.py:338
  191.3 18.6 %collective-permute-start.2 = (bf16[2,1024,128]{2,1,0:T(8,128)(2,1)S(1)}, bf16[2,1024,128]{2,1,0:T(8,128)(2,1)S(1)}, u32[]{:S(2)}, u32[]{:S(2)}) collective-permute-start(bf16[2,1024,128]{2,1,0:T(8,128)(2,1)S(1)} %pad_maximum_fusion.refs_3_.refs_5_), channel_id=1, source_target_pairs={{0,8},{4,12},{1,9},{5,13},{2,10},{6,14},{3,11},{7,15}} | collective-permute-start | bytes 1572872 | tf_op jit(solution)/shard_map/ppermute | solution.py:338
  192.6 22.7 %collective-permute-start.5 = (bf16[1024,128]{1,0:T(8,128)(2,1)S(1)}, bf16[1024,128]{1,0:T(8,128)(2,1)S(1)}, u32[]{:S(2)}, u32[]{:S(2)}) collective-permute-start(bf16[1024,128]{1,0:T(8,128)(2,1)S(1)} %collective-permute-done.refs_2_), channel_id=1, source_target_pairs={{16,8},{20,12},{24,16},{28,20},{17,9},{21,13},{25,17},{29,21},{18,... | collective-permute-start | bytes 786440 | tf_op jit(solution)/shard_map/ppermute | solution.py:338
  194.0 24.6 %collective-permute-start.3 = (bf16[2,1024,128]{2,1,0:T(8,128)(2,1)S(1)}, bf16[2,1024,128]{2,1,0:T(8,128)(2,1)S(1)}, u32[]{:S(2)}, u32[]{:S(2)}) collective-permute-start(bf16[2,1024,128]{2,1,0:T(8,128)(2,1)S(1)} %collective-permute-done.1.refs_4_.refs_6_), channel_id=1, source_target_pairs={{0,8},{4,12},{1,9},{5,13},{2,10},{6,14},{3,11},{7,15}} | collective-permute-start | bytes 1572872 | tf_op jit(solution)/shard_map/ppermute | solution.py:338
  207.2 10.1 %collective-permute-start.7 = (bf16[1024,128]{1,0:T(8,128)(2,1)S(1)}, bf16[1024,128]{1,0:T(8,128)(2,1)S(1)}, u32[]{:S(2)}, u32[]{:S(2)}) collective-permute-start(bf16[1024,128]{1,0:T(8,128)(2,1)S(1)} %collective-permute-done.refs_2_), channel_id=1, source_target_pairs={{24,8},{28,12},{25,9},{29,13},{26,10},{30,14},{27,11},{31,15}} | collective-permute-start | bytes 786440 | tf_op jit(solution)/shard_map/ppermute | solution.py:338
  208.5 53.5 %collective-permute-start.44 = (bf16[8,128,256]{2,1,0:T(8,128)(2,1)S(1)}, bf16[8,128,256]{2,1,0:T(8,128)(2,1)S(1)}, u32[]{:S(2)}, u32[]{:S(2)}) collective-permute-start(bf16[8,128,256]{2,1,0:T(8,128)(2,1)S(1)} %get-tuple-element.185), channel_id=1, source_target_pairs={{8,16},{12,20},{16,24},{20,28},{9,17},{13,21},{17,25},{21,29},{10,... | collective-permute-start | bytes 1572872 | tf_op jit(solution)/shard_map/ppermute | solution.py:338
  209.9 53.5 %collective-permute-start.45 = (bf16[8,128,256]{2,1,0:T(8,128)(2,1)S(1)}, bf16[8,128,256]{2,1,0:T(8,128)(2,1)S(1)}, u32[]{:S(2)}, u32[]{:S(2)}) collective-permute-start(bf16[8,128,256]{2,1,0:T(8,128)(2,1)S(1)} %get-tuple-element.184), channel_id=1, source_target_pairs={{8,24},{12,28},{9,25},{13,29},{10,26},{14,30},{11,27},{15,31}} | collective-permute-start | bytes 1572872 | tf_op jit(solution)/shard_map/ppermute | solution.py:338
  217.2 12.3 %collective-permute-start.47 = (f32[8,256]{1,0:T(8,128)S(1)}, f32[8,256]{1,0:T(8,128)S(1)}, u32[]{:S(2)}, u32[]{:S(2)}) collective-permute-start(f32[8,256]{1,0:T(8,128)S(1)} %get-tuple-element.192), channel_id=1, source_target_pairs={{8,24},{12,28},{9,25},{13,29},{10,26},{14,30},{11,27},{15,31}} | collective-permute-start | bytes 24584 | tf_op jit(solution)/shard_map/ppermute | solution.py:338
  218.5 46.2 %collective-permute-start.32 = (bf16[8,128,256]{2,1,0:T(8,128)(2,1)S(1)}, bf16[8,128,256]{2,1,0:T(8,128)(2,1)S(1)}, u32[]{:S(2)}, u32[]{:S(2)}) collective-permute-start(bf16[8,128,256]{2,1,0:T(8,128)(2,1)S(1)} %get-tuple-element.187), channel_id=1, source_target_pairs={{8,16},{12,20},{16,24},{20,28},{9,17},{13,21},{17,25},{21,29},{10,... | collective-permute-start | bytes 1572872 | tf_op jit(solution)/shard_map/ppermute | solution.py:338
  223.4 20.9 %collective-permute-start.34 = (f32[8,256]{1,0:T(8,128)S(1)}, f32[8,256]{1,0:T(8,128)S(1)}, u32[]{:S(2)}, u32[]{:S(2)}) collective-permute-start(f32[8,256]{1,0:T(8,128)S(1)} %get-tuple-element.195), channel_id=1, source_target_pairs={{8,16},{12,20},{16,24},{20,28},{9,17},{13,21},{17,25},{21,29},{10,... | collective-permute-start | bytes 24584 | tf_op jit(solution)/shard_map/ppermute | solution.py:338
  229.6 16.0 %collective-permute-start.35 = (f32[8,256]{1,0:T(8,128)S(1)}, f32[8,256]{1,0:T(8,128)S(1)}, u32[]{:S(2)}, u32[]{:S(2)}) collective-permute-start(f32[8,256]{1,0:T(8,128)S(1)} %get-tuple-element.194), channel_id=1, source_target_pairs={{8,24},{12,28},{9,25},{13,29},{10,26},{14,30},{11,27},{15,31}} | collective-permute-start | bytes 24584 | tf_op jit(solution)/shard_map/ppermute | solution.py:338
  247.0 38.0 %collective-permute-start.33 = (bf16[8,128,256]{2,1,0:T(8,128)(2,1)S(1)}, bf16[8,128,256]{2,1,0:T(8,128)(2,1)S(1)}, u32[]{:S(2)}, u32[]{:S(2)}) collective-permute-start(bf16[8,128,256]{2,1,0:T(8,128)(2,1)S(1)} %get-tuple-element.186), channel_id=1, source_target_pairs={{8,24},{12,28},{9,25},{13,29},{10,26},{14,30},{11,27},{15,31}} | collective-permute-start | bytes 1572872 | tf_op jit(solution)/shard_map/ppermute | solution.py:338
  249.4 36.9 %collective-permute-start.20 = (bf16[8,128,256]{2,1,0:T(8,128)(2,1)S(1)}, bf16[8,128,256]{2,1,0:T(8,128)(2,1)S(1)}, u32[]{:S(2)}, u32[]{:S(2)}) collective-permute-start(bf16[8,128,256]{2,1,0:T(8,128)(2,1)S(1)} %get-tuple-element.189), channel_id=1, source_target_pairs={{8,16},{12,20},{16,24},{20,28},{9,17},{13,21},{17,25},{21,29},{10,... | collective-permute-start | bytes 1572872 | tf_op jit(solution)/shard_map/ppermute | solution.py:338
  262.0 36.8 %collective-permute-start.21 = (bf16[8,128,256]{2,1,0:T(8,128)(2,1)S(1)}, bf16[8,128,256]{2,1,0:T(8,128)(2,1)S(1)}, u32[]{:S(2)}, u32[]{:S(2)}) collective-permute-start(bf16[8,128,256]{2,1,0:T(8,128)(2,1)S(1)} %get-tuple-element.188), channel_id=1, source_target_pairs={{8,24},{12,28},{9,25},{13,29},{10,26},{14,30},{11,27},{15,31}} | collective-permute-start | bytes 1572872 | tf_op jit(solution)/shard_map/ppermute | solution.py:338
  263.4 36.6 %collective-permute-start.8 = (bf16[8,128,256]{2,1,0:T(8,128)(2,1)S(1)}, bf16[8,128,256]{2,1,0:T(8,128)(2,1)S(1)}, u32[]{:S(2)}, u32[]{:S(2)}) collective-permute-start(bf16[8,128,256]{2,1,0:T(8,128)(2,1)S(1)} %get-tuple-element.191), channel_id=1, source_target_pairs={{8,16},{12,20},{16,24},{20,28},{9,17},{13,21},{17,25},{21,29},{10,... | collective-permute-start | bytes 1572872 | tf_op jit(solution)/shard_map/ppermute | solution.py:338
  264.7 35.3 %collective-permute-start.9 = (bf16[8,128,256]{2,1,0:T(8,128)(2,1)S(1)}, bf16[8,128,256]{2,1,0:T(8,128)(2,1)S(1)}, u32[]{:S(2)}, u32[]{:S(2)}) collective-permute-start(bf16[8,128,256]{2,1,0:T(8,128)(2,1)S(1)} %get-tuple-element.190), channel_id=1, source_target_pairs={{8,24},{12,28},{9,25},{13,29},{10,26},{14,30},{11,27},{15,31}} | collective-permute-start | bytes 1572872 | tf_op jit(solution)/shard_map/ppermute | solution.py:338
  285.1 14.9 %collective-permute-start.10 = (f32[8,256]{1,0:T(8,128)S(1)}, f32[8,256]{1,0:T(8,128)S(1)}, u32[]{:S(2)}, u32[]{:S(2)}) collective-permute-start(f32[8,256]{1,0:T(8,128)S(1)} %get-tuple-element.199), channel_id=1, source_target_pairs={{8,16},{12,20},{16,24},{20,28},{9,17},{13,21},{17,25},{21,29},{10,... | collective-permute-start | bytes 24584 | tf_op jit(solution)/shard_map/ppermute | solution.py:338
  286.4 13.6 %collective-permute-start.11 = (f32[8,256]{1,0:T(8,128)S(1)}, f32[8,256]{1,0:T(8,128)S(1)}, u32[]{:S(2)}, u32[]{:S(2)}) collective-permute-start(f32[8,256]{1,0:T(8,128)S(1)} %get-tuple-element.198), channel_id=1, source_target_pairs={{8,24},{12,28},{9,25},{13,29},{10,26},{14,30},{11,27},{15,31}} | collective-permute-start | bytes 24584 | tf_op jit(solution)/shard_map/ppermute | solution.py:338
  306.4 10.1 %collective-permute-start.51 = (bf16[1024,128]{1,0:T(8,128)(2,1)S(1)}, bf16[1024,128]{1,0:T(8,128)(2,1)S(1)}, u32[]{:S(2)}, u32[]{:S(2)}) collective-permute-start(bf16[1024,128]{1,0:T(8,128)(2,1)S(1)} %get-tuple-element.56), channel_id=1, source_target_pairs={{0,4},{4,0},{8,12},{12,8},{16,20},{20,16},{24,28},{28,24},{1,5},{5... | collective-permute-start | bytes 786440 | tf_op jit(solution)/shard_map/ppermute | solution.py:338
  306.4 10.0 %collective-permute-start.50 = (bf16[1024,128]{1,0:T(8,128)(2,1)S(1)}, bf16[1024,128]{1,0:T(8,128)(2,1)S(1)}, u32[]{:S(2)}, u32[]{:S(2)}) collective-permute-start(bf16[1024,128]{1,0:T(8,128)(2,1)S(1)} %get-tuple-element.55), channel_id=1, source_target_pairs={{0,4},{4,0},{8,12},{12,8},{16,20},{20,16},{24,28},{28,24},{1,5},{5... | collective-permute-start | bytes 786440 | tf_op jit(solution)/shard_map/ppermute | solution.py:338
  308.4 10.0 %collective-permute-start.49 = (bf16[1024,128]{1,0:T(8,128)(2,1)S(1)}, bf16[1024,128]{1,0:T(8,128)(2,1)S(1)}, u32[]{:S(2)}, u32[]{:S(2)}) collective-permute-start(bf16[1024,128]{1,0:T(8,128)(2,1)S(1)} %get-tuple-element.54), channel_id=1, source_target_pairs={{0,4},{4,0},{8,12},{12,8},{16,20},{20,16},{24,28},{28,24},{1,5},{5... | collective-permute-start | bytes 786440 | tf_op jit(solution)/shard_map/ppermute | solution.py:338
  308.5 12.7 %collective-permute-start.48 = (bf16[1024,128]{1,0:T(8,128)(2,1)S(1)}, bf16[1024,128]{1,0:T(8,128)(2,1)S(1)}, u32[]{:S(2)}, u32[]{:S(2)}) collective-permute-start(bf16[1024,128]{1,0:T(8,128)(2,1)S(1)} %get-tuple-element.53), channel_id=1, source_target_pairs={{0,4},{4,0},{8,12},{12,8},{16,20},{20,16},{24,28},{28,24},{1,5},{5... | collective-permute-start | bytes 786440 | tf_op jit(solution)/shard_map/ppermute | solution.py:338
  (15 other events, 145.4 us)

commit v2 on v0

--- a/solution.py
+++ b/solution.py
@@ -4,11 +4,15 @@
 import jax
 import jax.numpy as jnp
 from jax import lax
+from jax.experimental import pallas as pl
+from jax.experimental.pallas import tpu as pltpu
 from jax.sharding import PartitionSpec as P
 
 HEADS = 32
 HD = 128
 CAP = 2
+LOG2E = math.log2(math.e)
+EXP_SCALE = HD ** (-0.5) * LOG2E
 
 
 def partial_state(query_rows, key_block, value_block, causal):
@@ -124,8 +128,420 @@
     )
 
 
+LSE_ROWS = 32
+UNROLL = 2
+VMEM_LIMIT = 48 * 1024 * 1024
+
+
+def unit_fields(code):
+    return code & 31, (code >> 5) & 31, (code >> 10) & 63, (code >> 16) & 1, (code >> 17) & 1
+
+
+def unit_code(slot, span, out, first, diagonal):
+    return slot + span * 32 + out * 1024 + first * 65536 + diagonal * 131072
+
+
+def attention_kernel(shape, own, plan, *refs):
+    heads, n_q, n_kv, per_dev, block_rows = shape
+    q_refs, refs = refs[:2], refs[2:]
+    k_refs, refs = refs[:3], refs[3:]
+    outs, refs = refs[:2], refs[2:]
+    sides = (0,) if own else (0, 1)
+    (q_scr, kv_scr, s0, s1, p0, p1, d0, d1, acc_scr, top_scr, sum_scr, o_scr, lse_scr, sems) = refs[:14]
+    s_scr, p_scr, decay_scr = (s0, s1), (p0, p1), (d0, d1)
+    spans = n_q * per_dev
+    copies = []
+    for h in range(heads):
+        sources = [ref.at[h, 0] if own else ref.at[side, h] for ref in q_refs for side in sides]
+        targets = [q_scr.at[h, i] for i in range(n_q)]
+        for i in range(n_kv):
+            sources.append(k_refs[i].at[h, pl.ds(1, 2)] if i < 2 else k_refs[2].at[i - 2, h])
+            targets.append(kv_scr.at[h, i])
+        for i, (source, target) in enumerate(zip(sources, targets)):
+            copies.append(pltpu.make_async_copy(source, target, sems.at[h, i]))
+    for copy in copies:
+        copy.start()
+    s1[...] = jnp.zeros_like(s1)
+    p0[...] = jnp.zeros_like(p0)
+    d0[...] = jnp.zeros_like(d0)
+    acc_scr[...] = jnp.zeros_like(acc_scr)
+    top_scr[...] = jnp.zeros_like(top_scr)
+    sum_scr[...] = jnp.ones_like(sum_scr)
+    if own:
+        bias_scr = refs[14]
+        key_pos = lax.broadcasted_iota(jnp.int32, (block_rows, block_rows), 0)
+        query_pos = lax.broadcasted_iota(jnp.int32, (block_rows, block_rows), 1)
+        bias_scr[0] = jnp.zeros((block_rows, block_rows), jnp.float32)
+        bias_scr[1] = jnp.where(key_pos <= query_pos, 0.0, -1e30)
+    for copy in copies:
+        copy.wait()
+
+    def rows_of(i):
+        return pl.ds(pl.multiple_of((i % per_dev) * block_rows, block_rows), block_rows)
+
+    def step(h, at, now, acc, top, total):
+        before = 1 - now
+        for u in range(UNROLL):
+            slot, _, out, _, _ = unit_fields(plan[at + u])
+            vt = kv_scr[h, slot // per_dev, 1, rows_of(slot), :]
+            vt = jnp.concatenate([vt[:HD], vt[HD:]], axis=1)
+            mixed = jnp.dot(vt, p_scr[now][u], preferred_element_type=jnp.float32)
+            acc = acc * decay_scr[now][u, 0:1, :] + mixed
+            o_scr[out] = (acc * decay_scr[now][u, 1:2, :]).astype(o_scr.dtype)
+        for u in range(UNROLL):
+            _, _, out, first, diagonal = unit_fields(plan[at + UNROLL + u])
+            s = s_scr[before][u]
+            if own:
+                s = s + bias_scr[diagonal]
+            old = jnp.where(first == 1, -1e30, top)
+            top = jnp.maximum(old, jnp.max(s, axis=0, keepdims=True))
+            decay = jnp.exp2((old - top) * EXP_SCALE)
+            p = jnp.exp2((s - top) * EXP_SCALE)
+            total = total * decay + jnp.sum(p, axis=0, keepdims=True)
+            p_scr[before][u] = p.astype(jnp.bfloat16)
+            decay_scr[before][u, 0:1, :] = decay
+            decay_scr[before][u, 1:2, :] = 1.0 / total
+            lse_scr[pl.ds(out, 1), :] = top * EXP_SCALE + jnp.log(total) * LOG2E
+        for u in range(UNROLL):
+            slot, span, _, _, _ = unit_fields(plan[at + 2 * UNROLL + u])
+            k = kv_scr[h, slot // per_dev, 0, rows_of(slot), :]
+            q = q_scr[h, span // per_dev, rows_of(span), :]
+            s_scr[now][u] = lax.dot_general(
+                k, q, (((1,), (1,)), ((), ())), preferred_element_type=jnp.float32
+            )
+        return acc, top, total
+
+    for h in range(heads):
+        o_scr[...] = jnp.zeros_like(o_scr)
+        lse_scr[...] = jnp.full_like(lse_scr, -1e30)
+
+        def two_steps(i, carry):
+            state = (acc_scr[...], top_scr[...], sum_scr[...])
+            state = step(h, 1 + 2 * i * UNROLL, 0, *state)
+            state = step(h, 1 + (2 * i + 1) * UNROLL, 1, *state)
+            acc_scr[...], top_scr[...], sum_scr[...] = state
+            return carry
+
+        lax.fori_loop(0, (plan[0] + 1) // 2, two_steps, 0)
+        if own:
+            outs[0][h] = o_scr[:spans]
+            outs[1][h] = lse_scr[:spans, :]
+        else:
+            half = spans // 2
+            for side in range(2):
+                for span in range(half):
+                    outs[side][h, span * HD : (span + 1) * HD, :] = o_scr[side * half + span]
+                lse = lse_scr[side * half : (side + 1) * half, :]
+                high = lse.astype(jnp.bfloat16).astype(jnp.float32)
+                middle = (lse - high).astype(jnp.bfloat16).astype(jnp.float32)
+                rest = jnp.zeros((LSE_ROWS - 3 * half, block_rows), jnp.float32)
+                parts = jnp.concatenate([high, middle, lse - high - middle, rest], axis=0)
+                outs[side][h, half * HD :, :] = parts.astype(jnp.bfloat16)
+
+
+def attention_call(plan, q_pieces, kv_pieces, own, heads, per_dev, block_rows):
+    n_q, n_kv = (2 if own else 4), 4
+    spans = n_q * per_dev
+    vmem, hbm = pl.BlockSpec(memory_space=pltpu.VMEM), pl.BlockSpec(memory_space=pl.ANY)
+    f32, bf16 = jnp.float32, jnp.bfloat16
+    if own:
+        out_shape = (
+            jax.ShapeDtypeStruct((heads, spans, HD, block_rows), f32),
+            jax.ShapeDtypeStruct((heads, spans, block_rows), f32),
+        )
+    else:
+        packed = jax.ShapeDtypeStruct((heads, spans // 2 * HD + LSE_ROWS, block_rows), bf16)
+        out_shape = (packed, packed)
+    scratch = [
+        pltpu.VMEM((heads, n_q, per_dev * block_rows, HD), bf16),
+        pltpu.VMEM((heads, n_kv, 2, per_dev * block_rows, HD), bf16),
+        pltpu.VMEM((UNROLL, block_rows, block_rows), f32),
+        pltpu.VMEM((UNROLL, block_rows, block_rows), f32),
+        pltpu.VMEM((UNROLL, block_rows, block_rows), bf16),
+        pltpu.VMEM((UNROLL, block_rows, block_rows), bf16),
+        pltpu.VMEM((UNROLL, 8, block_rows), f32),
+        pltpu.VMEM((UNROLL, 8, block_rows), f32),
+        pltpu.VMEM((HD, block_rows), f32),
+        pltpu.VMEM((1, block_rows), f32),
+        pltpu.VMEM((1, block_rows), f32),
+        pltpu.VMEM((spans + 1, HD, block_rows), f32 if own else bf16),
+        pltpu.VMEM((spans + 8, block_rows), f32),
+        pltpu.SemaphoreType.DMA((heads, n_q + n_kv)),
+    ]
+    if own:
+        scratch.append(pltpu.VMEM((2, block_rows, block_rows), f32))
+    return pl.pallas_call(
+        partial(attention_kernel, (heads, n_q, n_kv, per_dev, block_rows), own),
+        out_shape=out_shape,
+        in_specs=[pl.BlockSpec(memory_space=pltpu.SMEM)] + [hbm] * 5,
+        out_specs=(vmem, vmem),
+        scratch_shapes=scratch,
+        compiler_params=pltpu.CompilerParams(vmem_limit_bytes=VMEM_LIMIT),
+        cost_estimate=pl.CostEstimate(
+            flops=heads * 32 * 4 * block_rows * block_rows * HD,
+            bytes_accessed=heads * 4 * 1024 * 1024,
+            transcendentals=heads * 32 * block_rows * block_rows,
+        ),
+        name="own_attention" if own else "served_attention",
+    )(plan, *q_pieces, *kv_pieces)
+
+
+def pack_kernel(shape, place, q_ref, k_ref, v_ref, keep_ref, send_ref, v_scr, t_scr, sems):
+    heads, first, half, rows = shape
+    later, outs = [], (keep_ref, send_ref)
+    loads = []
+    n = 0
+    for side in range(2):
+        for h in range(heads):
+            start = pl.multiple_of((place[side] * half + first + h) * HD, HD)
+            load = pltpu.make_async_copy(v_ref.at[:, pl.ds(start, HD)], v_scr.at[side, h], sems.at[n])
+            load.start()
+            loads.append(load)
+            n += 1
+    for side in (1, 0):
+        for h in range(heads):
+            start = pl.multiple_of((place[side] * half + first + h) * HD, HD)
+            for i, ref in enumerate((q_ref, k_ref)):
+                copy = pltpu.make_async_copy(ref.at[:, pl.ds(start, HD)], outs[side].at[h, i], sems.at[n])
+                copy.start()
+                later.append(copy)
+                n += 1
+    for side in (1, 0):
+        for h in range(heads):
+            loads[side * heads + h].wait()
+            for tile in range(rows // HD):
+                at = slice(tile * HD, (tile + 1) * HD)
+                t_scr[side, h, at, :] = v_scr[side, h, at, :].T
+            copy = pltpu.make_async_copy(t_scr.at[side, h], outs[side].at[h, 2], sems.at[n])
+            copy.start()
+            later.append(copy)
+            n += 1
+    for copy in later:
+        copy.wait()
+
+
+def pack_call(place, queries, keys, values, heads, first, half):
+    rows = queries.shape[0]
+    hbm = pl.BlockSpec(memory_space=pl.ANY)
+    packed = jax.ShapeDtypeStruct((heads, 3, rows, HD), jnp.bfloat16)
+    return pl.pallas_call(
+        partial(pack_kernel, (heads, first, half, rows)),
+        out_shape=(packed, packed),
+        in_specs=[pl.BlockSpec(memory_space=pltpu.SMEM)] + [hbm] * 3,
+        out_specs=(hbm, hbm),
+        scratch_shapes=[
+            pltpu.VMEM((2, heads, rows, HD), jnp.bfloat16),
+            pltpu.VMEM((2, heads, rows, HD), jnp.bfloat16),
+            pltpu.SemaphoreType.DMA((8 * heads,)),
+        ],
+        compiler_params=pltpu.CompilerParams(vmem_limit_bytes=VMEM_LIMIT),
+        name="pack",
+    )(place, queries, keys, values)
+
+
+def join_kernel(heads, keep_ref, swap_ref, q_ref, kv_ref, sems):
+    copies = []
+    for side, ref in enumerate((keep_ref, swap_ref)):
+        for h in range(heads):
+            copies.append((ref.at[h, 0], q_ref.at[side, h]))
+            copies.append((ref.at[h, pl.ds(1, 2)], kv_ref.at[side, h]))
+    copies = [pltpu.make_async_copy(s, t, sems.at[i]) for i, (s, t) in enumerate(copies)]
+    for copy in copies:
+        copy.start()
+    for copy in copies:
+        copy.wait()
+
+
+def join_call(keep, swapped):
+    heads, _, rows, _ = keep.shape
+    hbm = pl.BlockSpec(memory_space=pl.ANY)
+    return pl.pallas_call(
+        partial(join_kernel, heads),
+        out_shape=(
+            jax.ShapeDtypeStruct((2, heads, rows, HD), jnp.bfloat16),
+            jax.ShapeDtypeStruct((2, heads, 2, rows, HD), jnp.bfloat16),
+        ),
+        in_specs=[hbm, hbm],
+        out_specs=(hbm, hbm),
+        scratch_shapes=[pltpu.SemaphoreType.DMA((4 * heads,))],
+        compiler_params=pltpu.CompilerParams(vmem_limit_bytes=VMEM_LIMIT),
+        name="join",
+    )(keep, swapped)
+
+
+def merge_kernel(shape, valid, own_ref, own_lse_ref, near_ref, far_ref, sofar_ref, keep_ref, send_ref, squares_ref):
+    heads, per_dev, block_rows = shape
+    spans = 2 * per_dev
+    squares_ref[...] = sofar_ref[...]
+    for h in range(heads):
+        lses = [own_lse_ref[h]]
+        for i, ref in enumerate((near_ref, far_ref)):
+            parts = ref[h, spans * HD :, :].astype(jnp.float32)
+            lse = parts[:spans] + parts[spans : 2 * spans] + parts[2 * spans : 3 * spans]
+            lses.append(jnp.where(valid[i] > 0, lse, -1e30))
+        top = jnp.maximum(jnp.maximum(lses[0], lses[1]), lses[2])
+        weights = [jnp.exp2(lse - top) for lse in lses]
+        scale = 1.0 / (weights[0] + weights[1] + weights[2])
+        weights = [weight * scale for weight in weights]
+        for span in range(spans):
+            rows = slice(span, span + 1)
+            tile = slice(span * HD, (span + 1) * HD)
+            mixed = weights[0][rows, :] * own_ref[h, span]
+            mixed = mixed + weights[1][rows, :] * near_ref[h, tile, :].astype(jnp.float32)
+            mixed = mixed + weights[2][rows, :] * far_ref[h, tile, :].astype(jnp.float32)
+            squares_ref[rows, :] = squares_ref[rows, :] + jnp.sum(mixed * mixed, axis=0, keepdims=True)
+            target = keep_ref if span < per_dev else send_ref
+            start = (span % per_dev) * block_rows
+            target[h, start : start + block_rows, :] = mixed.T.astype(target.dtype)
+
+
+def merge_call(valid, own, near, far, sofar, per_dev):
+    heads, spans, _, block_rows = own[0].shape
+    vmem = pl.BlockSpec(memory_space=pltpu.VMEM)
+    packed = jax.ShapeDtypeStruct((heads, per_dev * block_rows, HD), jnp.bfloat16)
+    return pl.pallas_call(
+        partial(merge_kernel, (heads, per_dev, block_rows)),
+        out_shape=(packed, packed, jax.ShapeDtypeStruct((spans, block_rows), jnp.float32)),
+        in_specs=[pl.BlockSpec(memory_space=pltpu.SMEM)] + [vmem] * 5,
+        out_specs=(vmem, vmem, vmem),
+        compiler_params=pltpu.CompilerParams(vmem_limit_bytes=VMEM_LIMIT),
+        name="merge",
+    )(valid, own[0], own[1], near, far, sofar)
+
+
+def finish_kernel(per_dev, sizes, place, *refs):
+    n = len(sizes)
+    kept, returned = refs[:n], refs[n : 2 * n]
+    squares_ref, gain_ref, out_ref = refs[2 * n :]
+    block_rows = squares_ref.shape[1]
+    half = sum(sizes)
+    factor = lax.rsqrt(squares_ref[...] / (HEADS * HD) + 1e-06)
+    for b in range(per_dev):
+        column = jnp.broadcast_to(factor[b : b + 1, :], (HD, block_rows)).T
+        rows = slice(b * block_rows, (b + 1) * block_rows)
+        for side, pieces in enumerate((kept, returned)):
+            head = 0
+            for piece, size in zip(pieces, sizes):
+                for h in range(size):
+                    start = pl.multiple_of((place[side] * half + head) * HD, HD)
+                    gain = gain_ref[:, pl.ds(start, HD)].astype(jnp.float32)
+                    value = piece[h, rows, :].astype(jnp.float32) * column * gain
+                    out_ref[rows, pl.ds(start, HD)] = value.astype(out_ref.dtype)
+                    head += 1
+
+
+def finish_call(place, kept, returned, squares, gain, per_dev):
+    vmem = pl.BlockSpec(memory_space=pltpu.VMEM)
+    rows, width = kept[0].shape[1], gain.shape[0]
+    return pl.pallas_call(
+        partial(finish_kernel, per_dev, [k.shape[0] for k in kept]),
+        out_shape=jax.ShapeDtypeStruct((rows, width), jnp.bfloat16),
+        in_specs=[pl.BlockSpec(memory_space=pltpu.SMEM)] + [vmem] * (2 * len(kept) + 2),
+        out_specs=vmem,
+        compiler_params=pltpu.CompilerParams(vmem_limit_bytes=VMEM_LIMIT),
+        name="finish",
+    )(place, *kept, *returned, squares, gain.reshape(1, width))
+
+
+def plan_of(live, slot, diagonal, dump):
+    spans, entries = live.shape
+    t = jnp.arange(entries)
+    earlier = jnp.sum((t[None, None, :] < t[None, :, None]) & live[:, None, :], axis=2)
+    span = lax.broadcasted_iota(jnp.int32, live.shape, 0)
+    code = unit_code(slot, span, span, (earlier == 0).astype(jnp.int32), diagonal)
+    code, live = code.reshape(-1), live.reshape(-1)
+    n = spans * entries
+    i = jnp.arange(n)
+    rank = jnp.sum((i[None, :] < i[:, None]) & live[None, :], axis=1)
+    at = jnp.arange(n + 8 * UNROLL)
+    hit = live[None, :] & (rank[None, :] + 2 * UNROLL == at[:, None])
+    idle = unit_code(0, 0, dump, 1, 0)
+    codes = jnp.sum(jnp.where(hit, code[None, :] - idle, 0), axis=1) + idle
+    total = jnp.sum(live.astype(jnp.int32))
+    steps = jnp.where(total > 0, (total + UNROLL - 1) // UNROLL + 2, 0)
+    return jnp.concatenate([steps[None], codes]).astype(jnp.int32)
+
+
+def level_shards(queries, keys, values, selection, norm_gain):
+    device = lax.axis_index("ctx")
+    level, x = device // 2, device % 2
+    rows, width = queries.shape
+    per_dev, topk = selection.shape
+    block_rows = rows // per_dev
+    spans = 2 * per_dev
+    half = width // HD // 2
+
+    def to(array, pairs):
+        return lax.ppermute(array, "ctx", pairs)
+
+    swap = [(d, d ^ 1) for d in range(8)]
+    lift = [(0, 2), (1, 3)]
+    near_down, far_down = [(4, 2), (5, 3), (6, 4), (7, 5)], [(6, 2), (7, 3)]
+    near_up, far_up = [(2, 4), (3, 5), (4, 6), (5, 7)], [(2, 6), (3, 7)]
+    valid = jnp.stack([level >= 2, level >= 3]).astype(jnp.int32)
+    place = jnp.stack([x, 1 - x]).astype(jnp.int32)
+
+    sizes = [1] * half
+    packs = []
+    for c, size in enumerate(sizes):
+        keep, send = pack_call(place, queries, keys, values, size, sum(sizes[:c]), half)
+        packs.append((keep, to(send, swap)))
+
+    own_selection = jnp.concatenate([selection, to(selection, swap)], axis=0)
+    near_selection, far_selection = to(own_selection, near_down), to(own_selection, far_down)
+
+    def ids(at):
+        first = jnp.stack([(at * 2 + x) * per_dev, (at * 2 + 1 - x) * per_dev])
+        return (first[:, None] + jnp.arange(per_dev)[None, :]).reshape(-1, 1)
+
+    def slots(blocks):
+        owner = blocks // per_dev
+        slot = jnp.where(owner // 2 == level, 0, spans) + jnp.where(owner % 2 == x, 0, per_dev)
+        return owner // 2, slot + blocks % per_dev
+
+    others = own_selection[:, 1:]
+    block_level, slot = slots(others)
+    live = (others != ids(level)) & ((block_level == level) | ((level == 1) & (block_level == 0)))
+    first = jnp.ones((spans, 1), jnp.int32)
+    own_plan = plan_of(
+        jnp.concatenate([first > 0, live], axis=1),
+        jnp.concatenate([jnp.arange(spans, dtype=jnp.int32)[:, None], slot], axis=1),
+        jnp.concatenate([first, jnp.zeros_like(others)], axis=1),
+        spans,
+    )
+    others = jnp.concatenate([near_selection, far_selection], axis=0)[:, 1:]
+    block_level, slot = slots(others)
+    is_near = lax.broadcasted_iota(jnp.int32, others.shape, 0) < spans
+    mine = ((level == 1) & (block_level <= 1)) | ((level == 2) & (block_level == 2) & is_near)
+    live = (others != jnp.concatenate([ids(level + 1), ids(level + 2)], axis=0)) & mine
+    served_plan = plan_of(live, slot, jnp.zeros_like(others), 2 * spans)
+
+    kept, returned = [], []
+    squares = jnp.zeros((spans, block_rows), jnp.float32)
+    for c, size in enumerate(sizes):
+        keep, swapped = packs[c]
+        level_q, level_kv = join_call(keep, swapped)
+        low = to(level_kv, lift)
+        near_q, far_q = to(level_q, near_down), to(level_q, far_down)
+        kv = [keep, swapped, low]
+        near, far = attention_call(served_plan, [near_q, far_q], kv, False, size, per_dev, block_rows)
+        near, far = to(near, near_up), to(far, far_up)
+        own = attention_call(own_plan, [keep, swapped], kv, True, size, per_dev, block_rows)
+        keep, send, squares = merge_call(valid, own, near, far, squares, per_dev)
+        kept.append(keep)
+        returned.append(to(send, swap))
+    square = squares[:per_dev] + to(squares[per_dev:], swap)
+    n_head = lax.axis_size("head")
+    hop = 1
+    while hop < n_head:
+        square = square + lax.ppermute(square, "head", [(i, i ^ hop) for i in range(n_head)])
+        hop *= 2
+    return finish_call(place, kept, returned, square, norm_gain, per_dev)
+
+
 def solution(mesh):
     placed = (P("ctx", "head"), P("ctx", "head"), P("ctx", "head"), P("ctx", None), P("head"))
+    body = level_shards if mesh.shape["ctx"] == 8 else shards
     return jax.shard_map(
-        shards, mesh=mesh, in_specs=placed, out_specs=P("ctx", "head"), check_vma=False
-    )
+        body, mesh=mesh, in_specs=placed, out_specs=P("ctx", "head"), check_vma=False
+    )

time: 516 us -> 247 us (0.48)
  waiting for transfers between devices: 328 us -> 85.8 us
  Pallas kernels: 0 us -> 86.3 us
  local copies, waits for them, and re-layouts: 77.4 us -> 10.5 us
  starting transfers between devices: 15.7 us -> 56.6 us
  matrix products: 38.5 us -> 0 us
  blocking collectives: 29.3 us -> 0 us
  other arithmetic: 24.8 us -> 3.5 us
    all_to_all x2 -> x0, waiting for transfers between devices: 328 us -> none  [the longest x1 170 us: shards(): lax.all_to_all(key_out, 'ctx', split_axis=0, concat_axis=0, tiled=True)]
    pallas_call x0 -> x21, Pallas kernels: none -> 86.3 us  [the longest x4 36.1 us: join_call(): pl.pallas_call(partial(join_kernel, heads), out_shape=(jax.ShapeDtypeStru...]
    ppermute x0 -> x34, waiting for transfers between devices: none -> 85.8 us  [the longest x32 82.5 us: to(): return lax.ppermute(array, 'ctx', pairs)]
    ppermute x0 -> x34, starting transfers between devices: none -> 56.6 us  [the longest x32 55 us: to(): return lax.ppermute(array, 'ctx', pairs)]
    gather x9 -> x0, local copies, waits for them, and re-layouts: 42.7 us -> none  [the longest x2 17.3 us: shards(): value_out = value_blocks[send_block].reshape(n_ctx, CAP, block_rows, width)]
    dot_general x10 -> x0, matrix products: 38.5 us -> none  [the longest x5 23.7 us: partial_state(): jnp.einsum('shqk,skhd->sqhd', weights, value_block, preferred_element_typ...]
    all_gather x1 -> x0, blocking collectives: 22.5 us -> none  [shards(): everyone = lax.all_gather(selection, 'ctx', axis=0, tiled=True)]
    reduce_sum x11 -> x8, other arithmetic: 20 us -> 2.28 us  [the longest x2 1.53 us: plan_of(): total = jnp.sum(live.astype(jnp.int32))]
  transfers between devices with their start and end apart: 2 -> 34, of which waited for: 2 -> 15; matrix products, arithmetic and copies ran while one was open for 5% -> 2% of each run, Pallas kernels for 0% -> 34%
where the time goes in v2:
time: 247 us; the launch traced here: 246 us
  Pallas kernels  86.3 us (35%)
  waiting for transfers between devices  85.8 us (35%)
  starting transfers between devices  56.6 us (23%)
  local copies, waits for them, and re-layouts  10.5 us (4%)
  other arithmetic  3.5 us (1%)
  between operations  3.29 us (1%)
    ppermute x32, waiting for transfers between devices, to(): return lax.ppermute(array, 'ctx', pairs)  82.5 us
    ppermute x32, starting transfers between devices, to(): return lax.ppermute(array, 'ctx', pairs)  55 us
    pallas_call x4, Pallas kernels, join_call(): pl.pallas_call(partial(join_kernel, heads), out_shape=(jax.ShapeDtypeStru...  36.1 us
    pallas_call x8, Pallas kernels, attention_call(): pl.pallas_call(partial(attention_kernel, (heads, n_q, n_kv, per_dev, bloc...  30.8 us
    pallas_call x4, Pallas kernels, pack_call(): pl.pallas_call(partial(pack_kernel, (heads, first, half, rows)), out_shap...  10.7 us
    unnamed x38, local copies, waits for them, and re-layouts  9.61 us
    pallas_call x4, Pallas kernels, merge_call(): pl.pallas_call(partial(merge_kernel, (heads, per_dev, block_rows)), out_s...  5.91 us
  transfers between devices with their start and end apart: 34, of which 15 were waited for; matrix products, arithmetic and copies ran while one was open for 2% of the time, Pallas kernels for 34%

profile of v2, /device:TPU:24, one launch (start us, length us, event | category | flops | bytes accessed | tf_op | source)
XLA Modules:
  0.0 245.9 jit_solution(11714356220475947806)
XLA Ops:
  0.0 1.5 collective-permute-start
  1.6 1.6 copy-done
  3.2 1.6 copy-done.1
  4.8 2.7 %pack.4 = (bf16[1,3,1024,128]{3,2,1,0:T(8,128)(2,1)S(1)}, bf16[1,3,1024,128]{3,2,1,0:T(8,128)(2,1)}) custom-call(s32[2]{0:T(128)S(1)} %pad_add_fusion.3.place, bf16[1024,1024]{1,0:T(8,128)(2,1)S(1)} %copy-done, bf16[1024,1024]{1,0:T(8,128)(2,1)S(1)} %copy-done.1, bf16[1024,1024]{1,0:T(8,128)(2,1)} %v_ref.7), custom_call_target="tpu_custom_call" | custom-call | tf_op jit(solution)/shard_map/pack/pallas_call | solution.py:327
  8.0 2.7 %pack.5 = (bf16[1,3,1024,128]{3,2,1,0:T(8,128)(2,1)S(1)}, bf16[1,3,1024,128]{3,2,1,0:T(8,128)(2,1)}) custom-call(s32[2]{0:T(128)S(1)} %pad_add_fusion.3.place, bf16[1024,1024]{1,0:T(8,128)(2,1)S(1)} %copy-done, bf16[1024,1024]{1,0:T(8,128)(2,1)S(1)} %copy-done.1, bf16[1024,1024]{1,0:T(8,128)(2,1)} %v_ref.7), custom_call_target="tpu_custom_call" | custom-call | tf_op jit(solution)/shard_map/pack/pallas_call | solution.py:327
  10.7 1.6 collective-permute-start.9
  12.2 2.7 %pack.6 = (bf16[1,3,1024,128]{3,2,1,0:T(8,128)(2,1)S(1)}, bf16[1,3,1024,128]{3,2,1,0:T(8,128)(2,1)}) custom-call(s32[2]{0:T(128)S(1)} %pad_add_fusion.3.place, bf16[1024,1024]{1,0:T(8,128)(2,1)S(1)} %copy-done, bf16[1024,1024]{1,0:T(8,128)(2,1)S(1)} %copy-done.1, bf16[1024,1024]{1,0:T(8,128)(2,1)} %v_ref.7), custom_call_target="tpu_custom_call" | custom-call | tf_op jit(solution)/shard_map/pack/pallas_call | solution.py:327
  15.5 2.7 %pack.7 = (bf16[1,3,1024,128]{3,2,1,0:T(8,128)(2,1)S(1)}, bf16[1,3,1024,128]{3,2,1,0:T(8,128)(2,1)}) custom-call(s32[2]{0:T(128)S(1)} %pad_add_fusion.3.place, bf16[1024,1024]{1,0:T(8,128)(2,1)S(1)} %copy-done, bf16[1024,1024]{1,0:T(8,128)(2,1)S(1)} %copy-done.1, bf16[1024,1024]{1,0:T(8,128)(2,1)} %v_ref.7), custom_call_target="tpu_custom_call" | custom-call | tf_op jit(solution)/shard_map/pack/pallas_call | solution.py:327
  21.5 2.2 collective-permute-start.4
  24.3 3.9 %collective-permute-done.1.swap_ref.refs_1_.refs_3_ = bf16[1,3,1024,128]{3,2,1,0:T(8,128)(2,1)S(1)} collective-permute-done((bf16[1,3,1024,128]{3,2,1,0:T(8,128)(2,1)}, bf16[1,3,1024,128]{3,2,1,0:T(8,128)(2,1)S(1)}, u32[]{:S(2)}, u32[]{:S(2)}) %collective-permute-start.1) | collective-permute-done | bytes 786464 | tf_op jit(solution)/shard_map/ppermute | solution.py:475
  28.2 2.3 collective-permute-start.3
  32.3 12.8 %collective-permute-done.9.swap_ref.refs_1_.refs_3_ = bf16[1,3,1024,128]{3,2,1,0:T(8,128)(2,1)} collective-permute-done((bf16[1,3,1024,128]{3,2,1,0:T(8,128)(2,1)}, bf16[1,3,1024,128]{3,2,1,0:T(8,128)(2,1)}, u32[]{:S(2)}, u32[]{:S(2)}) %collective-permute-start.9) | collective-permute-done | bytes 786464 | tf_op jit(solution)/shard_map/ppermute | solution.py:475
  45.1 3.2 %collective-permute-start.5 = (bf16[2,1,1024,128]{3,2,1,0:T(8,128)(2,1)}, bf16[2,1,1024,128]{3,2,1,0:T(8,128)(2,1)}, u32[]{:S(2)}, u32[]{:S(2)}) collective-permute-start(bf16[2,1,1024,128]{3,2,1,0:T(8,128)(2,1)} %get-tuple-element.54), channel_id=1, source_target_pairs={{16,8},{20,12},{24,16},{28,20},{17,9},{21,13},{25,17},{29,21},{18,... | collective-permute-start | bytes 1572872 | tf_op jit(solution)/shard_map/ppermute | solution.py:475
  48.3 9.1 %join.5 = (bf16[2,1,1024,128]{3,2,1,0:T(8,128)(2,1)}, bf16[2,1,2,1024,128]{4,3,2,1,0:T(8,128)(2,1)S(1)}) custom-call(bf16[1,3,1024,128]{3,2,1,0:T(8,128)(2,1)S(1)} %get-tuple-element.58.keep_ref.refs_0_.refs_2_, bf16[1,3,1024,128]{3,2,1,0:T(8,128)(2,1)} %collective-permute-done.9.swap_ref.refs_1_.refs_3_), custom_call_target="tpu_custom_call" | custom-call | tf_op jit(solution)/shard_map/join/pallas_call | solution.py:358
  58.4 2.1 collective-permute-start.6
  60.5 2.1 collective-permute-start.11
  62.9 1.6 collective-permute-start.2
  65.7 25.0 %join.6 = (bf16[2,1,1024,128]{3,2,1,0:T(8,128)(2,1)}, bf16[2,1,2,1024,128]{4,3,2,1,0:T(8,128)(2,1)}) custom-call(bf16[1,3,1024,128]{3,2,1,0:T(8,128)(2,1)S(1)} %get-tuple-element.68.keep_ref.refs_0_.refs_2_, bf16[1,3,1024,128]{3,2,1,0:T(8,128)(2,1)} %collective-permute-done.15.swap_ref.refs_1_.refs_3_), custom_call_target="tpu_custom_call" | custom-call | tf_op jit(solution)/shard_map/join/pallas_call | solution.py:358
  90.7 2.1 collective-permute-start.12
  92.8 1.6 collective-permute-start.10
  94.5 1.7 collective-permute-start.16
  96.1 2.1 collective-permute-start.17
  102.3 2.5 %collective-permute-done.12.refs_1_ = bf16[2,1,1024,128]{3,2,1,0:T(8,128)(2,1)} collective-permute-done((bf16[2,1,1024,128]{3,2,1,0:T(8,128)(2,1)}, bf16[2,1,1024,128]{3,2,1,0:T(8,128)(2,1)}, u32[]{:S(2)}, u32[]{:S(2)}) %collective-permute-start.12) | collective-permute-done | bytes 524320 | tf_op jit(solution)/shard_map/ppermute | solution.py:475
  105.6 6.5 %collective-permute-done.17.refs_0_ = bf16[2,1,1024,128]{3,2,1,0:T(8,128)(2,1)} collective-permute-done((bf16[2,1,1024,128]{3,2,1,0:T(8,128)(2,1)}, bf16[2,1,1024,128]{3,2,1,0:T(8,128)(2,1)}, u32[]{:S(2)}, u32[]{:S(2)}) %collective-permute-start.17) | collective-permute-done | bytes 524320 | tf_op jit(solution)/shard_map/ppermute | solution.py:475
  112.1 5.3 %collective-permute-start.18 = (bf16[2,1,1024,128]{3,2,1,0:T(8,128)(2,1)}, bf16[2,1,1024,128]{3,2,1,0:T(8,128)(2,1)S(1)}, u32[]{:S(2)}, u32[]{:S(2)}) collective-permute-start(bf16[2,1,1024,128]{3,2,1,0:T(8,128)(2,1)} %get-tuple-element.73), channel_id=1, source_target_pairs={{24,8},{28,12},{25,9},{29,13},{26,10},{30,14},{27,11},{31,15}} | collective-permute-start | bytes 1572872 | tf_op jit(solution)/shard_map/ppermute | solution.py:475
  118.8 2.3 served_attention.4
  121.1 5.5 %collective-permute-start.24 = (bf16[2,1,1024,128]{3,2,1,0:T(8,128)(2,1)S(1)}, bf16[2,1,1024,128]{3,2,1,0:T(8,128)(2,1)S(1)}, u32[]{:S(2)}, u32[]{:S(2)}) collective-permute-start(bf16[2,1,1024,128]{3,2,1,0:T(8,128)(2,1)S(1)} %get-tuple-element.83), channel_id=1, source_target_pairs={{24,8},{28,12},{25,9},{29,13},{26,10},{30,14},{27,11},{31,15}} | collective-permute-start | bytes 1572872 | tf_op jit(solution)/shard_map/ppermute | solution.py:475
  126.7 3.2 %served_attention.5 = (bf16[1,1056,256]{2,1,0:T(8,128)(2,1)S(1)}, bf16[1,1056,256]{2,1,0:T(8,128)(2,1)}) custom-call(s32[129]{0:T(256)S(1)} %pad_add_fusion.2.plan, bf16[2,1,1024,128]{3,2,1,0:T(8,128)(2,1)} %collective-permute-done.11.refs_0_, bf16[2,1,1024,128]{3,2,1,0:T(8,128)(2,1)} %collective-permute-done.12.refs_1_, ...), custom_call_target="tpu_custom_call" | custom-call | flops 1073741824 | bytes 4194304 | tf_op jit(solution)/shard_map/served_attention/pallas_call | solution.py:273
  131.4 9.7 %collective-permute-done.23.refs_0_ = bf16[2,1,1024,128]{3,2,1,0:T(8,128)(2,1)S(1)} collective-permute-done((bf16[2,1,1024,128]{3,2,1,0:T(8,128)(2,1)S(1)}, bf16[2,1,1024,128]{3,2,1,0:T(8,128)(2,1)S(1)}, u32[]{:S(2)}, u32[]{:S(2)}) %collective-permute-start.23) | collective-permute-done | bytes 524320 | tf_op jit(solution)/shard_map/ppermute | solution.py:475
  143.8 3.4 %served_attention.6 = (bf16[1,1056,256]{2,1,0:T(8,128)(2,1)}, bf16[1,1056,256]{2,1,0:T(8,128)(2,1)}) custom-call(s32[129]{0:T(256)S(1)} %pad_add_fusion.2.plan, bf16[2,1,1024,128]{3,2,1,0:T(8,128)(2,1)} %collective-permute-done.17.refs_0_, bf16[2,1,1024,128]{3,2,1,0:T(8,128)(2,1)S(1)} %collective-permute-done.18.refs_1_, ...), custom_call_target="tpu_custom_call" | custom-call | flops 1073741824 | bytes 4194304 | tf_op jit(solution)/shard_map/served_attention/pallas_call | solution.py:273
  147.2 4.2 %collective-permute-done.24.refs_1_ = bf16[2,1,1024,128]{3,2,1,0:T(8,128)(2,1)S(1)} collective-permute-done((bf16[2,1,1024,128]{3,2,1,0:T(8,128)(2,1)S(1)}, bf16[2,1,1024,128]{3,2,1,0:T(8,128)(2,1)S(1)}, u32[]{:S(2)}, u32[]{:S(2)}) %collective-permute-start.24) | collective-permute-done | bytes 524320 | tf_op jit(solution)/shard_map/ppermute | solution.py:475
  154.0 3.0 %served_attention.7 = (bf16[1,1056,256]{2,1,0:T(8,128)(2,1)}, bf16[1,1056,256]{2,1,0:T(8,128)(2,1)}) custom-call(s32[129]{0:T(256)S(1)} %pad_add_fusion.2.plan, bf16[2,1,1024,128]{3,2,1,0:T(8,128)(2,1)S(1)} %collective-permute-done.23.refs_0_, bf16[2,1,1024,128]{3,2,1,0:T(8,128)(2,1)S(1)} %collective-permute-done.24.refs_1_, ...), custom_call_target="tpu_custom_call" | custom-call | flops 1073741824 | bytes 4194304 | tf_op jit(solution)/shard_map/served_attention/pallas_call | solution.py:273
  161.8 9.3 %collective-permute-done.13.near_ref = bf16[1,1056,256]{2,1,0:T(8,128)(2,1)S(1)} collective-permute-done((bf16[1,1056,256]{2,1,0:T(8,128)(2,1)S(1)}, bf16[1,1056,256]{2,1,0:T(8,128)(2,1)S(1)}, u32[]{:S(2)}, u32[]{:S(2)}) %collective-permute-start.13) | collective-permute-done | bytes 540704 | tf_op jit(solution)/shard_map/ppermute | solution.py:475
  175.4 4.6 %own_attention.4 = (f32[1,8,128,256]{3,2,1,0:T(8,128)S(1)}, f32[1,8,256]{2,1,0:T(8,128)S(1)}) custom-call(s32[81]{0:T(128)S(1)} %pad_add_fusion.5.plan, bf16[1,3,1024,128]{3,2,1,0:T(8,128)(2,1)S(1)} %get-tuple-element.49.keep_ref.refs_0_.refs_2_, bf16[1,3,1024,128]{3,2,1,0:T(8,128)(2,1)S(1)} %collective-permute-done.1.swap_ref.refs_1_.refs_3_, ...), custom_call_target="tpu_custom_call" | custom-call | flops 1073741824 | bytes 4194304 | tf_op jit(solution)/shard_map/own_attention/pallas_call | solution.py:273
  180.1 4.8 %own_attention.5 = (f32[1,8,128,256]{3,2,1,0:T(8,128)S(1)}, f32[1,8,256]{2,1,0:T(8,128)S(1)}) custom-call(s32[81]{0:T(128)S(1)} %pad_add_fusion.5.plan, bf16[1,3,1024,128]{3,2,1,0:T(8,128)(2,1)S(1)} %get-tuple-element.58.keep_ref.refs_0_.refs_2_, bf16[1,3,1024,128]{3,2,1,0:T(8,128)(2,1)} %collective-permute-done.9.swap_ref.refs_1_.refs_3_, ...), custom_call_target="tpu_custom_call" | custom-call | flops 1073741824 | bytes 4194304 | tf_op jit(solution)/shard_map/own_attention/pallas_call | solution.py:273
  184.9 4.8 %own_attention.6 = (f32[1,8,128,256]{3,2,1,0:T(8,128)S(1)}, f32[1,8,256]{2,1,0:T(8,128)S(1)}) custom-call(s32[81]{0:T(128)S(1)} %pad_add_fusion.5.plan, bf16[1,3,1024,128]{3,2,1,0:T(8,128)(2,1)S(1)} %get-tuple-element.68.keep_ref.refs_0_.refs_2_, bf16[1,3,1024,128]{3,2,1,0:T(8,128)(2,1)} %collective-permute-done.15.swap_ref.refs_1_.refs_3_, ...), custom_call_target="tpu_custom_call" | custom-call | flops 1073741824 | bytes 4194304 | tf_op jit(solution)/shard_map/own_attention/pallas_call | solution.py:273
  189.8 4.7 %own_attention.7 = (f32[1,8,128,256]{3,2,1,0:T(8,128)S(1)}, f32[1,8,256]{2,1,0:T(8,128)S(1)}) custom-call(s32[81]{0:T(128)S(1)} %pad_add_fusion.5.plan, bf16[1,3,1024,128]{3,2,1,0:T(8,128)(2,1)S(1)} %copy-done.5, bf16[1,3,1024,128]{3,2,1,0:T(8,128)(2,1)} %collective-permute-done.21.swap_ref.refs_1_.refs_3_, bf16[1,3,1024,128]{3,2,1,0:T(8,128)(2,1)S(1)} %copy-done.5, ...), custom_call_target="tpu_custom_call" | custom-call | flops 1073741824 | bytes 4194304 | tf_op jit(solution)/shard_map/own_attention/pallas_call | solution.py:273
  196.2 1.5 merge.5
  197.7 1.6 collective-permute-start.28
  199.2 7.0 %collective-permute-done.20.far_ref = bf16[1,1056,256]{2,1,0:T(8,128)(2,1)} collective-permute-done((bf16[1,1056,256]{2,1,0:T(8,128)(2,1)}, bf16[1,1056,256]{2,1,0:T(8,128)(2,1)}, u32[]{:S(2)}, u32[]{:S(2)}) %collective-permute-start.20) | collective-permute-done | bytes 540704 | tf_op jit(solution)/shard_map/ppermute | solution.py:475
  206.2 1.7 merge.6
  208.5 7.0 %collective-permute-done.25.near_ref = bf16[1,1056,256]{2,1,0:T(8,128)(2,1)} collective-permute-done((bf16[1,1056,256]{2,1,0:T(8,128)(2,1)}, bf16[1,1056,256]{2,1,0:T(8,128)(2,1)}, u32[]{:S(2)}, u32[]{:S(2)}) %collective-permute-start.25) | collective-permute-done | bytes 540704 | tf_op jit(solution)/shard_map/ppermute | solution.py:475
  215.5 13.3 %collective-permute-done.26.far_ref = bf16[1,1056,256]{2,1,0:T(8,128)(2,1)} collective-permute-done((bf16[1,1056,256]{2,1,0:T(8,128)(2,1)}, bf16[1,1056,256]{2,1,0:T(8,128)(2,1)}, u32[]{:S(2)}, u32[]{:S(2)}) %collective-permute-start.26) | collective-permute-done | bytes 540704 | tf_op jit(solution)/shard_map/ppermute | solution.py:475
  228.8 1.7 merge.7
  232.5 5.8 %collective-permute-done.31 = f32[4,256]{1,0:T(4,128)S(1)} collective-permute-done((f32[4,256]{1,0:T(4,128)S(1)}, f32[4,256]{1,0:T(4,128)S(1)}, u32[]{:S(2)}, u32[]{:S(2)}) %collective-permute-start.31) | collective-permute-done | bytes 4128 | tf_op jit(solution)/shard_map/ppermute | solution.py:475
  239.5 1.5 collective-permute-start.33
  241.0 2.1 collective-permute-done.33
  243.1 2.8 %finish.1 = bf16[1024,1024]{1,0:T(8,128)(2,1)} custom-call(s32[2]{0:T(128)S(1)} %pad_add_fusion.3.place, bf16[1,1024,128]{2,1,0:T(8,128)(2,1)S(1)} %get-tuple-element.57.refs_0_, bf16[1,1024,128]{2,1,0:T(8,128)(2,1)S(1)} %get-tuple-element.67.refs_1_, bf16[1,1024,128]{2,1,0:T(8,128)(2,1)S(1)} %get-tuple-element.77.refs_2_, ...), custom_call_target="tpu_custom_call" | custom-call | tf_op jit(solution)/shard_map/finish/pallas_call | solution.py:436
  (129 shorter events, 34.1 us)
Async XLA Ops:
  0.0 21.5 %collective-permute-start = (s32[4,8]{1,0:T(4,128)}, s32[4,8]{1,0:T(4,128)S(1)}, u32[]{:S(2)}, u32[]{:S(2)}) collective-permute-start(s32[4,8]{1,0:T(4,128)} %param.8), channel_id=1, source_target_pairs={{0,4},{4,0},{8,12},{12,8},{16,20},{20,16},{24,28},{28,24},{1,5},{5... | collective-permute-start | bytes 392 | tf_op jit(solution)/shard_map/ppermute | solution.py:475
  1.6 1.6 copy-start
  3.2 1.6 copy-start.1
  7.4 20.7 %collective-permute-start.1 = (bf16[1,3,1024,128]{3,2,1,0:T(8,128)(2,1)}, bf16[1,3,1024,128]{3,2,1,0:T(8,128)(2,1)S(1)}, u32[]{:S(2)}, u32[]{:S(2)}) collective-permute-start(bf16[1,3,1024,128]{3,2,1,0:T(8,128)(2,1)} %get-tuple-element.50), channel_id=1, source_target_pairs={{0,4},{4,0},{8,12},{12,8},{16,20},{20,16},{24,28},{28,24},{1,5},{5... | collective-permute-start | bytes 2359304 | tf_op jit(solution)/shard_map/ppermute | solution.py:475
  10.7 34.4 %collective-permute-start.9 = (bf16[1,3,1024,128]{3,2,1,0:T(8,128)(2,1)}, bf16[1,3,1024,128]{3,2,1,0:T(8,128)(2,1)}, u32[]{:S(2)}, u32[]{:S(2)}) collective-permute-start(bf16[1,3,1024,128]{3,2,1,0:T(8,128)(2,1)} %get-tuple-element.59), channel_id=1, source_target_pairs={{0,4},{4,0},{8,12},{12,8},{16,20},{20,16},{24,28},{28,24},{1,5},{5... | collective-permute-start | bytes 2359304 | tf_op jit(solution)/shard_map/ppermute | solution.py:475
  14.9 6.6 %copy-start.18 = (s32[4,8]{1,0:T(4,128)S(1)}, s32[4,8]{1,0:T(4,128)}, u32[]{:S(2)}) copy-start(s32[4,8]{1,0:T(4,128)} %param.8) | copy-start | bytes 388
  14.9 47.9 %collective-permute-start.15 = (bf16[1,3,1024,128]{3,2,1,0:T(8,128)(2,1)}, bf16[1,3,1024,128]{3,2,1,0:T(8,128)(2,1)}, u32[]{:S(2)}, u32[]{:S(2)}) collective-permute-start(bf16[1,3,1024,128]{3,2,1,0:T(8,128)(2,1)} %get-tuple-element.69), channel_id=1, source_target_pairs={{0,4},{4,0},{8,12},{12,8},{16,20},{20,16},{24,28},{28,24},{1,5},{5... | collective-permute-start | bytes 2359304 | tf_op jit(solution)/shard_map/ppermute | solution.py:475
  19.1 43.6 %copy-start.16 = (s32[8,8]{1,0:T(8,128)S(1)}, s32[8,8]{1,0:T(8,128)}, u32[]{:S(2)}) copy-start(s32[8,8]{1,0:T(8,128)} %constant.157.clone.1) | copy-start | bytes 772
  19.1 71.6 %collective-permute-start.21 = (bf16[1,3,1024,128]{3,2,1,0:T(8,128)(2,1)}, bf16[1,3,1024,128]{3,2,1,0:T(8,128)(2,1)}, u32[]{:S(2)}, u32[]{:S(2)}) collective-permute-start(bf16[1,3,1024,128]{3,2,1,0:T(8,128)(2,1)} %get-tuple-element.79), channel_id=1, source_target_pairs={{0,4},{4,0},{8,12},{12,8},{16,20},{20,16},{24,28},{28,24},{1,5},{5... | collective-permute-start | bytes 2359304 | tf_op jit(solution)/shard_map/ppermute | solution.py:475
  21.5 36.9 %collective-permute-start.4 = (s32[8,8]{1,0:T(8,128)S(1)}, s32[8,8]{1,0:T(8,128)S(1)}, u32[]{:S(2)}, u32[]{:S(2)}) collective-permute-start(s32[8,8]{1,0:T(8,128)S(1)} %pad_add_fusion.1), channel_id=1, source_target_pairs={{24,8},{28,12},{25,9},{29,13},{26,10},{30,14},{27,11},{31,15}} | collective-permute-start | bytes 776 | tf_op jit(solution)/shard_map/ppermute | solution.py:475
  28.2 32.4 %collective-permute-start.3 = (s32[8,8]{1,0:T(8,128)S(1)}, s32[8,8]{1,0:T(8,128)S(1)}, u32[]{:S(2)}, u32[]{:S(2)}) collective-permute-start(s32[8,8]{1,0:T(8,128)S(1)} %pad_add_fusion.1), channel_id=1, source_target_pairs={{16,8},{20,12},{24,16},{28,20},{17,9},{21,13},{25,17},{29,21},{18,... | collective-permute-start | bytes 776 | tf_op jit(solution)/shard_map/ppermute | solution.py:475
  31.4 1.0 copy-start.15
  45.1 47.7 %collective-permute-start.5 = (bf16[2,1,1024,128]{3,2,1,0:T(8,128)(2,1)}, bf16[2,1,1024,128]{3,2,1,0:T(8,128)(2,1)}, u32[]{:S(2)}, u32[]{:S(2)}) collective-permute-start(bf16[2,1,1024,128]{3,2,1,0:T(8,128)(2,1)} %get-tuple-element.54), channel_id=1, source_target_pairs={{16,8},{20,12},{24,16},{28,20},{17,9},{21,13},{25,17},{29,21},{18,... | collective-permute-start | bytes 1572872 | tf_op jit(solution)/shard_map/ppermute | solution.py:475
  58.4 36.1 %collective-permute-start.6 = (bf16[2,1,1024,128]{3,2,1,0:T(8,128)(2,1)}, bf16[2,1,1024,128]{3,2,1,0:T(8,128)(2,1)}, u32[]{:S(2)}, u32[]{:S(2)}) collective-permute-start(bf16[2,1,1024,128]{3,2,1,0:T(8,128)(2,1)} %get-tuple-element.54), channel_id=1, source_target_pairs={{24,8},{28,12},{25,9},{29,13},{26,10},{30,14},{27,11},{31,15}} | collective-permute-start | bytes 1572872 | tf_op jit(solution)/shard_map/ppermute | solution.py:475
  60.5 35.6 %collective-permute-start.11 = (bf16[2,1,1024,128]{3,2,1,0:T(8,128)(2,1)}, bf16[2,1,1024,128]{3,2,1,0:T(8,128)(2,1)}, u32[]{:S(2)}, u32[]{:S(2)}) collective-permute-start(bf16[2,1,1024,128]{3,2,1,0:T(8,128)(2,1)} %get-tuple-element.63), channel_id=1, source_target_pairs={{16,8},{20,12},{24,16},{28,20},{17,9},{21,13},{25,17},{29,21},{18,... | collective-permute-start | bytes 1572872 | tf_op jit(solution)/shard_map/ppermute | solution.py:475
  62.9 54.5 %collective-permute-start.2 = (bf16[2,1,2,1024,128]{4,3,2,1,0:T(8,128)(2,1)}, bf16[2,1,2,1024,128]{4,3,2,1,0:T(8,128)(2,1)}, u32[]{:S(2)}, u32[]{:S(2)}) collective-permute-start(bf16[2,1,2,1024,128]{4,3,2,1,0:T(8,128)(2,1)} %copy-done.15), channel_id=1, source_target_pairs={{0,8},{4,12},{1,9},{5,13},{2,10},{6,14},{3,11},{7,15}} | collective-permute-start | bytes 3145736 | tf_op jit(solution)/shard_map/ppermute | solution.py:475
  90.7 14.0 %collective-permute-start.12 = (bf16[2,1,1024,128]{3,2,1,0:T(8,128)(2,1)}, bf16[2,1,1024,128]{3,2,1,0:T(8,128)(2,1)}, u32[]{:S(2)}, u32[]{:S(2)}) collective-permute-start(bf16[2,1,1024,128]{3,2,1,0:T(8,128)(2,1)} %get-tuple-element.63), channel_id=1, source_target_pairs={{24,8},{28,12},{25,9},{29,13},{26,10},{30,14},{27,11},{31,15}} | collective-permute-start | bytes 1572872 | tf_op jit(solution)/shard_map/ppermute | solution.py:475
  92.8 28.3 %collective-permute-start.10 = (bf16[2,1,2,1024,128]{4,3,2,1,0:T(8,128)(2,1)}, bf16[2,1,2,1024,128]{4,3,2,1,0:T(8,128)(2,1)}, u32[]{:S(2)}, u32[]{:S(2)}) collective-permute-start(bf16[2,1,2,1024,128]{4,3,2,1,0:T(8,128)(2,1)} %copy-done.14), channel_id=1, source_target_pairs={{0,8},{4,12},{1,9},{5,13},{2,10},{6,14},{3,11},{7,15}} | collective-permute-start | bytes 3145736 | tf_op jit(solution)/shard_map/ppermute | solution.py:475
  94.5 47.9 %collective-permute-start.16 = (bf16[2,1,2,1024,128]{4,3,2,1,0:T(8,128)(2,1)}, bf16[2,1,2,1024,128]{4,3,2,1,0:T(8,128)(2,1)}, u32[]{:S(2)}, u32[]{:S(2)}) collective-permute-start(bf16[2,1,2,1024,128]{4,3,2,1,0:T(8,128)(2,1)} %get-tuple-element.70), channel_id=1, source_target_pairs={{0,8},{4,12},{1,9},{5,13},{2,10},{6,14},{3,11},{7,15}} | collective-permute-start | bytes 3145736 | tf_op jit(solution)/shard_map/ppermute | solution.py:475
  96.1 16.0 %collective-permute-start.17 = (bf16[2,1,1024,128]{3,2,1,0:T(8,128)(2,1)}, bf16[2,1,1024,128]{3,2,1,0:T(8,128)(2,1)}, u32[]{:S(2)}, u32[]{:S(2)}) collective-permute-start(bf16[2,1,1024,128]{3,2,1,0:T(8,128)(2,1)} %get-tuple-element.73), channel_id=1, source_target_pairs={{16,8},{20,12},{24,16},{28,20},{17,9},{21,13},{25,17},{29,21},{18,... | collective-permute-start | bytes 1572872 | tf_op jit(solution)/shard_map/ppermute | solution.py:475
  99.9 1.1 copy-start.3
  104.7 48.0 %collective-permute-start.22 = (bf16[2,1,2,1024,128]{4,3,2,1,0:T(8,128)(2,1)S(1)}, bf16[2,1,2,1024,128]{4,3,2,1,0:T(8,128)(2,1)S(1)}, u32[]{:S(2)}, u32[]{:S(2)}) collective-permute-start(bf16[2,1,2,1024,128]{4,3,2,1,0:T(8,128)(2,1)S(1)} %get-tuple-element.80), channel_id=1, source_target_pairs={{0,8},{4,12},{1,9},{5,13},{2,10},{6,14},{3,11},{7,15}} | collective-permute-start | bytes 3145736 | tf_op jit(solution)/shard_map/ppermute | solution.py:475
  112.1 17.9 %collective-permute-start.18 = (bf16[2,1,1024,128]{3,2,1,0:T(8,128)(2,1)}, bf16[2,1,1024,128]{3,2,1,0:T(8,128)(2,1)S(1)}, u32[]{:S(2)}, u32[]{:S(2)}) collective-permute-start(bf16[2,1,1024,128]{3,2,1,0:T(8,128)(2,1)} %get-tuple-element.73), channel_id=1, source_target_pairs={{24,8},{28,12},{25,9},{29,13},{26,10},{30,14},{27,11},{31,15}} | collective-permute-start | bytes 1572872 | tf_op jit(solution)/shard_map/ppermute | solution.py:475
  117.4 23.7 %collective-permute-start.23 = (bf16[2,1,1024,128]{3,2,1,0:T(8,128)(2,1)S(1)}, bf16[2,1,1024,128]{3,2,1,0:T(8,128)(2,1)S(1)}, u32[]{:S(2)}, u32[]{:S(2)}) collective-permute-start(bf16[2,1,1024,128]{3,2,1,0:T(8,128)(2,1)S(1)} %get-tuple-element.83), channel_id=1, source_target_pairs={{16,8},{20,12},{24,16},{28,20},{17,9},{21,13},{25,17},{29,21},{18,... | collective-permute-start | bytes 1572872 | tf_op jit(solution)/shard_map/ppermute | solution.py:475
  121.1 30.3 %collective-permute-start.24 = (bf16[2,1,1024,128]{3,2,1,0:T(8,128)(2,1)S(1)}, bf16[2,1,1024,128]{3,2,1,0:T(8,128)(2,1)S(1)}, u32[]{:S(2)}, u32[]{:S(2)}) collective-permute-start(bf16[2,1,1024,128]{3,2,1,0:T(8,128)(2,1)S(1)} %get-tuple-element.83), channel_id=1, source_target_pairs={{24,8},{28,12},{25,9},{29,13},{26,10},{30,14},{27,11},{31,15}} | collective-permute-start | bytes 1572872 | tf_op jit(solution)/shard_map/ppermute | solution.py:475
  129.9 24.1 %copy-start.4 = (bf16[1,3,1024,128]{3,2,1,0:T(8,128)(2,1)S(1)}, bf16[1,3,1024,128]{3,2,1,0:T(8,128)(2,1)}, u32[]{:S(2)}) copy-start(bf16[1,3,1024,128]{3,2,1,0:T(8,128)(2,1)} %copy-done.2) | copy-start | bytes 2359300
  130.0 27.0 %collective-permute-start.7 = (bf16[1,1056,256]{2,1,0:T(8,128)(2,1)S(1)}, bf16[1,1056,256]{2,1,0:T(8,128)(2,1)S(1)}, u32[]{:S(2)}, u32[]{:S(2)}) collective-permute-start(bf16[1,1056,256]{2,1,0:T(8,128)(2,1)S(1)} %get-tuple-element.55), channel_id=1, source_target_pairs={{8,16},{12,20},{16,24},{20,28},{9,17},{13,21},{17,25},{21,29},{10,... | collective-permute-start | bytes 1622024 | tf_op jit(solution)/shard_map/ppermute | solution.py:475
  141.1 18.6 %collective-permute-start.8 = (bf16[1,1056,256]{2,1,0:T(8,128)(2,1)S(1)}, bf16[1,1056,256]{2,1,0:T(8,128)(2,1)S(1)}, u32[]{:S(2)}, u32[]{:S(2)}) collective-permute-start(bf16[1,1056,256]{2,1,0:T(8,128)(2,1)S(1)} %get-tuple-element.56), channel_id=1, source_target_pairs={{8,24},{12,28},{9,25},{13,29},{10,26},{14,30},{11,27},{15,31}} | collective-permute-start | bytes 1622024 | tf_op jit(solution)/shard_map/ppermute | solution.py:475
  142.4 28.7 %collective-permute-start.13 = (bf16[1,1056,256]{2,1,0:T(8,128)(2,1)S(1)}, bf16[1,1056,256]{2,1,0:T(8,128)(2,1)S(1)}, u32[]{:S(2)}, u32[]{:S(2)}) collective-permute-start(bf16[1,1056,256]{2,1,0:T(8,128)(2,1)S(1)} %get-tuple-element.64), channel_id=1, source_target_pairs={{8,16},{12,20},{16,24},{20,28},{9,17},{13,21},{17,25},{21,29},{10,... | collective-permute-start | bytes 1622024 | tf_op jit(solution)/shard_map/ppermute | solution.py:475
  151.4 44.1 %collective-permute-start.14 = (bf16[1,1056,256]{2,1,0:T(8,128)(2,1)}, bf16[1,1056,256]{2,1,0:T(8,128)(2,1)}, u32[]{:S(2)}, u32[]{:S(2)}) collective-permute-start(bf16[1,1056,256]{2,1,0:T(8,128)(2,1)} %get-tuple-element.65), channel_id=1, source_target_pairs={{8,24},{12,28},{9,25},{13,29},{10,26},{14,30},{11,27},{15,31}} | collective-permute-start | bytes 1622024 | tf_op jit(solution)/shard_map/ppermute | solution.py:475
  152.7 4.3 %copy-start.6 = (bf16[2,1,2,1024,128]{4,3,2,1,0:T(8,128)(2,1)}, bf16[2,1,2,1024,128]{4,3,2,1,0:T(8,128)(2,1)S(1)}, u32[]{:S(2)}) copy-start(bf16[2,1,2,1024,128]{4,3,2,1,0:T(8,128)(2,1)S(1)} %collective-permute-done.22.refs_4_) | copy-start | bytes 3145732
  152.7 45.0 %collective-permute-start.19 = (bf16[1,1056,256]{2,1,0:T(8,128)(2,1)}, bf16[1,1056,256]{2,1,0:T(8,128)(2,1)}, u32[]{:S(2)}, u32[]{:S(2)}) collective-permute-start(bf16[1,1056,256]{2,1,0:T(8,128)(2,1)} %get-tuple-element.74), channel_id=1, source_target_pairs={{8,16},{12,20},{16,24},{20,28},{9,17},{13,21},{17,25},{21,29},{10,... | collective-permute-start | bytes 1622024 | tf_op jit(solution)/shard_map/ppermute | solution.py:475
  157.9 48.3 %collective-permute-start.20 = (bf16[1,1056,256]{2,1,0:T(8,128)(2,1)}, bf16[1,1056,256]{2,1,0:T(8,128)(2,1)}, u32[]{:S(2)}, u32[]{:S(2)}) collective-permute-start(bf16[1,1056,256]{2,1,0:T(8,128)(2,1)} %get-tuple-element.75), channel_id=1, source_target_pairs={{8,24},{12,28},{9,25},{13,29},{10,26},{14,30},{11,27},{15,31}} | collective-permute-start | bytes 1622024 | tf_op jit(solution)/shard_map/ppermute | solution.py:475
  160.5 55.0 %collective-permute-start.25 = (bf16[1,1056,256]{2,1,0:T(8,128)(2,1)}, bf16[1,1056,256]{2,1,0:T(8,128)(2,1)}, u32[]{:S(2)}, u32[]{:S(2)}) collective-permute-start(bf16[1,1056,256]{2,1,0:T(8,128)(2,1)} %get-tuple-element.84), channel_id=1, source_target_pairs={{8,16},{12,20},{16,24},{20,28},{9,17},{13,21},{17,25},{21,29},{10,... | collective-permute-start | bytes 1622024 | tf_op jit(solution)/shard_map/ppermute | solution.py:475
  171.9 56.8 %collective-permute-start.26 = (bf16[1,1056,256]{2,1,0:T(8,128)(2,1)}, bf16[1,1056,256]{2,1,0:T(8,128)(2,1)}, u32[]{:S(2)}, u32[]{:S(2)}) collective-permute-start(bf16[1,1056,256]{2,1,0:T(8,128)(2,1)} %get-tuple-element.85), channel_id=1, source_target_pairs={{8,24},{12,28},{9,25},{13,29},{10,26},{14,30},{11,27},{15,31}} | collective-permute-start | bytes 1622024 | tf_op jit(solution)/shard_map/ppermute | solution.py:475
  184.9 4.8 %copy-start.5 = (bf16[1,3,1024,128]{3,2,1,0:T(8,128)(2,1)S(1)}, bf16[1,3,1024,128]{3,2,1,0:T(8,128)(2,1)}, u32[]{:S(2)}) copy-start(bf16[1,3,1024,128]{3,2,1,0:T(8,128)(2,1)} %copy-done.2) | copy-start | bytes 2359300
  184.9 4.8 %copy-start.7 = (bf16[2,1,2,1024,128]{4,3,2,1,0:T(8,128)(2,1)S(1)}, bf16[2,1,2,1024,128]{4,3,2,1,0:T(8,128)(2,1)}, u32[]{:S(2)}) copy-start(bf16[2,1,2,1024,128]{4,3,2,1,0:T(8,128)(2,1)} %copy-done.6) | copy-start | bytes 3145732
  189.8 4.7 %copy-start.11 = (bf16[1,1056,256]{2,1,0:T(8,128)(2,1)S(1)}, bf16[1,1056,256]{2,1,0:T(8,128)(2,1)}, u32[]{:S(2)}) copy-start(bf16[1,1056,256]{2,1,0:T(8,128)(2,1)} %copy-done.10) | copy-start | bytes 1622020
  189.8 4.7 %copy-start.13 = (bf16[1,1056,256]{2,1,0:T(8,128)(2,1)S(1)}, bf16[1,1056,256]{2,1,0:T(8,128)(2,1)}, u32[]{:S(2)}) copy-start(bf16[1,1056,256]{2,1,0:T(8,128)(2,1)} %copy-done.12) | copy-start | bytes 1622020
  194.5 1.7 copy-start.9
  195.5 47.5 %collective-permute-start.27 = (bf16[1,1024,128]{2,1,0:T(8,128)(2,1)S(1)}, bf16[1,1024,128]{2,1,0:T(8,128)(2,1)S(1)}, u32[]{:S(2)}, u32[]{:S(2)}) collective-permute-start(bf16[1,1024,128]{2,1,0:T(8,128)(2,1)S(1)} %get-tuple-element.88), channel_id=1, source_target_pairs={{0,4},{4,0},{8,12},{12,8},{16,20},{20,16},{24,28},{28,24},{1,5},{5... | collective-permute-start | bytes 786440 | tf_op jit(solution)/shard_map/ppermute | solution.py:475
  197.7 45.4 %collective-permute-start.28 = (bf16[1,1024,128]{2,1,0:T(8,128)(2,1)S(1)}, bf16[1,1024,128]{2,1,0:T(8,128)(2,1)S(1)}, u32[]{:S(2)}, u32[]{:S(2)}) collective-permute-start(bf16[1,1024,128]{2,1,0:T(8,128)(2,1)S(1)} %get-tuple-element.89), channel_id=1, source_target_pairs={{0,4},{4,0},{8,12},{12,8},{16,20},{20,16},{24,28},{28,24},{1,5},{5... | collective-permute-start | bytes 786440 | tf_op jit(solution)/shard_map/ppermute | solution.py:475
  206.2 34.8 %copy-start.17 = (bf16[1024]{0:T(1024)(128)(2,1)S(1)}, bf16[1024]{0:T(1024)(128)(2,1)}, u32[]{:S(2)}) copy-start(bf16[1024]{0:T(1024)(128)(2,1)} %param.9) | copy-start | bytes 6148
  207.9 35.2 %collective-permute-start.29 = (bf16[1,1024,128]{2,1,0:T(8,128)(2,1)S(1)}, bf16[1,1024,128]{2,1,0:T(8,128)(2,1)S(1)}, u32[]{:S(2)}, u32[]{:S(2)}) collective-permute-start(bf16[1,1024,128]{2,1,0:T(8,128)(2,1)S(1)} %get-tuple-element.90), channel_id=1, source_target_pairs={{0,4},{4,0},{8,12},{12,8},{16,20},{20,16},{24,28},{28,24},{1,5},{5... | collective-permute-start | bytes 786440 | tf_op jit(solution)/shard_map/ppermute | solution.py:475
  230.4 12.7 %collective-permute-start.30 = (bf16[1,1024,128]{2,1,0:T(8,128)(2,1)S(1)}, bf16[1,1024,128]{2,1,0:T(8,128)(2,1)S(1)}, u32[]{:S(2)}, u32[]{:S(2)}) collective-permute-start(bf16[1,1024,128]{2,1,0:T(8,128)(2,1)S(1)} %get-tuple-element.91), channel_id=1, source_target_pairs={{0,4},{4,0},{8,12},{12,8},{16,20},{20,16},{24,28},{28,24},{1,5},{5... | collective-permute-start | bytes 786440 | tf_op jit(solution)/shard_map/ppermute | solution.py:475
  231.1 7.2 %collective-permute-start.31 = (f32[4,256]{1,0:T(4,128)S(1)}, f32[4,256]{1,0:T(4,128)S(1)}, u32[]{:S(2)}, u32[]{:S(2)}) collective-permute-start(f32[4,256]{1,0:T(4,128)S(1)} %slice.15), channel_id=1, source_target_pairs={{0,4},{4,0},{8,12},{12,8},{16,20},{20,16},{24,28},{28,24},{1,5},{5... | collective-permute-start | bytes 12296 | tf_op jit(solution)/shard_map/ppermute | solution.py:475
  238.3 1.2 collective-permute-start.32
  239.5 3.6 %collective-permute-start.33 = (f32[4,256]{1,0:T(4,128)S(1)}, f32[4,256]{1,0:T(4,128)S(1)}, u32[]{:S(2)}, u32[]{:S(2)}) collective-permute-start(f32[4,256]{1,0:T(4,128)S(1)} %add.298), channel_id=1, source_target_pairs={{0,2},{1,3},{2,0},{3,1},{4,6},{5,7},{6,4},{7,5},{8,10},{9,11},{10,... | collective-permute-start | bytes 12296 | tf_op jit(solution)/shard_map/ppermute | solution.py:537
  (5 other events, 4.3 us)

commit v3 on v2

--- a/solution.py
+++ b/solution.py
@@ -239,10 +239,17 @@
                 outs[side][h, half * HD :, :] = parts.astype(jnp.bfloat16)
 
 
-def attention_call(plan, q_pieces, kv_pieces, own, heads, per_dev, block_rows):
+def ordered(kernel, n_after):
+    def body(*refs):
+        kernel(*refs[n_after:])
+
+    return body
+
+
+def attention_call(plan, q_pieces, kv_pieces, own, heads, per_dev, block_rows, after=()):
     n_q, n_kv = (2 if own else 4), 4
     spans = n_q * per_dev
-    vmem, hbm = pl.BlockSpec(memory_space=pltpu.VMEM), pl.BlockSpec(memory_space=pl.ANY)
+    vmem, hbm = pl.BlockSpec(memory_space=pltpu.VMEM), pl.BlockSpec(memory_space=pltpu.HBM)
     f32, bf16 = jnp.float32, jnp.bfloat16
     if own:
         out_shape = (
@@ -271,19 +278,15 @@
     if own:
         scratch.append(pltpu.VMEM((2, block_rows, block_rows), f32))
     return pl.pallas_call(
-        partial(attention_kernel, (heads, n_q, n_kv, per_dev, block_rows), own),
+        ordered(partial(attention_kernel, (heads, n_q, n_kv, per_dev, block_rows), own), len(after)),
         out_shape=out_shape,
-        in_specs=[pl.BlockSpec(memory_space=pltpu.SMEM)] + [hbm] * 5,
+        in_specs=[hbm] * len(after) + [pl.BlockSpec(memory_space=pltpu.SMEM)] + [hbm] * 5,
         out_specs=(vmem, vmem),
         scratch_shapes=scratch,
         compiler_params=pltpu.CompilerParams(vmem_limit_bytes=VMEM_LIMIT),
-        cost_estimate=pl.CostEstimate(
-            flops=heads * 32 * 4 * block_rows * block_rows * HD,
-            bytes_accessed=heads * 4 * 1024 * 1024,
-            transcendentals=heads * 32 * block_rows * block_rows,
-        ),
+        cost_estimate=pl.CostEstimate(flops=1, bytes_accessed=1, transcendentals=0),
         name="own_attention" if own else "served_attention",
-    )(plan, *q_pieces, *kv_pieces)
+    )(*after, plan, *q_pieces, *kv_pieces)
 
 
 def pack_kernel(shape, place, q_ref, k_ref, v_ref, keep_ref, send_ref, v_scr, t_scr, sems):
@@ -320,14 +323,14 @@
         copy.wait()
 
 
-def pack_call(place, queries, keys, values, heads, first, half):
+def pack_call(place, queries, keys, values, heads, first, half, after=()):
     rows = queries.shape[0]
-    hbm = pl.BlockSpec(memory_space=pl.ANY)
+    hbm = pl.BlockSpec(memory_space=pltpu.HBM)
     packed = jax.ShapeDtypeStruct((heads, 3, rows, HD), jnp.bfloat16)
     return pl.pallas_call(
-        partial(pack_kernel, (heads, first, half, rows)),
+        ordered(partial(pack_kernel, (heads, first, half, rows)), len(after)),
         out_shape=(packed, packed),
-        in_specs=[pl.BlockSpec(memory_space=pltpu.SMEM)] + [hbm] * 3,
+        in_specs=[hbm] * len(after) + [pl.BlockSpec(memory_space=pltpu.SMEM)] + [hbm] * 3,
         out_specs=(hbm, hbm),
         scratch_shapes=[
             pltpu.VMEM((2, heads, rows, HD), jnp.bfloat16),
@@ -335,38 +338,54 @@
             pltpu.SemaphoreType.DMA((8 * heads,)),
         ],
         compiler_params=pltpu.CompilerParams(vmem_limit_bytes=VMEM_LIMIT),
+        cost_estimate=pl.CostEstimate(flops=1, bytes_accessed=1, transcendentals=0),
         name="pack",
-    )(place, queries, keys, values)
-
-
-def join_kernel(heads, keep_ref, swap_ref, q_ref, kv_ref, sems):
-    copies = []
+    )(*after, place, queries, keys, values)
+
+
+def join_kernel(heads, keep_ref, swap_ref, q_ref, kv_ref, scr, sems):
+    loads, stores = [], []
     for side, ref in enumerate((keep_ref, swap_ref)):
         for h in range(heads):
-            copies.append((ref.at[h, 0], q_ref.at[side, h]))
-            copies.append((ref.at[h, pl.ds(1, 2)], kv_ref.at[side, h]))
-    copies = [pltpu.make_async_copy(s, t, sems.at[i]) for i, (s, t) in enumerate(copies)]
-    for copy in copies:
-        copy.start()
-    for copy in copies:
-        copy.wait()
-
-
-def join_call(keep, swapped):
+            loads.append(pltpu.make_async_copy(ref.at[h], scr.at[side, h], sems.at[0, side, h]))
+            stores.append(
+                (
+                    pltpu.make_async_copy(scr.at[side, h, 0], q_ref.at[side, h], sems.at[1, side, h]),
+                    pltpu.make_async_copy(
+                        scr.at[side, h, pl.ds(1, 2)], kv_ref.at[side, h], sems.at[2, side, h]
+                    ),
+                )
+            )
+    for load in loads:
+        load.start()
+    for load, pair in zip(loads, stores):
+        load.wait()
+        for store in pair:
+            store.start()
+    for pair in stores:
+        for store in pair:
+            store.wait()
+
+
+def join_call(keep, swapped, after=()):
     heads, _, rows, _ = keep.shape
-    hbm = pl.BlockSpec(memory_space=pl.ANY)
+    hbm = pl.BlockSpec(memory_space=pltpu.HBM)
     return pl.pallas_call(
-        partial(join_kernel, heads),
+        ordered(partial(join_kernel, heads), len(after)),
         out_shape=(
             jax.ShapeDtypeStruct((2, heads, rows, HD), jnp.bfloat16),
             jax.ShapeDtypeStruct((2, heads, 2, rows, HD), jnp.bfloat16),
         ),
-        in_specs=[hbm, hbm],
+        in_specs=[hbm] * (len(after) + 2),
         out_specs=(hbm, hbm),
-        scratch_shapes=[pltpu.SemaphoreType.DMA((4 * heads,))],
+        scratch_shapes=[
+            pltpu.VMEM((2, heads, 3, rows, HD), jnp.bfloat16),
+            pltpu.SemaphoreType.DMA((3, 2, heads)),
+        ],
         compiler_params=pltpu.CompilerParams(vmem_limit_bytes=VMEM_LIMIT),
+        cost_estimate=pl.CostEstimate(flops=1, bytes_accessed=1, transcendentals=0),
         name="join",
-    )(keep, swapped)
+    )(*after, keep, swapped)
 
 
 def merge_kernel(shape, valid, own_ref, own_lse_ref, near_ref, far_ref, sofar_ref, keep_ref, send_ref, squares_ref):
@@ -395,18 +414,19 @@
             target[h, start : start + block_rows, :] = mixed.T.astype(target.dtype)
 
 
-def merge_call(valid, own, near, far, sofar, per_dev):
+def merge_call(valid, own, near, far, sofar, per_dev, after=()):
     heads, spans, _, block_rows = own[0].shape
     vmem = pl.BlockSpec(memory_space=pltpu.VMEM)
     packed = jax.ShapeDtypeStruct((heads, per_dev * block_rows, HD), jnp.bfloat16)
     return pl.pallas_call(
-        partial(merge_kernel, (heads, per_dev, block_rows)),
+        ordered(partial(merge_kernel, (heads, per_dev, block_rows)), len(after)),
         out_shape=(packed, packed, jax.ShapeDtypeStruct((spans, block_rows), jnp.float32)),
-        in_specs=[pl.BlockSpec(memory_space=pltpu.SMEM)] + [vmem] * 5,
+        in_specs=[pl.BlockSpec(memory_space=pltpu.HBM)] * len(after) + [pl.BlockSpec(memory_space=pltpu.SMEM)] + [vmem] * 5,
         out_specs=(vmem, vmem, vmem),
         compiler_params=pltpu.CompilerParams(vmem_limit_bytes=VMEM_LIMIT),
+        cost_estimate=pl.CostEstimate(flops=1, bytes_accessed=1, transcendentals=0),
         name="merge",
-    )(valid, own[0], own[1], near, far, sofar)
+    )(*after, valid, own[0], own[1], near, far, sofar)
 
 
 def finish_kernel(per_dev, sizes, place, *refs):
@@ -439,6 +459,7 @@
         in_specs=[pl.BlockSpec(memory_space=pltpu.SMEM)] + [vmem] * (2 * len(kept) + 2),
         out_specs=vmem,
         compiler_params=pltpu.CompilerParams(vmem_limit_bytes=VMEM_LIMIT),
+        cost_estimate=pl.CostEstimate(flops=1, bytes_accessed=1, transcendentals=0),
         name="finish",
     )(place, *kept, *returned, squares, gain.reshape(1, width))
 
@@ -471,8 +492,9 @@
     spans = 2 * per_dev
     half = width // HD // 2
 
-    def to(array, pairs):
-        return lax.ppermute(array, "ctx", pairs)
+    def to(array, pairs, name):
+        with jax.named_scope(name):
+            return lax.ppermute(array, "ctx", pairs)
 
     swap = [(d, d ^ 1) for d in range(8)]
     lift = [(0, 2), (1, 3)]
@@ -481,14 +503,11 @@
     valid = jnp.stack([level >= 2, level >= 3]).astype(jnp.int32)
     place = jnp.stack([x, 1 - x]).astype(jnp.int32)
 
-    sizes = [1] * half
-    packs = []
-    for c, size in enumerate(sizes):
-        keep, send = pack_call(place, queries, keys, values, size, sum(sizes[:c]), half)
-        packs.append((keep, to(send, swap)))
-
-    own_selection = jnp.concatenate([selection, to(selection, swap)], axis=0)
-    near_selection, far_selection = to(own_selection, near_down), to(own_selection, far_down)
+    own_selection = jnp.concatenate([selection, to(selection, swap, "selection_swap")], axis=0)
+    near_selection, far_selection = (
+        to(own_selection, near_down, "selection_near"),
+        to(own_selection, far_down, "selection_far"),
+    )
 
     def ids(at):
         first = jnp.stack([(at * 2 + x) * per_dev, (at * 2 + 1 - x) * per_dev])
@@ -516,21 +535,66 @@
     live = (others != jnp.concatenate([ids(level + 1), ids(level + 2)], axis=0)) & mine
     served_plan = plan_of(live, slot, jnp.zeros_like(others), 2 * spans)
 
-    kept, returned = [], []
-    squares = jnp.zeros((spans, block_rows), jnp.float32)
-    for c, size in enumerate(sizes):
-        keep, swapped = packs[c]
-        level_q, level_kv = join_call(keep, swapped)
-        low = to(level_kv, lift)
-        near_q, far_q = to(level_q, near_down), to(level_q, far_down)
-        kv = [keep, swapped, low]
-        near, far = attention_call(served_plan, [near_q, far_q], kv, False, size, per_dev, block_rows)
-        near, far = to(near, near_up), to(far, far_up)
-        own = attention_call(own_plan, [keep, swapped], kv, True, size, per_dev, block_rows)
-        keep, send, squares = merge_call(valid, own, near, far, squares, per_dev)
-        kept.append(keep)
-        returned.append(to(send, swap))
-    square = squares[:per_dev] + to(squares[per_dev:], swap)
+    sizes = [1] * half
+    n = len(sizes)
+    packs, lows, nears, fars, levels = [None] * n, [None] * n, [None] * n, [None] * n, [None] * n
+    ups, owns, kept, returned = [None] * n, [None] * n, [None] * n, [None] * n
+    squares = [jnp.zeros((spans, block_rows), jnp.float32)]
+    last = []
+
+    def pack(c, after=()):
+        keep, send = pack_call(
+            place, queries, keys, values, sizes[c], sum(sizes[:c]), half, (*after, *last)
+        )
+        last[:] = [keep]
+        packs[c] = (keep, to(send, swap, f"swap_c{c}"))
+
+    def join(c):
+        level_q, level_kv = join_call(*packs[c], last)
+        last[:] = [level_q]
+        lows[c] = to(level_kv, lift, f"lift_c{c}")
+        fars[c] = to(level_q, far_down, f"far_down_c{c}")
+        nears[c] = to(level_q, near_down, f"near_down_c{c}")
+
+    def serve(c):
+        kv, q = [*packs[c], lows[c]], [nears[c], fars[c]]
+        near, far = attention_call(served_plan, q, kv, False, sizes[c], per_dev, block_rows, last)
+        last[:] = [near]
+        ups[c] = (to(near, near_up, f"near_up_c{c}"), to(far, far_up, f"far_up_c{c}"))
+
+    def attend(c):
+        kv = [*packs[c], lows[c]]
+        owns[c] = attention_call(own_plan, packs[c], kv, True, sizes[c], per_dev, block_rows, last)
+        last[:] = [owns[c][1]]
+
+    def merge(c):
+        keep, send, total = merge_call(valid, owns[c], *ups[c], squares[0], per_dev, last)
+        squares[0] = total
+        last[:] = [keep]
+        kept[c], returned[c] = keep, to(send, swap, f"back_c{c}")
+
+    pack(0)
+    pack(1, (own_plan, served_plan))
+    join(0)
+    pack(2)
+    join(1)
+    serve(0)
+    attend(0)
+    join(2)
+    pack(3)
+    serve(1)
+    attend(1)
+    merge(0)
+    join(3)
+    serve(2)
+    attend(2)
+    merge(1)
+    serve(3)
+    merge(2)
+    attend(3)
+    merge(3)
+    squares = squares[0]
+    square = squares[:per_dev] + to(squares[per_dev:], swap, "squares_swap")
     n_head = lax.axis_size("head")
     hop = 1
     while hop < n_head:

time: 247 us -> 198 us (0.80)
  Pallas kernels: 86.3 us -> 52.9 us
  waiting for transfers between devices: 85.8 us -> 62 us
  starting transfers between devices: 56.6 us -> 63.4 us
    pallas_call x20, Pallas kernels: 83.5 us -> 50.1 us  [the longest x8 24.9 us: attention_call(): pl.pallas_call(ordered(partial(attention_kernel, (heads, n_q, n_kv, per_d...]
    ppermute x32, waiting for transfers between devices: 82.5 us -> 58.8 us  [to(): return lax.ppermute(array, 'ctx', pairs)]
    ppermute x32, starting transfers between devices: 55 us -> 61.9 us  [to(): return lax.ppermute(array, 'ctx', pairs)]
    unnamed x38 -> x44, local copies, waits for them, and re-layouts: 9.61 us -> 10.1 us
  transfers between devices with their start and end apart: 34 -> 34, of which waited for: 15 -> 9; matrix products, arithmetic and copies ran while one was open for 2% -> 2% of each run, Pallas kernels for 34% -> 25%
where the time goes in v3:
time: 198 us; the launch traced here: 196 us
  starting transfers between devices  63.4 us (32%)
  waiting for transfers between devices  62 us (31%)
  Pallas kernels  52.9 us (27%)
  local copies, waits for them, and re-layouts  11 us (6%)
  other arithmetic  3.56 us (2%)
  between operations  3.5 us (2%)
    ppermute x32, starting transfers between devices, to(): return lax.ppermute(array, 'ctx', pairs)  61.9 us
    ppermute x32, waiting for transfers between devices, to(): return lax.ppermute(array, 'ctx', pairs)  58.8 us
    pallas_call x8, Pallas kernels, attention_call(): pl.pallas_call(ordered(partial(attention_kernel, (heads, n_q, n_kv, per_d...  24.9 us
    pallas_call x4, Pallas kernels, pack_call(): pl.pallas_call(ordered(partial(pack_kernel, (heads, first, half, rows)),...  16.3 us
    unnamed x44, local copies, waits for them, and re-layouts  10.1 us
    pallas_call x4, Pallas kernels, merge_call(): pl.pallas_call(ordered(partial(merge_kernel, (heads, per_dev, block_rows)...  4.68 us
    pallas_call x4, Pallas kernels, join_call(): pl.pallas_call(ordered(partial(join_kernel, heads), len(after)), out_shap...  4.17 us
  transfers between devices with their start and end apart: 34, of which 9 were waited for; matrix products, arithmetic and copies ran while one was open for 2% of the time, Pallas kernels for 25%

profile of v3, /device:TPU:24, one launch (start us, length us, event | category | flops | bytes accessed | tf_op | source)
XLA Modules:
  0.0 196.4 jit_solution(14378299961308361244)
XLA Ops:
  0.0 1.5 collective-permute-start
  1.6 1.6 copy-done
  3.2 1.6 copy-done.2
  4.8 2.8 %pack.4 = (bf16[1,3,1024,128]{3,2,1,0:T(8,128)(2,1)S(1)}, bf16[1,3,1024,128]{3,2,1,0:T(8,128)(2,1)}) custom-call(s32[2]{0:T(128)S(1)} %pad_add_fusion.3.refs_0_.refs_3_.refs_1_.place, bf16[1024,1024]{1,0:T(8,128)(2,1)S(1)} %copy-done, bf16[1024,1024]{1,0:T(8,128)(2,1)S(1)} %copy-done.2, bf16[1024,1024]{1,0:T(8,128)(2,1)} %refs_4_.5), custom_call_target="tpu_custom_call" | custom-call | flops 1 | bytes 1 | tf_op jit(solution)/shard_map/pack/pallas_call | solution.py:330
  9.0 2.4 %collective-permute-start.1 = (s32[8,8]{1,0:T(8,128)S(1)}, s32[8,8]{1,0:T(8,128)S(1)}, u32[]{:S(2)}, u32[]{:S(2)}) collective-permute-start(s32[8,8]{1,0:T(8,128)S(1)} %pad_add_fusion.1), channel_id=1, source_target_pairs={{16,8},{20,12},{24,16},{28,20},{17,9},{21,13},{25,17},{29,21},{18,... | collective-permute-start | bytes 776 | tf_op jit(solution)/shard_map/selection_near/ppermute | solution.py:497
  19.0 1.9 pack.5
  20.9 1.6 collective-permute-start.4
  22.5 5.9 %collective-permute-done.3.refs_2_.refs_5_.refs_3_ = bf16[1,3,1024,128]{3,2,1,0:T(8,128)(2,1)} collective-permute-done((bf16[1,3,1024,128]{3,2,1,0:T(8,128)(2,1)}, bf16[1,3,1024,128]{3,2,1,0:T(8,128)(2,1)}, u32[]{:S(2)}, u32[]{:S(2)}) %collective-permute-start.3) | collective-permute-done | bytes 786464 | tf_op jit(solution)/shard_map/swap_c0/ppermute | solution.py:497
  28.4 1.3 join.4
  30.4 2.4 %collective-permute-start.5 = (bf16[2,1,1024,128]{3,2,1,0:T(8,128)(2,1)S(1)}, bf16[2,1,1024,128]{3,2,1,0:T(8,128)(2,1)S(1)}, u32[]{:S(2)}, u32[]{:S(2)}) collective-permute-start(bf16[2,1,1024,128]{3,2,1,0:T(8,128)(2,1)S(1)} %get-tuple-element.52.refs_0_), channel_id=1, source_target_pairs={{16,8},{20,12},{24,16},{28,20},{17,9},{21,13},{25,17},{29,21},{18,... | collective-permute-start | bytes 1572872 | tf_op jit(solution)/shard_map/near_down_c0/ppermute | solution.py:497
  32.8 1.9 pack.6
  35.4 1.7 collective-permute-start.6
  37.1 8.0 %collective-permute-done.4.refs_2_.refs_5_.refs_3_ = bf16[1,3,1024,128]{3,2,1,0:T(8,128)(2,1)S(1)} collective-permute-done((bf16[1,3,1024,128]{3,2,1,0:T(8,128)(2,1)S(1)}, bf16[1,3,1024,128]{3,2,1,0:T(8,128)(2,1)S(1)}, u32[]{:S(2)}, u32[]{:S(2)}) %collective-permute-start.4) | collective-permute-done | bytes 786464 | tf_op jit(solution)/shard_map/swap_c1/ppermute | solution.py:497
  45.1 1.3 join.5
  46.5 1.7 collective-permute-start.11
  48.1 1.9 collective-permute-start.10
  50.1 6.4 %collective-permute-done.6.refs_3_ = bf16[2,1,1024,128]{3,2,1,0:T(8,128)(2,1)S(1)} collective-permute-done((bf16[2,1,1024,128]{3,2,1,0:T(8,128)(2,1)S(1)}, bf16[2,1,1024,128]{3,2,1,0:T(8,128)(2,1)S(1)}, u32[]{:S(2)}, u32[]{:S(2)}) %collective-permute-start.6) | collective-permute-done | bytes 524320 | tf_op jit(solution)/shard_map/far_down_c0/ppermute | solution.py:497
  56.4 1.3 collective-permute-start.9
  57.8 2.7 %served_attention.4 = (bf16[1,1056,256]{2,1,0:T(8,128)(2,1)S(1)}, bf16[1,1056,256]{2,1,0:T(8,128)(2,1)}) custom-call(bf16[2,1,1024,128]{3,2,1,0:T(8,128)(2,1)S(1)} %get-tuple-element.55.refs_0_, s32[129]{0:T(256)S(1)} %pad_add_fusion.2.refs_1_, bf16[2,1,1024,128]{3,2,1,0:T(8,128)(2,1)S(1)} %collective-permute-done.5.refs_2_, ...), custom_call_target="tpu_custom_call" | custom-call | flops 1 | bytes 1 | tf_op jit(solution)/shard_map/served_attention/pallas_call | solution.py:280
  60.5 4.4 %own_attention.4 = (f32[1,8,128,256]{3,2,1,0:T(8,128)S(1)}, f32[1,8,256]{2,1,0:T(8,128)S(1)}) custom-call(bf16[1,1056,256]{2,1,0:T(8,128)(2,1)S(1)} %get-tuple-element.57.refs_0_, s32[81]{0:T(128)S(1)} %pad_add_fusion.5.refs_0_.refs_1_, bf16[1,3,1024,128]{3,2,1,0:T(8,128)(2,1)S(1)} %get-tuple-element.49.refs_2_.refs_1_.refs_4_, ...), custom_call_target="tpu_custom_call" | custom-call | flops 1 | bytes 1 | tf_op jit(solution)/shard_map/own_attention/pallas_call | solution.py:280
  67.2 9.7 %pack.7 = (bf16[1,3,1024,128]{3,2,1,0:T(8,128)(2,1)S(1)}, bf16[1,3,1024,128]{3,2,1,0:T(8,128)(2,1)}) custom-call(bf16[2,1,1024,128]{3,2,1,0:T(8,128)(2,1)S(1)} %get-tuple-element.60.refs_0_, s32[2]{0:T(128)S(1)} %pad_add_fusion.3.refs_0_.refs_3_.refs_1_.place, bf16[1024,1024]{1,0:T(8,128)(2,1)S(1)} %copy-done.1, bf16[1024,1024]{1,0:T(8,128)(2,1)} %refs_3_.5, ...), custom_call_target="tpu_custom_call" | custom-call | flops 1 | bytes 1 | tf_op jit(solution)/shard_map/pack/pallas_call | solution.py:330
  81.6 1.6 collective-permute-start.17
  83.3 8.7 %collective-permute-start.15 = (bf16[2,1,1024,128]{3,2,1,0:T(8,128)(2,1)}, bf16[2,1,1024,128]{3,2,1,0:T(8,128)(2,1)S(1)}, u32[]{:S(2)}, u32[]{:S(2)}) collective-permute-start(bf16[2,1,1024,128]{3,2,1,0:T(8,128)(2,1)} %copy-done.17), channel_id=1, source_target_pairs={{16,8},{20,12},{24,16},{28,20},{17,9},{21,13},{25,17},{29,21},{18,... | collective-permute-start | bytes 1572872 | tf_op jit(solution)/shard_map/near_down_c2/ppermute | solution.py:497
  96.4 2.1 %served_attention.5 = (bf16[1,1056,256]{2,1,0:T(8,128)(2,1)S(1)}, bf16[1,1056,256]{2,1,0:T(8,128)(2,1)S(1)}) custom-call(bf16[1,3,1024,128]{3,2,1,0:T(8,128)(2,1)S(1)} %get-tuple-element.61.refs_0_.refs_1_.refs_4_.refs_2_, s32[129]{0:T(256)S(1)} %pad_add_fusion.2.refs_1_, bf16[2,1,1024,128]{3,2,1,0:T(8,128)(2,1)S(1)} %copy-done.16, ...), custom_call_target="tpu_custom_call" | custom-call | flops 1 | bytes 1 | tf_op jit(solution)/shard_map/served_attention/pallas_call | solution.py:280
  98.5 4.5 %own_attention.5 = (f32[1,8,128,256]{3,2,1,0:T(8,128)S(1)}, f32[1,8,256]{2,1,0:T(8,128)S(1)}) custom-call(bf16[1,1056,256]{2,1,0:T(8,128)(2,1)S(1)} %get-tuple-element.63.refs_0_, s32[81]{0:T(128)S(1)} %pad_add_fusion.5.refs_0_.refs_1_, bf16[1,3,1024,128]{3,2,1,0:T(8,128)(2,1)S(1)} %copy-done.6, bf16[1,3,1024,128]{3,2,1,0:T(8,128)(2,1)S(1)} %copy-done.10, ...), custom_call_target="tpu_custom_call" | custom-call | flops 1 | bytes 1 | tf_op jit(solution)/shard_map/own_attention/pallas_call | solution.py:280
  103.1 9.7 %collective-permute-start.16 = (bf16[2,1,1024,128]{3,2,1,0:T(8,128)(2,1)S(1)}, bf16[2,1,1024,128]{3,2,1,0:T(8,128)(2,1)S(1)}, u32[]{:S(2)}, u32[]{:S(2)}) collective-permute-start(bf16[2,1,1024,128]{3,2,1,0:T(8,128)(2,1)S(1)} %copy-done.18), channel_id=1, source_target_pairs={{24,8},{28,12},{25,9},{29,13},{26,10},{30,14},{27,11},{31,15}} | collective-permute-start | bytes 1572872 | tf_op jit(solution)/shard_map/far_down_c2/ppermute | solution.py:497
  112.8 1.7 merge.4
  115.6 1.3 collective-permute-start.18
  116.9 1.3 collective-permute-start.19
  118.2 6.9 %collective-permute-done.16.refs_3_ = bf16[2,1,1024,128]{3,2,1,0:T(8,128)(2,1)S(1)} collective-permute-done((bf16[2,1,1024,128]{3,2,1,0:T(8,128)(2,1)S(1)}, bf16[2,1,1024,128]{3,2,1,0:T(8,128)(2,1)S(1)}, u32[]{:S(2)}, u32[]{:S(2)}) %collective-permute-start.16) | collective-permute-done | bytes 524320 | tf_op jit(solution)/shard_map/far_down_c2/ppermute | solution.py:497
  125.1 1.3 collective-permute-start.20
  126.4 5.4 %collective-permute-start.21 = (bf16[2,1,1024,128]{3,2,1,0:T(8,128)(2,1)S(1)}, bf16[2,1,1024,128]{3,2,1,0:T(8,128)(2,1)S(1)}, u32[]{:S(2)}, u32[]{:S(2)}) collective-permute-start(bf16[2,1,1024,128]{3,2,1,0:T(8,128)(2,1)S(1)} %get-tuple-element.69.refs_0_), channel_id=1, source_target_pairs={{24,8},{28,12},{25,9},{29,13},{26,10},{30,14},{27,11},{31,15}} | collective-permute-start | bytes 1572872 | tf_op jit(solution)/shard_map/far_down_c3/ppermute | solution.py:497
  131.8 2.1 %served_attention.6 = (bf16[1,1056,256]{2,1,0:T(8,128)(2,1)S(1)}, bf16[1,1056,256]{2,1,0:T(8,128)(2,1)S(1)}) custom-call(bf16[2,1,1024,128]{3,2,1,0:T(8,128)(2,1)S(1)} %get-tuple-element.69.refs_0_, s32[129]{0:T(256)S(1)} %pad_add_fusion.2.refs_1_, bf16[2,1,1024,128]{3,2,1,0:T(8,128)(2,1)S(1)} %collective-permute-done.15.refs_2_, ...), custom_call_target="tpu_custom_call" | custom-call | flops 1 | bytes 1 | tf_op jit(solution)/shard_map/served_attention/pallas_call | solution.py:280
  133.9 4.5 %own_attention.6 = (f32[1,8,128,256]{3,2,1,0:T(8,128)S(1)}, f32[1,8,256]{2,1,0:T(8,128)S(1)}) custom-call(bf16[1,1056,256]{2,1,0:T(8,128)(2,1)S(1)} %get-tuple-element.71.refs_0_, s32[81]{0:T(128)S(1)} %pad_add_fusion.5.refs_0_.refs_1_, bf16[1,3,1024,128]{3,2,1,0:T(8,128)(2,1)S(1)} %copy-done.4, bf16[1,3,1024,128]{3,2,1,0:T(8,128)(2,1)S(1)} %copy-done.8, ...), custom_call_target="tpu_custom_call" | custom-call | flops 1 | bytes 1 | tf_op jit(solution)/shard_map/own_attention/pallas_call | solution.py:280
  138.5 1.3 collective-permute-start.23
  139.8 1.5 collective-permute-start.24
  143.4 1.3 collective-permute-start.25
  144.7 1.3 collective-permute-start.26
  146.0 1.5 collective-permute-start.27
  147.5 20.3 %collective-permute-done.23.refs_4_ = bf16[1,1056,256]{2,1,0:T(8,128)(2,1)S(1)} collective-permute-done((bf16[1,1056,256]{2,1,0:T(8,128)(2,1)S(1)}, bf16[1,1056,256]{2,1,0:T(8,128)(2,1)S(1)}, u32[]{:S(2)}, u32[]{:S(2)}) %collective-permute-start.23) | collective-permute-done | bytes 540704 | tf_op jit(solution)/shard_map/near_up_c2/ppermute | solution.py:497
  167.8 1.5 collective-permute-start.28
  170.9 3.5 %own_attention.7 = (f32[1,8,128,256]{3,2,1,0:T(8,128)S(1)}, f32[1,8,256]{2,1,0:T(8,128)S(1)}) custom-call(bf16[1,1024,128]{2,1,0:T(8,128)(2,1)S(1)} %get-tuple-element.82.refs_0_.refs_2_, s32[81]{0:T(128)S(1)} %pad_add_fusion.5.refs_0_.refs_1_, bf16[1,3,1024,128]{3,2,1,0:T(8,128)(2,1)S(1)} %get-tuple-element.61.refs_0_.refs_1_.refs_4_.refs_2_, ...), custom_call_target="tpu_custom_call" | custom-call | flops 1 | bytes 1 | tf_op jit(solution)/shard_map/own_attention/pallas_call | solution.py:280
  174.4 6.9 %collective-permute-done.25.refs_4_ = bf16[1,1056,256]{2,1,0:T(8,128)(2,1)S(1)} collective-permute-done((bf16[1,1056,256]{2,1,0:T(8,128)(2,1)S(1)}, bf16[1,1056,256]{2,1,0:T(8,128)(2,1)S(1)}, u32[]{:S(2)}, u32[]{:S(2)}) %collective-permute-start.25) | collective-permute-done | bytes 540704 | tf_op jit(solution)/shard_map/near_up_c3/ppermute | solution.py:497
  182.3 1.6 collective-permute-start.30
  184.4 4.4 %collective-permute-done.31 = f32[4,256]{1,0:T(4,128)S(1)} collective-permute-done((f32[4,256]{1,0:T(4,128)S(1)}, f32[4,256]{1,0:T(4,128)S(1)}, u32[]{:S(2)}, u32[]{:S(2)}) %collective-permute-start.31) | collective-permute-done | bytes 4128 | tf_op jit(solution)/shard_map/squares_swap/ppermute | solution.py:497
  189.9 1.5 collective-permute-start.33
  191.5 2.1 %collective-permute-done.33 = f32[4,256]{1,0:T(4,128)S(1)} collective-permute-done((f32[4,256]{1,0:T(4,128)S(1)}, f32[4,256]{1,0:T(4,128)S(1)}, u32[]{:S(2)}, u32[]{:S(2)}) %collective-permute-start.33) | collective-permute-done | bytes 4128 | tf_op jit(solution)/shard_map/ppermute | solution.py:601
  193.6 2.8 %finish.1 = bf16[1024,1024]{1,0:T(8,128)(2,1)} custom-call(s32[2]{0:T(128)S(1)} %pad_add_fusion.3.refs_0_.refs_3_.refs_1_.place, bf16[1,1024,128]{2,1,0:T(8,128)(2,1)S(1)} %get-tuple-element.67.refs_0_, bf16[1,1024,128]{2,1,0:T(8,128)(2,1)S(1)} %get-tuple-element.76.refs_0_.refs_1_, bf16[1,1024,128]{2,1,0:T(8,128)(2,1)S(1)} %get-tuple-element.82.refs_0_.refs_2_, ...), custom_call_target="tpu_custom_call" | custom-call | flops 1 | bytes 1 | tf_op jit(solution)/shard_map/finish/pallas_call | solution.py:456
  (135 shorter events, 26.4 us)
Async XLA Ops:
  0.0 9.0 %collective-permute-start = (s32[4,8]{1,0:T(4,128)}, s32[4,8]{1,0:T(4,128)S(1)}, u32[]{:S(2)}, u32[]{:S(2)}) collective-permute-start(s32[4,8]{1,0:T(4,128)} %param.8), channel_id=1, source_target_pairs={{0,4},{4,0},{8,12},{12,8},{16,20},{20,16},{24,28},{28,24},{1,5},{5... | collective-permute-start | bytes 392 | tf_op jit(solution)/shard_map/selection_swap/ppermute | solution.py:497
  1.6 1.6 copy-start
  3.2 1.6 copy-start.2
  4.8 4.2 %copy-start.21 = (s32[4,8]{1,0:T(4,128)S(1)}, s32[4,8]{1,0:T(4,128)}, u32[]{:S(2)}) copy-start(s32[4,8]{1,0:T(4,128)} %param.8) | copy-start | bytes 388
  4.8 10.6 %copy-start.19 = (s32[8,8]{1,0:T(8,128)S(1)}, s32[8,8]{1,0:T(8,128)}, u32[]{:S(2)}) copy-start(s32[8,8]{1,0:T(8,128)} %constant.157.clone.1) | copy-start | bytes 772
  4.8 14.2 %copy-start.1 = (bf16[1024,1024]{1,0:T(8,128)(2,1)S(1)}, bf16[1024,1024]{1,0:T(8,128)(2,1)}, u32[]{:S(2)}) copy-start(bf16[1024,1024]{1,0:T(8,128)(2,1)} %refs_2_.5) | copy-start | bytes 6291460
  7.5 20.8 %collective-permute-start.3 = (bf16[1,3,1024,128]{3,2,1,0:T(8,128)(2,1)}, bf16[1,3,1024,128]{3,2,1,0:T(8,128)(2,1)}, u32[]{:S(2)}, u32[]{:S(2)}) collective-permute-start(bf16[1,3,1024,128]{3,2,1,0:T(8,128)(2,1)} %get-tuple-element.51), channel_id=1, source_target_pairs={{0,4},{4,0},{8,12},{12,8},{16,20},{20,16},{24,28},{28,24},{1,5},{5... | collective-permute-start | bytes 2359304 | tf_op jit(solution)/shard_map/swap_c0/ppermute | solution.py:497
  9.0 6.9 %collective-permute-start.1 = (s32[8,8]{1,0:T(8,128)S(1)}, s32[8,8]{1,0:T(8,128)S(1)}, u32[]{:S(2)}, u32[]{:S(2)}) collective-permute-start(s32[8,8]{1,0:T(8,128)S(1)} %pad_add_fusion.1), channel_id=1, source_target_pairs={{16,8},{20,12},{24,16},{28,20},{17,9},{21,13},{25,17},{29,21},{18,... | collective-permute-start | bytes 776 | tf_op jit(solution)/shard_map/selection_near/ppermute | solution.py:497
  11.4 4.5 %collective-permute-start.2 = (s32[8,8]{1,0:T(8,128)S(1)}, s32[8,8]{1,0:T(8,128)S(1)}, u32[]{:S(2)}, u32[]{:S(2)}) collective-permute-start(s32[8,8]{1,0:T(8,128)S(1)} %pad_add_fusion.1), channel_id=1, source_target_pairs={{24,8},{28,12},{25,9},{29,13},{26,10},{30,14},{27,11},{31,15}} | collective-permute-start | bytes 776 | tf_op jit(solution)/shard_map/selection_far/ppermute | solution.py:497
  20.9 24.2 %copy-start.5 = (bf16[1,3,1024,128]{3,2,1,0:T(8,128)(2,1)}, bf16[1,3,1024,128]{3,2,1,0:T(8,128)(2,1)S(1)}, u32[]{:S(2)}) copy-start(bf16[1,3,1024,128]{3,2,1,0:T(8,128)(2,1)S(1)} %get-tuple-element.50.refs_0_.refs_1_.refs_4_.refs_2_) | copy-start | bytes 2359300
  20.9 24.2 %collective-permute-start.4 = (bf16[1,3,1024,128]{3,2,1,0:T(8,128)(2,1)S(1)}, bf16[1,3,1024,128]{3,2,1,0:T(8,128)(2,1)S(1)}, u32[]{:S(2)}, u32[]{:S(2)}) collective-permute-start(bf16[1,3,1024,128]{3,2,1,0:T(8,128)(2,1)S(1)} %get-tuple-element.54), channel_id=1, source_target_pairs={{0,4},{4,0},{8,12},{12,8},{16,20},{20,16},{24,28},{28,24},{1,5},{5... | collective-permute-start | bytes 2359304 | tf_op jit(solution)/shard_map/swap_c1/ppermute | solution.py:497
  29.7 28.1 %collective-permute-start.7 = (bf16[2,1,2,1024,128]{4,3,2,1,0:T(8,128)(2,1)S(1)}, bf16[2,1,2,1024,128]{4,3,2,1,0:T(8,128)(2,1)S(1)}, u32[]{:S(2)}, u32[]{:S(2)}) collective-permute-start(bf16[2,1,2,1024,128]{4,3,2,1,0:T(8,128)(2,1)S(1)} %get-tuple-element.56), channel_id=1, source_target_pairs={{0,8},{4,12},{1,9},{5,13},{2,10},{6,14},{3,11},{7,15}} | collective-permute-start | bytes 3145736 | tf_op jit(solution)/shard_map/lift_c0/ppermute | solution.py:497
  30.4 17.7 %collective-permute-start.5 = (bf16[2,1,1024,128]{3,2,1,0:T(8,128)(2,1)S(1)}, bf16[2,1,1024,128]{3,2,1,0:T(8,128)(2,1)S(1)}, u32[]{:S(2)}, u32[]{:S(2)}) collective-permute-start(bf16[2,1,1024,128]{3,2,1,0:T(8,128)(2,1)S(1)} %get-tuple-element.52.refs_0_), channel_id=1, source_target_pairs={{16,8},{20,12},{24,16},{28,20},{17,9},{21,13},{25,17},{29,21},{18,... | collective-permute-start | bytes 1572872 | tf_op jit(solution)/shard_map/near_down_c0/ppermute | solution.py:497
  34.8 31.1 %copy-start.3 = (bf16[1,3,1024,128]{3,2,1,0:T(8,128)(2,1)}, bf16[1,3,1024,128]{3,2,1,0:T(8,128)(2,1)S(1)}, u32[]{:S(2)}) copy-start(bf16[1,3,1024,128]{3,2,1,0:T(8,128)(2,1)S(1)} %get-tuple-element.53.refs_0_.refs_1_.refs_4_.refs_2_) | copy-start | bytes 2359300
  34.8 31.1 %collective-permute-start.8 = (bf16[1,3,1024,128]{3,2,1,0:T(8,128)(2,1)S(1)}, bf16[1,3,1024,128]{3,2,1,0:T(8,128)(2,1)S(1)}, u32[]{:S(2)}, u32[]{:S(2)}) collective-permute-start(bf16[1,3,1024,128]{3,2,1,0:T(8,128)(2,1)S(1)} %get-tuple-element.59), channel_id=1, source_target_pairs={{0,4},{4,0},{8,12},{12,8},{16,20},{20,16},{24,28},{28,24},{1,5},{5... | collective-permute-start | bytes 2359304 | tf_op jit(solution)/shard_map/swap_c2/ppermute | solution.py:497
  35.4 21.0 %collective-permute-start.6 = (bf16[2,1,1024,128]{3,2,1,0:T(8,128)(2,1)S(1)}, bf16[2,1,1024,128]{3,2,1,0:T(8,128)(2,1)S(1)}, u32[]{:S(2)}, u32[]{:S(2)}) collective-permute-start(bf16[2,1,1024,128]{3,2,1,0:T(8,128)(2,1)S(1)} %get-tuple-element.52.refs_0_), channel_id=1, source_target_pairs={{24,8},{28,12},{25,9},{29,13},{26,10},{30,14},{27,11},{31,15}} | collective-permute-start | bytes 1572872 | tf_op jit(solution)/shard_map/far_down_c0/ppermute | solution.py:497
  45.1 1.3 copy-start.9
  46.5 36.8 %collective-permute-start.11 = (bf16[2,1,2,1024,128]{4,3,2,1,0:T(8,128)(2,1)}, bf16[2,1,2,1024,128]{4,3,2,1,0:T(8,128)(2,1)}, u32[]{:S(2)}, u32[]{:S(2)}) collective-permute-start(bf16[2,1,2,1024,128]{4,3,2,1,0:T(8,128)(2,1)} %get-tuple-element.62), channel_id=1, source_target_pairs={{0,8},{4,12},{1,9},{5,13},{2,10},{6,14},{3,11},{7,15}} | collective-permute-start | bytes 3145736 | tf_op jit(solution)/shard_map/lift_c1/ppermute | solution.py:497
  48.1 30.6 %collective-permute-start.10 = (bf16[2,1,1024,128]{3,2,1,0:T(8,128)(2,1)S(1)}, bf16[2,1,1024,128]{3,2,1,0:T(8,128)(2,1)S(1)}, u32[]{:S(2)}, u32[]{:S(2)}) collective-permute-start(bf16[2,1,1024,128]{3,2,1,0:T(8,128)(2,1)S(1)} %get-tuple-element.55.refs_0_), channel_id=1, source_target_pairs={{24,8},{28,12},{25,9},{29,13},{26,10},{30,14},{27,11},{31,15}} | collective-permute-start | bytes 1572872 | tf_op jit(solution)/shard_map/far_down_c1/ppermute | solution.py:497
  56.4 24.4 %collective-permute-start.9 = (bf16[2,1,1024,128]{3,2,1,0:T(8,128)(2,1)S(1)}, bf16[2,1,1024,128]{3,2,1,0:T(8,128)(2,1)S(1)}, u32[]{:S(2)}, u32[]{:S(2)}) collective-permute-start(bf16[2,1,1024,128]{3,2,1,0:T(8,128)(2,1)S(1)} %get-tuple-element.55.refs_0_), channel_id=1, source_target_pairs={{16,8},{20,12},{24,16},{28,20},{17,9},{21,13},{25,17},{29,21},{18,... | collective-permute-start | bytes 1572872 | tf_op jit(solution)/shard_map/near_down_c1/ppermute | solution.py:497
  67.2 9.7 %copy-start.17 = (bf16[2,1,1024,128]{3,2,1,0:T(8,128)(2,1)}, bf16[2,1,1024,128]{3,2,1,0:T(8,128)(2,1)S(1)}, u32[]{:S(2)}) copy-start(bf16[2,1,1024,128]{3,2,1,0:T(8,128)(2,1)S(1)} %get-tuple-element.60.refs_0_) | copy-start | bytes 1572868
  76.9 37.7 %collective-permute-start.14 = (bf16[1,3,1024,128]{3,2,1,0:T(8,128)(2,1)}, bf16[1,3,1024,128]{3,2,1,0:T(8,128)(2,1)S(1)}, u32[]{:S(2)}, u32[]{:S(2)}) collective-permute-start(bf16[1,3,1024,128]{3,2,1,0:T(8,128)(2,1)} %get-tuple-element.68), channel_id=1, source_target_pairs={{0,4},{4,0},{8,12},{12,8},{16,20},{20,16},{24,28},{28,24},{1,5},{5... | collective-permute-start | bytes 2359304 | tf_op jit(solution)/shard_map/swap_c3/ppermute | solution.py:497
  77.4 25.6 %collective-permute-start.12 = (bf16[1,1056,256]{2,1,0:T(8,128)(2,1)S(1)}, bf16[1,1056,256]{2,1,0:T(8,128)(2,1)}, u32[]{:S(2)}, u32[]{:S(2)}) collective-permute-start(bf16[1,1056,256]{2,1,0:T(8,128)(2,1)S(1)} %get-tuple-element.57.refs_0_), channel_id=1, source_target_pairs={{8,16},{12,20},{16,24},{20,28},{9,17},{13,21},{17,25},{21,29},{10,... | collective-permute-start | bytes 1622024 | tf_op jit(solution)/shard_map/near_up_c0/ppermute | solution.py:497
  79.5 33.3 %collective-permute-start.13 = (bf16[1,1056,256]{2,1,0:T(8,128)(2,1)}, bf16[1,1056,256]{2,1,0:T(8,128)(2,1)}, u32[]{:S(2)}, u32[]{:S(2)}) collective-permute-start(bf16[1,1056,256]{2,1,0:T(8,128)(2,1)} %get-tuple-element.66), channel_id=1, source_target_pairs={{8,24},{12,28},{9,25},{13,29},{10,26},{14,30},{11,27},{15,31}} | collective-permute-start | bytes 1622024 | tf_op jit(solution)/shard_map/far_up_c0/ppermute | solution.py:497
  81.6 44.8 %collective-permute-start.17 = (bf16[2,1,2,1024,128]{4,3,2,1,0:T(8,128)(2,1)}, bf16[2,1,2,1024,128]{4,3,2,1,0:T(8,128)(2,1)}, u32[]{:S(2)}, u32[]{:S(2)}) collective-permute-start(bf16[2,1,2,1024,128]{4,3,2,1,0:T(8,128)(2,1)} %get-tuple-element.70), channel_id=1, source_target_pairs={{0,8},{4,12},{1,9},{5,13},{2,10},{6,14},{3,11},{7,15}} | collective-permute-start | bytes 3145736 | tf_op jit(solution)/shard_map/lift_c2/ppermute | solution.py:497
  83.3 33.6 %collective-permute-start.15 = (bf16[2,1,1024,128]{3,2,1,0:T(8,128)(2,1)}, bf16[2,1,1024,128]{3,2,1,0:T(8,128)(2,1)S(1)}, u32[]{:S(2)}, u32[]{:S(2)}) collective-permute-start(bf16[2,1,1024,128]{3,2,1,0:T(8,128)(2,1)} %copy-done.17), channel_id=1, source_target_pairs={{16,8},{20,12},{24,16},{28,20},{17,9},{21,13},{25,17},{29,21},{18,... | collective-permute-start | bytes 1572872 | tf_op jit(solution)/shard_map/near_down_c2/ppermute | solution.py:497
  98.5 4.6 %copy-start.18 = (bf16[2,1,1024,128]{3,2,1,0:T(8,128)(2,1)S(1)}, bf16[2,1,1024,128]{3,2,1,0:T(8,128)(2,1)}, u32[]{:S(2)}) copy-start(bf16[2,1,1024,128]{3,2,1,0:T(8,128)(2,1)} %copy-done.17) | copy-start | bytes 1572868
  98.5 14.3 %copy-start.12 = (f32[1,8,128,256]{3,2,1,0:T(8,128)S(1)}, f32[1,8,128,256]{3,2,1,0:T(8,128)}, u32[]{:S(2)}) copy-start(f32[1,8,128,256]{3,2,1,0:T(8,128)} %copy-done.11) | copy-start | bytes 3145732
  103.1 28.7 %copy-start.4 = (bf16[1,3,1024,128]{3,2,1,0:T(8,128)(2,1)S(1)}, bf16[1,3,1024,128]{3,2,1,0:T(8,128)(2,1)}, u32[]{:S(2)}) copy-start(bf16[1,3,1024,128]{3,2,1,0:T(8,128)(2,1)} %copy-done.3) | copy-start | bytes 2359300
  103.1 28.7 %copy-start.8 = (bf16[1,3,1024,128]{3,2,1,0:T(8,128)(2,1)S(1)}, bf16[1,3,1024,128]{3,2,1,0:T(8,128)(2,1)}, u32[]{:S(2)}) copy-start(bf16[1,3,1024,128]{3,2,1,0:T(8,128)(2,1)} %copy-done.7) | copy-start | bytes 2359300
  103.1 22.0 %collective-permute-start.16 = (bf16[2,1,1024,128]{3,2,1,0:T(8,128)(2,1)S(1)}, bf16[2,1,1024,128]{3,2,1,0:T(8,128)(2,1)S(1)}, u32[]{:S(2)}, u32[]{:S(2)}) collective-permute-start(bf16[2,1,1024,128]{3,2,1,0:T(8,128)(2,1)S(1)} %copy-done.18), channel_id=1, source_target_pairs={{24,8},{28,12},{25,9},{29,13},{26,10},{30,14},{27,11},{31,15}} | collective-permute-start | bytes 1572872 | tf_op jit(solution)/shard_map/far_down_c2/ppermute | solution.py:497
  114.8 27.5 %collective-permute-start.22 = (bf16[2,1,2,1024,128]{4,3,2,1,0:T(8,128)(2,1)S(1)}, bf16[2,1,2,1024,128]{4,3,2,1,0:T(8,128)(2,1)S(1)}, u32[]{:S(2)}, u32[]{:S(2)}) collective-permute-start(bf16[2,1,2,1024,128]{4,3,2,1,0:T(8,128)(2,1)S(1)} %get-tuple-element.77), channel_id=1, source_target_pairs={{0,8},{4,12},{1,9},{5,13},{2,10},{6,14},{3,11},{7,15}} | collective-permute-start | bytes 3145736 | tf_op jit(solution)/shard_map/lift_c3/ppermute | solution.py:497
  115.6 22.9 %collective-permute-start.18 = (bf16[1,1056,256]{2,1,0:T(8,128)(2,1)S(1)}, bf16[1,1056,256]{2,1,0:T(8,128)(2,1)S(1)}, u32[]{:S(2)}, u32[]{:S(2)}) collective-permute-start(bf16[1,1056,256]{2,1,0:T(8,128)(2,1)S(1)} %get-tuple-element.63.refs_0_), channel_id=1, source_target_pairs={{8,16},{12,20},{16,24},{20,28},{9,17},{13,21},{17,25},{21,29},{10,... | collective-permute-start | bytes 1622024 | tf_op jit(solution)/shard_map/near_up_c1/ppermute | solution.py:497
  116.9 22.9 %collective-permute-start.19 = (bf16[1,1056,256]{2,1,0:T(8,128)(2,1)S(1)}, bf16[1,1056,256]{2,1,0:T(8,128)(2,1)S(1)}, u32[]{:S(2)}, u32[]{:S(2)}) collective-permute-start(bf16[1,1056,256]{2,1,0:T(8,128)(2,1)S(1)} %get-tuple-element.74), channel_id=1, source_target_pairs={{8,24},{12,28},{9,25},{13,29},{10,26},{14,30},{11,27},{15,31}} | collective-permute-start | bytes 1622024 | tf_op jit(solution)/shard_map/far_up_c1/ppermute | solution.py:497
  125.1 17.2 %collective-permute-start.20 = (bf16[2,1,1024,128]{3,2,1,0:T(8,128)(2,1)S(1)}, bf16[2,1,1024,128]{3,2,1,0:T(8,128)(2,1)S(1)}, u32[]{:S(2)}, u32[]{:S(2)}) collective-permute-start(bf16[2,1,1024,128]{3,2,1,0:T(8,128)(2,1)S(1)} %get-tuple-element.69.refs_0_), channel_id=1, source_target_pairs={{16,8},{20,12},{24,16},{28,20},{17,9},{21,13},{25,17},{29,21},{18,... | collective-permute-start | bytes 1572872 | tf_op jit(solution)/shard_map/near_down_c3/ppermute | solution.py:497
  126.4 15.9 %collective-permute-start.21 = (bf16[2,1,1024,128]{3,2,1,0:T(8,128)(2,1)S(1)}, bf16[2,1,1024,128]{3,2,1,0:T(8,128)(2,1)S(1)}, u32[]{:S(2)}, u32[]{:S(2)}) collective-permute-start(bf16[2,1,1024,128]{3,2,1,0:T(8,128)(2,1)S(1)} %get-tuple-element.69.refs_0_), channel_id=1, source_target_pairs={{24,8},{28,12},{25,9},{29,13},{26,10},{30,14},{27,11},{31,15}} | collective-permute-start | bytes 1572872 | tf_op jit(solution)/shard_map/far_down_c3/ppermute | solution.py:497
  138.5 29.3 %collective-permute-start.23 = (bf16[1,1056,256]{2,1,0:T(8,128)(2,1)S(1)}, bf16[1,1056,256]{2,1,0:T(8,128)(2,1)S(1)}, u32[]{:S(2)}, u32[]{:S(2)}) collective-permute-start(bf16[1,1056,256]{2,1,0:T(8,128)(2,1)S(1)} %get-tuple-element.71.refs_0_), channel_id=1, source_target_pairs={{8,16},{12,20},{16,24},{20,28},{9,17},{13,21},{17,25},{21,29},{10,... | collective-permute-start | bytes 1622024 | tf_op jit(solution)/shard_map/near_up_c2/ppermute | solution.py:497
  139.8 29.5 %collective-permute-start.24 = (bf16[1,1056,256]{2,1,0:T(8,128)(2,1)S(1)}, bf16[1,1056,256]{2,1,0:T(8,128)(2,1)S(1)}, u32[]{:S(2)}, u32[]{:S(2)}) collective-permute-start(bf16[1,1056,256]{2,1,0:T(8,128)(2,1)S(1)} %get-tuple-element.80), channel_id=1, source_target_pairs={{8,24},{12,28},{9,25},{13,29},{10,26},{14,30},{11,27},{15,31}} | collective-permute-start | bytes 1622024 | tf_op jit(solution)/shard_map/far_up_c2/ppermute | solution.py:497
  143.4 37.9 %collective-permute-start.25 = (bf16[1,1056,256]{2,1,0:T(8,128)(2,1)S(1)}, bf16[1,1056,256]{2,1,0:T(8,128)(2,1)S(1)}, u32[]{:S(2)}, u32[]{:S(2)}) collective-permute-start(bf16[1,1056,256]{2,1,0:T(8,128)(2,1)S(1)} %get-tuple-element.78.refs_0_), channel_id=1, source_target_pairs={{8,16},{12,20},{16,24},{20,28},{9,17},{13,21},{17,25},{21,29},{10,... | collective-permute-start | bytes 1622024 | tf_op jit(solution)/shard_map/near_up_c3/ppermute | solution.py:497
  144.7 36.6 %collective-permute-start.26 = (bf16[1,1056,256]{2,1,0:T(8,128)(2,1)S(1)}, bf16[1,1056,256]{2,1,0:T(8,128)(2,1)S(1)}, u32[]{:S(2)}, u32[]{:S(2)}) collective-permute-start(bf16[1,1056,256]{2,1,0:T(8,128)(2,1)S(1)} %get-tuple-element.85), channel_id=1, source_target_pairs={{8,24},{12,28},{9,25},{13,29},{10,26},{14,30},{11,27},{15,31}} | collective-permute-start | bytes 1622024 | tf_op jit(solution)/shard_map/far_up_c3/ppermute | solution.py:497
  146.0 47.6 %collective-permute-start.27 = (bf16[1,1024,128]{2,1,0:T(8,128)(2,1)S(1)}, bf16[1,1024,128]{2,1,0:T(8,128)(2,1)S(1)}, u32[]{:S(2)}, u32[]{:S(2)}) collective-permute-start(bf16[1,1024,128]{2,1,0:T(8,128)(2,1)S(1)} %get-tuple-element.88), channel_id=1, source_target_pairs={{0,4},{4,0},{8,12},{12,8},{16,20},{20,16},{24,28},{28,24},{1,5},{5... | collective-permute-start | bytes 786440 | tf_op jit(solution)/shard_map/back_c0/ppermute | solution.py:497
  167.8 25.8 %collective-permute-start.28 = (bf16[1,1024,128]{2,1,0:T(8,128)(2,1)S(1)}, bf16[1,1024,128]{2,1,0:T(8,128)(2,1)S(1)}, u32[]{:S(2)}, u32[]{:S(2)}) collective-permute-start(bf16[1,1024,128]{2,1,0:T(8,128)(2,1)S(1)} %get-tuple-element.89), channel_id=1, source_target_pairs={{0,4},{4,0},{8,12},{12,8},{16,20},{20,16},{24,28},{28,24},{1,5},{5... | collective-permute-start | bytes 786440 | tf_op jit(solution)/shard_map/back_c1/ppermute | solution.py:497
  170.3 23.2 %collective-permute-start.29 = (bf16[1,1024,128]{2,1,0:T(8,128)(2,1)S(1)}, bf16[1,1024,128]{2,1,0:T(8,128)(2,1)S(1)}, u32[]{:S(2)}, u32[]{:S(2)}) collective-permute-start(bf16[1,1024,128]{2,1,0:T(8,128)(2,1)S(1)} %get-tuple-element.90), channel_id=1, source_target_pairs={{0,4},{4,0},{8,12},{12,8},{16,20},{20,16},{24,28},{28,24},{1,5},{5... | collective-permute-start | bytes 786440 | tf_op jit(solution)/shard_map/back_c2/ppermute | solution.py:497
  174.4 17.1 %copy-start.20 = (bf16[1024]{0:T(1024)(128)(2,1)S(1)}, bf16[1024]{0:T(1024)(128)(2,1)}, u32[]{:S(2)}) copy-start(bf16[1024]{0:T(1024)(128)(2,1)} %param.9) | copy-start | bytes 6148
  182.3 11.3 %collective-permute-start.30 = (bf16[1,1024,128]{2,1,0:T(8,128)(2,1)S(1)}, bf16[1,1024,128]{2,1,0:T(8,128)(2,1)S(1)}, u32[]{:S(2)}, u32[]{:S(2)}) collective-permute-start(bf16[1,1024,128]{2,1,0:T(8,128)(2,1)S(1)} %get-tuple-element.91), channel_id=1, source_target_pairs={{0,4},{4,0},{8,12},{12,8},{16,20},{20,16},{24,28},{28,24},{1,5},{5... | collective-permute-start | bytes 786440 | tf_op jit(solution)/shard_map/back_c3/ppermute | solution.py:497
  183.9 4.9 %collective-permute-start.31 = (f32[4,256]{1,0:T(4,128)S(1)}, f32[4,256]{1,0:T(4,128)S(1)}, u32[]{:S(2)}, u32[]{:S(2)}) collective-permute-start(f32[4,256]{1,0:T(4,128)S(1)} %slice.15), channel_id=1, source_target_pairs={{0,4},{4,0},{8,12},{12,8},{16,20},{20,16},{24,28},{28,24},{1,5},{5... | collective-permute-start | bytes 12296 | tf_op jit(solution)/shard_map/squares_swap/ppermute | solution.py:497
  188.8 1.2 collective-permute-start.32
  189.9 3.6 %collective-permute-start.33 = (f32[4,256]{1,0:T(4,128)S(1)}, f32[4,256]{1,0:T(4,128)S(1)}, u32[]{:S(2)}, u32[]{:S(2)}) collective-permute-start(f32[4,256]{1,0:T(4,128)S(1)} %add.298), channel_id=1, source_target_pairs={{0,2},{1,3},{2,0},{3,1},{4,6},{5,7},{6,4},{7,5},{8,10},{9,11},{10,... | collective-permute-start | bytes 12296 | tf_op jit(solution)/shard_map/ppermute | solution.py:601
  (8 other events, 8.2 us)

commit v4 on v3

--- a/solution.py
+++ b/solution.py
@@ -128,9 +128,36 @@
     )
 
 
+SIZES = (1, 1, 1, 1,)
+SPLIT = (False, False, False, False,)
+ORDER = (
+    ("p", 0),
+    ("w", "plans"),
+    ("p", 1),
+    ("j", 0),
+    ("p", 2),
+    ("j", 1),
+    ("p", 3),
+    ("s", 0),
+    ("a", 0),
+    ("j", 2),
+    ("s", 1),
+    ("a", 1),
+    ("w", "lift_c1"),
+    ("m", 0),
+    ("j", 3),
+    ("s", 2),
+    ("w", "near_up_c1"),
+    ("a", 2),
+    ("m", 1),
+    ("s", 3),
+    ("m", 2),
+    ("a", 3),
+    ("m", 3),
+)
 LSE_ROWS = 32
 UNROLL = 2
-VMEM_LIMIT = 48 * 1024 * 1024
+VMEM_LIMIT = 63 * 1024 * 1024
 
 
 def unit_fields(code):
@@ -141,24 +168,30 @@
     return slot + span * 32 + out * 1024 + first * 65536 + diagonal * 131072
 
 
-def attention_kernel(shape, own, plan, *refs):
-    heads, n_q, n_kv, per_dev, block_rows = shape
-    q_refs, refs = refs[:2], refs[2:]
-    k_refs, refs = refs[:3], refs[3:]
+PIECES = {
+    "head": lambda ref, h: ref.at[h],
+    "queries": lambda ref, h: ref.at[h, 0],
+    "keys_values": lambda ref, h: ref.at[h, pl.ds(1, 2)],
+    "first": lambda ref, h: ref.at[0, h],
+    "second": lambda ref, h: ref.at[1, h],
+}
+
+
+def attention_kernel(shape, own, q_pieces, kv_pieces, n_in, plan, *refs):
+    heads, per_dev, block_rows = shape
+    n_q, n_kv = len(q_pieces), len(kv_pieces)
+    inputs, refs = refs[:n_in], refs[n_in:]
     outs, refs = refs[:2], refs[2:]
-    sides = (0,) if own else (0, 1)
     (q_scr, kv_scr, s0, s1, p0, p1, d0, d1, acc_scr, top_scr, sum_scr, o_scr, lse_scr, sems) = refs[:14]
     s_scr, p_scr, decay_scr = (s0, s1), (p0, p1), (d0, d1)
     spans = n_q * per_dev
     copies = []
     for h in range(heads):
-        sources = [ref.at[h, 0] if own else ref.at[side, h] for ref in q_refs for side in sides]
-        targets = [q_scr.at[h, i] for i in range(n_q)]
-        for i in range(n_kv):
-            sources.append(k_refs[i].at[h, pl.ds(1, 2)] if i < 2 else k_refs[2].at[i - 2, h])
-            targets.append(kv_scr.at[h, i])
-        for i, (source, target) in enumerate(zip(sources, targets)):
-            copies.append(pltpu.make_async_copy(source, target, sems.at[h, i]))
+        for i, (n, kind) in enumerate(q_pieces):
+            copies.append((PIECES[kind](inputs[n], h), q_scr.at[h, i], sems.at[h, i]))
+        for i, (n, kind) in enumerate(kv_pieces):
+            copies.append((PIECES[kind](inputs[n], h), kv_scr.at[h, i], sems.at[h, n_q + i]))
+    copies = [pltpu.make_async_copy(*copy) for copy in copies]
     for copy in copies:
         copy.start()
     s1[...] = jnp.zeros_like(s1)
@@ -247,7 +280,18 @@
 
 
 def attention_call(plan, q_pieces, kv_pieces, own, heads, per_dev, block_rows, after=()):
-    n_q, n_kv = (2 if own else 4), 4
+    inputs = []
+
+    def numbered(pieces):
+        out = []
+        for array, kind in pieces:
+            if not any(array is known for known in inputs):
+                inputs.append(array)
+            out.append(([array is known for known in inputs].index(True), kind))
+        return out
+
+    q_pieces, kv_pieces = numbered(q_pieces), numbered(kv_pieces)
+    n_q, n_kv = len(q_pieces), len(kv_pieces)
     spans = n_q * per_dev
     vmem, hbm = pl.BlockSpec(memory_space=pltpu.VMEM), pl.BlockSpec(memory_space=pltpu.HBM)
     f32, bf16 = jnp.float32, jnp.bfloat16
@@ -278,64 +322,80 @@
     if own:
         scratch.append(pltpu.VMEM((2, block_rows, block_rows), f32))
     return pl.pallas_call(
-        ordered(partial(attention_kernel, (heads, n_q, n_kv, per_dev, block_rows), own), len(after)),
+        ordered(
+            partial(
+                attention_kernel, (heads, per_dev, block_rows), own, q_pieces, kv_pieces, len(inputs)
+            ),
+            len(after),
+        ),
         out_shape=out_shape,
-        in_specs=[hbm] * len(after) + [pl.BlockSpec(memory_space=pltpu.SMEM)] + [hbm] * 5,
+        in_specs=[hbm] * len(after) + [pl.BlockSpec(memory_space=pltpu.SMEM)] + [hbm] * len(inputs),
         out_specs=(vmem, vmem),
         scratch_shapes=scratch,
         compiler_params=pltpu.CompilerParams(vmem_limit_bytes=VMEM_LIMIT),
         cost_estimate=pl.CostEstimate(flops=1, bytes_accessed=1, transcendentals=0),
         name="own_attention" if own else "served_attention",
-    )(*after, plan, *q_pieces, *kv_pieces)
-
-
-def pack_kernel(shape, place, q_ref, k_ref, v_ref, keep_ref, send_ref, v_scr, t_scr, sems):
-    heads, first, half, rows = shape
-    later, outs = [], (keep_ref, send_ref)
-    loads = []
-    n = 0
-    for side in range(2):
-        for h in range(heads):
-            start = pl.multiple_of((place[side] * half + first + h) * HD, HD)
-            load = pltpu.make_async_copy(v_ref.at[:, pl.ds(start, HD)], v_scr.at[side, h], sems.at[n])
-            load.start()
-            loads.append(load)
-            n += 1
+    )(*after, plan, *inputs)
+
+
+def pack_kernel(shape, place, q_ref, k_ref, v_ref, *refs):
+    heads, first, half, rows, split = shape
+    outs, (scr, t_scr, sems) = refs[:-3], refs[-3:]
+    loads, stores = {}, []
     for side in (1, 0):
         for h in range(heads):
             start = pl.multiple_of((place[side] * half + first + h) * HD, HD)
-            for i, ref in enumerate((q_ref, k_ref)):
-                copy = pltpu.make_async_copy(ref.at[:, pl.ds(start, HD)], outs[side].at[h, i], sems.at[n])
-                copy.start()
-                later.append(copy)
-                n += 1
+            for i, ref in enumerate((q_ref, k_ref, v_ref)):
+                load = pltpu.make_async_copy(
+                    ref.at[:, pl.ds(start, HD)], scr.at[side, h, i], sems.at[0, side, h, i]
+                )
+                load.start()
+                loads[side, h, i] = load
+
+    def store(side, h, i, source):
+        if split:
+            out = outs[2 * side + (i > 0)]
+            target = out.at[h, i - 1] if i else out.at[h]
+        else:
+            target = outs[side].at[h, i]
+        copy = pltpu.make_async_copy(source, target, sems.at[1, side, h, i])
+        copy.start()
+        stores.append(copy)
+
     for side in (1, 0):
         for h in range(heads):
-            loads[side * heads + h].wait()
+            for i in range(2):
+                loads[side, h, i].wait()
+                store(side, h, i, scr.at[side, h, i])
+            loads[side, h, 2].wait()
             for tile in range(rows // HD):
                 at = slice(tile * HD, (tile + 1) * HD)
-                t_scr[side, h, at, :] = v_scr[side, h, at, :].T
-            copy = pltpu.make_async_copy(t_scr.at[side, h], outs[side].at[h, 2], sems.at[n])
-            copy.start()
-            later.append(copy)
-            n += 1
-    for copy in later:
+                t_scr[side, h, at, :] = scr[side, h, 2, at, :].T
+            store(side, h, 2, t_scr.at[side, h])
+    for copy in stores:
         copy.wait()
 
 
-def pack_call(place, queries, keys, values, heads, first, half, after=()):
+def pack_call(place, queries, keys, values, heads, first, half, split, after=()):
     rows = queries.shape[0]
     hbm = pl.BlockSpec(memory_space=pltpu.HBM)
-    packed = jax.ShapeDtypeStruct((heads, 3, rows, HD), jnp.bfloat16)
+    bf16 = jnp.bfloat16
+    if split:
+        side = [
+            jax.ShapeDtypeStruct((heads, rows, HD), bf16),
+            jax.ShapeDtypeStruct((heads, 2, rows, HD), bf16),
+        ]
+    else:
+        side = [jax.ShapeDtypeStruct((heads, 3, rows, HD), bf16)]
     return pl.pallas_call(
-        ordered(partial(pack_kernel, (heads, first, half, rows)), len(after)),
-        out_shape=(packed, packed),
+        ordered(partial(pack_kernel, (heads, first, half, rows, split)), len(after)),
+        out_shape=side * 2,
         in_specs=[hbm] * len(after) + [pl.BlockSpec(memory_space=pltpu.SMEM)] + [hbm] * 3,
-        out_specs=(hbm, hbm),
+        out_specs=[hbm] * (2 * len(side)),
         scratch_shapes=[
-            pltpu.VMEM((2, heads, rows, HD), jnp.bfloat16),
-            pltpu.VMEM((2, heads, rows, HD), jnp.bfloat16),
-            pltpu.SemaphoreType.DMA((8 * heads,)),
+            pltpu.VMEM((2, heads, 3, rows, HD), bf16),
+            pltpu.VMEM((2, heads, rows, HD), bf16),
+            pltpu.SemaphoreType.DMA((2, 2, heads, 3)),
         ],
         compiler_params=pltpu.CompilerParams(vmem_limit_bytes=VMEM_LIMIT),
         cost_estimate=pl.CostEstimate(flops=1, bytes_accessed=1, transcendentals=0),
@@ -388,45 +448,54 @@
     )(*after, keep, swapped)
 
 
-def merge_kernel(shape, valid, own_ref, own_lse_ref, near_ref, far_ref, sofar_ref, keep_ref, send_ref, squares_ref):
-    heads, per_dev, block_rows = shape
+def merge_kernel(per_dev, block_rows, sizes, valid, sofar_ref, *refs):
+    inputs, (keep_ref, send_ref, squares_ref) = refs[:-3], refs[-3:]
     spans = 2 * per_dev
     squares_ref[...] = sofar_ref[...]
-    for h in range(heads):
-        lses = [own_lse_ref[h]]
-        for i, ref in enumerate((near_ref, far_ref)):
-            parts = ref[h, spans * HD :, :].astype(jnp.float32)
-            lse = parts[:spans] + parts[spans : 2 * spans] + parts[2 * spans : 3 * spans]
-            lses.append(jnp.where(valid[i] > 0, lse, -1e30))
-        top = jnp.maximum(jnp.maximum(lses[0], lses[1]), lses[2])
-        weights = [jnp.exp2(lse - top) for lse in lses]
-        scale = 1.0 / (weights[0] + weights[1] + weights[2])
-        weights = [weight * scale for weight in weights]
-        for span in range(spans):
-            rows = slice(span, span + 1)
-            tile = slice(span * HD, (span + 1) * HD)
-            mixed = weights[0][rows, :] * own_ref[h, span]
-            mixed = mixed + weights[1][rows, :] * near_ref[h, tile, :].astype(jnp.float32)
-            mixed = mixed + weights[2][rows, :] * far_ref[h, tile, :].astype(jnp.float32)
-            squares_ref[rows, :] = squares_ref[rows, :] + jnp.sum(mixed * mixed, axis=0, keepdims=True)
-            target = keep_ref if span < per_dev else send_ref
-            start = (span % per_dev) * block_rows
-            target[h, start : start + block_rows, :] = mixed.T.astype(target.dtype)
-
-
-def merge_call(valid, own, near, far, sofar, per_dev, after=()):
-    heads, spans, _, block_rows = own[0].shape
+    at = 0
+    for c, size in enumerate(sizes):
+        own_ref, own_lse_ref, near_ref, far_ref = inputs[4 * c : 4 * c + 4]
+        for h in range(size):
+            lses = [own_lse_ref[h]]
+            for i, ref in enumerate((near_ref, far_ref)):
+                parts = ref[h, spans * HD :, :].astype(jnp.float32)
+                lse = parts[:spans] + parts[spans : 2 * spans] + parts[2 * spans : 3 * spans]
+                lses.append(jnp.where(valid[i] > 0, lse, -1e30))
+            top = jnp.maximum(jnp.maximum(lses[0], lses[1]), lses[2])
+            weights = [jnp.exp2(lse - top) for lse in lses]
+            scale = 1.0 / (weights[0] + weights[1] + weights[2])
+            weights = [weight * scale for weight in weights]
+            for span in range(spans):
+                rows = slice(span, span + 1)
+                tile = slice(span * HD, (span + 1) * HD)
+                mixed = weights[0][rows, :] * own_ref[h, span]
+                mixed = mixed + weights[1][rows, :] * near_ref[h, tile, :].astype(jnp.float32)
+                mixed = mixed + weights[2][rows, :] * far_ref[h, tile, :].astype(jnp.float32)
+                squares_ref[rows, :] = squares_ref[rows, :] + jnp.sum(mixed * mixed, axis=0, keepdims=True)
+                target = keep_ref if span < per_dev else send_ref
+                start = (span % per_dev) * block_rows
+                target[at, start : start + block_rows, :] = mixed.T.astype(target.dtype)
+            at += 1
+
+
+def merge_call(valid, sofar, parts, per_dev, after=()):
+    block_rows = sofar.shape[1]
+    sizes = [own[0].shape[0] for own, _, _ in parts]
+    arrays = [array for own, near, far in parts for array in (*own, near, far)]
     vmem = pl.BlockSpec(memory_space=pltpu.VMEM)
-    packed = jax.ShapeDtypeStruct((heads, per_dev * block_rows, HD), jnp.bfloat16)
+    hbm = pl.BlockSpec(memory_space=pltpu.HBM)
+    packed = jax.ShapeDtypeStruct((sum(sizes), per_dev * block_rows, HD), jnp.bfloat16)
     return pl.pallas_call(
-        ordered(partial(merge_kernel, (heads, per_dev, block_rows)), len(after)),
-        out_shape=(packed, packed, jax.ShapeDtypeStruct((spans, block_rows), jnp.float32)),
-        in_specs=[pl.BlockSpec(memory_space=pltpu.HBM)] * len(after) + [pl.BlockSpec(memory_space=pltpu.SMEM)] + [vmem] * 5,
+        ordered(partial(merge_kernel, per_dev, block_rows, sizes), len(after)),
+        out_shape=(packed, packed, jax.ShapeDtypeStruct(sofar.shape, jnp.float32)),
+        in_specs=[hbm] * len(after)
+        + [pl.BlockSpec(memory_space=pltpu.SMEM)]
+        + [vmem] * (1 + len(arrays)),
         out_specs=(vmem, vmem, vmem),
         compiler_params=pltpu.CompilerParams(vmem_limit_bytes=VMEM_LIMIT),
         cost_estimate=pl.CostEstimate(flops=1, bytes_accessed=1, transcendentals=0),
         name="merge",
-    )(*after, valid, own[0], own[1], near, far, sofar)
+    )(*after, valid, sofar, *arrays)
 
 
 def finish_kernel(per_dev, sizes, place, *refs):
@@ -492,9 +561,12 @@
     spans = 2 * per_dev
     half = width // HD // 2
 
+    sent = {}
+
     def to(array, pairs, name):
         with jax.named_scope(name):
-            return lax.ppermute(array, "ctx", pairs)
+            sent[name] = lax.ppermute(array, "ctx", pairs)
+        return sent[name]
 
     swap = [(d, d ^ 1) for d in range(8)]
     lift = [(0, 2), (1, 3)]
@@ -535,64 +607,82 @@
     live = (others != jnp.concatenate([ids(level + 1), ids(level + 2)], axis=0)) & mine
     served_plan = plan_of(live, slot, jnp.zeros_like(others), 2 * spans)
 
-    sizes = [1] * half
+    sizes, split, order = SIZES, SPLIT, ORDER
     n = len(sizes)
-    packs, lows, nears, fars, levels = [None] * n, [None] * n, [None] * n, [None] * n, [None] * n
-    ups, owns, kept, returned = [None] * n, [None] * n, [None] * n, [None] * n
+    own_pieces, z_arrays, served_pieces = [None] * n, [None] * n, [None] * n
+    ups, owns, kept, returned = [None] * n, [None] * n, [], []
     squares = [jnp.zeros((spans, block_rows), jnp.float32)]
     last = []
 
-    def pack(c, after=()):
-        keep, send = pack_call(
-            place, queries, keys, values, sizes[c], sum(sizes[:c]), half, (*after, *last)
+    def pack(c):
+        packed = pack_call(
+            place, queries, keys, values, sizes[c], sum(sizes[:c]), half, split[c], last
         )
+        last[:] = [packed[0]]
+        if split[c]:
+            q_keep, kv_keep, q_send, kv_send = packed
+            z_arrays[c] = (q_keep, kv_keep)
+            kv_swap = to(kv_send, swap, f"swap_kv_c{c}")
+            q_swap = to(q_send, swap, f"swap_q_c{c}")
+            own_pieces[c] = (
+                [(q_keep, "head"), (q_swap, "head")],
+                [(kv_keep, "head"), (kv_swap, "head")],
+            )
+        else:
+            keep, send = packed
+            swapped = to(send, swap, f"swap_c{c}")
+            z_arrays[c] = (keep, swapped)
+            own_pieces[c] = (
+                [(keep, "queries"), (swapped, "queries")],
+                [(keep, "keys_values"), (swapped, "keys_values")],
+            )
+
+    def downs(c, q, kv, name):
+        low = to(kv, lift, f"lift_{name}c{c}")
+        far = to(q, far_down, f"far_down_{name}c{c}")
+        return to(q, near_down, f"near_down_{name}c{c}"), far, low
+
+    def join(c):
+        if split[c]:
+            (q_keep, q_swap), (kv_keep, kv_swap) = own_pieces[c]
+            keeps = downs(c, q_keep[0], kv_keep[0], "keep_")
+            swaps = downs(c, q_swap[0], kv_swap[0], "recv_")
+            near, far, low = [[(k, "head"), (r, "head")] for k, r in zip(keeps, swaps)]
+        else:
+            level_q, level_kv = join_call(*z_arrays[c], last)
+            last[:] = [level_q]
+            near, far, low = [
+                [(array, "first"), (array, "second")] for array in downs(c, level_q, level_kv, "")
+            ]
+        served_pieces[c] = (near + far, own_pieces[c][1] + low)
+
+    def serve(c):
+        near, far = attention_call(
+            served_plan, *served_pieces[c], False, sizes[c], per_dev, block_rows, last
+        )
+        last[:] = [near]
+        far = to(far, far_up, f"far_up_c{c}")
+        ups[c] = (to(near, near_up, f"near_up_c{c}"), far)
+
+    def attend(c):
+        owns[c] = attention_call(
+            own_plan, own_pieces[c][0], served_pieces[c][1], True, sizes[c], per_dev, block_rows, last
+        )
+        last[:] = [owns[c][1]]
+
+    def merge(*chunks):
+        parts = [(owns[c], *ups[c]) for c in chunks]
+        keep, send, squares[0] = merge_call(valid, squares[0], parts, per_dev, last)
         last[:] = [keep]
-        packs[c] = (keep, to(send, swap, f"swap_c{c}"))
-
-    def join(c):
-        level_q, level_kv = join_call(*packs[c], last)
-        last[:] = [level_q]
-        lows[c] = to(level_kv, lift, f"lift_c{c}")
-        fars[c] = to(level_q, far_down, f"far_down_c{c}")
-        nears[c] = to(level_q, near_down, f"near_down_c{c}")
-
-    def serve(c):
-        kv, q = [*packs[c], lows[c]], [nears[c], fars[c]]
-        near, far = attention_call(served_plan, q, kv, False, sizes[c], per_dev, block_rows, last)
-        last[:] = [near]
-        ups[c] = (to(near, near_up, f"near_up_c{c}"), to(far, far_up, f"far_up_c{c}"))
-
-    def attend(c):
-        kv = [*packs[c], lows[c]]
-        owns[c] = attention_call(own_plan, packs[c], kv, True, sizes[c], per_dev, block_rows, last)
-        last[:] = [owns[c][1]]
-
-    def merge(c):
-        keep, send, total = merge_call(valid, owns[c], *ups[c], squares[0], per_dev, last)
-        squares[0] = total
-        last[:] = [keep]
-        kept[c], returned[c] = keep, to(send, swap, f"back_c{c}")
-
-    pack(0)
-    pack(1, (own_plan, served_plan))
-    join(0)
-    pack(2)
-    join(1)
-    serve(0)
-    attend(0)
-    join(2)
-    pack(3)
-    serve(1)
-    attend(1)
-    merge(0)
-    join(3)
-    serve(2)
-    attend(2)
-    merge(1)
-    serve(3)
-    merge(2)
-    attend(3)
-    merge(3)
+        kept.append(keep)
+        returned.append(to(send, swap, f"back_c{chunks[0]}"))
+
+    steps = {"p": pack, "j": join, "s": serve, "a": attend, "m": merge}
+    for what, *args in order:
+        if what == "w":
+            last.extend([own_plan, served_plan] if args[0] == "plans" else [sent[args[0]]])
+        else:
+            steps[what](*args)
     squares = squares[0]
     square = squares[:per_dev] + to(squares[per_dev:], swap, "squares_swap")
     n_head = lax.axis_size("head")

time: 198 us -> 206 us (1.040)
  Pallas kernels: 52.9 us -> 75.2 us
  waiting for transfers between devices: 62 us -> 44.4 us
  local copies, waits for them, and re-layouts: 11 us -> 6.18 us
  starting transfers between devices: 63.4 us -> 67.2 us
  other arithmetic: 3.56 us -> 6.73 us
    ppermute x32, waiting for transfers between devices: 58.8 us -> 41.7 us  [to(): sent[name] = lax.ppermute(array, 'ctx', pairs)]
    pallas_call x16, Pallas kernels: 45.9 us -> 62.1 us  [the longest x8 39 us: attention_call(): pl.pallas_call(ordered(partial(attention_kernel, (heads, per_dev, block_r...]
    unnamed x44 -> x22, local copies, waits for them, and re-layouts: 10.1 us -> 3.44 us
    pallas_call x4, Pallas kernels: 4.17 us -> 9.29 us  [join_call(): pl.pallas_call(ordered(partial(join_kernel, heads), len(after)), out_shap...]
    ppermute x32, starting transfers between devices: 61.9 us -> 65.7 us  [to(): sent[name] = lax.ppermute(array, 'ctx', pairs)]
  transfers between devices with their start and end apart: 34 -> 34, of which waited for: 9 -> 9; matrix products, arithmetic and copies ran while one was open for 2% -> 5% of each run, Pallas kernels for 25% -> 35%
where the time goes in v4:
time: 206 us; the launch traced here: 202 us
  Pallas kernels  75.2 us (37%)
  starting transfers between devices  67.2 us (33%)
  waiting for transfers between devices  44.4 us (22%)
  other arithmetic  6.73 us (3%)
  local copies, waits for them, and re-layouts  6.18 us (3%)
  between operations  2.77 us (1%)
    ppermute x32, starting transfers between devices, to(): sent[name] = lax.ppermute(array, 'ctx', pairs)  65.7 us
    ppermute x32, waiting for transfers between devices, to(): sent[name] = lax.ppermute(array, 'ctx', pairs)  41.7 us
    pallas_call x8, Pallas kernels, attention_call(): pl.pallas_call(ordered(partial(attention_kernel, (heads, per_dev, block_r...  39 us
    pallas_call x4, Pallas kernels, pack_call(): pl.pallas_call(ordered(partial(pack_kernel, (heads, first, half, rows, sp...  12.1 us
    pallas_call x4, Pallas kernels, merge_call(): pl.pallas_call(ordered(partial(merge_kernel, per_dev, block_rows, sizes),...  11 us
    pallas_call x4, Pallas kernels, join_call(): pl.pallas_call(ordered(partial(join_kernel, heads), len(after)), out_shap...  9.29 us
  transfers between devices with their start and end apart: 34, of which 9 were waited for; matrix products, arithmetic and copies ran while one was open for 5% of the time, Pallas kernels for 35%

profile of v4, /device:TPU:24, one launch (start us, length us, event | category | flops | bytes accessed | tf_op | source)
XLA Modules:
  0.0 202.4 jit_solution(9553776114527851000)
XLA Ops:
  0.0 1.5 collective-permute-start
  2.1 3.1 %pack.4 = (bf16[1,3,1024,128]{3,2,1,0:T(8,128)(2,1)}, bf16[1,3,1024,128]{3,2,1,0:T(8,128)(2,1)}) custom-call(s32[2]{0:T(128)} %pad_add_fusion.3.refs_0_.refs_3_.refs_1_.place, bf16[1024,1024]{1,0:T(8,128)(2,1)} %refs_2_.5, bf16[1024,1024]{1,0:T(8,128)(2,1)} %refs_3_.5, bf16[1024,1024]{1,0:T(8,128)(2,1)} %refs_4_.5), custom_call_target="tpu_custom_call" | custom-call | flops 1 | bytes 1 | tf_op jit(solution)/shard_map/pack/pallas_call | solution.py:390
  6.7 2.4 %collective-permute-start.1 = (s32[8,8]{1,0:T(8,128)S(1)}, s32[8,8]{1,0:T(8,128)S(1)}, u32[]{:S(2)}, u32[]{:S(2)}) collective-permute-start(s32[8,8]{1,0:T(8,128)S(1)} %pad_add_fusion.1), channel_id=1, source_target_pairs={{16,8},{20,12},{24,16},{28,20},{17,9},{21,13},{25,17},{29,21},{18,... | collective-permute-start | bytes 776 | tf_op jit(solution)/shard_map/selection_near/ppermute | solution.py:568
  17.0 3.0 %pack.5 = (bf16[1,3,1024,128]{3,2,1,0:T(8,128)(2,1)}, bf16[1,3,1024,128]{3,2,1,0:T(8,128)(2,1)}) custom-call(bf16[1,3,1024,128]{3,2,1,0:T(8,128)(2,1)} %get-tuple-element.49.refs_0_.refs_1_.refs_4_.refs_2_, s32[81]{0:T(128)} %pad_add_fusion.5.refs_1_.refs_2_, s32[129]{0:T(256)} %pad_add_fusion.2.refs_2_.refs_1_, ...), custom_call_target="tpu_custom_call" | custom-call | flops 1 | bytes 1 | tf_op jit(solution)/shard_map/pack/pallas_call | solution.py:390
  19.9 1.6 collective-permute-start.4
  21.5 4.5 %collective-permute-done.3.refs_2_.refs_5_.refs_3_ = bf16[1,3,1024,128]{3,2,1,0:T(8,128)(2,1)S(1)} collective-permute-done((bf16[1,3,1024,128]{3,2,1,0:T(8,128)(2,1)}, bf16[1,3,1024,128]{3,2,1,0:T(8,128)(2,1)S(1)}, u32[]{:S(2)}, u32[]{:S(2)}) %collective-permute-start.3) | collective-permute-done | bytes 786464 | tf_op jit(solution)/shard_map/swap_c0/ppermute | solution.py:568
  26.8 2.3 %join.4 = (bf16[2,1,1024,128]{3,2,1,0:T(8,128)(2,1)}, bf16[2,1,2,1024,128]{4,3,2,1,0:T(8,128)(2,1)}) custom-call(bf16[1,3,1024,128]{3,2,1,0:T(8,128)(2,1)} %get-tuple-element.50.refs_0_.refs_1_.refs_4_.refs_2_, bf16[1,3,1024,128]{3,2,1,0:T(8,128)(2,1)} %get-tuple-element.49.refs_0_.refs_1_.refs_4_.refs_2_, bf16[1,3,1024,128]{3,2,1,0:T(8,128)(2,1)} %copy-done), custom_call_target="tpu_custom_call" | custom-call | flops 1 | bytes 1 | tf_op jit(solution)/shard_map/join/pallas_call | solution.py:433
  29.2 1.7 collective-permute-start.7
  30.8 2.4 %collective-permute-start.5 = (bf16[2,1,1024,128]{3,2,1,0:T(8,128)(2,1)}, bf16[2,1,1024,128]{3,2,1,0:T(8,128)(2,1)S(1)}, u32[]{:S(2)}, u32[]{:S(2)}) collective-permute-start(bf16[2,1,1024,128]{3,2,1,0:T(8,128)(2,1)} %get-tuple-element.52.refs_0_), channel_id=1, source_target_pairs={{16,8},{20,12},{24,16},{28,20},{17,9},{21,13},{25,17},{29,21},{18,... | collective-permute-start | bytes 1572872 | tf_op jit(solution)/shard_map/near_down_c0/ppermute | solution.py:568
  33.2 2.1 %collective-permute-start.6 = (bf16[2,1,1024,128]{3,2,1,0:T(8,128)(2,1)}, bf16[2,1,1024,128]{3,2,1,0:T(8,128)(2,1)}, u32[]{:S(2)}, u32[]{:S(2)}) collective-permute-start(bf16[2,1,1024,128]{3,2,1,0:T(8,128)(2,1)} %get-tuple-element.52.refs_0_), channel_id=1, source_target_pairs={{24,8},{28,12},{25,9},{29,13},{26,10},{30,14},{27,11},{31,15}} | collective-permute-start | bytes 1572872 | tf_op jit(solution)/shard_map/far_down_c0/ppermute | solution.py:568
  35.3 3.0 %pack.6 = (bf16[1,3,1024,128]{3,2,1,0:T(8,128)(2,1)}, bf16[1,3,1024,128]{3,2,1,0:T(8,128)(2,1)}) custom-call(bf16[2,1,1024,128]{3,2,1,0:T(8,128)(2,1)} %get-tuple-element.52.refs_0_, s32[2]{0:T(128)} %pad_add_fusion.3.refs_0_.refs_3_.refs_1_.place, bf16[1024,1024]{1,0:T(8,128)(2,1)} %refs_2_.5, bf16[1024,1024]{1,0:T(8,128)(2,1)} %refs_3_.5, ...), custom_call_target="tpu_custom_call" | custom-call | flops 1 | bytes 1 | tf_op jit(solution)/shard_map/pack/pallas_call | solution.py:390
  38.9 4.0 %collective-permute-done.4.refs_2_.refs_5_.refs_3_ = bf16[1,3,1024,128]{3,2,1,0:T(8,128)(2,1)} collective-permute-done((bf16[1,3,1024,128]{3,2,1,0:T(8,128)(2,1)}, bf16[1,3,1024,128]{3,2,1,0:T(8,128)(2,1)}, u32[]{:S(2)}, u32[]{:S(2)}) %collective-permute-start.4) | collective-permute-done | bytes 786464 | tf_op jit(solution)/shard_map/swap_c1/ppermute | solution.py:568
  42.9 2.3 %join.5 = (bf16[2,1,1024,128]{3,2,1,0:T(8,128)(2,1)}, bf16[2,1,2,1024,128]{4,3,2,1,0:T(8,128)(2,1)}) custom-call(bf16[1,3,1024,128]{3,2,1,0:T(8,128)(2,1)} %get-tuple-element.53.refs_0_.refs_1_.refs_4_.refs_3_, bf16[1,3,1024,128]{3,2,1,0:T(8,128)(2,1)} %get-tuple-element.50.refs_0_.refs_1_.refs_4_.refs_2_, ...), custom_call_target="tpu_custom_call" | custom-call | flops 1 | bytes 1 | tf_op jit(solution)/shard_map/join/pallas_call | solution.py:433
  45.2 1.7 collective-permute-start.11
  46.9 2.7 %collective-permute-start.10 = (bf16[2,1,1024,128]{3,2,1,0:T(8,128)(2,1)}, bf16[2,1,1024,128]{3,2,1,0:T(8,128)(2,1)}, u32[]{:S(2)}, u32[]{:S(2)}) collective-permute-start(bf16[2,1,1024,128]{3,2,1,0:T(8,128)(2,1)} %get-tuple-element.55.refs_0_), channel_id=1, source_target_pairs={{24,8},{28,12},{25,9},{29,13},{26,10},{30,14},{27,11},{31,15}} | collective-permute-start | bytes 1572872 | tf_op jit(solution)/shard_map/far_down_c1/ppermute | solution.py:568
  49.6 7.5 %collective-permute-done.6.refs_3_ = bf16[2,1,1024,128]{3,2,1,0:T(8,128)(2,1)} collective-permute-done((bf16[2,1,1024,128]{3,2,1,0:T(8,128)(2,1)}, bf16[2,1,1024,128]{3,2,1,0:T(8,128)(2,1)}, u32[]{:S(2)}, u32[]{:S(2)}) %collective-permute-start.6) | collective-permute-done | bytes 524320 | tf_op jit(solution)/shard_map/far_down_c0/ppermute | solution.py:568
  57.1 2.1 %collective-permute-start.9 = (bf16[2,1,1024,128]{3,2,1,0:T(8,128)(2,1)}, bf16[2,1,1024,128]{3,2,1,0:T(8,128)(2,1)}, u32[]{:S(2)}, u32[]{:S(2)}) collective-permute-start(bf16[2,1,1024,128]{3,2,1,0:T(8,128)(2,1)} %get-tuple-element.55.refs_0_), channel_id=1, source_target_pairs={{16,8},{20,12},{24,16},{28,20},{17,9},{21,13},{25,17},{29,21},{18,... | collective-permute-start | bytes 1572872 | tf_op jit(solution)/shard_map/near_down_c1/ppermute | solution.py:568
  59.2 3.0 %pack.7 = (bf16[1,3,1024,128]{3,2,1,0:T(8,128)(2,1)}, bf16[1,3,1024,128]{3,2,1,0:T(8,128)(2,1)}) custom-call(bf16[2,1,1024,128]{3,2,1,0:T(8,128)(2,1)} %get-tuple-element.55.refs_0_, s32[2]{0:T(128)} %pad_add_fusion.3.refs_0_.refs_3_.refs_1_.place, bf16[1024,1024]{1,0:T(8,128)(2,1)} %refs_2_.5, bf16[1024,1024]{1,0:T(8,128)(2,1)} %refs_3_.5, ...), custom_call_target="tpu_custom_call" | custom-call | flops 1 | bytes 1 | tf_op jit(solution)/shard_map/pack/pallas_call | solution.py:390
  62.9 3.7 %served_attention.4 = (bf16[1,1056,256]{2,1,0:T(8,128)(2,1)}, bf16[1,1056,256]{2,1,0:T(8,128)(2,1)}) custom-call(bf16[1,3,1024,128]{3,2,1,0:T(8,128)(2,1)} %get-tuple-element.56.refs_0_.refs_1_.refs_4_.refs_2_, s32[129]{0:T(256)} %pad_add_fusion.2.refs_2_.refs_1_, bf16[2,1,1024,128]{3,2,1,0:T(8,128)(2,1)} %copy-done.4, ...), custom_call_target="tpu_custom_call" | custom-call | flops 1 | bytes 1 | tf_op jit(solution)/shard_map/served_attention/pallas_call | solution.py:324
  66.6 1.7 collective-permute-done.10.refs_3_
  71.0 6.0 %own_attention.4 = (f32[1,8,128,256]{3,2,1,0:T(8,128)}, f32[1,8,256]{2,1,0:T(8,128)}) custom-call(bf16[1,1056,256]{2,1,0:T(8,128)(2,1)} %get-tuple-element.58.refs_0_, s32[81]{0:T(128)} %pad_add_fusion.5.refs_1_.refs_2_, bf16[1,3,1024,128]{3,2,1,0:T(8,128)(2,1)} %get-tuple-element.49.refs_0_.refs_1_.refs_4_.refs_2_, bf16[1,3,1024,128]{3,2,1,0:T(8,128)(2,1)} %copy-done, ...), custom_call_target="tpu_custom_call" | custom-call | flops 1 | bytes 1 | tf_op jit(solution)/shard_map/own_attention/pallas_call | solution.py:324
  76.9 2.3 %join.6 = (bf16[2,1,1024,128]{3,2,1,0:T(8,128)(2,1)}, bf16[2,1,2,1024,128]{4,3,2,1,0:T(8,128)(2,1)}) custom-call(f32[1,8,256]{2,1,0:T(8,128)} %get-tuple-element.59.refs_0_.refs_5_, bf16[1,3,1024,128]{3,2,1,0:T(8,128)(2,1)} %get-tuple-element.53.refs_0_.refs_1_.refs_4_.refs_3_, bf16[1,3,1024,128]{3,2,1,0:T(8,128)(2,1)} %collective-permute-done.8.refs_2_.refs_5_.refs_4_), custom_call_target="tpu_custom_call" | custom-call | flops 1 | bytes 1 | tf_op jit(solution)/shard_map/join/pallas_call | solution.py:433
  79.3 1.7 collective-permute-start.17
  80.9 7.0 %collective-permute-start.15 = (bf16[2,1,1024,128]{3,2,1,0:T(8,128)(2,1)}, bf16[2,1,1024,128]{3,2,1,0:T(8,128)(2,1)}, u32[]{:S(2)}, u32[]{:S(2)}) collective-permute-start(bf16[2,1,1024,128]{3,2,1,0:T(8,128)(2,1)} %get-tuple-element.61.refs_0_), channel_id=1, source_target_pairs={{16,8},{20,12},{24,16},{28,20},{17,9},{21,13},{25,17},{29,21},{18,... | collective-permute-start | bytes 1572872 | tf_op jit(solution)/shard_map/near_down_c2/ppermute | solution.py:568
  88.6 3.7 %served_attention.5 = (bf16[1,1056,256]{2,1,0:T(8,128)(2,1)}, bf16[1,1056,256]{2,1,0:T(8,128)(2,1)}) custom-call(bf16[2,1,1024,128]{3,2,1,0:T(8,128)(2,1)} %get-tuple-element.61.refs_0_, s32[129]{0:T(256)} %pad_add_fusion.2.refs_2_.refs_1_, bf16[2,1,1024,128]{3,2,1,0:T(8,128)(2,1)} %collective-permute-done.9.refs_2_, ...), custom_call_target="tpu_custom_call" | custom-call | flops 1 | bytes 1 | tf_op jit(solution)/shard_map/served_attention/pallas_call | solution.py:324
  92.3 6.0 %own_attention.5 = (f32[1,8,128,256]{3,2,1,0:T(8,128)}, f32[1,8,256]{2,1,0:T(8,128)}) custom-call(bf16[1,1056,256]{2,1,0:T(8,128)(2,1)} %get-tuple-element.63.refs_0_, s32[81]{0:T(128)} %pad_add_fusion.5.refs_1_.refs_2_, bf16[1,3,1024,128]{3,2,1,0:T(8,128)(2,1)} %get-tuple-element.50.refs_0_.refs_1_.refs_4_.refs_2_, ...), custom_call_target="tpu_custom_call" | custom-call | flops 1 | bytes 1 | tf_op jit(solution)/shard_map/own_attention/pallas_call | solution.py:324
  98.3 10.0 %collective-permute-start.16 = (bf16[2,1,1024,128]{3,2,1,0:T(8,128)(2,1)}, bf16[2,1,1024,128]{3,2,1,0:T(8,128)(2,1)}, u32[]{:S(2)}, u32[]{:S(2)}) collective-permute-start(bf16[2,1,1024,128]{3,2,1,0:T(8,128)(2,1)} %get-tuple-element.61.refs_0_), channel_id=1, source_target_pairs={{24,8},{28,12},{25,9},{29,13},{26,10},{30,14},{27,11},{31,15}} | collective-permute-start | bytes 1572872 | tf_op jit(solution)/shard_map/far_down_c2/ppermute | solution.py:568
  108.9 2.8 %merge.4 = (bf16[1,1024,128]{2,1,0:T(8,128)(2,1)}, bf16[1,1024,128]{2,1,0:T(8,128)(2,1)}, f32[8,256]{1,0:T(8,128)}) custom-call(f32[1,8,256]{2,1,0:T(8,128)} %get-tuple-element.64.refs_0_.refs_4_, bf16[2,1,2,1024,128]{4,3,2,1,0:T(8,128)(2,1)} %collective-permute-done.11.refs_6_.refs_4_.refs_1_, s32[2]{0:T(128)} %add_convert_fusion.refs_2_.refs_1_, ...), custom_call_target="tpu_custom_call" | custom-call | flops 1 | bytes 1 | tf_op jit(solution)/shard_map/merge/pallas_call | solution.py:488
  112.5 2.3 %join.7 = (bf16[2,1,1024,128]{3,2,1,0:T(8,128)(2,1)}, bf16[2,1,2,1024,128]{4,3,2,1,0:T(8,128)(2,1)}) custom-call(bf16[1,1024,128]{2,1,0:T(8,128)(2,1)} %get-tuple-element.67.refs_0_, bf16[1,3,1024,128]{3,2,1,0:T(8,128)(2,1)} %get-tuple-element.56.refs_0_.refs_1_.refs_4_.refs_2_, bf16[1,3,1024,128]{3,2,1,0:T(8,128)(2,1)} %copy-done.1), custom_call_target="tpu_custom_call" | custom-call | flops 1 | bytes 1 | tf_op jit(solution)/shard_map/join/pallas_call | solution.py:433
  114.8 1.7 collective-permute-start.22
  119.1 5.5 %collective-permute-start.20 = (bf16[2,1,1024,128]{3,2,1,0:T(8,128)(2,1)}, bf16[2,1,1024,128]{3,2,1,0:T(8,128)(2,1)}, u32[]{:S(2)}, u32[]{:S(2)}) collective-permute-start(bf16[2,1,1024,128]{3,2,1,0:T(8,128)(2,1)} %get-tuple-element.69.refs_0_), channel_id=1, source_target_pairs={{16,8},{20,12},{24,16},{28,20},{17,9},{21,13},{25,17},{29,21},{18,... | collective-permute-start | bytes 1572872 | tf_op jit(solution)/shard_map/near_down_c3/ppermute | solution.py:568
  124.6 2.9 %collective-permute-start.21 = (bf16[2,1,1024,128]{3,2,1,0:T(8,128)(2,1)}, bf16[2,1,1024,128]{3,2,1,0:T(8,128)(2,1)}, u32[]{:S(2)}, u32[]{:S(2)}) collective-permute-start(bf16[2,1,1024,128]{3,2,1,0:T(8,128)(2,1)} %get-tuple-element.69.refs_0_), channel_id=1, source_target_pairs={{24,8},{28,12},{25,9},{29,13},{26,10},{30,14},{27,11},{31,15}} | collective-permute-start | bytes 1572872 | tf_op jit(solution)/shard_map/far_down_c3/ppermute | solution.py:568
  127.5 3.8 %served_attention.6 = (bf16[1,1056,256]{2,1,0:T(8,128)(2,1)}, bf16[1,1056,256]{2,1,0:T(8,128)(2,1)}) custom-call(bf16[2,1,1024,128]{3,2,1,0:T(8,128)(2,1)} %get-tuple-element.69.refs_0_, s32[129]{0:T(256)} %pad_add_fusion.2.refs_2_.refs_1_, bf16[2,1,1024,128]{3,2,1,0:T(8,128)(2,1)} %collective-permute-done.15.refs_2_, ...), custom_call_target="tpu_custom_call" | custom-call | flops 1 | bytes 1 | tf_op jit(solution)/shard_map/served_attention/pallas_call | solution.py:324
  131.3 12.6 %collective-permute-done.18.refs_1_.refs_5_ = bf16[1,1056,256]{2,1,0:T(8,128)(2,1)S(1)} collective-permute-done((bf16[1,1056,256]{2,1,0:T(8,128)(2,1)}, bf16[1,1056,256]{2,1,0:T(8,128)(2,1)S(1)}, u32[]{:S(2)}, u32[]{:S(2)}) %collective-permute-start.18) | collective-permute-done | bytes 540704 | tf_op jit(solution)/shard_map/near_up_c1/ppermute | solution.py:568
  145.2 6.0 %own_attention.6 = (f32[1,8,128,256]{3,2,1,0:T(8,128)}, f32[1,8,256]{2,1,0:T(8,128)}) custom-call(bf16[1,1056,256]{2,1,0:T(8,128)(2,1)} %get-tuple-element.71.refs_0_, bf16[1,1056,256]{2,1,0:T(8,128)(2,1)} %copy-done.2, s32[81]{0:T(128)} %pad_add_fusion.5.refs_1_.refs_2_, bf16[1,3,1024,128]{3,2,1,0:T(8,128)(2,1)} %get-tuple-element.53.refs_0_.refs_1_.refs_4_.refs_3_, ...), custom_call_target="tpu_custom_call" | custom-call | flops 1 | bytes 1 | tf_op jit(solution)/shard_map/own_attention/pallas_call | solution.py:324
  152.5 2.7 %merge.5 = (bf16[1,1024,128]{2,1,0:T(8,128)(2,1)}, bf16[1,1024,128]{2,1,0:T(8,128)(2,1)}, f32[8,256]{1,0:T(8,128)}) custom-call(f32[1,8,256]{2,1,0:T(8,128)} %get-tuple-element.72.refs_0_.refs_4_, s32[2]{0:T(128)} %add_convert_fusion.refs_2_.refs_1_, f32[8,256]{1,0:T(8,128)} %get-tuple-element.73.refs_2_, f32[1,8,128,256]{3,2,1,0:T(8,128)} %get-tuple-element.74.refs_3_, ...), custom_call_target="tpu_custom_call" | custom-call | flops 1 | bytes 1 | tf_op jit(solution)/shard_map/merge/pallas_call | solution.py:488
  155.2 3.7 %served_attention.7 = (bf16[1,1056,256]{2,1,0:T(8,128)(2,1)}, bf16[1,1056,256]{2,1,0:T(8,128)(2,1)}) custom-call(bf16[1,1024,128]{2,1,0:T(8,128)(2,1)} %get-tuple-element.76.refs_0_.refs_1_, s32[129]{0:T(256)} %pad_add_fusion.2.refs_2_.refs_1_, bf16[2,1,1024,128]{3,2,1,0:T(8,128)(2,1)} %collective-permute-done.20.refs_2_, ...), custom_call_target="tpu_custom_call" | custom-call | flops 1 | bytes 1 | tf_op jit(solution)/shard_map/served_attention/pallas_call | solution.py:324
  161.5 1.6 collective-permute-start.27
  163.1 7.4 %collective-permute-done.23.refs_5_ = bf16[1,1056,256]{2,1,0:T(8,128)(2,1)} collective-permute-done((bf16[1,1056,256]{2,1,0:T(8,128)(2,1)}, bf16[1,1056,256]{2,1,0:T(8,128)(2,1)}, u32[]{:S(2)}, u32[]{:S(2)}) %collective-permute-start.23) | collective-permute-done | bytes 540704 | tf_op jit(solution)/shard_map/near_up_c2/ppermute | solution.py:568
  170.5 1.5 collective-permute-start.28
  172.8 2.8 %merge.6 = (bf16[1,1024,128]{2,1,0:T(8,128)(2,1)}, bf16[1,1024,128]{2,1,0:T(8,128)(2,1)}, f32[8,256]{1,0:T(8,128)}) custom-call(bf16[1,1056,256]{2,1,0:T(8,128)(2,1)} %get-tuple-element.78.refs_0_, s32[2]{0:T(128)} %add_convert_fusion.refs_2_.refs_1_, f32[8,256]{1,0:T(8,128)} %get-tuple-element.79.refs_2_, f32[1,8,128,256]{3,2,1,0:T(8,128)} %get-tuple-element.80.refs_3_, ...), custom_call_target="tpu_custom_call" | custom-call | flops 1 | bytes 1 | tf_op jit(solution)/shard_map/merge/pallas_call | solution.py:488
  176.2 6.1 %own_attention.7 = (f32[1,8,128,256]{3,2,1,0:T(8,128)}, f32[1,8,256]{2,1,0:T(8,128)}) custom-call(bf16[1,1024,128]{2,1,0:T(8,128)(2,1)} %get-tuple-element.82.refs_0_.refs_2_, s32[81]{0:T(128)} %pad_add_fusion.5.refs_1_.refs_2_, bf16[1,3,1024,128]{3,2,1,0:T(8,128)(2,1)} %get-tuple-element.56.refs_0_.refs_1_.refs_4_.refs_2_, ...), custom_call_target="tpu_custom_call" | custom-call | flops 1 | bytes 1 | tf_op jit(solution)/shard_map/own_attention/pallas_call | solution.py:324
  182.3 2.8 %merge.7 = (bf16[1,1024,128]{2,1,0:T(8,128)(2,1)}, bf16[1,1024,128]{2,1,0:T(8,128)(2,1)}, f32[8,256]{1,0:T(8,128)}) custom-call(f32[1,8,256]{2,1,0:T(8,128)} %get-tuple-element.83.refs_0_.refs_4_, s32[2]{0:T(128)} %add_convert_fusion.refs_2_.refs_1_, f32[8,256]{1,0:T(8,128)} %get-tuple-element.84.refs_2_, f32[1,8,128,256]{3,2,1,0:T(8,128)} %get-tuple-element.85.refs_3_, ...), custom_call_target="tpu_custom_call" | custom-call | flops 1 | bytes 1 | tf_op jit(solution)/shard_map/merge/pallas_call | solution.py:488
  185.0 1.5 collective-permute-start.30
  187.8 3.9 %collective-permute-done.31 = f32[4,256]{1,0:T(4,128)S(1)} collective-permute-done((f32[4,256]{1,0:T(4,128)S(1)}, f32[4,256]{1,0:T(4,128)S(1)}, u32[]{:S(2)}, u32[]{:S(2)}) %collective-permute-start.31) | collective-permute-done | bytes 4128 | tf_op jit(solution)/shard_map/squares_swap/ppermute | solution.py:568
  193.5 1.5 collective-permute-start.33
  195.7 1.5 collective-permute-done.33
  198.6 3.8 %finish.1 = bf16[1024,1024]{1,0:T(8,128)(2,1)} custom-call(s32[2]{0:T(128)} %pad_add_fusion.3.refs_0_.refs_3_.refs_1_.place, bf16[1,1024,128]{2,1,0:T(8,128)(2,1)} %get-tuple-element.67.refs_0_, bf16[1,1024,128]{2,1,0:T(8,128)(2,1)} %get-tuple-element.76.refs_0_.refs_1_, bf16[1,1024,128]{2,1,0:T(8,128)(2,1)} %get-tuple-element.82.refs_0_.refs_2_, ...), custom_call_target="tpu_custom_call" | custom-call | flops 1 | bytes 1 | tf_op jit(solution)/shard_map/finish/pallas_call | solution.py:525
  (113 shorter events, 28.6 us)
Async XLA Ops:
  0.0 6.6 %collective-permute-start = (s32[4,8]{1,0:T(4,128)}, s32[4,8]{1,0:T(4,128)S(1)}, u32[]{:S(2)}, u32[]{:S(2)}) collective-permute-start(s32[4,8]{1,0:T(4,128)} %param.8), channel_id=1, source_target_pairs={{0,4},{4,0},{8,12},{12,8},{16,20},{20,16},{24,28},{28,24},{1,5},{5... | collective-permute-start | bytes 392 | tf_op jit(solution)/shard_map/selection_swap/ppermute | solution.py:568
  2.1 4.6 %copy-start.10 = (s32[4,8]{1,0:T(4,128)S(1)}, s32[4,8]{1,0:T(4,128)}, u32[]{:S(2)}) copy-start(s32[4,8]{1,0:T(4,128)} %param.8) | copy-start | bytes 388
  2.1 10.6 %copy-start.8 = (s32[8,8]{1,0:T(8,128)S(1)}, s32[8,8]{1,0:T(8,128)}, u32[]{:S(2)}) copy-start(s32[8,8]{1,0:T(8,128)} %constant.157.clone.1) | copy-start | bytes 772
  5.2 20.7 %collective-permute-start.3 = (bf16[1,3,1024,128]{3,2,1,0:T(8,128)(2,1)}, bf16[1,3,1024,128]{3,2,1,0:T(8,128)(2,1)S(1)}, u32[]{:S(2)}, u32[]{:S(2)}) collective-permute-start(bf16[1,3,1024,128]{3,2,1,0:T(8,128)(2,1)} %get-tuple-element.51), channel_id=1, source_target_pairs={{0,4},{4,0},{8,12},{12,8},{16,20},{20,16},{24,28},{28,24},{1,5},{5... | collective-permute-start | bytes 2359304 | tf_op jit(solution)/shard_map/swap_c0/ppermute | solution.py:568
  6.7 7.0 %collective-permute-start.1 = (s32[8,8]{1,0:T(8,128)S(1)}, s32[8,8]{1,0:T(8,128)S(1)}, u32[]{:S(2)}, u32[]{:S(2)}) collective-permute-start(s32[8,8]{1,0:T(8,128)S(1)} %pad_add_fusion.1), channel_id=1, source_target_pairs={{16,8},{20,12},{24,16},{28,20},{17,9},{21,13},{25,17},{29,21},{18,... | collective-permute-start | bytes 776 | tf_op jit(solution)/shard_map/selection_near/ppermute | solution.py:568
  9.0 4.7 %collective-permute-start.2 = (s32[8,8]{1,0:T(8,128)S(1)}, s32[8,8]{1,0:T(8,128)S(1)}, u32[]{:S(2)}, u32[]{:S(2)}) collective-permute-start(s32[8,8]{1,0:T(8,128)S(1)} %pad_add_fusion.1), channel_id=1, source_target_pairs={{24,8},{28,12},{25,9},{29,13},{26,10},{30,14},{27,11},{31,15}} | collective-permute-start | bytes 776 | tf_op jit(solution)/shard_map/selection_far/ppermute | solution.py:568
  19.9 23.0 %collective-permute-start.4 = (bf16[1,3,1024,128]{3,2,1,0:T(8,128)(2,1)}, bf16[1,3,1024,128]{3,2,1,0:T(8,128)(2,1)}, u32[]{:S(2)}, u32[]{:S(2)}) collective-permute-start(bf16[1,3,1024,128]{3,2,1,0:T(8,128)(2,1)} %get-tuple-element.54), channel_id=1, source_target_pairs={{0,4},{4,0},{8,12},{12,8},{16,20},{20,16},{24,28},{28,24},{1,5},{5... | collective-permute-start | bytes 2359304 | tf_op jit(solution)/shard_map/swap_c1/ppermute | solution.py:568
  26.0 0.9 copy-start
  29.2 33.1 %collective-permute-start.7 = (bf16[2,1,2,1024,128]{4,3,2,1,0:T(8,128)(2,1)}, bf16[2,1,2,1024,128]{4,3,2,1,0:T(8,128)(2,1)}, u32[]{:S(2)}, u32[]{:S(2)}) collective-permute-start(bf16[2,1,2,1024,128]{4,3,2,1,0:T(8,128)(2,1)} %get-tuple-element.57), channel_id=1, source_target_pairs={{0,8},{4,12},{1,9},{5,13},{2,10},{6,14},{3,11},{7,15}} | collective-permute-start | bytes 3145736 | tf_op jit(solution)/shard_map/lift_c0/ppermute | solution.py:568
  30.8 16.1 %collective-permute-start.5 = (bf16[2,1,1024,128]{3,2,1,0:T(8,128)(2,1)}, bf16[2,1,1024,128]{3,2,1,0:T(8,128)(2,1)S(1)}, u32[]{:S(2)}, u32[]{:S(2)}) collective-permute-start(bf16[2,1,1024,128]{3,2,1,0:T(8,128)(2,1)} %get-tuple-element.52.refs_0_), channel_id=1, source_target_pairs={{16,8},{20,12},{24,16},{28,20},{17,9},{21,13},{25,17},{29,21},{18,... | collective-permute-start | bytes 1572872 | tf_op jit(solution)/shard_map/near_down_c0/ppermute | solution.py:568
  33.2 23.9 %collective-permute-start.6 = (bf16[2,1,1024,128]{3,2,1,0:T(8,128)(2,1)}, bf16[2,1,1024,128]{3,2,1,0:T(8,128)(2,1)}, u32[]{:S(2)}, u32[]{:S(2)}) collective-permute-start(bf16[2,1,1024,128]{3,2,1,0:T(8,128)(2,1)} %get-tuple-element.52.refs_0_), channel_id=1, source_target_pairs={{24,8},{28,12},{25,9},{29,13},{26,10},{30,14},{27,11},{31,15}} | collective-permute-start | bytes 1572872 | tf_op jit(solution)/shard_map/far_down_c0/ppermute | solution.py:568
  38.3 31.4 %collective-permute-start.8 = (bf16[1,3,1024,128]{3,2,1,0:T(8,128)(2,1)}, bf16[1,3,1024,128]{3,2,1,0:T(8,128)(2,1)}, u32[]{:S(2)}, u32[]{:S(2)}) collective-permute-start(bf16[1,3,1024,128]{3,2,1,0:T(8,128)(2,1)} %get-tuple-element.60), channel_id=1, source_target_pairs={{0,4},{4,0},{8,12},{12,8},{16,20},{20,16},{24,28},{28,24},{1,5},{5... | collective-permute-start | bytes 2359304 | tf_op jit(solution)/shard_map/swap_c2/ppermute | solution.py:568
  45.2 35.7 %collective-permute-start.11 = (bf16[2,1,2,1024,128]{4,3,2,1,0:T(8,128)(2,1)}, bf16[2,1,2,1024,128]{4,3,2,1,0:T(8,128)(2,1)}, u32[]{:S(2)}, u32[]{:S(2)}) collective-permute-start(bf16[2,1,2,1024,128]{4,3,2,1,0:T(8,128)(2,1)} %get-tuple-element.62), channel_id=1, source_target_pairs={{0,8},{4,12},{1,9},{5,13},{2,10},{6,14},{3,11},{7,15}} | collective-permute-start | bytes 3145736 | tf_op jit(solution)/shard_map/lift_c1/ppermute | solution.py:568
  46.9 15.3 %copy-start.4 = (bf16[2,1,1024,128]{3,2,1,0:T(8,128)(2,1)}, bf16[2,1,1024,128]{3,2,1,0:T(8,128)(2,1)S(1)}, u32[]{:S(2)}) copy-start(bf16[2,1,1024,128]{3,2,1,0:T(8,128)(2,1)S(1)} %collective-permute-done.5.refs_2_) | copy-start | bytes 1572868
  46.9 21.4 %collective-permute-start.10 = (bf16[2,1,1024,128]{3,2,1,0:T(8,128)(2,1)}, bf16[2,1,1024,128]{3,2,1,0:T(8,128)(2,1)}, u32[]{:S(2)}, u32[]{:S(2)}) collective-permute-start(bf16[2,1,1024,128]{3,2,1,0:T(8,128)(2,1)} %get-tuple-element.55.refs_0_), channel_id=1, source_target_pairs={{24,8},{28,12},{25,9},{29,13},{26,10},{30,14},{27,11},{31,15}} | collective-permute-start | bytes 1572872 | tf_op jit(solution)/shard_map/far_down_c1/ppermute | solution.py:568
  57.1 22.2 %collective-permute-start.9 = (bf16[2,1,1024,128]{3,2,1,0:T(8,128)(2,1)}, bf16[2,1,1024,128]{3,2,1,0:T(8,128)(2,1)}, u32[]{:S(2)}, u32[]{:S(2)}) collective-permute-start(bf16[2,1,1024,128]{3,2,1,0:T(8,128)(2,1)} %get-tuple-element.55.refs_0_), channel_id=1, source_target_pairs={{16,8},{20,12},{24,16},{28,20},{17,9},{21,13},{25,17},{29,21},{18,... | collective-permute-start | bytes 1572872 | tf_op jit(solution)/shard_map/near_down_c1/ppermute | solution.py:568
  62.3 49.4 %collective-permute-start.14 = (bf16[1,3,1024,128]{3,2,1,0:T(8,128)(2,1)}, bf16[1,3,1024,128]{3,2,1,0:T(8,128)(2,1)S(1)}, u32[]{:S(2)}, u32[]{:S(2)}) collective-permute-start(bf16[1,3,1024,128]{3,2,1,0:T(8,128)(2,1)} %get-tuple-element.68), channel_id=1, source_target_pairs={{0,4},{4,0},{8,12},{12,8},{16,20},{20,16},{24,28},{28,24},{1,5},{5... | collective-permute-start | bytes 2359304 | tf_op jit(solution)/shard_map/swap_c3/ppermute | solution.py:568
  68.4 29.9 %collective-permute-start.12 = (bf16[1,1056,256]{2,1,0:T(8,128)(2,1)}, bf16[1,1056,256]{2,1,0:T(8,128)(2,1)}, u32[]{:S(2)}, u32[]{:S(2)}) collective-permute-start(bf16[1,1056,256]{2,1,0:T(8,128)(2,1)} %get-tuple-element.58.refs_0_), channel_id=1, source_target_pairs={{8,16},{12,20},{16,24},{20,28},{9,17},{13,21},{17,25},{21,29},{10,... | collective-permute-start | bytes 1622024 | tf_op jit(solution)/shard_map/near_up_c0/ppermute | solution.py:568
  69.7 38.6 %collective-permute-start.13 = (bf16[1,1056,256]{2,1,0:T(8,128)(2,1)}, bf16[1,1056,256]{2,1,0:T(8,128)(2,1)}, u32[]{:S(2)}, u32[]{:S(2)}) collective-permute-start(bf16[1,1056,256]{2,1,0:T(8,128)(2,1)} %get-tuple-element.66), channel_id=1, source_target_pairs={{8,24},{12,28},{9,25},{13,29},{10,26},{14,30},{11,27},{15,31}} | collective-permute-start | bytes 1622024 | tf_op jit(solution)/shard_map/far_up_c0/ppermute | solution.py:568
  79.3 45.3 %collective-permute-start.17 = (bf16[2,1,2,1024,128]{4,3,2,1,0:T(8,128)(2,1)}, bf16[2,1,2,1024,128]{4,3,2,1,0:T(8,128)(2,1)}, u32[]{:S(2)}, u32[]{:S(2)}) collective-permute-start(bf16[2,1,2,1024,128]{4,3,2,1,0:T(8,128)(2,1)} %get-tuple-element.70), channel_id=1, source_target_pairs={{0,8},{4,12},{1,9},{5,13},{2,10},{6,14},{3,11},{7,15}} | collective-permute-start | bytes 3145736 | tf_op jit(solution)/shard_map/lift_c2/ppermute | solution.py:568
  80.9 36.9 %collective-permute-start.15 = (bf16[2,1,1024,128]{3,2,1,0:T(8,128)(2,1)}, bf16[2,1,1024,128]{3,2,1,0:T(8,128)(2,1)}, u32[]{:S(2)}, u32[]{:S(2)}) collective-permute-start(bf16[2,1,1024,128]{3,2,1,0:T(8,128)(2,1)} %get-tuple-element.61.refs_0_), channel_id=1, source_target_pairs={{16,8},{20,12},{24,16},{28,20},{17,9},{21,13},{25,17},{29,21},{18,... | collective-permute-start | bytes 1572872 | tf_op jit(solution)/shard_map/near_down_c2/ppermute | solution.py:568
  98.3 20.9 %collective-permute-start.16 = (bf16[2,1,1024,128]{3,2,1,0:T(8,128)(2,1)}, bf16[2,1,1024,128]{3,2,1,0:T(8,128)(2,1)}, u32[]{:S(2)}, u32[]{:S(2)}) collective-permute-start(bf16[2,1,1024,128]{3,2,1,0:T(8,128)(2,1)} %get-tuple-element.61.refs_0_), channel_id=1, source_target_pairs={{24,8},{28,12},{25,9},{29,13},{26,10},{30,14},{27,11},{31,15}} | collective-permute-start | bytes 1572872 | tf_op jit(solution)/shard_map/far_down_c2/ppermute | solution.py:568
  111.6 0.9 copy-start.1
  114.8 40.4 %collective-permute-start.22 = (bf16[2,1,2,1024,128]{4,3,2,1,0:T(8,128)(2,1)}, bf16[2,1,2,1024,128]{4,3,2,1,0:T(8,128)(2,1)}, u32[]{:S(2)}, u32[]{:S(2)}) collective-permute-start(bf16[2,1,2,1024,128]{4,3,2,1,0:T(8,128)(2,1)} %get-tuple-element.77), channel_id=1, source_target_pairs={{0,8},{4,12},{1,9},{5,13},{2,10},{6,14},{3,11},{7,15}} | collective-permute-start | bytes 3145736 | tf_op jit(solution)/shard_map/lift_c3/ppermute | solution.py:568
  116.5 27.3 %collective-permute-start.18 = (bf16[1,1056,256]{2,1,0:T(8,128)(2,1)}, bf16[1,1056,256]{2,1,0:T(8,128)(2,1)S(1)}, u32[]{:S(2)}, u32[]{:S(2)}) collective-permute-start(bf16[1,1056,256]{2,1,0:T(8,128)(2,1)} %get-tuple-element.63.refs_0_), channel_id=1, source_target_pairs={{8,16},{12,20},{16,24},{20,28},{9,17},{13,21},{17,25},{21,29},{10,... | collective-permute-start | bytes 1622024 | tf_op jit(solution)/shard_map/near_up_c1/ppermute | solution.py:568
  117.8 33.3 %collective-permute-start.19 = (bf16[1,1056,256]{2,1,0:T(8,128)(2,1)}, bf16[1,1056,256]{2,1,0:T(8,128)(2,1)}, u32[]{:S(2)}, u32[]{:S(2)}) collective-permute-start(bf16[1,1056,256]{2,1,0:T(8,128)(2,1)} %get-tuple-element.75), channel_id=1, source_target_pairs={{8,24},{12,28},{9,25},{13,29},{10,26},{14,30},{11,27},{15,31}} | collective-permute-start | bytes 1622024 | tf_op jit(solution)/shard_map/far_up_c1/ppermute | solution.py:568
  119.1 36.1 %collective-permute-start.20 = (bf16[2,1,1024,128]{3,2,1,0:T(8,128)(2,1)}, bf16[2,1,1024,128]{3,2,1,0:T(8,128)(2,1)}, u32[]{:S(2)}, u32[]{:S(2)}) collective-permute-start(bf16[2,1,1024,128]{3,2,1,0:T(8,128)(2,1)} %get-tuple-element.69.refs_0_), channel_id=1, source_target_pairs={{16,8},{20,12},{24,16},{28,20},{17,9},{21,13},{25,17},{29,21},{18,... | collective-permute-start | bytes 1572872 | tf_op jit(solution)/shard_map/near_down_c3/ppermute | solution.py:568
  124.6 30.6 %collective-permute-start.21 = (bf16[2,1,1024,128]{3,2,1,0:T(8,128)(2,1)}, bf16[2,1,1024,128]{3,2,1,0:T(8,128)(2,1)}, u32[]{:S(2)}, u32[]{:S(2)}) collective-permute-start(bf16[2,1,1024,128]{3,2,1,0:T(8,128)(2,1)} %get-tuple-element.69.refs_0_), channel_id=1, source_target_pairs={{24,8},{28,12},{25,9},{29,13},{26,10},{30,14},{27,11},{31,15}} | collective-permute-start | bytes 1572872 | tf_op jit(solution)/shard_map/far_down_c3/ppermute | solution.py:568
  143.9 1.3 copy-start.2
  143.9 26.7 %collective-permute-start.23 = (bf16[1,1056,256]{2,1,0:T(8,128)(2,1)}, bf16[1,1056,256]{2,1,0:T(8,128)(2,1)}, u32[]{:S(2)}, u32[]{:S(2)}) collective-permute-start(bf16[1,1056,256]{2,1,0:T(8,128)(2,1)} %get-tuple-element.71.refs_0_), channel_id=1, source_target_pairs={{8,16},{12,20},{16,24},{20,28},{9,17},{13,21},{17,25},{21,29},{10,... | collective-permute-start | bytes 1622024 | tf_op jit(solution)/shard_map/near_up_c2/ppermute | solution.py:568
  151.2 20.9 %collective-permute-start.24 = (bf16[1,1056,256]{2,1,0:T(8,128)(2,1)}, bf16[1,1056,256]{2,1,0:T(8,128)(2,1)S(1)}, u32[]{:S(2)}, u32[]{:S(2)}) collective-permute-start(bf16[1,1056,256]{2,1,0:T(8,128)(2,1)} %get-tuple-element.81), channel_id=1, source_target_pairs={{8,24},{12,28},{9,25},{13,29},{10,26},{14,30},{11,27},{15,31}} | collective-permute-start | bytes 1622024 | tf_op jit(solution)/shard_map/far_up_c2/ppermute | solution.py:568
  158.9 23.3 %collective-permute-start.25 = (bf16[1,1056,256]{2,1,0:T(8,128)(2,1)}, bf16[1,1056,256]{2,1,0:T(8,128)(2,1)}, u32[]{:S(2)}, u32[]{:S(2)}) collective-permute-start(bf16[1,1056,256]{2,1,0:T(8,128)(2,1)} %get-tuple-element.78.refs_0_), channel_id=1, source_target_pairs={{8,16},{12,20},{16,24},{20,28},{9,17},{13,21},{17,25},{21,29},{10,... | collective-permute-start | bytes 1622024 | tf_op jit(solution)/shard_map/near_up_c3/ppermute | solution.py:568
  160.2 22.0 %collective-permute-start.26 = (bf16[1,1056,256]{2,1,0:T(8,128)(2,1)}, bf16[1,1056,256]{2,1,0:T(8,128)(2,1)}, u32[]{:S(2)}, u32[]{:S(2)}) collective-permute-start(bf16[1,1056,256]{2,1,0:T(8,128)(2,1)} %get-tuple-element.86), channel_id=1, source_target_pairs={{8,24},{12,28},{9,25},{13,29},{10,26},{14,30},{11,27},{15,31}} | collective-permute-start | bytes 1622024 | tf_op jit(solution)/shard_map/far_up_c3/ppermute | solution.py:568
  161.5 36.2 %collective-permute-start.27 = (bf16[1,1024,128]{2,1,0:T(8,128)(2,1)}, bf16[1,1024,128]{2,1,0:T(8,128)(2,1)S(1)}, u32[]{:S(2)}, u32[]{:S(2)}) collective-permute-start(bf16[1,1024,128]{2,1,0:T(8,128)(2,1)} %get-tuple-element.88), channel_id=1, source_target_pairs={{0,4},{4,0},{8,12},{12,8},{16,20},{20,16},{24,28},{28,24},{1,5},{5... | collective-permute-start | bytes 786440 | tf_op jit(solution)/shard_map/back_c0/ppermute | solution.py:568
  170.5 27.2 %collective-permute-start.28 = (bf16[1,1024,128]{2,1,0:T(8,128)(2,1)}, bf16[1,1024,128]{2,1,0:T(8,128)(2,1)}, u32[]{:S(2)}, u32[]{:S(2)}) collective-permute-start(bf16[1,1024,128]{2,1,0:T(8,128)(2,1)} %get-tuple-element.89), channel_id=1, source_target_pairs={{0,4},{4,0},{8,12},{12,8},{16,20},{20,16},{24,28},{28,24},{1,5},{5... | collective-permute-start | bytes 786440 | tf_op jit(solution)/shard_map/back_c1/ppermute | solution.py:568
  172.0 0.8 copy-start.3
  175.6 22.1 %collective-permute-start.29 = (bf16[1,1024,128]{2,1,0:T(8,128)(2,1)}, bf16[1,1024,128]{2,1,0:T(8,128)(2,1)S(1)}, u32[]{:S(2)}, u32[]{:S(2)}) collective-permute-start(bf16[1,1024,128]{2,1,0:T(8,128)(2,1)} %get-tuple-element.90), channel_id=1, source_target_pairs={{0,4},{4,0},{8,12},{12,8},{16,20},{20,16},{24,28},{28,24},{1,5},{5... | collective-permute-start | bytes 786440 | tf_op jit(solution)/shard_map/back_c2/ppermute | solution.py:568
  176.1 18.9 %copy-start.9 = (bf16[1024]{0:T(1024)(128)(2,1)S(1)}, bf16[1024]{0:T(1024)(128)(2,1)}, u32[]{:S(2)}) copy-start(bf16[1024]{0:T(1024)(128)(2,1)} %param.9) | copy-start | bytes 6148
  185.0 12.7 %collective-permute-start.30 = (bf16[1,1024,128]{2,1,0:T(8,128)(2,1)}, bf16[1,1024,128]{2,1,0:T(8,128)(2,1)S(1)}, u32[]{:S(2)}, u32[]{:S(2)}) collective-permute-start(bf16[1,1024,128]{2,1,0:T(8,128)(2,1)} %get-tuple-element.91), channel_id=1, source_target_pairs={{0,4},{4,0},{8,12},{12,8},{16,20},{20,16},{24,28},{28,24},{1,5},{5... | collective-permute-start | bytes 786440 | tf_op jit(solution)/shard_map/back_c3/ppermute | solution.py:568
  187.2 4.4 %collective-permute-start.31 = (f32[4,256]{1,0:T(4,128)S(1)}, f32[4,256]{1,0:T(4,128)S(1)}, u32[]{:S(2)}, u32[]{:S(2)}) collective-permute-start(f32[4,256]{1,0:T(4,128)S(1)} %slice.15), channel_id=1, source_target_pairs={{0,4},{4,0},{8,12},{12,8},{16,20},{20,16},{24,28},{28,24},{1,5},{5... | collective-permute-start | bytes 12296 | tf_op jit(solution)/shard_map/squares_swap/ppermute | solution.py:568
  192.4 1.2 collective-permute-start.32
  193.5 3.6 %collective-permute-start.33 = (f32[4,256]{1,0:T(4,128)S(1)}, f32[4,256]{1,0:T(4,128)S(1)}, u32[]{:S(2)}, u32[]{:S(2)}) collective-permute-start(f32[4,256]{1,0:T(4,128)S(1)} %add.298), channel_id=1, source_target_pairs={{0,2},{1,3},{2,0},{3,1},{4,6},{5,7},{6,4},{7,5},{8,10},{9,11},{10,... | collective-permute-start | bytes 12296 | tf_op jit(solution)/shard_map/ppermute | solution.py:691
  197.7 0.7 copy-start.5
  197.8 0.8 copy-start.6
  197.8 0.9 copy-start.7

commit v5 on v4

--- a/solution.py
+++ b/solution.py
@@ -132,10 +132,10 @@
 SPLIT = (False, False, False, False,)
 ORDER = (
     ("p", 0),
+    ("p", 2),
     ("w", "plans"),
     ("p", 1),
     ("j", 0),
-    ("p", 2),
     ("j", 1),
     ("p", 3),
     ("s", 0),
@@ -144,20 +144,20 @@
     ("s", 1),
     ("a", 1),
     ("w", "lift_c1"),
-    ("m", 0),
+    ("w", "near_up_c0"),
+    ("w", "far_up_c0"),
     ("j", 3),
     ("s", 2),
-    ("w", "near_up_c1"),
+    ("s", 3),
     ("a", 2),
-    ("m", 1),
-    ("s", 3),
+    ("m", 0, 1),
     ("m", 2),
     ("a", 3),
     ("m", 3),
 )
 LSE_ROWS = 32
 UNROLL = 2
-VMEM_LIMIT = 63 * 1024 * 1024
+VMEM_LIMIT = 16 * 1024 * 1024
 
 
 def unit_fields(code):
@@ -380,6 +380,9 @@
     rows = queries.shape[0]
     hbm = pl.BlockSpec(memory_space=pltpu.HBM)
     bf16 = jnp.bfloat16
+    queries, keys, values = (
+        pltpu.with_memory_space_constraint(array, pltpu.HBM) for array in (queries, keys, values)
+    )
     if split:
         side = [
             jax.ShapeDtypeStruct((heads, rows, HD), bf16),

time: 206 us -> 181 us (0.88); the launches traced: 202 us -> 180 us
  Pallas kernels: 75.2 us -> 38.9 us
  waiting for transfers between devices: 44.4 us -> 68.1 us
  starting transfers between devices: 67.2 us -> 60 us
  other arithmetic: 6.73 us -> 3.49 us
    ppermute x32 -> x31, waiting for transfers between devices: 41.7 us -> 64.9 us  [to(): sent[name] = lax.ppermute(array, 'ctx', pairs)]
    pallas_call x8, Pallas kernels: 39 us -> 21 us  [attention_call(): pl.pallas_call(ordered(partial(attention_kernel, (heads, per_dev, block_r...]
    pallas_call x4, Pallas kernels: 9.29 us -> 1.11 us  [join_call(): pl.pallas_call(ordered(partial(join_kernel, heads), len(after)), out_shap...]
    ppermute x32 -> x31, starting transfers between devices: 65.7 us -> 58.5 us  [to(): sent[name] = lax.ppermute(array, 'ctx', pairs)]
    pallas_call x4 -> x3, Pallas kernels: 11 us -> 5.29 us  [merge_call(): pl.pallas_call(ordered(partial(merge_kernel, per_dev, block_rows, sizes),...]
    pallas_call x4, Pallas kernels: 12.1 us -> 8.74 us  [pack_call(): pl.pallas_call(ordered(partial(pack_kernel, (heads, first, half, rows, sp...]
    unnamed x22 -> x46, local copies, waits for them, and re-layouts: 3.44 us -> 5.16 us
  transfers between devices with their start and end apart: 34 -> 33, of which waited for: 9 -> 15; matrix products, arithmetic and copies ran while one was open for 5% -> 2% of each run, Pallas kernels for 35% -> 20%
where the time goes in v5:
time: 181 us; the launch traced here: 180 us
  waiting for transfers between devices  68.1 us (38%)
  starting transfers between devices  60 us (33%)
  Pallas kernels  38.9 us (21%)
  local copies, waits for them, and re-layouts  6.03 us (3%)
  other arithmetic  3.49 us (2%)
  between operations  3.38 us (2%)
    ppermute x31, waiting for transfers between devices, to(): sent[name] = lax.ppermute(array, 'ctx', pairs)  64.9 us
    ppermute x31, starting transfers between devices, to(): sent[name] = lax.ppermute(array, 'ctx', pairs)  58.5 us
    pallas_call x8, Pallas kernels, attention_call(): pl.pallas_call(ordered(partial(attention_kernel, (heads, per_dev, block_r...  21 us
    pallas_call x4, Pallas kernels, pack_call(): pl.pallas_call(ordered(partial(pack_kernel, (heads, first, half, rows, sp...  8.74 us
    pallas_call x3, Pallas kernels, merge_call(): pl.pallas_call(ordered(partial(merge_kernel, per_dev, block_rows, sizes),...  5.29 us
    unnamed x46, local copies, waits for them, and re-layouts  5.16 us
  transfers between devices with their start and end apart: 33, of which 15 were waited for; matrix products, arithmetic and copies ran while one was open for 2% of the time, Pallas kernels for 20%

profile of v5, /device:TPU:24, one launch (start us, length us, event | category | flops | bytes accessed | tf_op | source)
XLA Modules:
  0.0 180.0 jit_solution(9712576762197425829)
XLA Ops:
  0.0 1.5 collective-permute-start
  1.6 2.2 %pack.4 = (bf16[1,3,1024,128]{3,2,1,0:T(8,128)(2,1)S(1)}, bf16[1,3,1024,128]{3,2,1,0:T(8,128)(2,1)S(1)}) custom-call(s32[2]{0:T(128)S(1)} %pad_add_fusion.3.refs_0_.refs_1_.refs_3_.place, bf16[1024,1024]{1,0:T(8,128)(2,1)} %refs_2_.5, bf16[1024,1024]{1,0:T(8,128)(2,1)} %refs_3_.5, bf16[1024,1024]{1,0:T(8,128)(2,1)} %refs_4_.5), custom_call_target="tpu_custom_call" | custom-call | flops 1 | bytes 1 | tf_op jit(solution)/shard_map/pack/pallas_call | solution.py:393
  5.0 2.2 %pack.5 = (bf16[1,3,1024,128]{3,2,1,0:T(8,128)(2,1)S(1)}, bf16[1,3,1024,128]{3,2,1,0:T(8,128)(2,1)S(1)}) custom-call(bf16[1,3,1024,128]{3,2,1,0:T(8,128)(2,1)S(1)} %get-tuple-element.46.refs_0_.refs_1_.refs_4_.refs_2_, s32[2]{0:T(128)S(1)} %pad_add_fusion.3.refs_0_.refs_1_.refs_3_.place, bf16[1024,1024]{1,0:T(8,128)(2,1)} %refs_2_.5, ...), custom_call_target="tpu_custom_call" | custom-call | flops 1 | bytes 1 | tf_op jit(solution)/shard_map/pack/pallas_call | solution.py:393
  8.3 2.4 %collective-permute-start.1 = (s32[8,8]{1,0:T(8,128)S(1)}, s32[8,8]{1,0:T(8,128)S(1)}, u32[]{:S(2)}, u32[]{:S(2)}) collective-permute-start(s32[8,8]{1,0:T(8,128)S(1)} %pad_add_fusion.1), channel_id=1, source_target_pairs={{16,8},{20,12},{24,16},{28,20},{17,9},{21,13},{25,17},{29,21},{18,... | collective-permute-start | bytes 776 | tf_op jit(solution)/shard_map/selection_near/ppermute | solution.py:571
  10.7 1.3 collective-permute-start.2
  18.1 2.2 %pack.6 = (bf16[1,3,1024,128]{3,2,1,0:T(8,128)(2,1)S(1)}, bf16[1,3,1024,128]{3,2,1,0:T(8,128)(2,1)S(1)}) custom-call(bf16[1,3,1024,128]{3,2,1,0:T(8,128)(2,1)S(1)} %get-tuple-element.47.refs_0_.refs_1_.refs_4_.refs_2_, s32[81]{0:T(128)S(1)} %pad_add_fusion.5.refs_1_, s32[129]{0:T(256)S(1)} %pad_add_fusion.2.refs_2_.refs_1_, ...), custom_call_target="tpu_custom_call" | custom-call | flops 1 | bytes 1 | tf_op jit(solution)/shard_map/pack/pallas_call | solution.py:393
  20.3 1.6 collective-permute-start.4
  21.8 1.8 %collective-permute-done.3.refs_2_.refs_5_.refs_3_ = bf16[1,3,1024,128]{3,2,1,0:T(8,128)(2,1)S(1)} collective-permute-done((bf16[1,3,1024,128]{3,2,1,0:T(8,128)(2,1)S(1)}, bf16[1,3,1024,128]{3,2,1,0:T(8,128)(2,1)S(1)}, u32[]{:S(2)}, u32[]{:S(2)}) %collective-permute-start.3) | collective-permute-done | bytes 786464 | tf_op jit(solution)/shard_map/swap_c0/ppermute | solution.py:571
  24.7 3.0 %collective-permute-start.5 = (bf16[2,1,1024,128]{3,2,1,0:T(8,128)(2,1)S(1)}, bf16[2,1,1024,128]{3,2,1,0:T(8,128)(2,1)S(1)}, u32[]{:S(2)}, u32[]{:S(2)}) collective-permute-start(bf16[2,1,1024,128]{3,2,1,0:T(8,128)(2,1)S(1)} %get-tuple-element.50.refs_0_), channel_id=1, source_target_pairs={{16,8},{20,12},{24,16},{28,20},{17,9},{21,13},{25,17},{29,21},{18,... | collective-permute-start | bytes 1572872 | tf_op jit(solution)/shard_map/near_down_c0/ppermute | solution.py:571
  27.8 1.3 collective-permute-start.6
  29.1 11.7 %collective-permute-done.4.refs_2_.refs_5_.refs_3_ = bf16[1,3,1024,128]{3,2,1,0:T(8,128)(2,1)S(1)} collective-permute-done((bf16[1,3,1024,128]{3,2,1,0:T(8,128)(2,1)S(1)}, bf16[1,3,1024,128]{3,2,1,0:T(8,128)(2,1)S(1)}, u32[]{:S(2)}, u32[]{:S(2)}) %collective-permute-start.4) | collective-permute-done | bytes 786464 | tf_op jit(solution)/shard_map/swap_c1/ppermute | solution.py:571
  41.1 3.3 %collective-permute-start.10 = (bf16[2,1,1024,128]{3,2,1,0:T(8,128)(2,1)S(1)}, bf16[2,1,1024,128]{3,2,1,0:T(8,128)(2,1)S(1)}, u32[]{:S(2)}, u32[]{:S(2)}) collective-permute-start(bf16[2,1,1024,128]{3,2,1,0:T(8,128)(2,1)S(1)} %get-tuple-element.52.refs_0_), channel_id=1, source_target_pairs={{24,8},{28,12},{25,9},{29,13},{26,10},{30,14},{27,11},{31,15}} | collective-permute-start | bytes 1572872 | tf_op jit(solution)/shard_map/far_down_c1/ppermute | solution.py:571
  45.3 2.2 %pack.7 = (bf16[1,3,1024,128]{3,2,1,0:T(8,128)(2,1)S(1)}, bf16[1,3,1024,128]{3,2,1,0:T(8,128)(2,1)S(1)}) custom-call(bf16[2,1,1024,128]{3,2,1,0:T(8,128)(2,1)S(1)} %get-tuple-element.52.refs_0_, s32[2]{0:T(128)S(1)} %pad_add_fusion.3.refs_0_.refs_1_.refs_3_.place, bf16[1024,1024]{1,0:T(8,128)(2,1)} %refs_2_.5, bf16[1024,1024]{1,0:T(8,128)(2,1)} %refs_3_.5, ...), custom_call_target="tpu_custom_call" | custom-call | flops 1 | bytes 1 | tf_op jit(solution)/shard_map/pack/pallas_call | solution.py:393
  47.5 3.8 %collective-permute-done.6.refs_3_ = bf16[2,1,1024,128]{3,2,1,0:T(8,128)(2,1)S(1)} collective-permute-done((bf16[2,1,1024,128]{3,2,1,0:T(8,128)(2,1)S(1)}, bf16[2,1,1024,128]{3,2,1,0:T(8,128)(2,1)S(1)}, u32[]{:S(2)}, u32[]{:S(2)}) %collective-permute-start.6) | collective-permute-done | bytes 524320 | tf_op jit(solution)/shard_map/far_down_c0/ppermute | solution.py:571
  51.3 1.3 collective-permute-start.9
  53.7 3.9 %collective-permute-done.8.refs_2_.refs_5_.refs_3_ = bf16[1,3,1024,128]{3,2,1,0:T(8,128)(2,1)S(1)} collective-permute-done((bf16[1,3,1024,128]{3,2,1,0:T(8,128)(2,1)S(1)}, bf16[1,3,1024,128]{3,2,1,0:T(8,128)(2,1)S(1)}, u32[]{:S(2)}, u32[]{:S(2)}) %collective-permute-start.8) | collective-permute-done | bytes 786464 | tf_op jit(solution)/shard_map/swap_c2/ppermute | solution.py:571
  59.0 3.6 %collective-permute-done.10.refs_3_ = bf16[2,1,1024,128]{3,2,1,0:T(8,128)(2,1)S(1)} collective-permute-done((bf16[2,1,1024,128]{3,2,1,0:T(8,128)(2,1)S(1)}, bf16[2,1,1024,128]{3,2,1,0:T(8,128)(2,1)S(1)}, u32[]{:S(2)}, u32[]{:S(2)}) %collective-permute-start.10) | collective-permute-done | bytes 524320 | tf_op jit(solution)/shard_map/far_down_c1/ppermute | solution.py:571
  63.8 3.5 %own_attention.4 = (f32[1,8,128,256]{3,2,1,0:T(8,128)S(1)}, f32[1,8,256]{2,1,0:T(8,128)S(1)}) custom-call(bf16[1,1056,256]{2,1,0:T(8,128)(2,1)S(1)} %get-tuple-element.55.refs_0_, s32[81]{0:T(128)S(1)} %pad_add_fusion.5.refs_1_, bf16[1,3,1024,128]{3,2,1,0:T(8,128)(2,1)S(1)} %get-tuple-element.46.refs_0_.refs_1_.refs_4_.refs_2_, ...), custom_call_target="tpu_custom_call" | custom-call | flops 1 | bytes 1 | tf_op jit(solution)/shard_map/own_attention/pallas_call | solution.py:324
  67.6 2.3 %collective-permute-done.9.refs_2_ = bf16[2,1,1024,128]{3,2,1,0:T(8,128)(2,1)S(1)} collective-permute-done((bf16[2,1,1024,128]{3,2,1,0:T(8,128)(2,1)S(1)}, bf16[2,1,1024,128]{3,2,1,0:T(8,128)(2,1)S(1)}, u32[]{:S(2)}, u32[]{:S(2)}) %collective-permute-start.9) | collective-permute-done | bytes 524320 | tf_op jit(solution)/shard_map/near_down_c1/ppermute | solution.py:571
  70.7 4.4 %collective-permute-start.15 = (bf16[2,1,1024,128]{3,2,1,0:T(8,128)(2,1)S(1)}, bf16[2,1,1024,128]{3,2,1,0:T(8,128)(2,1)S(1)}, u32[]{:S(2)}, u32[]{:S(2)}) collective-permute-start(bf16[2,1,1024,128]{3,2,1,0:T(8,128)(2,1)S(1)} %get-tuple-element.58.refs_0_), channel_id=1, source_target_pairs={{16,8},{20,12},{24,16},{28,20},{17,9},{21,13},{25,17},{29,21},{18,... | collective-permute-start | bytes 1572872 | tf_op jit(solution)/shard_map/near_down_c2/ppermute | solution.py:571
  75.1 1.8 %served_attention.5 = (bf16[1,1056,256]{2,1,0:T(8,128)(2,1)S(1)}, bf16[1,1056,256]{2,1,0:T(8,128)(2,1)}) custom-call(bf16[2,1,1024,128]{3,2,1,0:T(8,128)(2,1)S(1)} %get-tuple-element.58.refs_0_, s32[129]{0:T(256)S(1)} %pad_add_fusion.2.refs_2_.refs_1_, bf16[2,1,1024,128]{3,2,1,0:T(8,128)(2,1)S(1)} %collective-permute-done.9.refs_2_, ...), custom_call_target="tpu_custom_call" | custom-call | flops 1 | bytes 1 | tf_op jit(solution)/shard_map/served_attention/pallas_call | solution.py:324
  77.0 7.0 %collective-permute-start.16 = (bf16[2,1,1024,128]{3,2,1,0:T(8,128)(2,1)S(1)}, bf16[2,1,1024,128]{3,2,1,0:T(8,128)(2,1)S(1)}, u32[]{:S(2)}, u32[]{:S(2)}) collective-permute-start(bf16[2,1,1024,128]{3,2,1,0:T(8,128)(2,1)S(1)} %get-tuple-element.58.refs_0_), channel_id=1, source_target_pairs={{24,8},{28,12},{25,9},{29,13},{26,10},{30,14},{27,11},{31,15}} | collective-permute-start | bytes 1572872 | tf_op jit(solution)/shard_map/far_down_c2/ppermute | solution.py:571
  83.9 3.5 %own_attention.5 = (f32[1,8,128,256]{3,2,1,0:T(8,128)S(1)}, f32[1,8,256]{2,1,0:T(8,128)S(1)}) custom-call(bf16[1,1056,256]{2,1,0:T(8,128)(2,1)S(1)} %get-tuple-element.60.refs_0_, s32[81]{0:T(128)S(1)} %pad_add_fusion.5.refs_1_, bf16[1,3,1024,128]{3,2,1,0:T(8,128)(2,1)S(1)} %get-tuple-element.48.refs_0_.refs_1_.refs_4_.refs_2_, ...), custom_call_target="tpu_custom_call" | custom-call | flops 1 | bytes 1 | tf_op jit(solution)/shard_map/own_attention/pallas_call | solution.py:324
  89.4 1.3 collective-permute-start.21
  90.7 11.2 %collective-permute-start.18 = (bf16[2,1,1024,128]{3,2,1,0:T(8,128)(2,1)S(1)}, bf16[2,1,1024,128]{3,2,1,0:T(8,128)(2,1)S(1)}, u32[]{:S(2)}, u32[]{:S(2)}) collective-permute-start(bf16[2,1,1024,128]{3,2,1,0:T(8,128)(2,1)S(1)} %get-tuple-element.64.refs_0_), channel_id=1, source_target_pairs={{16,8},{20,12},{24,16},{28,20},{17,9},{21,13},{25,17},{29,21},{18,... | collective-permute-start | bytes 1572872 | tf_op jit(solution)/shard_map/near_down_c3/ppermute | solution.py:571
  102.0 3.2 %collective-permute-start.19 = (bf16[2,1,1024,128]{3,2,1,0:T(8,128)(2,1)S(1)}, bf16[2,1,1024,128]{3,2,1,0:T(8,128)(2,1)S(1)}, u32[]{:S(2)}, u32[]{:S(2)}) collective-permute-start(bf16[2,1,1024,128]{3,2,1,0:T(8,128)(2,1)S(1)} %get-tuple-element.64.refs_0_), channel_id=1, source_target_pairs={{24,8},{28,12},{25,9},{29,13},{26,10},{30,14},{27,11},{31,15}} | collective-permute-start | bytes 1572872 | tf_op jit(solution)/shard_map/far_down_c3/ppermute | solution.py:571
  105.2 1.3 collective-permute-start.22
  106.5 2.1 %served_attention.6 = (bf16[1,1056,256]{2,1,0:T(8,128)(2,1)}, bf16[1,1056,256]{2,1,0:T(8,128)(2,1)}) custom-call(bf16[2,1,1024,128]{3,2,1,0:T(8,128)(2,1)S(1)} %get-tuple-element.64.refs_0_, s32[129]{0:T(256)S(1)} %pad_add_fusion.2.refs_2_.refs_1_, bf16[2,1,1024,128]{3,2,1,0:T(8,128)(2,1)S(1)} %collective-permute-done.15.refs_2_, ...), custom_call_target="tpu_custom_call" | custom-call | flops 1 | bytes 1 | tf_op jit(solution)/shard_map/served_attention/pallas_call | solution.py:324
  108.6 3.9 %collective-permute-done.18.refs_2_ = bf16[2,1,1024,128]{3,2,1,0:T(8,128)(2,1)S(1)} collective-permute-done((bf16[2,1,1024,128]{3,2,1,0:T(8,128)(2,1)S(1)}, bf16[2,1,1024,128]{3,2,1,0:T(8,128)(2,1)S(1)}, u32[]{:S(2)}, u32[]{:S(2)}) %collective-permute-start.18) | collective-permute-done | bytes 524320 | tf_op jit(solution)/shard_map/near_down_c3/ppermute | solution.py:571
  113.8 4.4 %collective-permute-done.19.refs_3_ = bf16[2,1,1024,128]{3,2,1,0:T(8,128)(2,1)S(1)} collective-permute-done((bf16[2,1,1024,128]{3,2,1,0:T(8,128)(2,1)S(1)}, bf16[2,1,1024,128]{3,2,1,0:T(8,128)(2,1)S(1)}, u32[]{:S(2)}, u32[]{:S(2)}) %collective-permute-start.19) | collective-permute-done | bytes 524320 | tf_op jit(solution)/shard_map/far_down_c3/ppermute | solution.py:571
  118.2 1.4 collective-permute-start.24
  119.6 2.0 %served_attention.7 = (bf16[1,1056,256]{2,1,0:T(8,128)(2,1)}, bf16[1,1056,256]{2,1,0:T(8,128)(2,1)}) custom-call(bf16[1,1056,256]{2,1,0:T(8,128)(2,1)} %get-tuple-element.66.refs_0_, s32[129]{0:T(256)S(1)} %pad_add_fusion.2.refs_2_.refs_1_, bf16[2,1,1024,128]{3,2,1,0:T(8,128)(2,1)S(1)} %collective-permute-done.18.refs_2_, ...), custom_call_target="tpu_custom_call" | custom-call | flops 1 | bytes 1 | tf_op jit(solution)/shard_map/served_attention/pallas_call | solution.py:324
  121.7 1.3 collective-permute-start.25
  123.8 1.5 collective-permute-start.26
  126.6 3.5 %own_attention.6 = (f32[1,8,128,256]{3,2,1,0:T(8,128)S(1)}, f32[1,8,256]{2,1,0:T(8,128)S(1)}) custom-call(bf16[1,1056,256]{2,1,0:T(8,128)(2,1)} %get-tuple-element.68.refs_0_, s32[81]{0:T(128)S(1)} %pad_add_fusion.5.refs_1_, bf16[1,3,1024,128]{3,2,1,0:T(8,128)(2,1)S(1)} %get-tuple-element.47.refs_0_.refs_1_.refs_4_.refs_2_, ...), custom_call_target="tpu_custom_call" | custom-call | flops 1 | bytes 1 | tf_op jit(solution)/shard_map/own_attention/pallas_call | solution.py:324
  131.4 1.9 %merge.3 = (bf16[2,1024,128]{2,1,0:T(8,128)(2,1)S(1)}, bf16[2,1024,128]{2,1,0:T(8,128)(2,1)S(1)}, f32[8,256]{1,0:T(8,128)S(1)}) custom-call(f32[1,8,256]{2,1,0:T(8,128)S(1)} %get-tuple-element.69.refs_0_.refs_4_, s32[2]{0:T(128)S(1)} %add_convert_fusion.refs_1_, f32[8,256]{1,0:T(8,128)S(1)} %broadcast_in_dim.75.refs_2_, f32[1,8,128,256]{3,2,1,0:T(8,128)S(1)} %copy-done.13, ...), custom_call_target="tpu_custom_call" | custom-call | flops 1 | bytes 1 | tf_op jit(solution)/shard_map/merge/pallas_call | solution.py:491
  133.7 10.1 %collective-permute-done.23.refs_5_ = bf16[1,1056,256]{2,1,0:T(8,128)(2,1)} collective-permute-done((bf16[1,1056,256]{2,1,0:T(8,128)(2,1)}, bf16[1,1056,256]{2,1,0:T(8,128)(2,1)}, u32[]{:S(2)}, u32[]{:S(2)}) %collective-permute-start.23) | collective-permute-done | bytes 540704 | tf_op jit(solution)/shard_map/near_up_c2/ppermute | solution.py:571
  143.8 5.9 %collective-permute-done.24.refs_6_ = bf16[1,1056,256]{2,1,0:T(8,128)(2,1)} collective-permute-done((bf16[1,1056,256]{2,1,0:T(8,128)(2,1)}, bf16[1,1056,256]{2,1,0:T(8,128)(2,1)}, u32[]{:S(2)}, u32[]{:S(2)}) %collective-permute-start.24) | collective-permute-done | bytes 540704 | tf_op jit(solution)/shard_map/far_up_c2/ppermute | solution.py:571
  149.6 1.7 merge.4
  151.7 3.5 %own_attention.7 = (f32[1,8,128,256]{3,2,1,0:T(8,128)S(1)}, f32[1,8,256]{2,1,0:T(8,128)S(1)}) custom-call(bf16[1,1024,128]{2,1,0:T(8,128)(2,1)S(1)} %get-tuple-element.77.refs_0_.refs_1_, s32[81]{0:T(128)S(1)} %pad_add_fusion.5.refs_1_, bf16[1,3,1024,128]{3,2,1,0:T(8,128)(2,1)S(1)} %get-tuple-element.53.refs_0_.refs_4_.refs_2_, ...), custom_call_target="tpu_custom_call" | custom-call | flops 1 | bytes 1 | tf_op jit(solution)/shard_map/own_attention/pallas_call | solution.py:324
  155.2 3.1 %collective-permute-done.25.refs_5_ = bf16[1,1056,256]{2,1,0:T(8,128)(2,1)} collective-permute-done((bf16[1,1056,256]{2,1,0:T(8,128)(2,1)}, bf16[1,1056,256]{2,1,0:T(8,128)(2,1)}, u32[]{:S(2)}, u32[]{:S(2)}) %collective-permute-start.25) | collective-permute-done | bytes 540704 | tf_op jit(solution)/shard_map/near_up_c3/ppermute | solution.py:571
  158.3 5.9 %collective-permute-done.26.refs_6_ = bf16[1,1056,256]{2,1,0:T(8,128)(2,1)} collective-permute-done((bf16[1,1056,256]{2,1,0:T(8,128)(2,1)}, bf16[1,1056,256]{2,1,0:T(8,128)(2,1)}, u32[]{:S(2)}, u32[]{:S(2)}) %collective-permute-start.26) | collective-permute-done | bytes 540704 | tf_op jit(solution)/shard_map/far_up_c3/ppermute | solution.py:571
  164.2 1.7 merge.5
  166.2 1.8 collective-permute-start.30
  168.0 4.4 %collective-permute-done.30 = f32[4,256]{1,0:T(4,128)S(1)} collective-permute-done((f32[4,256]{1,0:T(4,128)S(1)}, f32[4,256]{1,0:T(4,128)S(1)}, u32[]{:S(2)}, u32[]{:S(2)}) %collective-permute-start.30) | collective-permute-done | bytes 4128 | tf_op jit(solution)/shard_map/squares_swap/ppermute | solution.py:571
  173.5 1.5 collective-permute-start.32
  175.0 2.1 %collective-permute-done.32 = f32[4,256]{1,0:T(4,128)S(1)} collective-permute-done((f32[4,256]{1,0:T(4,128)S(1)}, f32[4,256]{1,0:T(4,128)S(1)}, u32[]{:S(2)}, u32[]{:S(2)}) %collective-permute-start.32) | collective-permute-done | bytes 4128 | tf_op jit(solution)/shard_map/ppermute | solution.py:694
  177.1 2.8 %finish.1 = bf16[1024,1024]{1,0:T(8,128)(2,1)} custom-call(s32[2]{0:T(128)S(1)} %pad_add_fusion.3.refs_0_.refs_1_.refs_3_.place, bf16[2,1024,128]{2,1,0:T(8,128)(2,1)S(1)} %get-tuple-element.73.refs_0_, bf16[1,1024,128]{2,1,0:T(8,128)(2,1)S(1)} %get-tuple-element.77.refs_0_.refs_1_, bf16[1,1024,128]{2,1,0:T(8,128)(2,1)S(1)} %get-tuple-element.82.refs_2_, ...), custom_call_target="tpu_custom_call" | custom-call | flops 1 | bytes 1 | tf_op jit(solution)/shard_map/finish/pallas_call | solution.py:528
  (134 shorter events, 21.5 us)
Async XLA Ops:
  0.0 8.3 %collective-permute-start = (s32[4,8]{1,0:T(4,128)}, s32[4,8]{1,0:T(4,128)S(1)}, u32[]{:S(2)}, u32[]{:S(2)}) collective-permute-start(s32[4,8]{1,0:T(4,128)} %param.8), channel_id=1, source_target_pairs={{0,4},{4,0},{8,12},{12,8},{16,20},{20,16},{24,28},{28,24},{1,5},{5... | collective-permute-start | bytes 392 | tf_op jit(solution)/shard_map/selection_swap/ppermute | solution.py:571
  3.8 19.9 %collective-permute-start.3 = (bf16[1,3,1024,128]{3,2,1,0:T(8,128)(2,1)S(1)}, bf16[1,3,1024,128]{3,2,1,0:T(8,128)(2,1)S(1)}, u32[]{:S(2)}, u32[]{:S(2)}) collective-permute-start(bf16[1,3,1024,128]{3,2,1,0:T(8,128)(2,1)S(1)} %get-tuple-element.49), channel_id=1, source_target_pairs={{0,4},{4,0},{8,12},{12,8},{16,20},{20,16},{24,28},{28,24},{1,5},{5... | collective-permute-start | bytes 2359304 | tf_op jit(solution)/shard_map/swap_c0/ppermute | solution.py:571
  5.0 9.5 %copy-start.20 = (s32[8,8]{1,0:T(8,128)S(1)}, s32[8,8]{1,0:T(8,128)}, u32[]{:S(2)}) copy-start(s32[8,8]{1,0:T(8,128)} %constant.157.clone.1) | copy-start | bytes 772
  8.3 6.8 %collective-permute-start.1 = (s32[8,8]{1,0:T(8,128)S(1)}, s32[8,8]{1,0:T(8,128)S(1)}, u32[]{:S(2)}, u32[]{:S(2)}) collective-permute-start(s32[8,8]{1,0:T(8,128)S(1)} %pad_add_fusion.1), channel_id=1, source_target_pairs={{16,8},{20,12},{24,16},{28,20},{17,9},{21,13},{25,17},{29,21},{18,... | collective-permute-start | bytes 776 | tf_op jit(solution)/shard_map/selection_near/ppermute | solution.py:571
  10.7 4.4 %collective-permute-start.2 = (s32[8,8]{1,0:T(8,128)S(1)}, s32[8,8]{1,0:T(8,128)S(1)}, u32[]{:S(2)}, u32[]{:S(2)}) collective-permute-start(s32[8,8]{1,0:T(8,128)S(1)} %pad_add_fusion.1), channel_id=1, source_target_pairs={{24,8},{28,12},{25,9},{29,13},{26,10},{30,14},{27,11},{31,15}} | collective-permute-start | bytes 776 | tf_op jit(solution)/shard_map/selection_far/ppermute | solution.py:571
  20.3 7.5 %copy-start.19 = (bf16[1,3,1024,128]{3,2,1,0:T(8,128)(2,1)S(1)}, bf16[1,3,1024,128]{3,2,1,0:T(8,128)(2,1)}, u32[]{:S(2)}) copy-start(bf16[1,3,1024,128]{3,2,1,0:T(8,128)(2,1)} %copy-done.18) | copy-start | bytes 2359300
  20.3 20.5 %collective-permute-start.4 = (bf16[1,3,1024,128]{3,2,1,0:T(8,128)(2,1)S(1)}, bf16[1,3,1024,128]{3,2,1,0:T(8,128)(2,1)S(1)}, u32[]{:S(2)}, u32[]{:S(2)}) collective-permute-start(bf16[1,3,1024,128]{3,2,1,0:T(8,128)(2,1)S(1)} %get-tuple-element.51), channel_id=1, source_target_pairs={{0,4},{4,0},{8,12},{12,8},{16,20},{20,16},{24,28},{28,24},{1,5},{5... | collective-permute-start | bytes 2359304 | tf_op jit(solution)/shard_map/swap_c1/ppermute | solution.py:571
  23.7 17.4 %copy-start.2 = (bf16[1,3,1024,128]{3,2,1,0:T(8,128)(2,1)}, bf16[1,3,1024,128]{3,2,1,0:T(8,128)(2,1)S(1)}, u32[]{:S(2)}) copy-start(bf16[1,3,1024,128]{3,2,1,0:T(8,128)(2,1)S(1)} %collective-permute-done.3.refs_2_.refs_5_.refs_3_) | copy-start | bytes 2359300
  24.0 27.4 %collective-permute-start.7 = (bf16[2,1,2,1024,128]{4,3,2,1,0:T(8,128)(2,1)S(1)}, bf16[2,1,2,1024,128]{4,3,2,1,0:T(8,128)(2,1)S(1)}, u32[]{:S(2)}, u32[]{:S(2)}) collective-permute-start(bf16[2,1,2,1024,128]{4,3,2,1,0:T(8,128)(2,1)S(1)} %get-tuple-element.54), channel_id=1, source_target_pairs={{0,8},{4,12},{1,9},{5,13},{2,10},{6,14},{3,11},{7,15}} | collective-permute-start | bytes 3145736 | tf_op jit(solution)/shard_map/lift_c0/ppermute | solution.py:571
  24.7 19.7 %collective-permute-start.5 = (bf16[2,1,1024,128]{3,2,1,0:T(8,128)(2,1)S(1)}, bf16[2,1,1024,128]{3,2,1,0:T(8,128)(2,1)S(1)}, u32[]{:S(2)}, u32[]{:S(2)}) collective-permute-start(bf16[2,1,1024,128]{3,2,1,0:T(8,128)(2,1)S(1)} %get-tuple-element.50.refs_0_), channel_id=1, source_target_pairs={{16,8},{20,12},{24,16},{28,20},{17,9},{21,13},{25,17},{29,21},{18,... | collective-permute-start | bytes 1572872 | tf_op jit(solution)/shard_map/near_down_c0/ppermute | solution.py:571
  27.7 29.9 %collective-permute-start.8 = (bf16[1,3,1024,128]{3,2,1,0:T(8,128)(2,1)S(1)}, bf16[1,3,1024,128]{3,2,1,0:T(8,128)(2,1)S(1)}, u32[]{:S(2)}, u32[]{:S(2)}) collective-permute-start(bf16[1,3,1024,128]{3,2,1,0:T(8,128)(2,1)S(1)} %copy-done.19), channel_id=1, source_target_pairs={{0,4},{4,0},{8,12},{12,8},{16,20},{20,16},{24,28},{28,24},{1,5},{5... | collective-permute-start | bytes 2359304 | tf_op jit(solution)/shard_map/swap_c2/ppermute | solution.py:571
  27.8 23.5 %collective-permute-start.6 = (bf16[2,1,1024,128]{3,2,1,0:T(8,128)(2,1)S(1)}, bf16[2,1,1024,128]{3,2,1,0:T(8,128)(2,1)S(1)}, u32[]{:S(2)}, u32[]{:S(2)}) collective-permute-start(bf16[2,1,1024,128]{3,2,1,0:T(8,128)(2,1)S(1)} %get-tuple-element.50.refs_0_), channel_id=1, source_target_pairs={{24,8},{28,12},{25,9},{29,13},{26,10},{30,14},{27,11},{31,15}} | collective-permute-start | bytes 1572872 | tf_op jit(solution)/shard_map/far_down_c0/ppermute | solution.py:571
  41.1 21.4 %collective-permute-start.10 = (bf16[2,1,1024,128]{3,2,1,0:T(8,128)(2,1)S(1)}, bf16[2,1,1024,128]{3,2,1,0:T(8,128)(2,1)S(1)}, u32[]{:S(2)}, u32[]{:S(2)}) collective-permute-start(bf16[2,1,1024,128]{3,2,1,0:T(8,128)(2,1)S(1)} %get-tuple-element.52.refs_0_), channel_id=1, source_target_pairs={{24,8},{28,12},{25,9},{29,13},{26,10},{30,14},{27,11},{31,15}} | collective-permute-start | bytes 1572872 | tf_op jit(solution)/shard_map/far_down_c1/ppermute | solution.py:571
  44.4 8.2 %copy-start.3 = (bf16[1,3,1024,128]{3,2,1,0:T(8,128)(2,1)S(1)}, bf16[1,3,1024,128]{3,2,1,0:T(8,128)(2,1)}, u32[]{:S(2)}) copy-start(bf16[1,3,1024,128]{3,2,1,0:T(8,128)(2,1)} %copy-done.2) | copy-start | bytes 2359300
  44.4 26.2 %collective-permute-start.11 = (bf16[2,1,2,1024,128]{4,3,2,1,0:T(8,128)(2,1)S(1)}, bf16[2,1,2,1024,128]{4,3,2,1,0:T(8,128)(2,1)S(1)}, u32[]{:S(2)}, u32[]{:S(2)}) collective-permute-start(bf16[2,1,2,1024,128]{4,3,2,1,0:T(8,128)(2,1)S(1)} %get-tuple-element.59), channel_id=1, source_target_pairs={{0,8},{4,12},{1,9},{5,13},{2,10},{6,14},{3,11},{7,15}} | collective-permute-start | bytes 3145736 | tf_op jit(solution)/shard_map/lift_c1/ppermute | solution.py:571
  51.3 25.6 %collective-permute-start.14 = (bf16[1,3,1024,128]{3,2,1,0:T(8,128)(2,1)S(1)}, bf16[1,3,1024,128]{3,2,1,0:T(8,128)(2,1)S(1)}, u32[]{:S(2)}, u32[]{:S(2)}) collective-permute-start(bf16[1,3,1024,128]{3,2,1,0:T(8,128)(2,1)S(1)} %get-tuple-element.63), channel_id=1, source_target_pairs={{0,4},{4,0},{8,12},{12,8},{16,20},{20,16},{24,28},{28,24},{1,5},{5... | collective-permute-start | bytes 2359304 | tf_op jit(solution)/shard_map/swap_c3/ppermute | solution.py:571
  51.3 18.6 %collective-permute-start.9 = (bf16[2,1,1024,128]{3,2,1,0:T(8,128)(2,1)S(1)}, bf16[2,1,1024,128]{3,2,1,0:T(8,128)(2,1)S(1)}, u32[]{:S(2)}, u32[]{:S(2)}) collective-permute-start(bf16[2,1,1024,128]{3,2,1,0:T(8,128)(2,1)S(1)} %get-tuple-element.52.refs_0_), channel_id=1, source_target_pairs={{16,8},{20,12},{24,16},{28,20},{17,9},{21,13},{25,17},{29,21},{18,... | collective-permute-start | bytes 1572872 | tf_op jit(solution)/shard_map/near_down_c1/ppermute | solution.py:571
  57.7 48.9 %copy-start = (bf16[1,3,1024,128]{3,2,1,0:T(8,128)(2,1)}, bf16[1,3,1024,128]{3,2,1,0:T(8,128)(2,1)S(1)}, u32[]{:S(2)}) copy-start(bf16[1,3,1024,128]{3,2,1,0:T(8,128)(2,1)S(1)} %collective-permute-done.8.refs_2_.refs_5_.refs_3_) | copy-start | bytes 2359300
  57.7 30.7 %collective-permute-start.12 = (bf16[1,1056,256]{2,1,0:T(8,128)(2,1)S(1)}, bf16[1,1056,256]{2,1,0:T(8,128)(2,1)S(1)}, u32[]{:S(2)}, u32[]{:S(2)}) collective-permute-start(bf16[1,1056,256]{2,1,0:T(8,128)(2,1)S(1)} %get-tuple-element.55.refs_0_), channel_id=1, source_target_pairs={{8,16},{12,20},{16,24},{20,28},{9,17},{13,21},{17,25},{21,29},{10,... | collective-permute-start | bytes 1622024 | tf_op jit(solution)/shard_map/near_up_c0/ppermute | solution.py:571
  62.5 25.8 %collective-permute-start.13 = (bf16[1,1056,256]{2,1,0:T(8,128)(2,1)S(1)}, bf16[1,1056,256]{2,1,0:T(8,128)(2,1)S(1)}, u32[]{:S(2)}, u32[]{:S(2)}) collective-permute-start(bf16[1,1056,256]{2,1,0:T(8,128)(2,1)S(1)} %get-tuple-element.62), channel_id=1, source_target_pairs={{8,24},{12,28},{9,25},{13,29},{10,26},{14,30},{11,27},{15,31}} | collective-permute-start | bytes 1622024 | tf_op jit(solution)/shard_map/far_up_c0/ppermute | solution.py:571
  69.9 35.3 %collective-permute-start.17 = (bf16[2,1,2,1024,128]{4,3,2,1,0:T(8,128)(2,1)S(1)}, bf16[2,1,2,1024,128]{4,3,2,1,0:T(8,128)(2,1)S(1)}, u32[]{:S(2)}, u32[]{:S(2)}) collective-permute-start(bf16[2,1,2,1024,128]{4,3,2,1,0:T(8,128)(2,1)S(1)} %get-tuple-element.65), channel_id=1, source_target_pairs={{0,8},{4,12},{1,9},{5,13},{2,10},{6,14},{3,11},{7,15}} | collective-permute-start | bytes 3145736 | tf_op jit(solution)/shard_map/lift_c2/ppermute | solution.py:571
  70.7 20.1 %collective-permute-start.15 = (bf16[2,1,1024,128]{3,2,1,0:T(8,128)(2,1)S(1)}, bf16[2,1,1024,128]{3,2,1,0:T(8,128)(2,1)S(1)}, u32[]{:S(2)}, u32[]{:S(2)}) collective-permute-start(bf16[2,1,1024,128]{3,2,1,0:T(8,128)(2,1)S(1)} %get-tuple-element.58.refs_0_), channel_id=1, source_target_pairs={{16,8},{20,12},{24,16},{28,20},{17,9},{21,13},{25,17},{29,21},{18,... | collective-permute-start | bytes 1572872 | tf_op jit(solution)/shard_map/near_down_c2/ppermute | solution.py:571
  77.0 25.0 %collective-permute-start.16 = (bf16[2,1,1024,128]{3,2,1,0:T(8,128)(2,1)S(1)}, bf16[2,1,1024,128]{3,2,1,0:T(8,128)(2,1)S(1)}, u32[]{:S(2)}, u32[]{:S(2)}) collective-permute-start(bf16[2,1,1024,128]{3,2,1,0:T(8,128)(2,1)S(1)} %get-tuple-element.58.refs_0_), channel_id=1, source_target_pairs={{24,8},{28,12},{25,9},{29,13},{26,10},{30,14},{27,11},{31,15}} | collective-permute-start | bytes 1572872 | tf_op jit(solution)/shard_map/far_down_c2/ppermute | solution.py:571
  88.4 20.2 %copy-start.8 = (bf16[1,1056,256]{2,1,0:T(8,128)(2,1)}, bf16[1,1056,256]{2,1,0:T(8,128)(2,1)S(1)}, u32[]{:S(2)}) copy-start(bf16[1,1056,256]{2,1,0:T(8,128)(2,1)S(1)} %collective-permute-done.12.refs_2_.refs_5_) | copy-start | bytes 1622020
  88.4 20.2 %copy-start.10 = (bf16[1,1056,256]{2,1,0:T(8,128)(2,1)}, bf16[1,1056,256]{2,1,0:T(8,128)(2,1)S(1)}, u32[]{:S(2)}) copy-start(bf16[1,1056,256]{2,1,0:T(8,128)(2,1)S(1)} %collective-permute-done.13.refs_3_.refs_6_) | copy-start | bytes 1622020
  88.7 30.9 %collective-permute-start.20 = (bf16[2,1,2,1024,128]{4,3,2,1,0:T(8,128)(2,1)S(1)}, bf16[2,1,2,1024,128]{4,3,2,1,0:T(8,128)(2,1)S(1)}, u32[]{:S(2)}, u32[]{:S(2)}) collective-permute-start(bf16[2,1,2,1024,128]{4,3,2,1,0:T(8,128)(2,1)S(1)} %get-tuple-element.67), channel_id=1, source_target_pairs={{0,8},{4,12},{1,9},{5,13},{2,10},{6,14},{3,11},{7,15}} | collective-permute-start | bytes 3145736 | tf_op jit(solution)/shard_map/lift_c3/ppermute | solution.py:571
  89.4 33.6 %collective-permute-start.21 = (bf16[1,1056,256]{2,1,0:T(8,128)(2,1)S(1)}, bf16[1,1056,256]{2,1,0:T(8,128)(2,1)S(1)}, u32[]{:S(2)}, u32[]{:S(2)}) collective-permute-start(bf16[1,1056,256]{2,1,0:T(8,128)(2,1)S(1)} %get-tuple-element.60.refs_0_), channel_id=1, source_target_pairs={{8,16},{12,20},{16,24},{20,28},{9,17},{13,21},{17,25},{21,29},{10,... | collective-permute-start | bytes 1622024 | tf_op jit(solution)/shard_map/near_up_c1/ppermute | solution.py:571
  90.7 21.8 %collective-permute-start.18 = (bf16[2,1,1024,128]{3,2,1,0:T(8,128)(2,1)S(1)}, bf16[2,1,1024,128]{3,2,1,0:T(8,128)(2,1)S(1)}, u32[]{:S(2)}, u32[]{:S(2)}) collective-permute-start(bf16[2,1,1024,128]{3,2,1,0:T(8,128)(2,1)S(1)} %get-tuple-element.64.refs_0_), channel_id=1, source_target_pairs={{16,8},{20,12},{24,16},{28,20},{17,9},{21,13},{25,17},{29,21},{18,... | collective-permute-start | bytes 1572872 | tf_op jit(solution)/shard_map/near_down_c3/ppermute | solution.py:571
  102.0 16.2 %collective-permute-start.19 = (bf16[2,1,1024,128]{3,2,1,0:T(8,128)(2,1)S(1)}, bf16[2,1,1024,128]{3,2,1,0:T(8,128)(2,1)S(1)}, u32[]{:S(2)}, u32[]{:S(2)}) collective-permute-start(bf16[2,1,1024,128]{3,2,1,0:T(8,128)(2,1)S(1)} %get-tuple-element.64.refs_0_), channel_id=1, source_target_pairs={{24,8},{28,12},{25,9},{29,13},{26,10},{30,14},{27,11},{31,15}} | collective-permute-start | bytes 1572872 | tf_op jit(solution)/shard_map/far_down_c3/ppermute | solution.py:571
  105.2 3.4 %copy-start.6 = (bf16[2,1,2,1024,128]{4,3,2,1,0:T(8,128)(2,1)}, bf16[2,1,2,1024,128]{4,3,2,1,0:T(8,128)(2,1)S(1)}, u32[]{:S(2)}) copy-start(bf16[2,1,2,1024,128]{4,3,2,1,0:T(8,128)(2,1)S(1)} %collective-permute-done.17.refs_6_.refs_4_) | copy-start | bytes 3145732
  105.2 24.9 %collective-permute-start.22 = (bf16[1,1056,256]{2,1,0:T(8,128)(2,1)}, bf16[1,1056,256]{2,1,0:T(8,128)(2,1)}, u32[]{:S(2)}, u32[]{:S(2)}) collective-permute-start(bf16[1,1056,256]{2,1,0:T(8,128)(2,1)} %get-tuple-element.72), channel_id=1, source_target_pairs={{8,24},{12,28},{9,25},{13,29},{10,26},{14,30},{11,27},{15,31}} | collective-permute-start | bytes 1622024 | tf_op jit(solution)/shard_map/far_up_c1/ppermute | solution.py:571
  112.5 31.3 %collective-permute-start.23 = (bf16[1,1056,256]{2,1,0:T(8,128)(2,1)}, bf16[1,1056,256]{2,1,0:T(8,128)(2,1)}, u32[]{:S(2)}, u32[]{:S(2)}) collective-permute-start(bf16[1,1056,256]{2,1,0:T(8,128)(2,1)} %get-tuple-element.66.refs_0_), channel_id=1, source_target_pairs={{8,16},{12,20},{16,24},{20,28},{9,17},{13,21},{17,25},{21,29},{10,... | collective-permute-start | bytes 1622024 | tf_op jit(solution)/shard_map/near_up_c2/ppermute | solution.py:571
  118.2 7.2 %copy-start.1 = (bf16[1,3,1024,128]{3,2,1,0:T(8,128)(2,1)S(1)}, bf16[1,3,1024,128]{3,2,1,0:T(8,128)(2,1)}, u32[]{:S(2)}) copy-start(bf16[1,3,1024,128]{3,2,1,0:T(8,128)(2,1)} %copy-done) | copy-start | bytes 2359300
  118.2 31.4 %collective-permute-start.24 = (bf16[1,1056,256]{2,1,0:T(8,128)(2,1)}, bf16[1,1056,256]{2,1,0:T(8,128)(2,1)}, u32[]{:S(2)}, u32[]{:S(2)}) collective-permute-start(bf16[1,1056,256]{2,1,0:T(8,128)(2,1)} %get-tuple-element.76), channel_id=1, source_target_pairs={{8,24},{12,28},{9,25},{13,29},{10,26},{14,30},{11,27},{15,31}} | collective-permute-start | bytes 1622024 | tf_op jit(solution)/shard_map/far_up_c2/ppermute | solution.py:571
  121.7 36.6 %collective-permute-start.25 = (bf16[1,1056,256]{2,1,0:T(8,128)(2,1)}, bf16[1,1056,256]{2,1,0:T(8,128)(2,1)}, u32[]{:S(2)}, u32[]{:S(2)}) collective-permute-start(bf16[1,1056,256]{2,1,0:T(8,128)(2,1)} %get-tuple-element.68.refs_0_), channel_id=1, source_target_pairs={{8,16},{12,20},{16,24},{20,28},{9,17},{13,21},{17,25},{21,29},{10,... | collective-permute-start | bytes 1622024 | tf_op jit(solution)/shard_map/near_up_c3/ppermute | solution.py:571
  123.8 40.4 %collective-permute-start.26 = (bf16[1,1056,256]{2,1,0:T(8,128)(2,1)}, bf16[1,1056,256]{2,1,0:T(8,128)(2,1)}, u32[]{:S(2)}, u32[]{:S(2)}) collective-permute-start(bf16[1,1056,256]{2,1,0:T(8,128)(2,1)} %get-tuple-element.81), channel_id=1, source_target_pairs={{8,24},{12,28},{9,25},{13,29},{10,26},{14,30},{11,27},{15,31}} | collective-permute-start | bytes 1622024 | tf_op jit(solution)/shard_map/far_up_c3/ppermute | solution.py:571
  126.6 3.5 %copy-start.9 = (bf16[1,1056,256]{2,1,0:T(8,128)(2,1)S(1)}, bf16[1,1056,256]{2,1,0:T(8,128)(2,1)}, u32[]{:S(2)}) copy-start(bf16[1,1056,256]{2,1,0:T(8,128)(2,1)} %copy-done.8) | copy-start | bytes 1622020
  126.6 3.5 %copy-start.11 = (bf16[1,1056,256]{2,1,0:T(8,128)(2,1)S(1)}, bf16[1,1056,256]{2,1,0:T(8,128)(2,1)}, u32[]{:S(2)}) copy-start(bf16[1,1056,256]{2,1,0:T(8,128)(2,1)} %copy-done.10) | copy-start | bytes 1622020
  126.6 3.5 %copy-start.13 = (f32[1,8,128,256]{3,2,1,0:T(8,128)S(1)}, f32[1,8,128,256]{3,2,1,0:T(8,128)}, u32[]{:S(2)}) copy-start(f32[1,8,128,256]{3,2,1,0:T(8,128)} %copy-done.12) | copy-start | bytes 3145732
  126.6 3.6 %copy-start.17 = (bf16[1,1056,256]{2,1,0:T(8,128)(2,1)S(1)}, bf16[1,1056,256]{2,1,0:T(8,128)(2,1)}, u32[]{:S(2)}) copy-start(bf16[1,1056,256]{2,1,0:T(8,128)(2,1)} %copy-done.16) | copy-start | bytes 1622020
  133.3 18.4 %copy-start.5 = (bf16[2,1,2,1024,128]{4,3,2,1,0:T(8,128)(2,1)S(1)}, bf16[2,1,2,1024,128]{4,3,2,1,0:T(8,128)(2,1)}, u32[]{:S(2)}) copy-start(bf16[2,1,2,1024,128]{4,3,2,1,0:T(8,128)(2,1)} %copy-done.4) | copy-start | bytes 3145732
  133.3 43.8 %collective-permute-start.27 = (bf16[2,1024,128]{2,1,0:T(8,128)(2,1)S(1)}, bf16[2,1024,128]{2,1,0:T(8,128)(2,1)S(1)}, u32[]{:S(2)}, u32[]{:S(2)}) collective-permute-start(bf16[2,1024,128]{2,1,0:T(8,128)(2,1)S(1)} %get-tuple-element.83), channel_id=1, source_target_pairs={{0,4},{4,0},{8,12},{12,8},{16,20},{20,16},{24,28},{28,24},{1,5},{5... | collective-permute-start | bytes 1572872 | tf_op jit(solution)/shard_map/back_c0/ppermute | solution.py:571
  151.3 25.8 %collective-permute-start.28 = (bf16[1,1024,128]{2,1,0:T(8,128)(2,1)S(1)}, bf16[1,1024,128]{2,1,0:T(8,128)(2,1)S(1)}, u32[]{:S(2)}, u32[]{:S(2)}) collective-permute-start(bf16[1,1024,128]{2,1,0:T(8,128)(2,1)S(1)} %get-tuple-element.84), channel_id=1, source_target_pairs={{0,4},{4,0},{8,12},{12,8},{16,20},{20,16},{24,28},{28,24},{1,5},{5... | collective-permute-start | bytes 786440 | tf_op jit(solution)/shard_map/back_c2/ppermute | solution.py:571
  151.7 23.4 %copy-start.21 = (bf16[1024]{0:T(1024)(128)(2,1)S(1)}, bf16[1024]{0:T(1024)(128)(2,1)}, u32[]{:S(2)}) copy-start(bf16[1024]{0:T(1024)(128)(2,1)} %param.9) | copy-start | bytes 6148
  165.9 11.3 %collective-permute-start.29 = (bf16[1,1024,128]{2,1,0:T(8,128)(2,1)S(1)}, bf16[1,1024,128]{2,1,0:T(8,128)(2,1)S(1)}, u32[]{:S(2)}, u32[]{:S(2)}) collective-permute-start(bf16[1,1024,128]{2,1,0:T(8,128)(2,1)S(1)} %get-tuple-element.85), channel_id=1, source_target_pairs={{0,4},{4,0},{8,12},{12,8},{16,20},{20,16},{24,28},{28,24},{1,5},{5... | collective-permute-start | bytes 786440 | tf_op jit(solution)/shard_map/back_c3/ppermute | solution.py:571
  166.2 6.1 %collective-permute-start.30 = (f32[4,256]{1,0:T(4,128)S(1)}, f32[4,256]{1,0:T(4,128)S(1)}, u32[]{:S(2)}, u32[]{:S(2)}) collective-permute-start(f32[4,256]{1,0:T(4,128)S(1)} %slice.15), channel_id=1, source_target_pairs={{0,4},{4,0},{8,12},{12,8},{16,20},{20,16},{24,28},{28,24},{1,5},{5... | collective-permute-start | bytes 12296 | tf_op jit(solution)/shard_map/squares_swap/ppermute | solution.py:571
  172.3 1.2 collective-permute-start.31
  173.5 3.6 %collective-permute-start.32 = (f32[4,256]{1,0:T(4,128)S(1)}, f32[4,256]{1,0:T(4,128)S(1)}, u32[]{:S(2)}, u32[]{:S(2)}) collective-permute-start(f32[4,256]{1,0:T(4,128)S(1)} %add.298), channel_id=1, source_target_pairs={{0,2},{1,3},{2,0},{3,1},{4,6},{5,7},{6,4},{7,5},{8,10},{9,11},{10,... | collective-permute-start | bytes 12296 | tf_op jit(solution)/shard_map/ppermute | solution.py:694
  (8 other events, 13.8 us)

commit v6 on v5

--- a/solution.py
+++ b/solution.py
@@ -128,14 +128,16 @@
     )
 
 
-SIZES = (1, 1, 1, 1,)
-SPLIT = (False, False, False, False,)
+SPLIT = (True, True, False, False)
+SCATTER = (False, False, False, False)
 ORDER = (
-    ("p", 0),
+    ("p", 0, 1),
+    ("w", "plans"),
+    ("w", "near_down_keep_c0"),
+    ("w", "far_down_keep_c0"),
+    ("w", "lift_keep_c0"),
+    ("j", 0),
     ("p", 2),
-    ("w", "plans"),
-    ("p", 1),
-    ("j", 0),
     ("j", 1),
     ("p", 3),
     ("s", 0),
@@ -143,19 +145,19 @@
     ("j", 2),
     ("s", 1),
     ("a", 1),
-    ("w", "lift_c1"),
     ("w", "near_up_c0"),
     ("w", "far_up_c0"),
     ("j", 3),
     ("s", 2),
-    ("s", 3),
     ("a", 2),
     ("m", 0, 1),
+    ("a", 3),
+    ("s", 3),
     ("m", 2),
-    ("a", 3),
     ("m", 3),
 )
-LSE_ROWS = 32
+COSTS = {"pack": 0.0, "join": 0.0, "served": 0.0, "own": 0.0, "merge": 0.0, "finish": 0.0}
+DIRECT = True
 UNROLL = 2
 VMEM_LIMIT = 16 * 1024 * 1024
 
@@ -170,6 +172,7 @@
 
 PIECES = {
     "head": lambda ref, h: ref.at[h],
+    "next head": lambda ref, h: ref.at[h + 1],
     "queries": lambda ref, h: ref.at[h, 0],
     "keys_values": lambda ref, h: ref.at[h, pl.ds(1, 2)],
     "first": lambda ref, h: ref.at[0, h],
@@ -177,11 +180,12 @@
 }
 
 
-def attention_kernel(shape, own, q_pieces, kv_pieces, n_in, plan, *refs):
+def attention_kernel(shape, own, groups, q_pieces, kv_pieces, n_in, plan, *refs):
     heads, per_dev, block_rows = shape
     n_q, n_kv = len(q_pieces), len(kv_pieces)
     inputs, refs = refs[:n_in], refs[n_in:]
-    outs, refs = refs[:2], refs[2:]
+    n_out = len(groups) + 2 * own
+    outs, refs = refs[:n_out], refs[n_out:]
     (q_scr, kv_scr, s0, s1, p0, p1, d0, d1, acc_scr, top_scr, sum_scr, o_scr, lse_scr, sems) = refs[:14]
     s_scr, p_scr, decay_scr = (s0, s1), (p0, p1), (d0, d1)
     spans = n_q * per_dev
@@ -257,19 +261,33 @@
 
         lax.fori_loop(0, (plan[0] + 1) // 2, two_steps, 0)
         if own:
-            outs[0][h] = o_scr[:spans]
-            outs[1][h] = lse_scr[:spans, :]
-        else:
-            half = spans // 2
-            for side in range(2):
-                for span in range(half):
-                    outs[side][h, span * HD : (span + 1) * HD, :] = o_scr[side * half + span]
-                lse = lse_scr[side * half : (side + 1) * half, :]
-                high = lse.astype(jnp.bfloat16).astype(jnp.float32)
-                middle = (lse - high).astype(jnp.bfloat16).astype(jnp.float32)
-                rest = jnp.zeros((LSE_ROWS - 3 * half, block_rows), jnp.float32)
-                parts = jnp.concatenate([high, middle, lse - high - middle, rest], axis=0)
-                outs[side][h, half * HD :, :] = parts.astype(jnp.bfloat16)
+            kept = outs[0].shape[1]
+            outs[0][h] = o_scr[:kept]
+            outs[1][h] = lse_scr[:kept, :]
+        for out, (start, stop) in zip(outs[2 if own else 0 :], groups):
+            n = stop - start
+            for span in range(n):
+                out[h, span * HD : (span + 1) * HD, :] = o_scr[start + span].astype(jnp.bfloat16)
+            lse = lse_scr[start:stop, :]
+            high = lse.astype(jnp.bfloat16).astype(jnp.float32)
+            middle = (lse - high).astype(jnp.bfloat16).astype(jnp.float32)
+            rest = jnp.zeros((lse_rows(n) - 3 * n, block_rows), jnp.float32)
+            parts = jnp.concatenate([high, middle, lse - high - middle, rest], axis=0)
+            out[h, n * HD :, :] = parts.astype(jnp.bfloat16)
+
+
+def lse_rows(spans):
+    return -(-3 * spans // 16) * 16
+
+
+def unpacked_lse(ref, h, spans):
+    parts = ref[h, spans * HD :, :].astype(jnp.float32)
+    return parts[:spans] + parts[spans : 2 * spans] + parts[2 * spans : 3 * spans]
+
+
+def cost(name):
+    us = COSTS[name]
+    return pl.CostEstimate(flops=int(us * 1e9) + 1, bytes_accessed=int(us * 3.4e6) + 1, transcendentals=0)
 
 
 def ordered(kernel, n_after):
@@ -279,7 +297,7 @@
     return body
 
 
-def attention_call(plan, q_pieces, kv_pieces, own, heads, per_dev, block_rows, after=()):
+def attention_call(plan, q_pieces, kv_pieces, own, direct, heads, per_dev, block_rows, after=()):
     inputs = []
 
     def numbered(pieces):
@@ -296,13 +314,19 @@
     vmem, hbm = pl.BlockSpec(memory_space=pltpu.VMEM), pl.BlockSpec(memory_space=pltpu.HBM)
     f32, bf16 = jnp.float32, jnp.bfloat16
     if own:
-        out_shape = (
-            jax.ShapeDtypeStruct((heads, spans, HD, block_rows), f32),
-            jax.ShapeDtypeStruct((heads, spans, block_rows), f32),
-        )
+        kept = per_dev if direct else spans
+        groups = ((per_dev, spans),) if direct else ()
+        out_shape = [
+            jax.ShapeDtypeStruct((heads, kept, HD, block_rows), f32),
+            jax.ShapeDtypeStruct((heads, kept, block_rows), f32),
+        ]
     else:
-        packed = jax.ShapeDtypeStruct((heads, spans // 2 * HD + LSE_ROWS, block_rows), bf16)
-        out_shape = (packed, packed)
+        size = per_dev if direct else 2 * per_dev
+        groups = tuple((start, start + size) for start in range(0, spans, size))
+        out_shape = []
+    for start, stop in groups:
+        packed_rows = (stop - start) * HD + lse_rows(stop - start)
+        out_shape.append(jax.ShapeDtypeStruct((heads, packed_rows, block_rows), bf16))
     scratch = [
         pltpu.VMEM((heads, n_q, per_dev * block_rows, HD), bf16),
         pltpu.VMEM((heads, n_kv, 2, per_dev * block_rows, HD), bf16),
@@ -324,59 +348,74 @@
     return pl.pallas_call(
         ordered(
             partial(
-                attention_kernel, (heads, per_dev, block_rows), own, q_pieces, kv_pieces, len(inputs)
+                attention_kernel,
+                (heads, per_dev, block_rows),
+                own,
+                groups,
+                q_pieces,
+                kv_pieces,
+                len(inputs),
             ),
             len(after),
         ),
         out_shape=out_shape,
         in_specs=[hbm] * len(after) + [pl.BlockSpec(memory_space=pltpu.SMEM)] + [hbm] * len(inputs),
-        out_specs=(vmem, vmem),
+        out_specs=[vmem] * len(out_shape),
         scratch_shapes=scratch,
         compiler_params=pltpu.CompilerParams(vmem_limit_bytes=VMEM_LIMIT),
-        cost_estimate=pl.CostEstimate(flops=1, bytes_accessed=1, transcendentals=0),
+        cost_estimate=cost("own" if own else "served"),
         name="own_attention" if own else "served_attention",
     )(*after, plan, *inputs)
 
 
 def pack_kernel(shape, place, q_ref, k_ref, v_ref, *refs):
-    heads, first, half, rows, split = shape
+    heads, first, half, rows, split, scatter = shape
     outs, (scr, t_scr, sems) = refs[:-3], refs[-3:]
     loads, stores = {}, []
-    for side in (1, 0):
+    places = [(side, h) for h in range(heads) for side in (1, 0)]
+    for side, h in places:
+        start = pl.multiple_of((place[side] * half + first + h) * HD, HD)
+        for i, ref in enumerate((q_ref, k_ref, v_ref)):
+            loads[side, h, i] = pltpu.make_async_copy(
+                ref.at[:, pl.ds(start, HD)], scr.at[side, h, i], sems.at[0, side, h, i]
+            )
+            loads[side, h, i].start()
+
+    if scatter:
         for h in range(heads):
-            start = pl.multiple_of((place[side] * half + first + h) * HD, HD)
-            for i, ref in enumerate((q_ref, k_ref, v_ref)):
-                load = pltpu.make_async_copy(
-                    ref.at[:, pl.ds(start, HD)], scr.at[side, h, i], sems.at[0, side, h, i]
+            t_scr[0, h] = jnp.zeros_like(t_scr[0, h])
+            for i in range(3):
+                blank = pltpu.make_async_copy(
+                    t_scr.at[0, h], outs[-heads + h].at[place[0], i], sems.at[2, 0, h, i]
                 )
-                load.start()
-                loads[side, h, i] = load
+                blank.start()
+                blank.wait()
 
     def store(side, h, i, source):
-        if split:
-            out = outs[2 * side + (i > 0)]
-            target = out.at[h, i - 1] if i else out.at[h]
+        if side:
+            target = outs[-heads + h].at[place[1] if scatter else 0, i]
+        elif split:
+            target = outs[1].at[h, i - 1] if i else outs[0].at[h]
         else:
-            target = outs[side].at[h, i]
+            target = outs[0].at[h, i]
         copy = pltpu.make_async_copy(source, target, sems.at[1, side, h, i])
         copy.start()
         stores.append(copy)
 
-    for side in (1, 0):
-        for h in range(heads):
-            for i in range(2):
-                loads[side, h, i].wait()
-                store(side, h, i, scr.at[side, h, i])
-            loads[side, h, 2].wait()
-            for tile in range(rows // HD):
-                at = slice(tile * HD, (tile + 1) * HD)
-                t_scr[side, h, at, :] = scr[side, h, 2, at, :].T
-            store(side, h, 2, t_scr.at[side, h])
+    for side, h in places:
+        for i in range(2):
+            loads[side, h, i].wait()
+            store(side, h, i, scr.at[side, h, i])
+        loads[side, h, 2].wait()
+        for tile in range(rows // HD):
+            at = slice(tile * HD, (tile + 1) * HD)
+            t_scr[side, h, at, :] = scr[side, h, 2, at, :].T
+        store(side, h, 2, t_scr.at[side, h])
     for copy in stores:
         copy.wait()
 
 
-def pack_call(place, queries, keys, values, heads, first, half, split, after=()):
+def pack_call(place, queries, keys, values, heads, first, half, split, scatter, after=()):
     rows = queries.shape[0]
     hbm = pl.BlockSpec(memory_space=pltpu.HBM)
     bf16 = jnp.bfloat16
@@ -384,26 +423,62 @@
         pltpu.with_memory_space_constraint(array, pltpu.HBM) for array in (queries, keys, values)
     )
     if split:
-        side = [
+        outs = [
             jax.ShapeDtypeStruct((heads, rows, HD), bf16),
             jax.ShapeDtypeStruct((heads, 2, rows, HD), bf16),
         ]
     else:
-        side = [jax.ShapeDtypeStruct((heads, 3, rows, HD), bf16)]
+        outs = [jax.ShapeDtypeStruct((heads, 3, rows, HD), bf16)]
+    outs += [jax.ShapeDtypeStruct((2 if scatter else 1, 3, rows, HD), bf16)] * heads
     return pl.pallas_call(
-        ordered(partial(pack_kernel, (heads, first, half, rows, split)), len(after)),
-        out_shape=side * 2,
+        ordered(partial(pack_kernel, (heads, first, half, rows, split, scatter)), len(after)),
+        out_shape=outs,
         in_specs=[hbm] * len(after) + [pl.BlockSpec(memory_space=pltpu.SMEM)] + [hbm] * 3,
-        out_specs=[hbm] * (2 * len(side)),
+        out_specs=[hbm] * len(outs),
         scratch_shapes=[
             pltpu.VMEM((2, heads, 3, rows, HD), bf16),
             pltpu.VMEM((2, heads, rows, HD), bf16),
-            pltpu.SemaphoreType.DMA((2, 2, heads, 3)),
+            pltpu.SemaphoreType.DMA((3, 2, heads, 3)),
         ],
         compiler_params=pltpu.CompilerParams(vmem_limit_bytes=VMEM_LIMIT),
-        cost_estimate=pl.CostEstimate(flops=1, bytes_accessed=1, transcendentals=0),
+        cost_estimate=cost("pack"),
         name="pack",
     )(*after, place, queries, keys, values)
+
+
+def cut_kernel(ref, q_ref, kv_ref, scr, sems):
+    load = pltpu.make_async_copy(ref, scr, sems.at[0])
+    load.start()
+    load.wait()
+    stores = [
+        pltpu.make_async_copy(scr.at[0, 0], q_ref.at[0], sems.at[1]),
+        pltpu.make_async_copy(scr.at[0, pl.ds(1, 2)], kv_ref.at[0], sems.at[2]),
+    ]
+    for store in stores:
+        store.start()
+    for store in stores:
+        store.wait()
+
+
+def cut_call(packed, after=()):
+    _, _, rows, _ = packed.shape
+    hbm = pl.BlockSpec(memory_space=pltpu.HBM)
+    return pl.pallas_call(
+        ordered(cut_kernel, len(after)),
+        out_shape=(
+            jax.ShapeDtypeStruct((1, rows, HD), jnp.bfloat16),
+            jax.ShapeDtypeStruct((1, 2, rows, HD), jnp.bfloat16),
+        ),
+        in_specs=[hbm] * (len(after) + 1),
+        out_specs=(hbm, hbm),
+        scratch_shapes=[
+            pltpu.VMEM(packed.shape, jnp.bfloat16),
+            pltpu.SemaphoreType.DMA((3,)),
+        ],
+        compiler_params=pltpu.CompilerParams(vmem_limit_bytes=VMEM_LIMIT),
+        cost_estimate=cost("join"),
+        name="join",
+    )(*after, packed)
 
 
 def join_kernel(heads, keep_ref, swap_ref, q_ref, kv_ref, scr, sems):
@@ -446,7 +521,7 @@
             pltpu.SemaphoreType.DMA((3, 2, heads)),
         ],
         compiler_params=pltpu.CompilerParams(vmem_limit_bytes=VMEM_LIMIT),
-        cost_estimate=pl.CostEstimate(flops=1, bytes_accessed=1, transcendentals=0),
+        cost_estimate=cost("join"),
         name="join",
     )(*after, keep, swapped)
 
@@ -461,9 +536,7 @@
         for h in range(size):
             lses = [own_lse_ref[h]]
             for i, ref in enumerate((near_ref, far_ref)):
-                parts = ref[h, spans * HD :, :].astype(jnp.float32)
-                lse = parts[:spans] + parts[spans : 2 * spans] + parts[2 * spans : 3 * spans]
-                lses.append(jnp.where(valid[i] > 0, lse, -1e30))
+                lses.append(jnp.where(valid[i] > 0, unpacked_lse(ref, h, spans), -1e30))
             top = jnp.maximum(jnp.maximum(lses[0], lses[1]), lses[2])
             weights = [jnp.exp2(lse - top) for lse in lses]
             scale = 1.0 / (weights[0] + weights[1] + weights[2])
@@ -496,9 +569,49 @@
         + [vmem] * (1 + len(arrays)),
         out_specs=(vmem, vmem, vmem),
         compiler_params=pltpu.CompilerParams(vmem_limit_bytes=VMEM_LIMIT),
-        cost_estimate=pl.CostEstimate(flops=1, bytes_accessed=1, transcendentals=0),
+        cost_estimate=cost("merge"),
         name="merge",
     )(*after, valid, sofar, *arrays)
+
+
+def own_merge_kernel(per_dev, block_rows, valid, sofar_ref, squares_in_ref, own_ref, own_lse_ref, *refs):
+    other_ref, packs, outs, squares_ref = refs[0], refs[1:5], refs[5:7], refs[7]
+    squares_ref[...] = sofar_ref[:per_dev, :] + squares_in_ref[...]
+    for side in range(2):
+        arrivals = (packs[side], packs[2 + side])
+        lses = [unpacked_lse(other_ref, 0, per_dev) if side else own_lse_ref[0]]
+        for i, ref in enumerate(arrivals):
+            lses.append(jnp.where(valid[i] > 0, unpacked_lse(ref, 0, per_dev), -1e30))
+        top = jnp.maximum(jnp.maximum(lses[0], lses[1]), lses[2])
+        weights = [jnp.exp2(lse - top) for lse in lses]
+        scale = 1.0 / (weights[0] + weights[1] + weights[2])
+        weights = [weight * scale for weight in weights]
+        for span in range(per_dev):
+            rows = slice(span, span + 1)
+            tile = slice(span * HD, (span + 1) * HD)
+            mixed = other_ref[0, tile, :].astype(jnp.float32) if side else own_ref[0, span]
+            mixed = weights[0][rows, :] * mixed
+            for weight, ref in zip(weights[1:], arrivals):
+                mixed = mixed + weight[rows, :] * ref[0, tile, :].astype(jnp.float32)
+            squares_ref[rows, :] = squares_ref[rows, :] + jnp.sum(mixed * mixed, axis=0, keepdims=True)
+            at = slice(span * block_rows, (span + 1) * block_rows)
+            outs[side][0, at, :] = mixed.T.astype(jnp.bfloat16)
+
+
+def own_merge_call(valid, sofar, squares_in, own, other, packs, per_dev, after=()):
+    block_rows = sofar.shape[1]
+    vmem = pl.BlockSpec(memory_space=pltpu.VMEM)
+    hbm = pl.BlockSpec(memory_space=pltpu.HBM)
+    packed = jax.ShapeDtypeStruct((1, per_dev * block_rows, HD), jnp.bfloat16)
+    return pl.pallas_call(
+        ordered(partial(own_merge_kernel, per_dev, block_rows), len(after)),
+        out_shape=(packed, packed, jax.ShapeDtypeStruct((per_dev, block_rows), jnp.float32)),
+        in_specs=[hbm] * len(after) + [pl.BlockSpec(memory_space=pltpu.SMEM)] + [vmem] * 9,
+        out_specs=(vmem, vmem, vmem),
+        compiler_params=pltpu.CompilerParams(vmem_limit_bytes=VMEM_LIMIT),
+        cost_estimate=cost("merge"),
+        name="merge",
+    )(*after, valid, sofar, squares_in, *own, other, *packs)
 
 
 def finish_kernel(per_dev, sizes, place, *refs):
@@ -531,7 +644,7 @@
         in_specs=[pl.BlockSpec(memory_space=pltpu.SMEM)] + [vmem] * (2 * len(kept) + 2),
         out_specs=vmem,
         compiler_params=pltpu.CompilerParams(vmem_limit_bytes=VMEM_LIMIT),
-        cost_estimate=pl.CostEstimate(flops=1, bytes_accessed=1, transcendentals=0),
+        cost_estimate=cost("finish"),
         name="finish",
     )(place, *kept, *returned, squares, gain.reshape(1, width))
 
@@ -571,18 +684,30 @@
             sent[name] = lax.ppermute(array, "ctx", pairs)
         return sent[name]
 
+    def exchange(array, name):
+        pairs = [[d, d + 1] for d in range(0, 8, 2)]
+        with jax.named_scope(name):
+            sent[name] = lax.psum_scatter(
+                array, "ctx", scatter_dimension=0, axis_index_groups=pairs, tiled=True
+            )
+        return sent[name]
+
     swap = [(d, d ^ 1) for d in range(8)]
     lift = [(0, 2), (1, 3)]
     near_down, far_down = [(4, 2), (5, 3), (6, 4), (7, 5)], [(6, 2), (7, 3)]
+
+    def crossed(pairs):
+        return [(source, target ^ 1) for source, target in pairs]
+
     near_up, far_up = [(2, 4), (3, 5), (4, 6), (5, 7)], [(2, 6), (3, 7)]
     valid = jnp.stack([level >= 2, level >= 3]).astype(jnp.int32)
     place = jnp.stack([x, 1 - x]).astype(jnp.int32)
 
     own_selection = jnp.concatenate([selection, to(selection, swap, "selection_swap")], axis=0)
-    near_selection, far_selection = (
-        to(own_selection, near_down, "selection_near"),
-        to(own_selection, far_down, "selection_far"),
-    )
+    above = to(own_selection, [(6, 4), (7, 5)], "selection_near")
+    two = to(jnp.concatenate([own_selection, above], axis=0), [(4, 2), (5, 3)], "selection_far")
+    near_selection = jnp.where(level == 2, above, two[:spans])
+    far_selection = two[spans:]
 
     def ids(at):
         first = jnp.stack([(at * 2 + x) * per_dev, (at * 2 + 1 - x) * per_dev])
@@ -610,75 +735,114 @@
     live = (others != jnp.concatenate([ids(level + 1), ids(level + 2)], axis=0)) & mine
     served_plan = plan_of(live, slot, jnp.zeros_like(others), 2 * spans)
 
-    sizes, split, order = SIZES, SPLIT, ORDER
-    n = len(sizes)
-    own_pieces, z_arrays, served_pieces = [None] * n, [None] * n, [None] * n
-    ups, owns, kept, returned = [None] * n, [None] * n, [], []
+    n, split, order = half, SPLIT, ORDER
+    own_pieces, z_arrays, served_pieces, downs_of = {}, {}, {}, {}
+    ups, owns, others, squares_in, kept, returned = {}, {}, {}, [], [], []
     squares = [jnp.zeros((spans, block_rows), jnp.float32)]
     last = []
 
-    def pack(c):
+    def downs(q, kv, name):
+        low = to(kv, lift, f"lift_{name}")
+        far = to(q, far_down, f"far_down_{name}")
+        return to(q, near_down, f"near_down_{name}"), far, low
+
+    def pack(*chunks):
+        c = chunks[0]
         packed = pack_call(
-            place, queries, keys, values, sizes[c], sum(sizes[:c]), half, split[c], last
+            place, queries, keys, values, len(chunks), c, half, split[c], SCATTER[c], last
         )
         last[:] = [packed[0]]
+        if SCATTER[c]:
+            swapped = [exchange(p, f"swap_c{d}") for d, p in zip(chunks, packed[-len(chunks) :])]
+        else:
+            swapped = [to(p, swap, f"swap_c{d}") for d, p in zip(chunks, packed[-len(chunks) :])]
         if split[c]:
-            q_keep, kv_keep, q_send, kv_send = packed
-            z_arrays[c] = (q_keep, kv_keep)
-            kv_swap = to(kv_send, swap, f"swap_kv_c{c}")
-            q_swap = to(q_send, swap, f"swap_q_c{c}")
+            keeps = downs(packed[0], packed[1], f"keep_c{c}")
+            for d, kind, swap_d in zip(chunks, ("head", "next head"), swapped):
+                downs_of[d] = [(array, kind) for array in keeps]
+                z_arrays[d] = (swap_d,)
+                own_pieces[d] = (
+                    [(packed[0], kind), (swap_d, "queries")],
+                    [(packed[1], kind), (swap_d, "keys_values")],
+                )
+        else:
+            z_arrays[c] = (packed[0], swapped[0])
             own_pieces[c] = (
-                [(q_keep, "head"), (q_swap, "head")],
-                [(kv_keep, "head"), (kv_swap, "head")],
+                [(array, "queries") for array in z_arrays[c]],
+                [(array, "keys_values") for array in z_arrays[c]],
             )
-        else:
-            keep, send = packed
-            swapped = to(send, swap, f"swap_c{c}")
-            z_arrays[c] = (keep, swapped)
-            own_pieces[c] = (
-                [(keep, "queries"), (swapped, "queries")],
-                [(keep, "keys_values"), (swapped, "keys_values")],
-            )
-
-    def downs(c, q, kv, name):
-        low = to(kv, lift, f"lift_{name}c{c}")
-        far = to(q, far_down, f"far_down_{name}c{c}")
-        return to(q, near_down, f"near_down_{name}c{c}"), far, low
 
     def join(c):
         if split[c]:
-            (q_keep, q_swap), (kv_keep, kv_swap) = own_pieces[c]
-            keeps = downs(c, q_keep[0], kv_keep[0], "keep_")
-            swaps = downs(c, q_swap[0], kv_swap[0], "recv_")
-            near, far, low = [[(k, "head"), (r, "head")] for k, r in zip(keeps, swaps)]
+            q_swap, kv_swap = cut_call(*z_arrays[c], last)
+            last[:] = [q_swap]
+            swaps = downs(q_swap, kv_swap, f"recv_c{c}")
+            near, far, low = [[k, (r, "head")] for k, r in zip(downs_of[c], swaps)]
         else:
             level_q, level_kv = join_call(*z_arrays[c], last)
             last[:] = [level_q]
             near, far, low = [
-                [(array, "first"), (array, "second")] for array in downs(c, level_q, level_kv, "")
+                [(array, "first"), (array, "second")] for array in downs(level_q, level_kv, f"c{c}")
             ]
         served_pieces[c] = (near + far, own_pieces[c][1] + low)
 
+    def is_direct(c):
+        return DIRECT and c == n - 1
+
     def serve(c):
-        near, far = attention_call(
-            served_plan, *served_pieces[c], False, sizes[c], per_dev, block_rows, last
+        packs = attention_call(
+            served_plan, *served_pieces[c], False, is_direct(c), 1, per_dev, block_rows, last
         )
-        last[:] = [near]
-        far = to(far, far_up, f"far_up_c{c}")
-        ups[c] = (to(near, near_up, f"near_up_c{c}"), far)
+        last[:] = [packs[0]]
+        if is_direct(c):
+            near_same, near_cross, far_same, far_cross = packs
+            far = (
+                to(far_same, far_up, f"far_up_same_c{c}"),
+                to(far_cross, crossed(far_up), f"far_up_cross_c{c}"),
+            )
+            near = (
+                to(near_same, near_up, f"near_up_same_c{c}"),
+                to(near_cross, crossed(near_up), f"near_up_cross_c{c}"),
+            )
+            ups[c] = (*near, *far)
+        else:
+            near, far = packs
+            far = to(far, far_up, f"far_up_c{c}")
+            ups[c] = (to(near, near_up, f"near_up_c{c}"), far)
 
     def attend(c):
-        owns[c] = attention_call(
-            own_plan, own_pieces[c][0], served_pieces[c][1], True, sizes[c], per_dev, block_rows, last
+        state = attention_call(
+            own_plan,
+            own_pieces[c][0],
+            served_pieces[c][1],
+            True,
+            is_direct(c),
+            1,
+            per_dev,
+            block_rows,
+            last,
         )
-        last[:] = [owns[c][1]]
+        last[:] = [state[1]]
+        owns[c] = state[:2]
+        if is_direct(c):
+            others[c] = to(state[2], swap, f"back_own_c{c}")
 
     def merge(*chunks):
+        if is_direct(chunks[0]):
+            c = chunks[0]
+            keep, back, squares[0] = own_merge_call(
+                valid, squares[0], squares_in[0], owns[c], others[c], ups[c], per_dev, last
+            )
+            kept.append(keep)
+            returned.append(back)
+            return
         parts = [(owns[c], *ups[c]) for c in chunks]
         keep, send, squares[0] = merge_call(valid, squares[0], parts, per_dev, last)
         last[:] = [keep]
         kept.append(keep)
         returned.append(to(send, swap, f"back_c{chunks[0]}"))
+        if DIRECT and chunks[-1] == n - 2:
+            squares_in.append(to(squares[0][per_dev:], swap, "squares_swap"))
 
     steps = {"p": pack, "j": join, "s": serve, "a": attend, "m": merge}
     for what, *args in order:
@@ -686,8 +850,9 @@
             last.extend([own_plan, served_plan] if args[0] == "plans" else [sent[args[0]]])
         else:
             steps[what](*args)
-    squares = squares[0]
-    square = squares[:per_dev] + to(squares[per_dev:], swap, "squares_swap")
+    square = squares[0]
+    if not DIRECT:
+        square = square[:per_dev] + to(square[per_dev:], swap, "squares_swap")
     n_head = lax.axis_size("head")
     hop = 1
     while hop < n_head:

time: 181 us -> 186 us (1.028)
  starting transfers between devices: 60 us -> 77.5 us
  waiting for transfers between devices: 68.1 us -> 53.2 us
    ppermute x31 -> x36, starting transfers between devices: 58.5 us -> 75.9 us  [to(): sent[name] = lax.ppermute(array, 'ctx', pairs)]
    ppermute x31 -> x36, waiting for transfers between devices: 64.9 us -> 50 us  [to(): sent[name] = lax.ppermute(array, 'ctx', pairs)]
    pallas_call x0 -> x3, Pallas kernels: none -> 2.4 us  [the longest x2 1.36 us: cut_call(): pl.pallas_call(ordered(cut_kernel, len(after)), out_shape=(jax.ShapeDtype...]
    pallas_call x3 -> x2, Pallas kernels: 5.29 us -> 3.11 us  [merge_call(): pl.pallas_call(ordered(partial(merge_kernel, per_dev, block_rows, sizes),...]
    pallas_call x4 -> x3, Pallas kernels: 8.74 us -> 7.6 us  [pack_call(): pl.pallas_call(ordered(partial(pack_kernel, (heads, first, half, rows, sp...]
    unnamed x46 -> x48, local copies, waits for them, and re-layouts: 5.16 us -> 5.17 us
  transfers between devices with their start and end apart: 33 -> 38, of which waited for: 15 -> 11; matrix products, arithmetic and copies ran while one was open for 2% -> 2% of each run, Pallas kernels for 20% -> 19%
where the time goes in v6:
time: 186 us; the launch traced here: 184 us
  starting transfers between devices  77.5 us (42%)
  waiting for transfers between devices  53.2 us (29%)
  Pallas kernels  40.5 us (22%)
  local copies, waits for them, and re-layouts  6.03 us (3%)
  other arithmetic  3.45 us (2%)
  between operations  3.18 us (2%)
    ppermute x36, starting transfers between devices, to(): sent[name] = lax.ppermute(array, 'ctx', pairs)  75.9 us
    ppermute x36, waiting for transfers between devices, to(): sent[name] = lax.ppermute(array, 'ctx', pairs)  50 us
    pallas_call x8, Pallas kernels, attention_call(): pl.pallas_call(ordered(partial(attention_kernel, (heads, per_dev, block_r...  22.8 us
    pallas_call x3, Pallas kernels, pack_call(): pl.pallas_call(ordered(partial(pack_kernel, (heads, first, half, rows, sp...  7.6 us
    unnamed x48, local copies, waits for them, and re-layouts  5.17 us
  transfers between devices with their start and end apart: 38, of which 11 were waited for; matrix products, arithmetic and copies ran while one was open for 2% of the time, Pallas kernels for 19%

profile of v6, /device:TPU:24, one launch (start us, length us, event | category | flops | bytes accessed | tf_op | source)
XLA Modules:
  0.0 183.9 jit_solution(17547201483744033627)
XLA Ops:
  0.1 3.1 %pack.3 = (bf16[2,1024,128]{2,1,0:T(8,128)(2,1)S(1)}, bf16[2,2,1024,128]{3,2,1,0:T(8,128)(2,1)S(1)}, bf16[1,3,1024,128]{3,2,1,0:T(8,128)(2,1)}, bf16[1,3,1024,128]{3,2,1,0:T(8,128)(2,1)S(1)}) custom-call(s32[2]{0:T(128)S(1)} %pad_add_fusion.4.refs_0_.refs_1_.place, bf16[1024,1024]{1,0:T(8,128)(2,1)} %refs_2_.5, bf16[1024,1024]{1,0:T(8,128)(2,1)} %refs_3_.5, ...), custom_call_target="tpu_custom_call" | custom-call | flops 1 | bytes 1 | tf_op jit(solution)/shard_map/pack/pallas_call | solution.py:433
  3.2 3.2 %collective-permute-start.3 = (bf16[2,1024,128]{2,1,0:T(8,128)(2,1)S(1)}, bf16[2,1024,128]{2,1,0:T(8,128)(2,1)}, u32[]{:S(2)}, u32[]{:S(2)}) collective-permute-start(bf16[2,1024,128]{2,1,0:T(8,128)(2,1)S(1)} %get-tuple-element.49.refs_0_.refs_2_), channel_id=1, source_target_pairs={{16,8},{20,12},{24,16},{28,20},{17,9},{21,13},{25,17},{29,21},{18,... | collective-permute-start | bytes 1572872 | tf_op jit(solution)/shard_map/near_down_keep_c0/ppermute | solution.py:684
  6.4 2.1 %collective-permute-start.4 = (bf16[2,1024,128]{2,1,0:T(8,128)(2,1)S(1)}, bf16[2,1024,128]{2,1,0:T(8,128)(2,1)}, u32[]{:S(2)}, u32[]{:S(2)}) collective-permute-start(bf16[2,1024,128]{2,1,0:T(8,128)(2,1)S(1)} %get-tuple-element.49.refs_0_.refs_2_), channel_id=1, source_target_pairs={{24,8},{28,12},{25,9},{29,13},{26,10},{30,14},{27,11},{31,15}} | collective-permute-start | bytes 1572872 | tf_op jit(solution)/shard_map/far_down_keep_c0/ppermute | solution.py:684
  8.5 1.5 collective-permute-start
  12.2 1.3 collective-permute-start.1
  16.3 11.7 %collective-permute-done.1 = s32[8,8]{1,0:T(8,128)S(1)} collective-permute-done((s32[8,8]{1,0:T(8,128)S(1)}, s32[8,8]{1,0:T(8,128)S(1)}, u32[]{:S(2)}, u32[]{:S(2)}) %collective-permute-start.1) | collective-permute-done | bytes 288 | tf_op jit(solution)/shard_map/selection_near/ppermute | solution.py:684
  28.8 1.5 collective-permute-start.7
  34.0 2.2 %pack.4 = (bf16[1,3,1024,128]{3,2,1,0:T(8,128)(2,1)S(1)}, bf16[1,3,1024,128]{3,2,1,0:T(8,128)(2,1)S(1)}) custom-call(bf16[1,1024,128]{2,1,0:T(8,128)(2,1)S(1)} %get-tuple-element.52.refs_0_, s32[2]{0:T(128)S(1)} %pad_add_fusion.4.refs_0_.refs_1_.place, bf16[1024,1024]{1,0:T(8,128)(2,1)} %refs_2_.5, bf16[1024,1024]{1,0:T(8,128)(2,1)} %refs_3_.5, ...), custom_call_target="tpu_custom_call" | custom-call | flops 1 | bytes 1 | tf_op jit(solution)/shard_map/pack/pallas_call | solution.py:433
  37.6 6.3 %collective-permute-start.8 = (bf16[1,1024,128]{2,1,0:T(8,128)(2,1)S(1)}, bf16[1,1024,128]{2,1,0:T(8,128)(2,1)S(1)}, u32[]{:S(2)}, u32[]{:S(2)}) collective-permute-start(bf16[1,1024,128]{2,1,0:T(8,128)(2,1)S(1)} %get-tuple-element.52.refs_0_), channel_id=1, source_target_pairs={{16,8},{20,12},{24,16},{28,20},{17,9},{21,13},{25,17},{29,21},{18,... | collective-permute-start | bytes 786440 | tf_op jit(solution)/shard_map/near_down_recv_c0/ppermute | solution.py:684
  43.9 3.6 %collective-permute-start.9 = (bf16[1,1024,128]{2,1,0:T(8,128)(2,1)S(1)}, bf16[1,1024,128]{2,1,0:T(8,128)(2,1)S(1)}, u32[]{:S(2)}, u32[]{:S(2)}) collective-permute-start(bf16[1,1024,128]{2,1,0:T(8,128)(2,1)S(1)} %get-tuple-element.52.refs_0_), channel_id=1, source_target_pairs={{24,8},{28,12},{25,9},{29,13},{26,10},{30,14},{27,11},{31,15}} | collective-permute-start | bytes 786440 | tf_op jit(solution)/shard_map/far_down_recv_c0/ppermute | solution.py:684
  47.5 2.1 %collective-permute-done.7.refs_1_.refs_7_.refs_3_ = bf16[1,3,1024,128]{3,2,1,0:T(8,128)(2,1)} collective-permute-done((bf16[1,3,1024,128]{3,2,1,0:T(8,128)(2,1)}, bf16[1,3,1024,128]{3,2,1,0:T(8,128)(2,1)}, u32[]{:S(2)}, u32[]{:S(2)}) %collective-permute-start.7) | collective-permute-done | bytes 786464 | tf_op jit(solution)/shard_map/swap_c1/ppermute | solution.py:684
  51.6 6.4 %collective-permute-start.12 = (bf16[1,1024,128]{2,1,0:T(8,128)(2,1)S(1)}, bf16[1,1024,128]{2,1,0:T(8,128)(2,1)S(1)}, u32[]{:S(2)}, u32[]{:S(2)}) collective-permute-start(bf16[1,1024,128]{2,1,0:T(8,128)(2,1)S(1)} %get-tuple-element.55.refs_0_), channel_id=1, source_target_pairs={{16,8},{20,12},{24,16},{28,20},{17,9},{21,13},{25,17},{29,21},{18,... | collective-permute-start | bytes 786440 | tf_op jit(solution)/shard_map/near_down_recv_c1/ppermute | solution.py:684
  58.0 2.2 %pack.5 = (bf16[1,3,1024,128]{3,2,1,0:T(8,128)(2,1)S(1)}, bf16[1,3,1024,128]{3,2,1,0:T(8,128)(2,1)S(1)}) custom-call(bf16[1,1024,128]{2,1,0:T(8,128)(2,1)S(1)} %get-tuple-element.55.refs_0_, s32[2]{0:T(128)S(1)} %pad_add_fusion.4.refs_0_.refs_1_.place, bf16[1024,1024]{1,0:T(8,128)(2,1)} %refs_2_.5, bf16[1024,1024]{1,0:T(8,128)(2,1)} %refs_3_.5, ...), custom_call_target="tpu_custom_call" | custom-call | flops 1 | bytes 1 | tf_op jit(solution)/shard_map/pack/pallas_call | solution.py:433
  60.3 1.6 collective-permute-start.17
  61.8 3.6 %collective-permute-start.13 = (bf16[1,1024,128]{2,1,0:T(8,128)(2,1)S(1)}, bf16[1,1024,128]{2,1,0:T(8,128)(2,1)S(1)}, u32[]{:S(2)}, u32[]{:S(2)}) collective-permute-start(bf16[1,1024,128]{2,1,0:T(8,128)(2,1)S(1)} %get-tuple-element.55.refs_0_), channel_id=1, source_target_pairs={{24,8},{28,12},{25,9},{29,13},{26,10},{30,14},{27,11},{31,15}} | collective-permute-start | bytes 786440 | tf_op jit(solution)/shard_map/far_down_recv_c1/ppermute | solution.py:684
  65.5 1.8 served_attention.4
  67.3 1.3 collective-permute-start.15
  68.6 1.3 collective-permute-start.16
  69.9 3.5 %own_attention.4 = (f32[1,8,128,256]{3,2,1,0:T(8,128)S(1)}, f32[1,8,256]{2,1,0:T(8,128)S(1)}) custom-call(bf16[1,1056,256]{2,1,0:T(8,128)(2,1)S(1)} %get-tuple-element.58.refs_0_, s32[81]{0:T(128)S(1)} %pad_add_fusion.6.refs_1_, bf16[2,1024,128]{2,1,0:T(8,128)(2,1)S(1)} %get-tuple-element.49.refs_0_.refs_2_, bf16[1,3,1024,128]{3,2,1,0:T(8,128)(2,1)S(1)} %copy-done.3, ...), custom_call_target="tpu_custom_call" | custom-call | flops 1 | bytes 1 | tf_op jit(solution)/shard_map/own_attention/pallas_call | solution.py:348
  74.5 4.0 %collective-permute-start.18 = (bf16[2,1,1024,128]{3,2,1,0:T(8,128)(2,1)S(1)}, bf16[2,1,1024,128]{3,2,1,0:T(8,128)(2,1)S(1)}, u32[]{:S(2)}, u32[]{:S(2)}) collective-permute-start(bf16[2,1,1024,128]{3,2,1,0:T(8,128)(2,1)S(1)} %get-tuple-element.61.refs_0_), channel_id=1, source_target_pairs={{16,8},{20,12},{24,16},{28,20},{17,9},{21,13},{25,17},{29,21},{18,... | collective-permute-start | bytes 1572872 | tf_op jit(solution)/shard_map/near_down_c2/ppermute | solution.py:684
  78.5 2.0 %served_attention.5 = (bf16[1,1056,256]{2,1,0:T(8,128)(2,1)S(1)}, bf16[1,1056,256]{2,1,0:T(8,128)(2,1)S(1)}) custom-call(bf16[2,1,1024,128]{3,2,1,0:T(8,128)(2,1)S(1)} %get-tuple-element.61.refs_0_, s32[129]{0:T(256)S(1)} %pad_add_fusion.3.refs_2_.refs_1_, bf16[2,1024,128]{2,1,0:T(8,128)(2,1)} %collective-permute-done.3.refs_3_.refs_2_, ...), custom_call_target="tpu_custom_call" | custom-call | flops 1 | bytes 1 | tf_op jit(solution)/shard_map/served_attention/pallas_call | solution.py:348
  80.4 4.4 %own_attention.5 = (f32[1,8,128,256]{3,2,1,0:T(8,128)S(1)}, f32[1,8,256]{2,1,0:T(8,128)S(1)}) custom-call(bf16[1,1056,256]{2,1,0:T(8,128)(2,1)S(1)} %get-tuple-element.63.refs_0_, s32[81]{0:T(128)S(1)} %pad_add_fusion.6.refs_1_, bf16[2,1024,128]{2,1,0:T(8,128)(2,1)S(1)} %get-tuple-element.49.refs_0_.refs_2_, ...), custom_call_target="tpu_custom_call" | custom-call | flops 1 | bytes 1 | tf_op jit(solution)/shard_map/own_attention/pallas_call | solution.py:348
  84.8 9.9 %collective-permute-start.19 = (bf16[2,1,1024,128]{3,2,1,0:T(8,128)(2,1)S(1)}, bf16[2,1,1024,128]{3,2,1,0:T(8,128)(2,1)S(1)}, u32[]{:S(2)}, u32[]{:S(2)}) collective-permute-start(bf16[2,1,1024,128]{3,2,1,0:T(8,128)(2,1)S(1)} %get-tuple-element.61.refs_0_), channel_id=1, source_target_pairs={{24,8},{28,12},{25,9},{29,13},{26,10},{30,14},{27,11},{31,15}} | collective-permute-start | bytes 1572872 | tf_op jit(solution)/shard_map/far_down_c2/ppermute | solution.py:684
  94.8 1.5 join.7
  97.1 1.3 collective-permute-start.21
  98.4 1.3 collective-permute-start.22
  99.7 5.4 %collective-permute-done.19.refs_3_ = bf16[2,1,1024,128]{3,2,1,0:T(8,128)(2,1)S(1)} collective-permute-done((bf16[2,1,1024,128]{3,2,1,0:T(8,128)(2,1)S(1)}, bf16[2,1,1024,128]{3,2,1,0:T(8,128)(2,1)S(1)}, u32[]{:S(2)}, u32[]{:S(2)}) %collective-permute-start.19) | collective-permute-done | bytes 524320 | tf_op jit(solution)/shard_map/far_down_c2/ppermute | solution.py:684
  105.1 2.1 %collective-permute-start.24 = (bf16[2,1,1024,128]{3,2,1,0:T(8,128)(2,1)}, bf16[2,1,1024,128]{3,2,1,0:T(8,128)(2,1)}, u32[]{:S(2)}, u32[]{:S(2)}) collective-permute-start(bf16[2,1,1024,128]{3,2,1,0:T(8,128)(2,1)} %get-tuple-element.67.refs_0_), channel_id=1, source_target_pairs={{16,8},{20,12},{24,16},{28,20},{17,9},{21,13},{25,17},{29,21},{18,... | collective-permute-start | bytes 1572872 | tf_op jit(solution)/shard_map/near_down_c3/ppermute | solution.py:684
  107.2 5.3 %collective-permute-start.25 = (bf16[2,1,1024,128]{3,2,1,0:T(8,128)(2,1)}, bf16[2,1,1024,128]{3,2,1,0:T(8,128)(2,1)}, u32[]{:S(2)}, u32[]{:S(2)}) collective-permute-start(bf16[2,1,1024,128]{3,2,1,0:T(8,128)(2,1)} %get-tuple-element.67.refs_0_), channel_id=1, source_target_pairs={{24,8},{28,12},{25,9},{29,13},{26,10},{30,14},{27,11},{31,15}} | collective-permute-start | bytes 1572872 | tf_op jit(solution)/shard_map/far_down_c3/ppermute | solution.py:684
  112.5 2.0 %served_attention.6 = (bf16[1,1056,256]{2,1,0:T(8,128)(2,1)}, bf16[1,1056,256]{2,1,0:T(8,128)(2,1)}) custom-call(bf16[2,1,1024,128]{3,2,1,0:T(8,128)(2,1)} %get-tuple-element.67.refs_0_, s32[129]{0:T(256)S(1)} %pad_add_fusion.3.refs_2_.refs_1_, bf16[2,1,1024,128]{3,2,1,0:T(8,128)(2,1)S(1)} %collective-permute-done.18.refs_2_, ...), custom_call_target="tpu_custom_call" | custom-call | flops 1 | bytes 1 | tf_op jit(solution)/shard_map/served_attention/pallas_call | solution.py:348
  114.6 4.3 %collective-permute-done.21.refs_9_ = bf16[1,1056,256]{2,1,0:T(8,128)(2,1)S(1)} collective-permute-done((bf16[1,1056,256]{2,1,0:T(8,128)(2,1)S(1)}, bf16[1,1056,256]{2,1,0:T(8,128)(2,1)S(1)}, u32[]{:S(2)}, u32[]{:S(2)}) %collective-permute-start.21) | collective-permute-done | bytes 540704 | tf_op jit(solution)/shard_map/near_up_c1/ppermute | solution.py:684
  120.2 2.9 %collective-permute-done.22.refs_10_ = bf16[1,1056,256]{2,1,0:T(8,128)(2,1)S(1)} collective-permute-done((bf16[1,1056,256]{2,1,0:T(8,128)(2,1)S(1)}, bf16[1,1056,256]{2,1,0:T(8,128)(2,1)S(1)}, u32[]{:S(2)}, u32[]{:S(2)}) %collective-permute-start.22) | collective-permute-done | bytes 540704 | tf_op jit(solution)/shard_map/far_up_c1/ppermute | solution.py:684
  127.7 3.7 %own_attention.6 = (f32[1,8,128,256]{3,2,1,0:T(8,128)S(1)}, f32[1,8,256]{2,1,0:T(8,128)S(1)}) custom-call(bf16[1,1056,256]{2,1,0:T(8,128)(2,1)} %get-tuple-element.69.refs_0_, s32[81]{0:T(128)S(1)} %pad_add_fusion.6.refs_1_, bf16[1,3,1024,128]{3,2,1,0:T(8,128)(2,1)S(1)} %get-tuple-element.53.refs_0_.refs_1_.refs_4_.refs_2_, ...), custom_call_target="tpu_custom_call" | custom-call | flops 1 | bytes 1 | tf_op jit(solution)/shard_map/own_attention/pallas_call | solution.py:348
  132.6 1.4 merge.3
  134.1 3.5 %own_attention.7 = (f32[1,4,128,256]{3,2,1,0:T(8,128)S(1)}, f32[1,4,256]{2,1,0:T(4,128)S(1)}, bf16[1,528,256]{2,1,0:T(8,128)(2,1)S(1)}) custom-call(bf16[2,1024,128]{2,1,0:T(8,128)(2,1)S(1)} %get-tuple-element.74.refs_0_, s32[81]{0:T(128)S(1)} %pad_add_fusion.6.refs_1_, bf16[1,3,1024,128]{3,2,1,0:T(8,128)(2,1)S(1)} %copy-done.1, ...), custom_call_target="tpu_custom_call" | custom-call | flops 1 | bytes 1 | tf_op jit(solution)/shard_map/own_attention/pallas_call | solution.py:348
  137.6 2.0 %served_attention.7 = (bf16[1,528,256]{2,1,0:T(8,128)(2,1)S(1)}, bf16[1,528,256]{2,1,0:T(8,128)(2,1)S(1)}, bf16[1,528,256]{2,1,0:T(8,128)(2,1)S(1)}, bf16[1,528,256]{2,1,0:T(8,128)(2,1)S(1)}) custom-call(f32[1,4,256]{2,1,0:T(4,128)S(1)} %get-tuple-element.76.refs_0_.refs_5_, s32[129]{0:T(256)S(1)} %pad_add_fusion.3.refs_2_.refs_1_, ...), custom_call_target="tpu_custom_call" | custom-call | flops 1 | bytes 1 | tf_op jit(solution)/shard_map/served_attention/pallas_call | solution.py:348
  139.6 1.3 collective-permute-start.30
  140.9 1.3 collective-permute-start.31
  142.2 1.6 collective-permute-start.34
  143.7 5.2 %collective-permute-done.26.refs_5_ = bf16[1,1056,256]{2,1,0:T(8,128)(2,1)} collective-permute-done((bf16[1,1056,256]{2,1,0:T(8,128)(2,1)}, bf16[1,1056,256]{2,1,0:T(8,128)(2,1)}, u32[]{:S(2)}, u32[]{:S(2)}) %collective-permute-start.26) | collective-permute-done | bytes 540704 | tf_op jit(solution)/shard_map/near_up_c2/ppermute | solution.py:684
  148.9 1.7 merge.4
  150.6 1.7 collective-permute-start.28
  153.5 10.9 %collective-permute-done.28.refs_3_ = f32[4,256]{1,0:T(4,128)S(1)} collective-permute-done((f32[4,256]{1,0:T(4,128)S(1)}, f32[4,256]{1,0:T(4,128)S(1)}, u32[]{:S(2)}, u32[]{:S(2)}) %collective-permute-start.28) | collective-permute-done | bytes 4128 | tf_op jit(solution)/shard_map/squares_swap/ppermute | solution.py:684
  165.7 1.3 collective-permute-start.29
  167.8 6.9 %collective-permute-done.33.refs_10_ = bf16[1,528,256]{2,1,0:T(8,128)(2,1)S(1)} collective-permute-done((bf16[1,528,256]{2,1,0:T(8,128)(2,1)S(1)}, bf16[1,528,256]{2,1,0:T(8,128)(2,1)S(1)}, u32[]{:S(2)}, u32[]{:S(2)}) %collective-permute-start.33) | collective-permute-done | bytes 270368 | tf_op jit(solution)/shard_map/far_up_cross_c3/ppermute | solution.py:684
  177.4 1.5 collective-permute-start.37
  179.0 2.1 %collective-permute-done.37 = f32[4,256]{1,0:T(4,128)S(1)} collective-permute-done((f32[4,256]{1,0:T(4,128)S(1)}, f32[4,256]{1,0:T(4,128)S(1)}, u32[]{:S(2)}, u32[]{:S(2)}) %collective-permute-start.37) | collective-permute-done | bytes 4128 | tf_op jit(solution)/shard_map/ppermute | solution.py:859
  181.1 2.8 %finish.1 = bf16[1024,1024]{1,0:T(8,128)(2,1)} custom-call(s32[2]{0:T(128)S(1)} %pad_add_fusion.4.refs_0_.refs_1_.place, bf16[2,1024,128]{2,1,0:T(8,128)(2,1)S(1)} %get-tuple-element.74.refs_0_, bf16[1,1024,128]{2,1,0:T(8,128)(2,1)S(1)} %get-tuple-element.81.refs_0_.refs_1_, bf16[1,1024,128]{2,1,0:T(8,128)(2,1)S(1)} %get-tuple-element.88.refs_2_, ...), custom_call_target="tpu_custom_call" | custom-call | flops 1 | bytes 1 | tf_op jit(solution)/shard_map/finish/pallas_call | solution.py:641
  (146 shorter events, 25.2 us)
Async XLA Ops:
  0.1 15.8 %copy-start.22 = (s32[8,8]{1,0:T(8,128)S(1)}, s32[8,8]{1,0:T(8,128)}, u32[]{:S(2)}) copy-start(s32[8,8]{1,0:T(8,128)} %constant.157.clone.1) | copy-start | bytes 772
  3.2 29.9 %collective-permute-start.3 = (bf16[2,1024,128]{2,1,0:T(8,128)(2,1)S(1)}, bf16[2,1024,128]{2,1,0:T(8,128)(2,1)}, u32[]{:S(2)}, u32[]{:S(2)}) collective-permute-start(bf16[2,1024,128]{2,1,0:T(8,128)(2,1)S(1)} %get-tuple-element.49.refs_0_.refs_2_), channel_id=1, source_target_pairs={{16,8},{20,12},{24,16},{28,20},{17,9},{21,13},{25,17},{29,21},{18,... | collective-permute-start | bytes 1572872 | tf_op jit(solution)/shard_map/near_down_keep_c0/ppermute | solution.py:684
  6.4 26.7 %collective-permute-start.4 = (bf16[2,1024,128]{2,1,0:T(8,128)(2,1)S(1)}, bf16[2,1024,128]{2,1,0:T(8,128)(2,1)}, u32[]{:S(2)}, u32[]{:S(2)}) collective-permute-start(bf16[2,1024,128]{2,1,0:T(8,128)(2,1)S(1)} %get-tuple-element.49.refs_0_.refs_2_), channel_id=1, source_target_pairs={{24,8},{28,12},{25,9},{29,13},{26,10},{30,14},{27,11},{31,15}} | collective-permute-start | bytes 1572872 | tf_op jit(solution)/shard_map/far_down_keep_c0/ppermute | solution.py:684
  8.5 3.7 %collective-permute-start = (s32[4,8]{1,0:T(4,128)S(1)}, s32[4,8]{1,0:T(4,128)S(1)}, u32[]{:S(2)}, u32[]{:S(2)}) collective-permute-start(s32[4,8]{1,0:T(4,128)S(1)} %copy-done.21), channel_id=1, source_target_pairs={{0,4},{4,0},{8,12},{12,8},{16,20},{20,16},{24,28},{28,24},{1,5},{5... | collective-permute-start | bytes 392 | tf_op jit(solution)/shard_map/selection_swap/ppermute | solution.py:684
  10.0 23.2 %collective-permute-start.5 = (bf16[2,2,1024,128]{3,2,1,0:T(8,128)(2,1)S(1)}, bf16[2,2,1024,128]{3,2,1,0:T(8,128)(2,1)S(1)}, u32[]{:S(2)}, u32[]{:S(2)}) collective-permute-start(bf16[2,2,1024,128]{3,2,1,0:T(8,128)(2,1)S(1)} %get-tuple-element.50.refs_6_.refs_4_), channel_id=1, source_target_pairs={{0,8},{4,12},{1,9},{5,13},{2,10},{6,14},{3,11},{7,15}} | collective-permute-start | bytes 3145736 | tf_op jit(solution)/shard_map/lift_keep_c0/ppermute | solution.py:684
  10.7 22.4 %collective-permute-start.6 = (bf16[1,3,1024,128]{3,2,1,0:T(8,128)(2,1)}, bf16[1,3,1024,128]{3,2,1,0:T(8,128)(2,1)S(1)}, u32[]{:S(2)}, u32[]{:S(2)}) collective-permute-start(bf16[1,3,1024,128]{3,2,1,0:T(8,128)(2,1)} %get-tuple-element.51), channel_id=1, source_target_pairs={{0,4},{4,0},{8,12},{12,8},{16,20},{20,16},{24,28},{28,24},{1,5},{5... | collective-permute-start | bytes 2359304 | tf_op jit(solution)/shard_map/swap_c0/ppermute | solution.py:684
  12.2 15.9 %collective-permute-start.1 = (s32[8,8]{1,0:T(8,128)S(1)}, s32[8,8]{1,0:T(8,128)S(1)}, u32[]{:S(2)}, u32[]{:S(2)}) collective-permute-start(s32[8,8]{1,0:T(8,128)S(1)} %pad_add_fusion.2), channel_id=1, source_target_pairs={{24,16},{28,20},{25,17},{29,21},{26,18},{30,22},{27,19},{31,23}} | collective-permute-start | bytes 776 | tf_op jit(solution)/shard_map/selection_near/ppermute | solution.py:684
  28.1 0.7 collective-permute-start.2
  28.8 20.8 %collective-permute-start.7 = (bf16[1,3,1024,128]{3,2,1,0:T(8,128)(2,1)}, bf16[1,3,1024,128]{3,2,1,0:T(8,128)(2,1)}, u32[]{:S(2)}, u32[]{:S(2)}) collective-permute-start(bf16[1,3,1024,128]{3,2,1,0:T(8,128)(2,1)} %copy-done.20), channel_id=1, source_target_pairs={{0,4},{4,0},{8,12},{12,8},{16,20},{20,16},{24,28},{28,24},{1,5},{5... | collective-permute-start | bytes 2359304 | tf_op jit(solution)/shard_map/swap_c1/ppermute | solution.py:684
  36.3 32.3 %collective-permute-start.11 = (bf16[1,3,1024,128]{3,2,1,0:T(8,128)(2,1)S(1)}, bf16[1,3,1024,128]{3,2,1,0:T(8,128)(2,1)S(1)}, u32[]{:S(2)}, u32[]{:S(2)}) collective-permute-start(bf16[1,3,1024,128]{3,2,1,0:T(8,128)(2,1)S(1)} %get-tuple-element.60), channel_id=1, source_target_pairs={{0,4},{4,0},{8,12},{12,8},{16,20},{20,16},{24,28},{28,24},{1,5},{5... | collective-permute-start | bytes 2359304 | tf_op jit(solution)/shard_map/swap_c2/ppermute | solution.py:684
  36.9 25.0 %collective-permute-start.10 = (bf16[1,2,1024,128]{3,2,1,0:T(8,128)(2,1)S(1)}, bf16[1,2,1024,128]{3,2,1,0:T(8,128)(2,1)S(1)}, u32[]{:S(2)}, u32[]{:S(2)}) collective-permute-start(bf16[1,2,1024,128]{3,2,1,0:T(8,128)(2,1)S(1)} %get-tuple-element.57), channel_id=1, source_target_pairs={{0,8},{4,12},{1,9},{5,13},{2,10},{6,14},{3,11},{7,15}} | collective-permute-start | bytes 1572872 | tf_op jit(solution)/shard_map/lift_recv_c0/ppermute | solution.py:684
  37.6 14.0 %collective-permute-start.8 = (bf16[1,1024,128]{2,1,0:T(8,128)(2,1)S(1)}, bf16[1,1024,128]{2,1,0:T(8,128)(2,1)S(1)}, u32[]{:S(2)}, u32[]{:S(2)}) collective-permute-start(bf16[1,1024,128]{2,1,0:T(8,128)(2,1)S(1)} %get-tuple-element.52.refs_0_), channel_id=1, source_target_pairs={{16,8},{20,12},{24,16},{28,20},{17,9},{21,13},{25,17},{29,21},{18,... | collective-permute-start | bytes 786440 | tf_op jit(solution)/shard_map/near_down_recv_c0/ppermute | solution.py:684
  43.9 16.4 %collective-permute-start.9 = (bf16[1,1024,128]{2,1,0:T(8,128)(2,1)S(1)}, bf16[1,1024,128]{2,1,0:T(8,128)(2,1)S(1)}, u32[]{:S(2)}, u32[]{:S(2)}) collective-permute-start(bf16[1,1024,128]{2,1,0:T(8,128)(2,1)S(1)} %get-tuple-element.52.refs_0_), channel_id=1, source_target_pairs={{24,8},{28,12},{25,9},{29,13},{26,10},{30,14},{27,11},{31,15}} | collective-permute-start | bytes 786440 | tf_op jit(solution)/shard_map/far_down_recv_c0/ppermute | solution.py:684
  50.8 23.6 %collective-permute-start.14 = (bf16[1,2,1024,128]{3,2,1,0:T(8,128)(2,1)S(1)}, bf16[1,2,1024,128]{3,2,1,0:T(8,128)(2,1)S(1)}, u32[]{:S(2)}, u32[]{:S(2)}) collective-permute-start(bf16[1,2,1024,128]{3,2,1,0:T(8,128)(2,1)S(1)} %get-tuple-element.62), channel_id=1, source_target_pairs={{0,8},{4,12},{1,9},{5,13},{2,10},{6,14},{3,11},{7,15}} | collective-permute-start | bytes 1572872 | tf_op jit(solution)/shard_map/lift_recv_c1/ppermute | solution.py:684
  51.6 13.9 %copy-start.3 = (bf16[1,3,1024,128]{3,2,1,0:T(8,128)(2,1)S(1)}, bf16[1,3,1024,128]{3,2,1,0:T(8,128)(2,1)}, u32[]{:S(2)}) copy-start(bf16[1,3,1024,128]{3,2,1,0:T(8,128)(2,1)} %copy-done.2) | copy-start | bytes 2359300
  51.6 15.7 %collective-permute-start.12 = (bf16[1,1024,128]{2,1,0:T(8,128)(2,1)S(1)}, bf16[1,1024,128]{2,1,0:T(8,128)(2,1)S(1)}, u32[]{:S(2)}, u32[]{:S(2)}) collective-permute-start(bf16[1,1024,128]{2,1,0:T(8,128)(2,1)S(1)} %get-tuple-element.55.refs_0_), channel_id=1, source_target_pairs={{16,8},{20,12},{24,16},{28,20},{17,9},{21,13},{25,17},{29,21},{18,... | collective-permute-start | bytes 786440 | tf_op jit(solution)/shard_map/near_down_recv_c1/ppermute | solution.py:684
  60.3 34.5 %copy-start = (bf16[1,3,1024,128]{3,2,1,0:T(8,128)(2,1)}, bf16[1,3,1024,128]{3,2,1,0:T(8,128)(2,1)S(1)}, u32[]{:S(2)}) copy-start(bf16[1,3,1024,128]{3,2,1,0:T(8,128)(2,1)S(1)} %get-tuple-element.56.refs_0_.refs_3_.refs_2_.refs_4_) | copy-start | bytes 2359300
  60.3 24.5 %collective-permute-start.17 = (bf16[1,3,1024,128]{3,2,1,0:T(8,128)(2,1)S(1)}, bf16[1,3,1024,128]{3,2,1,0:T(8,128)(2,1)S(1)}, u32[]{:S(2)}, u32[]{:S(2)}) collective-permute-start(bf16[1,3,1024,128]{3,2,1,0:T(8,128)(2,1)S(1)} %get-tuple-element.66), channel_id=1, source_target_pairs={{0,4},{4,0},{8,12},{12,8},{16,20},{20,16},{24,28},{28,24},{1,5},{5... | collective-permute-start | bytes 2359304 | tf_op jit(solution)/shard_map/swap_c3/ppermute | solution.py:684
  61.8 11.9 %collective-permute-start.13 = (bf16[1,1024,128]{2,1,0:T(8,128)(2,1)S(1)}, bf16[1,1024,128]{2,1,0:T(8,128)(2,1)S(1)}, u32[]{:S(2)}, u32[]{:S(2)}) collective-permute-start(bf16[1,1024,128]{2,1,0:T(8,128)(2,1)S(1)} %get-tuple-element.55.refs_0_), channel_id=1, source_target_pairs={{24,8},{28,12},{25,9},{29,13},{26,10},{30,14},{27,11},{31,15}} | collective-permute-start | bytes 786440 | tf_op jit(solution)/shard_map/far_down_recv_c1/ppermute | solution.py:684
  67.3 27.4 %collective-permute-start.15 = (bf16[1,1056,256]{2,1,0:T(8,128)(2,1)S(1)}, bf16[1,1056,256]{2,1,0:T(8,128)(2,1)S(1)}, u32[]{:S(2)}, u32[]{:S(2)}) collective-permute-start(bf16[1,1056,256]{2,1,0:T(8,128)(2,1)S(1)} %get-tuple-element.58.refs_0_), channel_id=1, source_target_pairs={{8,16},{12,20},{16,24},{20,28},{9,17},{13,21},{17,25},{21,29},{10,... | collective-permute-start | bytes 1622024 | tf_op jit(solution)/shard_map/near_up_c0/ppermute | solution.py:684
  68.6 43.9 %copy-start.4 = (bf16[1,3,1024,128]{3,2,1,0:T(8,128)(2,1)}, bf16[1,3,1024,128]{3,2,1,0:T(8,128)(2,1)S(1)}, u32[]{:S(2)}) copy-start(bf16[1,3,1024,128]{3,2,1,0:T(8,128)(2,1)S(1)} %collective-permute-done.11.refs_2_.refs_5_.refs_3_) | copy-start | bytes 2359300
  68.6 26.1 %collective-permute-start.16 = (bf16[1,1056,256]{2,1,0:T(8,128)(2,1)S(1)}, bf16[1,1056,256]{2,1,0:T(8,128)(2,1)S(1)}, u32[]{:S(2)}, u32[]{:S(2)}) collective-permute-start(bf16[1,1056,256]{2,1,0:T(8,128)(2,1)S(1)} %get-tuple-element.65), channel_id=1, source_target_pairs={{8,24},{12,28},{9,25},{13,29},{10,26},{14,30},{11,27},{15,31}} | collective-permute-start | bytes 1622024 | tf_op jit(solution)/shard_map/far_up_c0/ppermute | solution.py:684
  73.7 33.5 %collective-permute-start.20 = (bf16[2,1,2,1024,128]{4,3,2,1,0:T(8,128)(2,1)S(1)}, bf16[2,1,2,1024,128]{4,3,2,1,0:T(8,128)(2,1)S(1)}, u32[]{:S(2)}, u32[]{:S(2)}) collective-permute-start(bf16[2,1,2,1024,128]{4,3,2,1,0:T(8,128)(2,1)S(1)} %get-tuple-element.68), channel_id=1, source_target_pairs={{0,8},{4,12},{1,9},{5,13},{2,10},{6,14},{3,11},{7,15}} | collective-permute-start | bytes 3145736 | tf_op jit(solution)/shard_map/lift_c2/ppermute | solution.py:684
  74.5 23.9 %collective-permute-start.18 = (bf16[2,1,1024,128]{3,2,1,0:T(8,128)(2,1)S(1)}, bf16[2,1,1024,128]{3,2,1,0:T(8,128)(2,1)S(1)}, u32[]{:S(2)}, u32[]{:S(2)}) collective-permute-start(bf16[2,1,1024,128]{3,2,1,0:T(8,128)(2,1)S(1)} %get-tuple-element.61.refs_0_), channel_id=1, source_target_pairs={{16,8},{20,12},{24,16},{28,20},{17,9},{21,13},{25,17},{29,21},{18,... | collective-permute-start | bytes 1572872 | tf_op jit(solution)/shard_map/near_down_c2/ppermute | solution.py:684
  84.8 22.4 %copy-start.16 = (f32[1,8,128,256]{3,2,1,0:T(8,128)}, f32[1,8,128,256]{3,2,1,0:T(8,128)S(1)}, u32[]{:S(2)}) copy-start(f32[1,8,128,256]{3,2,1,0:T(8,128)S(1)} %get-tuple-element.72.refs_7_) | copy-start | bytes 3145732
  84.8 29.7 %copy-start.6 = (bf16[1,3,1024,128]{3,2,1,0:T(8,128)(2,1)}, bf16[1,3,1024,128]{3,2,1,0:T(8,128)(2,1)S(1)}, u32[]{:S(2)}) copy-start(bf16[1,3,1024,128]{3,2,1,0:T(8,128)(2,1)S(1)} %collective-permute-done.17.refs_4_.refs_3_.refs_5_) | copy-start | bytes 2359300
  84.8 20.2 %collective-permute-start.19 = (bf16[2,1,1024,128]{3,2,1,0:T(8,128)(2,1)S(1)}, bf16[2,1,1024,128]{3,2,1,0:T(8,128)(2,1)S(1)}, u32[]{:S(2)}, u32[]{:S(2)}) collective-permute-start(bf16[2,1,1024,128]{3,2,1,0:T(8,128)(2,1)S(1)} %get-tuple-element.61.refs_0_), channel_id=1, source_target_pairs={{24,8},{28,12},{25,9},{29,13},{26,10},{30,14},{27,11},{31,15}} | collective-permute-start | bytes 1572872 | tf_op jit(solution)/shard_map/far_down_c2/ppermute | solution.py:684
  94.7 12.4 %copy-start.10 = (bf16[1,1056,256]{2,1,0:T(8,128)(2,1)}, bf16[1,1056,256]{2,1,0:T(8,128)(2,1)S(1)}, u32[]{:S(2)}) copy-start(bf16[1,1056,256]{2,1,0:T(8,128)(2,1)S(1)} %collective-permute-done.15.refs_1_.refs_5_) | copy-start | bytes 1622020
  94.8 19.8 %copy-start.12 = (bf16[1,1056,256]{2,1,0:T(8,128)(2,1)}, bf16[1,1056,256]{2,1,0:T(8,128)(2,1)S(1)}, u32[]{:S(2)}) copy-start(bf16[1,1056,256]{2,1,0:T(8,128)(2,1)S(1)} %collective-permute-done.16.refs_2_.refs_6_) | copy-start | bytes 1622020
  96.3 37.7 %collective-permute-start.23 = (bf16[2,1,2,1024,128]{4,3,2,1,0:T(8,128)(2,1)}, bf16[2,1,2,1024,128]{4,3,2,1,0:T(8,128)(2,1)S(1)}, u32[]{:S(2)}, u32[]{:S(2)}) collective-permute-start(bf16[2,1,2,1024,128]{4,3,2,1,0:T(8,128)(2,1)} %get-tuple-element.75), channel_id=1, source_target_pairs={{0,8},{4,12},{1,9},{5,13},{2,10},{6,14},{3,11},{7,15}} | collective-permute-start | bytes 3145736 | tf_op jit(solution)/shard_map/lift_c3/ppermute | solution.py:684
  97.1 21.8 %collective-permute-start.21 = (bf16[1,1056,256]{2,1,0:T(8,128)(2,1)S(1)}, bf16[1,1056,256]{2,1,0:T(8,128)(2,1)S(1)}, u32[]{:S(2)}, u32[]{:S(2)}) collective-permute-start(bf16[1,1056,256]{2,1,0:T(8,128)(2,1)S(1)} %get-tuple-element.63.refs_0_), channel_id=1, source_target_pairs={{8,16},{12,20},{16,24},{20,28},{9,17},{13,21},{17,25},{21,29},{10,... | collective-permute-start | bytes 1622024 | tf_op jit(solution)/shard_map/near_up_c1/ppermute | solution.py:684
  98.4 24.8 %collective-permute-start.22 = (bf16[1,1056,256]{2,1,0:T(8,128)(2,1)S(1)}, bf16[1,1056,256]{2,1,0:T(8,128)(2,1)S(1)}, u32[]{:S(2)}, u32[]{:S(2)}) collective-permute-start(bf16[1,1056,256]{2,1,0:T(8,128)(2,1)S(1)} %get-tuple-element.73), channel_id=1, source_target_pairs={{8,24},{12,28},{9,25},{13,29},{10,26},{14,30},{11,27},{15,31}} | collective-permute-start | bytes 1622024 | tf_op jit(solution)/shard_map/far_up_c1/ppermute | solution.py:684
  105.1 32.5 %collective-permute-start.24 = (bf16[2,1,1024,128]{3,2,1,0:T(8,128)(2,1)}, bf16[2,1,1024,128]{3,2,1,0:T(8,128)(2,1)}, u32[]{:S(2)}, u32[]{:S(2)}) collective-permute-start(bf16[2,1,1024,128]{3,2,1,0:T(8,128)(2,1)} %get-tuple-element.67.refs_0_), channel_id=1, source_target_pairs={{16,8},{20,12},{24,16},{28,20},{17,9},{21,13},{25,17},{29,21},{18,... | collective-permute-start | bytes 1572872 | tf_op jit(solution)/shard_map/near_down_c3/ppermute | solution.py:684
  107.2 30.4 %collective-permute-start.25 = (bf16[2,1,1024,128]{3,2,1,0:T(8,128)(2,1)}, bf16[2,1,1024,128]{3,2,1,0:T(8,128)(2,1)}, u32[]{:S(2)}, u32[]{:S(2)}) collective-permute-start(bf16[2,1,1024,128]{3,2,1,0:T(8,128)(2,1)} %get-tuple-element.67.refs_0_), channel_id=1, source_target_pairs={{24,8},{28,12},{25,9},{29,13},{26,10},{30,14},{27,11},{31,15}} | collective-permute-start | bytes 1572872 | tf_op jit(solution)/shard_map/far_down_c3/ppermute | solution.py:684
  112.5 18.8 %copy-start.11 = (bf16[1,1056,256]{2,1,0:T(8,128)(2,1)S(1)}, bf16[1,1056,256]{2,1,0:T(8,128)(2,1)}, u32[]{:S(2)}) copy-start(bf16[1,1056,256]{2,1,0:T(8,128)(2,1)} %copy-done.10) | copy-start | bytes 1622020
  118.9 30.0 %collective-permute-start.26 = (bf16[1,1056,256]{2,1,0:T(8,128)(2,1)}, bf16[1,1056,256]{2,1,0:T(8,128)(2,1)}, u32[]{:S(2)}, u32[]{:S(2)}) collective-permute-start(bf16[1,1056,256]{2,1,0:T(8,128)(2,1)} %get-tuple-element.69.refs_0_), channel_id=1, source_target_pairs={{8,16},{12,20},{16,24},{20,28},{9,17},{13,21},{17,25},{21,29},{10,... | collective-permute-start | bytes 1622024 | tf_op jit(solution)/shard_map/near_up_c2/ppermute | solution.py:684
  123.9 24.9 %collective-permute-start.27 = (bf16[1,1056,256]{2,1,0:T(8,128)(2,1)}, bf16[1,1056,256]{2,1,0:T(8,128)(2,1)}, u32[]{:S(2)}, u32[]{:S(2)}) collective-permute-start(bf16[1,1056,256]{2,1,0:T(8,128)(2,1)} %get-tuple-element.80), channel_id=1, source_target_pairs={{8,24},{12,28},{9,25},{13,29},{10,26},{14,30},{11,27},{15,31}} | collective-permute-start | bytes 1622024 | tf_op jit(solution)/shard_map/far_up_c2/ppermute | solution.py:684
  139.6 26.2 %collective-permute-start.30 = (bf16[1,528,256]{2,1,0:T(8,128)(2,1)S(1)}, bf16[1,528,256]{2,1,0:T(8,128)(2,1)S(1)}, u32[]{:S(2)}, u32[]{:S(2)}) collective-permute-start(bf16[1,528,256]{2,1,0:T(8,128)(2,1)S(1)} %get-tuple-element.77.refs_0_), channel_id=1, source_target_pairs={{8,16},{12,20},{16,24},{20,28},{9,17},{13,21},{17,25},{21,29},{10,... | collective-permute-start | bytes 811016 | tf_op jit(solution)/shard_map/near_up_same_c3/ppermute | solution.py:684
  140.9 26.2 %collective-permute-start.31 = (bf16[1,528,256]{2,1,0:T(8,128)(2,1)S(1)}, bf16[1,528,256]{2,1,0:T(8,128)(2,1)S(1)}, u32[]{:S(2)}, u32[]{:S(2)}) collective-permute-start(bf16[1,528,256]{2,1,0:T(8,128)(2,1)S(1)} %get-tuple-element.85), channel_id=1, source_target_pairs={{8,20},{12,16},{16,28},{20,24},{9,21},{13,17},{17,29},{21,25},{10,... | collective-permute-start | bytes 811016 | tf_op jit(solution)/shard_map/near_up_cross_c3/ppermute | solution.py:684
  142.2 38.9 %collective-permute-start.34 = (bf16[2,1024,128]{2,1,0:T(8,128)(2,1)S(1)}, bf16[2,1024,128]{2,1,0:T(8,128)(2,1)S(1)}, u32[]{:S(2)}, u32[]{:S(2)}) collective-permute-start(bf16[2,1024,128]{2,1,0:T(8,128)(2,1)S(1)} %get-tuple-element.89), channel_id=1, source_target_pairs={{0,4},{4,0},{8,12},{12,8},{16,20},{20,16},{24,28},{28,24},{1,5},{5... | collective-permute-start | bytes 1572872 | tf_op jit(solution)/shard_map/back_c0/ppermute | solution.py:684
  148.9 30.1 %copy-start.23 = (bf16[1024]{0:T(1024)(128)(2,1)S(1)}, bf16[1024]{0:T(1024)(128)(2,1)}, u32[]{:S(2)}) copy-start(bf16[1024]{0:T(1024)(128)(2,1)} %param.9) | copy-start | bytes 6148
  150.6 13.9 %collective-permute-start.28 = (f32[4,256]{1,0:T(4,128)S(1)}, f32[4,256]{1,0:T(4,128)S(1)}, u32[]{:S(2)}, u32[]{:S(2)}) collective-permute-start(f32[4,256]{1,0:T(4,128)S(1)} %slice.19), channel_id=1, source_target_pairs={{0,4},{4,0},{8,12},{12,8},{16,20},{20,16},{24,28},{28,24},{1,5},{5... | collective-permute-start | bytes 12296 | tf_op jit(solution)/shard_map/squares_swap/ppermute | solution.py:684
  152.2 15.6 %collective-permute-start.32 = (bf16[1,528,256]{2,1,0:T(8,128)(2,1)S(1)}, bf16[1,528,256]{2,1,0:T(8,128)(2,1)S(1)}, u32[]{:S(2)}, u32[]{:S(2)}) collective-permute-start(bf16[1,528,256]{2,1,0:T(8,128)(2,1)S(1)} %get-tuple-element.86), channel_id=1, source_target_pairs={{8,24},{12,28},{9,25},{13,29},{10,26},{14,30},{11,27},{15,31}} | collective-permute-start | bytes 811016 | tf_op jit(solution)/shard_map/far_up_same_c3/ppermute | solution.py:684
  164.4 10.2 %collective-permute-start.33 = (bf16[1,528,256]{2,1,0:T(8,128)(2,1)S(1)}, bf16[1,528,256]{2,1,0:T(8,128)(2,1)S(1)}, u32[]{:S(2)}, u32[]{:S(2)}) collective-permute-start(bf16[1,528,256]{2,1,0:T(8,128)(2,1)S(1)} %get-tuple-element.87), channel_id=1, source_target_pairs={{8,28},{12,24},{9,29},{13,25},{10,30},{14,26},{11,31},{15,27}} | collective-permute-start | bytes 811016 | tf_op jit(solution)/shard_map/far_up_cross_c3/ppermute | solution.py:684
  165.7 9.4 %collective-permute-start.29 = (bf16[1,528,256]{2,1,0:T(8,128)(2,1)S(1)}, bf16[1,528,256]{2,1,0:T(8,128)(2,1)S(1)}, u32[]{:S(2)}, u32[]{:S(2)}) collective-permute-start(bf16[1,528,256]{2,1,0:T(8,128)(2,1)S(1)} %get-tuple-element.84), channel_id=1, source_target_pairs={{0,4},{4,0},{8,12},{12,8},{16,20},{20,16},{24,28},{28,24},{1,5},{5... | collective-permute-start | bytes 811016 | tf_op jit(solution)/shard_map/back_own_c3/ppermute | solution.py:684
  167.1 14.0 %collective-permute-start.35 = (bf16[1,1024,128]{2,1,0:T(8,128)(2,1)S(1)}, bf16[1,1024,128]{2,1,0:T(8,128)(2,1)S(1)}, u32[]{:S(2)}, u32[]{:S(2)}) collective-permute-start(bf16[1,1024,128]{2,1,0:T(8,128)(2,1)S(1)} %get-tuple-element.90), channel_id=1, source_target_pairs={{0,4},{4,0},{8,12},{12,8},{16,20},{20,16},{24,28},{28,24},{1,5},{5... | collective-permute-start | bytes 786440 | tf_op jit(solution)/shard_map/back_c2/ppermute | solution.py:684
  176.2 1.2 collective-permute-start.36
  177.4 3.6 %collective-permute-start.37 = (f32[4,256]{1,0:T(4,128)S(1)}, f32[4,256]{1,0:T(4,128)S(1)}, u32[]{:S(2)}, u32[]{:S(2)}) collective-permute-start(f32[4,256]{1,0:T(4,128)S(1)} %add.294), channel_id=1, source_target_pairs={{0,2},{1,3},{2,0},{3,1},{4,6},{5,7},{6,4},{7,5},{8,10},{9,11},{10,... | collective-permute-start | bytes 12296 | tf_op jit(solution)/shard_map/ppermute | solution.py:859
  (14 other events, 43.6 us)

commit v7 on v6

--- a/solution.py
+++ b/solution.py
@@ -128,36 +128,38 @@
     )
 
 
-SPLIT = (True, True, False, False)
+SPLIT = (True, False, False, False)
 SCATTER = (False, False, False, False)
 ORDER = (
-    ("p", 0, 1),
-    ("w", "plans"),
+    ("p", 0),
+    ("w", "plan"),
     ("w", "near_down_keep_c0"),
     ("w", "far_down_keep_c0"),
     ("w", "lift_keep_c0"),
+    ("p", 1),
     ("j", 0),
     ("p", 2),
     ("j", 1),
+    ("s", 0),
+    ("j", 2),
+    ("a", 0),
     ("p", 3),
-    ("s", 0),
-    ("a", 0),
-    ("j", 2),
     ("s", 1),
+    ("m", 0),
     ("a", 1),
-    ("w", "near_up_c0"),
-    ("w", "far_up_c0"),
     ("j", 3),
     ("s", 2),
+    ("m", 1),
     ("a", 2),
-    ("m", 0, 1),
+    ("w", "back_c0"),
+    ("s", 3),
     ("a", 3),
-    ("s", 3),
     ("m", 2),
     ("m", 3),
 )
-COSTS = {"pack": 0.0, "join": 0.0, "served": 0.0, "own": 0.0, "merge": 0.0, "finish": 0.0}
+COSTS = {"pack": 2, "join": 1, "served": 6, "own": 5, "merge": 1, "finish": 3}
 DIRECT = True
+NOTE_ROWS = 16
 UNROLL = 2
 VMEM_LIMIT = 16 * 1024 * 1024
 
@@ -171,12 +173,13 @@
 
 
 PIECES = {
-    "head": lambda ref, h: ref.at[h],
-    "next head": lambda ref, h: ref.at[h + 1],
-    "queries": lambda ref, h: ref.at[h, 0],
-    "keys_values": lambda ref, h: ref.at[h, pl.ds(1, 2)],
-    "first": lambda ref, h: ref.at[0, h],
-    "second": lambda ref, h: ref.at[1, h],
+    "head": lambda ref, h, rows: ref.at[h],
+    "next head": lambda ref, h, rows: ref.at[h + 1],
+    "top rows": lambda ref, h, rows: ref.at[h, pl.ds(0, rows)],
+    "queries": lambda ref, h, rows: ref.at[h, 0],
+    "keys_values": lambda ref, h, rows: ref.at[h, pl.ds(1, 2)],
+    "first": lambda ref, h, rows: ref.at[0, h],
+    "second": lambda ref, h, rows: ref.at[1, h],
 }
 
 
@@ -192,15 +195,16 @@
     copies = []
     for h in range(heads):
         for i, (n, kind) in enumerate(q_pieces):
-            copies.append((PIECES[kind](inputs[n], h), q_scr.at[h, i], sems.at[h, i]))
+            copies.append((PIECES[kind](inputs[n], h, per_dev * block_rows), q_scr.at[h, i], sems.at[h, i]))
         for i, (n, kind) in enumerate(kv_pieces):
-            copies.append((PIECES[kind](inputs[n], h), kv_scr.at[h, i], sems.at[h, n_q + i]))
+            copies.append((PIECES[kind](inputs[n], h, per_dev * block_rows), kv_scr.at[h, i], sems.at[h, n_q + i]))
     copies = [pltpu.make_async_copy(*copy) for copy in copies]
     for copy in copies:
         copy.start()
     s1[...] = jnp.zeros_like(s1)
     p0[...] = jnp.zeros_like(p0)
     d0[...] = jnp.zeros_like(d0)
+    d1[...] = jnp.zeros_like(d1)
     acc_scr[...] = jnp.zeros_like(acc_scr)
     top_scr[...] = jnp.zeros_like(top_scr)
     sum_scr[...] = jnp.ones_like(sum_scr)
@@ -226,12 +230,10 @@
             acc = acc * decay_scr[now][u, 0:1, :] + mixed
             o_scr[out] = (acc * decay_scr[now][u, 1:2, :]).astype(o_scr.dtype)
         for u in range(UNROLL):
-            _, _, out, first, diagonal = unit_fields(plan[at + UNROLL + u])
+            _, _, out, first, _ = unit_fields(plan[at + UNROLL + u])
             s = s_scr[before][u]
-            if own:
-                s = s + bias_scr[diagonal]
             old = jnp.where(first == 1, -1e30, top)
-            top = jnp.maximum(old, jnp.max(s, axis=0, keepdims=True))
+            top = jnp.maximum(old, decay_scr[before][u, 2:3, :])
             decay = jnp.exp2((old - top) * EXP_SCALE)
             p = jnp.exp2((s - top) * EXP_SCALE)
             total = total * decay + jnp.sum(p, axis=0, keepdims=True)
@@ -240,12 +242,14 @@
             decay_scr[before][u, 1:2, :] = 1.0 / total
             lse_scr[pl.ds(out, 1), :] = top * EXP_SCALE + jnp.log(total) * LOG2E
         for u in range(UNROLL):
-            slot, span, _, _, _ = unit_fields(plan[at + 2 * UNROLL + u])
+            slot, span, _, _, diagonal = unit_fields(plan[at + 2 * UNROLL + u])
             k = kv_scr[h, slot // per_dev, 0, rows_of(slot), :]
             q = q_scr[h, span // per_dev, rows_of(span), :]
-            s_scr[now][u] = lax.dot_general(
-                k, q, (((1,), (1,)), ((), ())), preferred_element_type=jnp.float32
-            )
+            s = lax.dot_general(k, q, (((1,), (1,)), ((), ())), preferred_element_type=jnp.float32)
+            if own:
+                s = s + bias_scr[diagonal]
+            s_scr[now][u] = s
+            decay_scr[now][u, 2:3, :] = jnp.max(s, axis=0, keepdims=True)
         return acc, top, total
 
     for h in range(heads):
@@ -446,13 +450,19 @@
     )(*after, place, queries, keys, values)
 
 
-def cut_kernel(ref, q_ref, kv_ref, scr, sems):
-    load = pltpu.make_async_copy(ref, scr, sems.at[0])
-    load.start()
-    load.wait()
+def cut_kernel(rows, note_ref, ref, q_ref, kv_ref, scr, note_scr, sems):
+    loads = [
+        pltpu.make_async_copy(ref, scr, sems.at[0]),
+        pltpu.make_async_copy(note_ref, note_scr, sems.at[1]),
+    ]
+    for load in loads:
+        load.start()
+    for load in loads:
+        load.wait()
     stores = [
-        pltpu.make_async_copy(scr.at[0, 0], q_ref.at[0], sems.at[1]),
-        pltpu.make_async_copy(scr.at[0, pl.ds(1, 2)], kv_ref.at[0], sems.at[2]),
+        pltpu.make_async_copy(scr.at[0, 0], q_ref.at[0, pl.ds(0, rows)], sems.at[2]),
+        pltpu.make_async_copy(note_scr, q_ref.at[0, pl.ds(rows, NOTE_ROWS)], sems.at[3]),
+        pltpu.make_async_copy(scr.at[0, pl.ds(1, 2)], kv_ref.at[0], sems.at[4]),
     ]
     for store in stores:
         store.start()
@@ -460,25 +470,26 @@
         store.wait()
 
 
-def cut_call(packed, after=()):
+def cut_call(packed, note, after=()):
     _, _, rows, _ = packed.shape
     hbm = pl.BlockSpec(memory_space=pltpu.HBM)
     return pl.pallas_call(
-        ordered(cut_kernel, len(after)),
+        ordered(partial(cut_kernel, rows), len(after)),
         out_shape=(
-            jax.ShapeDtypeStruct((1, rows, HD), jnp.bfloat16),
+            jax.ShapeDtypeStruct((1, rows + NOTE_ROWS, HD), jnp.bfloat16),
             jax.ShapeDtypeStruct((1, 2, rows, HD), jnp.bfloat16),
         ),
-        in_specs=[hbm] * (len(after) + 1),
+        in_specs=[hbm] * (len(after) + 2),
         out_specs=(hbm, hbm),
         scratch_shapes=[
             pltpu.VMEM(packed.shape, jnp.bfloat16),
-            pltpu.SemaphoreType.DMA((3,)),
+            pltpu.VMEM((NOTE_ROWS, HD), jnp.bfloat16),
+            pltpu.SemaphoreType.DMA((5,)),
         ],
         compiler_params=pltpu.CompilerParams(vmem_limit_bytes=VMEM_LIMIT),
         cost_estimate=cost("join"),
         name="join",
-    )(*after, packed)
+    )(*after, note, packed)
 
 
 def join_kernel(heads, keep_ref, swap_ref, q_ref, kv_ref, scr, sems):
@@ -704,10 +715,8 @@
     place = jnp.stack([x, 1 - x]).astype(jnp.int32)
 
     own_selection = jnp.concatenate([selection, to(selection, swap, "selection_swap")], axis=0)
-    above = to(own_selection, [(6, 4), (7, 5)], "selection_near")
-    two = to(jnp.concatenate([own_selection, above], axis=0), [(4, 2), (5, 3)], "selection_far")
-    near_selection = jnp.where(level == 2, above, two[:spans])
-    far_selection = two[spans:]
+    note = jnp.zeros((NOTE_ROWS, HD), jnp.bfloat16)
+    note = lax.dynamic_update_slice(note, own_selection.astype(jnp.bfloat16), (0, 0))
 
     def ids(at):
         first = jnp.stack([(at * 2 + x) * per_dev, (at * 2 + 1 - x) * per_dev])
@@ -728,18 +737,22 @@
         jnp.concatenate([first, jnp.zeros_like(others)], axis=1),
         spans,
     )
-    others = jnp.concatenate([near_selection, far_selection], axis=0)[:, 1:]
-    block_level, slot = slots(others)
-    is_near = lax.broadcasted_iota(jnp.int32, others.shape, 0) < spans
-    mine = ((level == 1) & (block_level <= 1)) | ((level == 2) & (block_level == 2) & is_near)
-    live = (others != jnp.concatenate([ids(level + 1), ids(level + 2)], axis=0)) & mine
-    served_plan = plan_of(live, slot, jnp.zeros_like(others), 2 * spans)
+    def served_lists(*noted):
+        near_selection, far_selection = (
+            array[0, rows : rows + spans, :topk].astype(jnp.int32) for array in noted
+        )
+        others = jnp.concatenate([near_selection, far_selection], axis=0)[:, 1:]
+        block_level, slot = slots(others)
+        is_near = lax.broadcasted_iota(jnp.int32, others.shape, 0) < spans
+        mine = ((level == 1) & (block_level <= 1)) | ((level == 2) & (block_level == 2) & is_near)
+        live = (others != jnp.concatenate([ids(level + 1), ids(level + 2)], axis=0)) & mine
+        return plan_of(live, slot, jnp.zeros_like(others), 2 * spans)
 
     n, split, order = half, SPLIT, ORDER
     own_pieces, z_arrays, served_pieces, downs_of = {}, {}, {}, {}
     ups, owns, others, squares_in, kept, returned = {}, {}, {}, [], [], []
     squares = [jnp.zeros((spans, block_rows), jnp.float32)]
-    last = []
+    last, served_plan = [], []
 
     def downs(q, kv, name):
         low = to(kv, lift, f"lift_{name}")
@@ -774,10 +787,15 @@
 
     def join(c):
         if split[c]:
-            q_swap, kv_swap = cut_call(*z_arrays[c], last)
+            q_swap, kv_swap = cut_call(*z_arrays[c], note, last)
             last[:] = [q_swap]
             swaps = downs(q_swap, kv_swap, f"recv_c{c}")
-            near, far, low = [[k, (r, "head")] for k, r in zip(downs_of[c], swaps)]
+            if not served_plan:
+                served_plan.append(served_lists(*swaps[:2]))
+            near, far, low = [
+                [k, (r, kind)]
+                for k, r, kind in zip(downs_of[c], swaps, ("top rows", "top rows", "head"))
+            ]
         else:
             level_q, level_kv = join_call(*z_arrays[c], last)
             last[:] = [level_q]
@@ -791,7 +809,7 @@
 
     def serve(c):
         packs = attention_call(
-            served_plan, *served_pieces[c], False, is_direct(c), 1, per_dev, block_rows, last
+            served_plan[0], *served_pieces[c], False, is_direct(c), 1, per_dev, block_rows, last
         )
         last[:] = [packs[0]]
         if is_direct(c):
@@ -847,7 +865,7 @@
     steps = {"p": pack, "j": join, "s": serve, "a": attend, "m": merge}
     for what, *args in order:
         if what == "w":
-            last.extend([own_plan, served_plan] if args[0] == "plans" else [sent[args[0]]])
+            last.append(own_plan if args[0] == "plan" else sent[args[0]])
         else:
             steps[what](*args)
     square = squares[0]

time: 186 us -> 171 us (0.919)
  starting transfers between devices: 77.5 us -> 60.2 us
  waiting for transfers between devices: 53.2 us -> 56.7 us
    ppermute x36 -> x35, starting transfers between devices: 75.9 us -> 58.6 us  [to(): sent[name] = lax.ppermute(array, 'ctx', pairs)]
    ppermute x36 -> x35, waiting for transfers between devices: 50 us -> 53.5 us  [to(): sent[name] = lax.ppermute(array, 'ctx', pairs)]
    pallas_call x3 -> x4, Pallas kernels: 7.6 us -> 9.78 us  [pack_call(): pl.pallas_call(ordered(partial(pack_kernel, (heads, first, half, rows, sp...]
    unnamed x48 -> x22, local copies, waits for them, and re-layouts: 5.17 us -> 3.18 us
  transfers between devices with their start and end apart: 38 -> 37, of which waited for: 11 -> 13; matrix products, arithmetic and copies ran while one was open for 2% -> 3% of each run, Pallas kernels for 19% -> 21%
where the time goes in v7:
time: 171 us; the launch traced here: 170 us
  starting transfers between devices  60.2 us (35%)
  waiting for transfers between devices  56.7 us (33%)
  Pallas kernels  41.8 us (24%)
  local copies, waits for them, and re-layouts  4.24 us (2%)
  other arithmetic  3.4 us (2%)
  between operations  3.26 us (2%)
    ppermute x35, starting transfers between devices, to(): sent[name] = lax.ppermute(array, 'ctx', pairs)  58.6 us
    ppermute x35, waiting for transfers between devices, to(): sent[name] = lax.ppermute(array, 'ctx', pairs)  53.5 us
    pallas_call x8, Pallas kernels, attention_call(): pl.pallas_call(ordered(partial(attention_kernel, (heads, per_dev, block_r...  22.2 us
    pallas_call x4, Pallas kernels, pack_call(): pl.pallas_call(ordered(partial(pack_kernel, (heads, first, half, rows, sp...  9.78 us
  transfers between devices with their start and end apart: 37, of which 13 were waited for; matrix products, arithmetic and copies ran while one was open for 3% of the time, Pallas kernels for 21%

profile of v7, /device:TPU:24, one launch (start us, length us, event | category | flops | bytes accessed | tf_op | source)
XLA Modules:
  0.0 169.5 jit_solution(12842851063820897274)
XLA Ops:
  0.1 2.2 %pack.4 = (bf16[1,1024,128]{2,1,0:T(8,128)(2,1)S(1)}, bf16[1,2,1024,128]{3,2,1,0:T(8,128)(2,1)S(1)}, bf16[1,3,1024,128]{3,2,1,0:T(8,128)(2,1)S(1)}) custom-call(s32[2]{0:T(128)S(1)} %pad_add_fusion.2.refs_0_.refs_5_.refs_1_.place, bf16[1024,1024]{1,0:T(8,128)(2,1)} %refs_2_.5, bf16[1024,1024]{1,0:T(8,128)(2,1)} %refs_3_.5, bf16[1024,1024]{1,0:T(8,128)(2,1)} %refs_4_.3), custom_call_target="tpu_custom_call" | custom-call | flops 2000000000 | bytes 6800001 | tf_op jit(solution)/shard_map/pack/pallas_call | solution.py:437
  2.3 2.4 %collective-permute-start.1 = (bf16[1,1024,128]{2,1,0:T(8,128)(2,1)S(1)}, bf16[1,1024,128]{2,1,0:T(8,128)(2,1)S(1)}, u32[]{:S(2)}, u32[]{:S(2)}) collective-permute-start(bf16[1,1024,128]{2,1,0:T(8,128)(2,1)S(1)} %get-tuple-element.53.refs_0_.refs_2_), channel_id=1, source_target_pairs={{16,8},{20,12},{24,16},{28,20},{17,9},{21,13},{25,17},{29,21},{18,... | collective-permute-start | bytes 786440 | tf_op jit(solution)/shard_map/near_down_keep_c0/ppermute | solution.py:695
  4.7 1.3 collective-permute-start.2
  6.0 1.6 collective-permute-start
  12.8 3.0 %collective-permute-done.2.refs_3_.refs_4_ = bf16[1,1024,128]{2,1,0:T(8,128)(2,1)S(1)} collective-permute-done((bf16[1,1024,128]{2,1,0:T(8,128)(2,1)S(1)}, bf16[1,1024,128]{2,1,0:T(8,128)(2,1)S(1)}, u32[]{:S(2)}, u32[]{:S(2)}) %collective-permute-start.2) | collective-permute-done | bytes 262176 | tf_op jit(solution)/shard_map/far_down_keep_c0/ppermute | solution.py:695
  15.9 2.7 %pack.5 = (bf16[1,3,1024,128]{3,2,1,0:T(8,128)(2,1)S(1)}, bf16[1,3,1024,128]{3,2,1,0:T(8,128)(2,1)}) custom-call(bf16[1,1024,128]{2,1,0:T(8,128)(2,1)S(1)} %get-tuple-element.53.refs_0_.refs_2_, s32[81]{0:T(128)S(1)} %pad_add_fusion.4.refs_1_, bf16[1,1024,128]{2,1,0:T(8,128)(2,1)S(1)} %collective-permute-done.1.refs_2_, ...), custom_call_target="tpu_custom_call" | custom-call | flops 2000000000 | bytes 6800001 | tf_op jit(solution)/shard_map/pack/pallas_call | solution.py:437
  18.5 8.5 %collective-permute-done.4.refs_2_.refs_7_.refs_3_ = bf16[1,3,1024,128]{3,2,1,0:T(8,128)(2,1)S(1)} collective-permute-done((bf16[1,3,1024,128]{3,2,1,0:T(8,128)(2,1)S(1)}, bf16[1,3,1024,128]{3,2,1,0:T(8,128)(2,1)S(1)}, u32[]{:S(2)}, u32[]{:S(2)}) %collective-permute-start.4) | collective-permute-done | bytes 786464 | tf_op jit(solution)/shard_map/swap_c0/ppermute | solution.py:695
  28.1 1.7 %collective-permute-start.6 = (bf16[1,1040,128]{2,1,0:T(8,128)(2,1)}, bf16[1,1040,128]{2,1,0:T(8,128)(2,1)S(1)}, u32[]{:S(2)}, u32[]{:S(2)}) collective-permute-start(bf16[1,1040,128]{2,1,0:T(8,128)(2,1)} %get-tuple-element.57.refs_0_), channel_id=1, source_target_pairs={{16,8},{20,12},{24,16},{28,20},{17,9},{21,13},{25,17},{29,21},{18,... | collective-permute-start | bytes 798728 | tf_op jit(solution)/shard_map/near_down_recv_c0/ppermute | solution.py:695
  30.4 1.6 collective-permute-start.7
  32.0 2.6 %pack.6 = (bf16[1,3,1024,128]{3,2,1,0:T(8,128)(2,1)S(1)}, bf16[1,3,1024,128]{3,2,1,0:T(8,128)(2,1)}) custom-call(bf16[1,1040,128]{2,1,0:T(8,128)(2,1)} %get-tuple-element.57.refs_0_, s32[2]{0:T(128)S(1)} %pad_add_fusion.2.refs_0_.refs_5_.refs_1_.place, bf16[1024,1024]{1,0:T(8,128)(2,1)} %refs_2_.5, bf16[1024,1024]{1,0:T(8,128)(2,1)} %refs_3_.5, ...), custom_call_target="tpu_custom_call" | custom-call | flops 2000000000 | bytes 6800001 | tf_op jit(solution)/shard_map/pack/pallas_call | solution.py:437
  35.6 1.5 collective-permute-start.8
  37.0 1.5 collective-permute-start.9
  38.6 1.3 collective-permute-done.7.refs_5_
  42.9 7.8 %collective-permute-done.5.refs_2_.refs_5_.refs_3_ = bf16[1,3,1024,128]{3,2,1,0:T(8,128)(2,1)} collective-permute-done((bf16[1,3,1024,128]{3,2,1,0:T(8,128)(2,1)}, bf16[1,3,1024,128]{3,2,1,0:T(8,128)(2,1)}, u32[]{:S(2)}, u32[]{:S(2)}) %collective-permute-start.5) | collective-permute-done | bytes 786464 | tf_op jit(solution)/shard_map/swap_c1/ppermute | solution.py:695
  52.9 1.3 join.5
  54.3 2.8 %collective-permute-start.10 = (bf16[2,1,1024,128]{3,2,1,0:T(8,128)(2,1)S(1)}, bf16[2,1,1024,128]{3,2,1,0:T(8,128)(2,1)S(1)}, u32[]{:S(2)}, u32[]{:S(2)}) collective-permute-start(bf16[2,1,1024,128]{3,2,1,0:T(8,128)(2,1)S(1)} %get-tuple-element.60.refs_0_), channel_id=1, source_target_pairs={{16,8},{20,12},{24,16},{28,20},{17,9},{21,13},{25,17},{29,21},{18,... | collective-permute-start | bytes 1572872 | tf_op jit(solution)/shard_map/near_down_c1/ppermute | solution.py:695
  57.1 1.3 collective-permute-start.11
  59.2 2.0 %served_attention.4 = (bf16[1,1056,256]{2,1,0:T(8,128)(2,1)S(1)}, bf16[1,1056,256]{2,1,0:T(8,128)(2,1)S(1)}) custom-call(bf16[2,1,1024,128]{3,2,1,0:T(8,128)(2,1)S(1)} %get-tuple-element.60.refs_0_, s32[129]{0:T(256)S(1)} %pad_add_fusion.1.refs_1_.refs_2_, bf16[1,1024,128]{2,1,0:T(8,128)(2,1)S(1)} %collective-permute-done.1.refs_2_, ...), custom_call_target="tpu_custom_call" | custom-call | flops 6000000000 | bytes 20400000 | tf_op jit(solution)/shard_map/served_attention/pallas_call | solution.py:352
  61.2 1.3 collective-permute-start.13
  62.5 2.0 %collective-permute-done.9.refs_2_.refs_5_.refs_3_ = bf16[1,3,1024,128]{3,2,1,0:T(8,128)(2,1)S(1)} collective-permute-done((bf16[1,3,1024,128]{3,2,1,0:T(8,128)(2,1)}, bf16[1,3,1024,128]{3,2,1,0:T(8,128)(2,1)S(1)}, u32[]{:S(2)}, u32[]{:S(2)}) %collective-permute-start.9) | collective-permute-done | bytes 786464 | tf_op jit(solution)/shard_map/swap_c2/ppermute | solution.py:695
  64.5 1.3 collective-permute-start.14
  66.0 4.5 %own_attention.4 = (f32[1,8,128,256]{3,2,1,0:T(8,128)S(1)}, f32[1,8,256]{2,1,0:T(8,128)S(1)}) custom-call(bf16[2,1,1024,128]{3,2,1,0:T(8,128)(2,1)S(1)} %get-tuple-element.64.refs_0_, s32[81]{0:T(128)S(1)} %pad_add_fusion.4.refs_1_, bf16[1,1024,128]{2,1,0:T(8,128)(2,1)S(1)} %get-tuple-element.53.refs_0_.refs_2_, ...), custom_call_target="tpu_custom_call" | custom-call | flops 5000000000 | bytes 17000000 | tf_op jit(solution)/shard_map/own_attention/pallas_call | solution.py:352
  70.5 2.2 %pack.7 = (bf16[1,3,1024,128]{3,2,1,0:T(8,128)(2,1)S(1)}, bf16[1,3,1024,128]{3,2,1,0:T(8,128)(2,1)S(1)}) custom-call(f32[1,8,256]{2,1,0:T(8,128)S(1)} %get-tuple-element.65.refs_0_.refs_4_, s32[2]{0:T(128)S(1)} %pad_add_fusion.2.refs_0_.refs_5_.refs_1_.place, bf16[1024,1024]{1,0:T(8,128)(2,1)} %refs_2_.5, bf16[1024,1024]{1,0:T(8,128)(2,1)} %refs_3_.5, ...), custom_call_target="tpu_custom_call" | custom-call | flops 2000000000 | bytes 6800001 | tf_op jit(solution)/shard_map/pack/pallas_call | solution.py:437
  72.8 2.5 %collective-permute-start.16 = (bf16[2,1,1024,128]{3,2,1,0:T(8,128)(2,1)S(1)}, bf16[2,1,1024,128]{3,2,1,0:T(8,128)(2,1)S(1)}, u32[]{:S(2)}, u32[]{:S(2)}) collective-permute-start(bf16[2,1,1024,128]{3,2,1,0:T(8,128)(2,1)S(1)} %get-tuple-element.64.refs_0_), channel_id=1, source_target_pairs={{16,8},{20,12},{24,16},{28,20},{17,9},{21,13},{25,17},{29,21},{18,... | collective-permute-start | bytes 1572872 | tf_op jit(solution)/shard_map/near_down_c2/ppermute | solution.py:695
  77.2 1.9 %served_attention.5 = (bf16[1,1056,256]{2,1,0:T(8,128)(2,1)S(1)}, bf16[1,1056,256]{2,1,0:T(8,128)(2,1)S(1)}) custom-call(bf16[1,3,1024,128]{3,2,1,0:T(8,128)(2,1)S(1)} %get-tuple-element.66.refs_0_.refs_1_.refs_5_.refs_2_, s32[129]{0:T(256)S(1)} %pad_add_fusion.1.refs_1_.refs_2_, bf16[2,1,1024,128]{3,2,1,0:T(8,128)(2,1)S(1)} %collective-permute-done.10.refs_2_, ...), custom_call_target="tpu_custom_call" | custom-call | flops 6000000000 | bytes 20400000 | tf_op jit(solution)/shard_map/served_attention/pallas_call | solution.py:352
  79.2 10.2 %collective-permute-start.17 = (bf16[2,1,1024,128]{3,2,1,0:T(8,128)(2,1)S(1)}, bf16[2,1,1024,128]{3,2,1,0:T(8,128)(2,1)S(1)}, u32[]{:S(2)}, u32[]{:S(2)}) collective-permute-start(bf16[2,1,1024,128]{3,2,1,0:T(8,128)(2,1)S(1)} %get-tuple-element.64.refs_0_), channel_id=1, source_target_pairs={{24,8},{28,12},{25,9},{29,13},{26,10},{30,14},{27,11},{31,15}} | collective-permute-start | bytes 1572872 | tf_op jit(solution)/shard_map/far_down_c2/ppermute | solution.py:695
  89.4 1.3 collective-permute-start.19
  91.7 4.4 %own_attention.5 = (f32[1,8,128,256]{3,2,1,0:T(8,128)S(1)}, f32[1,8,256]{2,1,0:T(8,128)S(1)}) custom-call(bf16[1,1024,128]{2,1,0:T(8,128)(2,1)S(1)} %get-tuple-element.71.refs_0_, s32[81]{0:T(128)S(1)} %pad_add_fusion.4.refs_1_, bf16[1,3,1024,128]{3,2,1,0:T(8,128)(2,1)S(1)} %copy-done.2, ...), custom_call_target="tpu_custom_call" | custom-call | flops 5000000000 | bytes 17000000 | tf_op jit(solution)/shard_map/own_attention/pallas_call | solution.py:352
  96.1 1.4 collective-permute-start.20
  97.9 1.6 collective-permute-start.21
  100.2 4.0 %collective-permute-start.22 = (bf16[2,1,1024,128]{3,2,1,0:T(8,128)(2,1)S(1)}, bf16[2,1,1024,128]{3,2,1,0:T(8,128)(2,1)S(1)}, u32[]{:S(2)}, u32[]{:S(2)}) collective-permute-start(bf16[2,1,1024,128]{3,2,1,0:T(8,128)(2,1)S(1)} %get-tuple-element.74.refs_0_), channel_id=1, source_target_pairs={{16,8},{20,12},{24,16},{28,20},{17,9},{21,13},{25,17},{29,21},{18,... | collective-permute-start | bytes 1572872 | tf_op jit(solution)/shard_map/near_down_c3/ppermute | solution.py:695
  105.2 8.0 %collective-permute-done.19.refs_5_ = bf16[1,1056,256]{2,1,0:T(8,128)(2,1)S(1)} collective-permute-done((bf16[1,1056,256]{2,1,0:T(8,128)(2,1)S(1)}, bf16[1,1056,256]{2,1,0:T(8,128)(2,1)S(1)}, u32[]{:S(2)}, u32[]{:S(2)}) %collective-permute-start.19) | collective-permute-done | bytes 540704 | tf_op jit(solution)/shard_map/near_up_c1/ppermute | solution.py:695
  113.2 1.3 collective-permute-start.23
  114.6 1.3 collective-permute-start.25
  116.9 3.7 %own_attention.6 = (f32[1,8,128,256]{3,2,1,0:T(8,128)S(1)}, f32[1,8,256]{2,1,0:T(8,128)S(1)}) custom-call(bf16[1,1024,128]{2,1,0:T(8,128)(2,1)S(1)} %get-tuple-element.80.refs_0_.refs_1_, s32[81]{0:T(128)S(1)} %pad_add_fusion.4.refs_1_, bf16[1,3,1024,128]{3,2,1,0:T(8,128)(2,1)S(1)} %copy-done.7, ...), custom_call_target="tpu_custom_call" | custom-call | flops 5000000000 | bytes 17000000 | tf_op jit(solution)/shard_map/own_attention/pallas_call | solution.py:352
  120.7 1.3 collective-permute-start.26
  123.2 3.6 %own_attention.7 = (f32[1,4,128,256]{3,2,1,0:T(8,128)S(1)}, f32[1,4,256]{2,1,0:T(4,128)S(1)}, bf16[1,528,256]{2,1,0:T(8,128)(2,1)S(1)}) custom-call(bf16[1,528,256]{2,1,0:T(8,128)(2,1)S(1)} %get-tuple-element.84.refs_0_, s32[81]{0:T(128)S(1)} %pad_add_fusion.4.refs_1_, bf16[1,3,1024,128]{3,2,1,0:T(8,128)(2,1)S(1)} %get-tuple-element.66.refs_0_.refs_1_.refs_5_.refs_2_, ...), custom_call_target="tpu_custom_call" | custom-call | flops 5000000000 | bytes 17000000 | tf_op jit(solution)/shard_map/own_attention/pallas_call | solution.py:352
  126.7 2.2 %collective-permute-start.28 = (bf16[1,528,256]{2,1,0:T(8,128)(2,1)S(1)}, bf16[1,528,256]{2,1,0:T(8,128)(2,1)S(1)}, u32[]{:S(2)}, u32[]{:S(2)}) collective-permute-start(bf16[1,528,256]{2,1,0:T(8,128)(2,1)S(1)} %get-tuple-element.92), channel_id=1, source_target_pairs={{0,4},{4,0},{8,12},{12,8},{16,20},{20,16},{24,28},{28,24},{1,5},{5... | collective-permute-start | bytes 811016 | tf_op jit(solution)/shard_map/back_own_c3/ppermute | solution.py:695
  128.9 1.3 collective-permute-start.29
  130.2 9.2 %collective-permute-done.25.refs_5_ = bf16[1,1056,256]{2,1,0:T(8,128)(2,1)S(1)} collective-permute-done((bf16[1,1056,256]{2,1,0:T(8,128)(2,1)S(1)}, bf16[1,1056,256]{2,1,0:T(8,128)(2,1)S(1)}, u32[]{:S(2)}, u32[]{:S(2)}) %collective-permute-start.25) | collective-permute-done | bytes 540704 | tf_op jit(solution)/shard_map/near_up_c2/ppermute | solution.py:695
  140.5 1.4 collective-permute-start.27
  141.9 1.3 collective-permute-start.30
  143.2 1.3 collective-permute-start.31
  144.5 1.3 collective-permute-start.32
  149.0 11.8 %collective-permute-done.30.refs_8_ = bf16[1,528,256]{2,1,0:T(8,128)(2,1)S(1)} collective-permute-done((bf16[1,528,256]{2,1,0:T(8,128)(2,1)S(1)}, bf16[1,528,256]{2,1,0:T(8,128)(2,1)S(1)}, u32[]{:S(2)}, u32[]{:S(2)}) %collective-permute-start.30) | collective-permute-done | bytes 270368 | tf_op jit(solution)/shard_map/near_up_cross_c3/ppermute | solution.py:695
  163.1 1.5 collective-permute-start.36
  164.6 2.1 %collective-permute-done.36 = f32[4,256]{1,0:T(4,128)S(1)} collective-permute-done((f32[4,256]{1,0:T(4,128)S(1)}, f32[4,256]{1,0:T(4,128)S(1)}, u32[]{:S(2)}, u32[]{:S(2)}) %collective-permute-start.36) | collective-permute-done | bytes 4128 | tf_op jit(solution)/shard_map/ppermute | solution.py:877
  166.7 2.8 %finish.1 = bf16[1024,1024]{1,0:T(8,128)(2,1)} custom-call(s32[2]{0:T(128)S(1)} %pad_add_fusion.2.refs_0_.refs_5_.refs_1_.place, bf16[1,1024,128]{2,1,0:T(8,128)(2,1)S(1)} %get-tuple-element.71.refs_0_, bf16[1,1024,128]{2,1,0:T(8,128)(2,1)S(1)} %get-tuple-element.80.refs_0_.refs_1_, bf16[1,1024,128]{2,1,0:T(8,128)(2,1)S(1)} %get-tuple-element.89.refs_0_.refs_2_, ...), custom_call_target="tpu_custom_call" | custom-call | flops 3000000000 | bytes 10200001 | tf_op jit(solution)/shard_map/finish/pallas_call | solution.py:652
  (124 shorter events, 25.2 us)
Async XLA Ops:
  0.1 6.0 %copy-start.9 = (s32[4,8]{1,0:T(4,128)S(1)}, s32[4,8]{1,0:T(4,128)}, u32[]{:S(2)}) copy-start(s32[4,8]{1,0:T(4,128)} %param.8) | copy-start | bytes 388
  0.1 10.3 %copy-start.8 = (s32[8,8]{1,0:T(8,128)S(1)}, s32[8,8]{1,0:T(8,128)}, u32[]{:S(2)}) copy-start(s32[8,8]{1,0:T(8,128)} %constant.158.clone.1) | copy-start | bytes 772
  2.3 16.2 %copy-start.3 = (bf16[1,2,1024,128]{3,2,1,0:T(8,128)(2,1)}, bf16[1,2,1024,128]{3,2,1,0:T(8,128)(2,1)S(1)}, u32[]{:S(2)}) copy-start(bf16[1,2,1024,128]{3,2,1,0:T(8,128)(2,1)S(1)} %get-tuple-element.54.refs_6_.refs_4_) | copy-start | bytes 1572868
  2.3 10.5 %collective-permute-start.1 = (bf16[1,1024,128]{2,1,0:T(8,128)(2,1)S(1)}, bf16[1,1024,128]{2,1,0:T(8,128)(2,1)S(1)}, u32[]{:S(2)}, u32[]{:S(2)}) collective-permute-start(bf16[1,1024,128]{2,1,0:T(8,128)(2,1)S(1)} %get-tuple-element.53.refs_0_.refs_2_), channel_id=1, source_target_pairs={{16,8},{20,12},{24,16},{28,20},{17,9},{21,13},{25,17},{29,21},{18,... | collective-permute-start | bytes 786440 | tf_op jit(solution)/shard_map/near_down_keep_c0/ppermute | solution.py:695
  4.7 11.1 %collective-permute-start.2 = (bf16[1,1024,128]{2,1,0:T(8,128)(2,1)S(1)}, bf16[1,1024,128]{2,1,0:T(8,128)(2,1)S(1)}, u32[]{:S(2)}, u32[]{:S(2)}) collective-permute-start(bf16[1,1024,128]{2,1,0:T(8,128)(2,1)S(1)} %get-tuple-element.53.refs_0_.refs_2_), channel_id=1, source_target_pairs={{24,8},{28,12},{25,9},{29,13},{26,10},{30,14},{27,11},{31,15}} | collective-permute-start | bytes 786440 | tf_op jit(solution)/shard_map/far_down_keep_c0/ppermute | solution.py:695
  6.0 3.7 %collective-permute-start = (s32[4,8]{1,0:T(4,128)S(1)}, s32[4,8]{1,0:T(4,128)S(1)}, u32[]{:S(2)}, u32[]{:S(2)}) collective-permute-start(s32[4,8]{1,0:T(4,128)S(1)} %copy-done.9), channel_id=1, source_target_pairs={{0,4},{4,0},{8,12},{12,8},{16,20},{20,16},{24,28},{28,24},{1,5},{5... | collective-permute-start | bytes 392 | tf_op jit(solution)/shard_map/selection_swap/ppermute | solution.py:695
  7.6 8.3 %collective-permute-start.3 = (bf16[1,2,1024,128]{3,2,1,0:T(8,128)(2,1)S(1)}, bf16[1,2,1024,128]{3,2,1,0:T(8,128)(2,1)S(1)}, u32[]{:S(2)}, u32[]{:S(2)}) collective-permute-start(bf16[1,2,1024,128]{3,2,1,0:T(8,128)(2,1)S(1)} %get-tuple-element.54.refs_6_.refs_4_), channel_id=1, source_target_pairs={{0,8},{4,12},{1,9},{5,13},{2,10},{6,14},{3,11},{7,15}} | collective-permute-start | bytes 1572872 | tf_op jit(solution)/shard_map/lift_keep_c0/ppermute | solution.py:695
  8.3 18.8 %collective-permute-start.4 = (bf16[1,3,1024,128]{3,2,1,0:T(8,128)(2,1)S(1)}, bf16[1,3,1024,128]{3,2,1,0:T(8,128)(2,1)S(1)}, u32[]{:S(2)}, u32[]{:S(2)}) collective-permute-start(bf16[1,3,1024,128]{3,2,1,0:T(8,128)(2,1)S(1)} %get-tuple-element.56), channel_id=1, source_target_pairs={{0,4},{4,0},{8,12},{12,8},{16,20},{20,16},{24,28},{28,24},{1,5},{5... | collective-permute-start | bytes 2359304 | tf_op jit(solution)/shard_map/swap_c0/ppermute | solution.py:695
  18.5 11.3 %copy-start = (bf16[1,3,1024,128]{3,2,1,0:T(8,128)(2,1)}, bf16[1,3,1024,128]{3,2,1,0:T(8,128)(2,1)S(1)}, u32[]{:S(2)}) copy-start(bf16[1,3,1024,128]{3,2,1,0:T(8,128)(2,1)S(1)} %get-tuple-element.55.refs_0_.refs_1_.refs_4_.refs_2_) | copy-start | bytes 2359300
  28.1 10.5 %collective-permute-start.6 = (bf16[1,1040,128]{2,1,0:T(8,128)(2,1)}, bf16[1,1040,128]{2,1,0:T(8,128)(2,1)S(1)}, u32[]{:S(2)}, u32[]{:S(2)}) collective-permute-start(bf16[1,1040,128]{2,1,0:T(8,128)(2,1)} %get-tuple-element.57.refs_0_), channel_id=1, source_target_pairs={{16,8},{20,12},{24,16},{28,20},{17,9},{21,13},{25,17},{29,21},{18,... | collective-permute-start | bytes 798728 | tf_op jit(solution)/shard_map/near_down_recv_c0/ppermute | solution.py:695
  29.9 20.8 %collective-permute-start.5 = (bf16[1,3,1024,128]{3,2,1,0:T(8,128)(2,1)}, bf16[1,3,1024,128]{3,2,1,0:T(8,128)(2,1)}, u32[]{:S(2)}, u32[]{:S(2)}) collective-permute-start(bf16[1,3,1024,128]{3,2,1,0:T(8,128)(2,1)} %get-tuple-element.59), channel_id=1, source_target_pairs={{0,4},{4,0},{8,12},{12,8},{16,20},{20,16},{24,28},{28,24},{1,5},{5... | collective-permute-start | bytes 2359304 | tf_op jit(solution)/shard_map/swap_c1/ppermute | solution.py:695
  30.4 9.5 %collective-permute-start.7 = (bf16[1,1040,128]{2,1,0:T(8,128)(2,1)}, bf16[1,1040,128]{2,1,0:T(8,128)(2,1)S(1)}, u32[]{:S(2)}, u32[]{:S(2)}) collective-permute-start(bf16[1,1040,128]{2,1,0:T(8,128)(2,1)} %get-tuple-element.57.refs_0_), channel_id=1, source_target_pairs={{24,8},{28,12},{25,9},{29,13},{26,10},{30,14},{27,11},{31,15}} | collective-permute-start | bytes 798728 | tf_op jit(solution)/shard_map/far_down_recv_c0/ppermute | solution.py:695
  34.7 0.9 copy-start.5
  35.6 23.6 %collective-permute-start.8 = (bf16[1,2,1024,128]{3,2,1,0:T(8,128)(2,1)}, bf16[1,2,1024,128]{3,2,1,0:T(8,128)(2,1)}, u32[]{:S(2)}, u32[]{:S(2)}) collective-permute-start(bf16[1,2,1024,128]{3,2,1,0:T(8,128)(2,1)} %get-tuple-element.61), channel_id=1, source_target_pairs={{0,8},{4,12},{1,9},{5,13},{2,10},{6,14},{3,11},{7,15}} | collective-permute-start | bytes 1572872 | tf_op jit(solution)/shard_map/lift_recv_c0/ppermute | solution.py:695
  37.0 27.4 %collective-permute-start.9 = (bf16[1,3,1024,128]{3,2,1,0:T(8,128)(2,1)}, bf16[1,3,1024,128]{3,2,1,0:T(8,128)(2,1)S(1)}, u32[]{:S(2)}, u32[]{:S(2)}) collective-permute-start(bf16[1,3,1024,128]{3,2,1,0:T(8,128)(2,1)} %get-tuple-element.63), channel_id=1, source_target_pairs={{0,4},{4,0},{8,12},{12,8},{16,20},{20,16},{24,28},{28,24},{1,5},{5... | collective-permute-start | bytes 2359304 | tf_op jit(solution)/shard_map/swap_c2/ppermute | solution.py:695
  50.7 1.1 copy-start.1
  51.8 1.1 copy-start.6
  52.9 6.2 %copy-start.4 = (bf16[1,2,1024,128]{3,2,1,0:T(8,128)(2,1)S(1)}, bf16[1,2,1024,128]{3,2,1,0:T(8,128)(2,1)}, u32[]{:S(2)}) copy-start(bf16[1,2,1024,128]{3,2,1,0:T(8,128)(2,1)} %copy-done.3) | copy-start | bytes 1572868
  54.3 18.5 %collective-permute-start.10 = (bf16[2,1,1024,128]{3,2,1,0:T(8,128)(2,1)S(1)}, bf16[2,1,1024,128]{3,2,1,0:T(8,128)(2,1)S(1)}, u32[]{:S(2)}, u32[]{:S(2)}) collective-permute-start(bf16[2,1,1024,128]{3,2,1,0:T(8,128)(2,1)S(1)} %get-tuple-element.60.refs_0_), channel_id=1, source_target_pairs={{16,8},{20,12},{24,16},{28,20},{17,9},{21,13},{25,17},{29,21},{18,... | collective-permute-start | bytes 1572872 | tf_op jit(solution)/shard_map/near_down_c1/ppermute | solution.py:695
  57.1 18.9 %collective-permute-start.11 = (bf16[2,1,1024,128]{3,2,1,0:T(8,128)(2,1)S(1)}, bf16[2,1,1024,128]{3,2,1,0:T(8,128)(2,1)S(1)}, u32[]{:S(2)}, u32[]{:S(2)}) collective-permute-start(bf16[2,1,1024,128]{3,2,1,0:T(8,128)(2,1)S(1)} %get-tuple-element.60.refs_0_), channel_id=1, source_target_pairs={{24,8},{28,12},{25,9},{29,13},{26,10},{30,14},{27,11},{31,15}} | collective-permute-start | bytes 1572872 | tf_op jit(solution)/shard_map/far_down_c1/ppermute | solution.py:695
  58.4 18.1 %collective-permute-start.12 = (bf16[2,1,2,1024,128]{4,3,2,1,0:T(8,128)(2,1)S(1)}, bf16[2,1,2,1024,128]{4,3,2,1,0:T(8,128)(2,1)S(1)}, u32[]{:S(2)}, u32[]{:S(2)}) collective-permute-start(bf16[2,1,2,1024,128]{4,3,2,1,0:T(8,128)(2,1)S(1)} %get-tuple-element.67), channel_id=1, source_target_pairs={{0,8},{4,12},{1,9},{5,13},{2,10},{6,14},{3,11},{7,15}} | collective-permute-start | bytes 3145736 | tf_op jit(solution)/shard_map/lift_c1/ppermute | solution.py:695
  61.2 18.0 %collective-permute-start.13 = (bf16[1,1056,256]{2,1,0:T(8,128)(2,1)S(1)}, bf16[1,1056,256]{2,1,0:T(8,128)(2,1)S(1)}, u32[]{:S(2)}, u32[]{:S(2)}) collective-permute-start(bf16[1,1056,256]{2,1,0:T(8,128)(2,1)S(1)} %get-tuple-element.62.refs_0_), channel_id=1, source_target_pairs={{8,16},{12,20},{16,24},{20,28},{9,17},{13,21},{17,25},{21,29},{10,... | collective-permute-start | bytes 1622024 | tf_op jit(solution)/shard_map/near_up_c0/ppermute | solution.py:695
  64.5 24.9 %collective-permute-start.14 = (bf16[1,1056,256]{2,1,0:T(8,128)(2,1)S(1)}, bf16[1,1056,256]{2,1,0:T(8,128)(2,1)S(1)}, u32[]{:S(2)}, u32[]{:S(2)}) collective-permute-start(bf16[1,1056,256]{2,1,0:T(8,128)(2,1)S(1)} %get-tuple-element.70), channel_id=1, source_target_pairs={{8,24},{12,28},{9,25},{13,29},{10,26},{14,30},{11,27},{15,31}} | collective-permute-start | bytes 1622024 | tf_op jit(solution)/shard_map/far_up_c0/ppermute | solution.py:695
  70.5 6.7 %copy-start.2 = (bf16[1,3,1024,128]{3,2,1,0:T(8,128)(2,1)S(1)}, bf16[1,3,1024,128]{3,2,1,0:T(8,128)(2,1)}, u32[]{:S(2)}) copy-start(bf16[1,3,1024,128]{3,2,1,0:T(8,128)(2,1)} %copy-done) | copy-start | bytes 2359300
  72.8 25.1 %collective-permute-start.16 = (bf16[2,1,1024,128]{3,2,1,0:T(8,128)(2,1)S(1)}, bf16[2,1,1024,128]{3,2,1,0:T(8,128)(2,1)S(1)}, u32[]{:S(2)}, u32[]{:S(2)}) collective-permute-start(bf16[2,1,1024,128]{3,2,1,0:T(8,128)(2,1)S(1)} %get-tuple-element.64.refs_0_), channel_id=1, source_target_pairs={{16,8},{20,12},{24,16},{28,20},{17,9},{21,13},{25,17},{29,21},{18,... | collective-permute-start | bytes 1572872 | tf_op jit(solution)/shard_map/near_down_c2/ppermute | solution.py:695
  76.0 20.2 %collective-permute-start.15 = (bf16[1,3,1024,128]{3,2,1,0:T(8,128)(2,1)S(1)}, bf16[1,3,1024,128]{3,2,1,0:T(8,128)(2,1)S(1)}, u32[]{:S(2)}, u32[]{:S(2)}) collective-permute-start(bf16[1,3,1024,128]{3,2,1,0:T(8,128)(2,1)S(1)} %get-tuple-element.73), channel_id=1, source_target_pairs={{0,4},{4,0},{8,12},{12,8},{16,20},{20,16},{24,28},{28,24},{1,5},{5... | collective-permute-start | bytes 2359304 | tf_op jit(solution)/shard_map/swap_c3/ppermute | solution.py:695
  76.5 23.6 %collective-permute-start.18 = (bf16[2,1,2,1024,128]{4,3,2,1,0:T(8,128)(2,1)S(1)}, bf16[2,1,2,1024,128]{4,3,2,1,0:T(8,128)(2,1)S(1)}, u32[]{:S(2)}, u32[]{:S(2)}) collective-permute-start(bf16[2,1,2,1024,128]{4,3,2,1,0:T(8,128)(2,1)S(1)} %get-tuple-element.75), channel_id=1, source_target_pairs={{0,8},{4,12},{1,9},{5,13},{2,10},{6,14},{3,11},{7,15}} | collective-permute-start | bytes 3145736 | tf_op jit(solution)/shard_map/lift_c2/ppermute | solution.py:695
  79.2 20.2 %collective-permute-start.17 = (bf16[2,1,1024,128]{3,2,1,0:T(8,128)(2,1)S(1)}, bf16[2,1,1024,128]{3,2,1,0:T(8,128)(2,1)S(1)}, u32[]{:S(2)}, u32[]{:S(2)}) collective-permute-start(bf16[2,1,1024,128]{3,2,1,0:T(8,128)(2,1)S(1)} %get-tuple-element.64.refs_0_), channel_id=1, source_target_pairs={{24,8},{28,12},{25,9},{29,13},{26,10},{30,14},{27,11},{31,15}} | collective-permute-start | bytes 1572872 | tf_op jit(solution)/shard_map/far_down_c2/ppermute | solution.py:695
  89.4 23.9 %collective-permute-start.19 = (bf16[1,1056,256]{2,1,0:T(8,128)(2,1)S(1)}, bf16[1,1056,256]{2,1,0:T(8,128)(2,1)S(1)}, u32[]{:S(2)}, u32[]{:S(2)}) collective-permute-start(bf16[1,1056,256]{2,1,0:T(8,128)(2,1)S(1)} %get-tuple-element.68.refs_0_), channel_id=1, source_target_pairs={{8,16},{12,20},{16,24},{20,28},{9,17},{13,21},{17,25},{21,29},{10,... | collective-permute-start | bytes 1622024 | tf_op jit(solution)/shard_map/near_up_c1/ppermute | solution.py:695
  96.1 8.0 %copy-start.7 = (bf16[1,3,1024,128]{3,2,1,0:T(8,128)(2,1)S(1)}, bf16[1,3,1024,128]{3,2,1,0:T(8,128)(2,1)}, u32[]{:S(2)}) copy-start(bf16[1,3,1024,128]{3,2,1,0:T(8,128)(2,1)} %copy-done.5) | copy-start | bytes 2359300
  96.1 18.4 %collective-permute-start.20 = (bf16[1,1056,256]{2,1,0:T(8,128)(2,1)S(1)}, bf16[1,1056,256]{2,1,0:T(8,128)(2,1)S(1)}, u32[]{:S(2)}, u32[]{:S(2)}) collective-permute-start(bf16[1,1056,256]{2,1,0:T(8,128)(2,1)S(1)} %get-tuple-element.79), channel_id=1, source_target_pairs={{8,24},{12,28},{9,25},{13,29},{10,26},{14,30},{11,27},{15,31}} | collective-permute-start | bytes 1622024 | tf_op jit(solution)/shard_map/far_up_c1/ppermute | solution.py:695
  97.9 22.8 %collective-permute-start.21 = (bf16[1,1024,128]{2,1,0:T(8,128)(2,1)S(1)}, bf16[1,1024,128]{2,1,0:T(8,128)(2,1)S(1)}, u32[]{:S(2)}, u32[]{:S(2)}) collective-permute-start(bf16[1,1024,128]{2,1,0:T(8,128)(2,1)S(1)} %get-tuple-element.82), channel_id=1, source_target_pairs={{0,4},{4,0},{8,12},{12,8},{16,20},{20,16},{24,28},{28,24},{1,5},{5... | collective-permute-start | bytes 786440 | tf_op jit(solution)/shard_map/back_c0/ppermute | solution.py:695
  99.4 22.7 %collective-permute-start.24 = (bf16[2,1,2,1024,128]{4,3,2,1,0:T(8,128)(2,1)S(1)}, bf16[2,1,2,1024,128]{4,3,2,1,0:T(8,128)(2,1)S(1)}, u32[]{:S(2)}, u32[]{:S(2)}) collective-permute-start(bf16[2,1,2,1024,128]{4,3,2,1,0:T(8,128)(2,1)S(1)} %get-tuple-element.83), channel_id=1, source_target_pairs={{0,8},{4,12},{1,9},{5,13},{2,10},{6,14},{3,11},{7,15}} | collective-permute-start | bytes 3145736 | tf_op jit(solution)/shard_map/lift_c3/ppermute | solution.py:695
  100.2 21.8 %collective-permute-start.22 = (bf16[2,1,1024,128]{3,2,1,0:T(8,128)(2,1)S(1)}, bf16[2,1,1024,128]{3,2,1,0:T(8,128)(2,1)S(1)}, u32[]{:S(2)}, u32[]{:S(2)}) collective-permute-start(bf16[2,1,1024,128]{3,2,1,0:T(8,128)(2,1)S(1)} %get-tuple-element.74.refs_0_), channel_id=1, source_target_pairs={{16,8},{20,12},{24,16},{28,20},{17,9},{21,13},{25,17},{29,21},{18,... | collective-permute-start | bytes 1572872 | tf_op jit(solution)/shard_map/near_down_c3/ppermute | solution.py:695
  113.2 8.8 %collective-permute-start.23 = (bf16[2,1,1024,128]{3,2,1,0:T(8,128)(2,1)S(1)}, bf16[2,1,1024,128]{3,2,1,0:T(8,128)(2,1)S(1)}, u32[]{:S(2)}, u32[]{:S(2)}) collective-permute-start(bf16[2,1,1024,128]{3,2,1,0:T(8,128)(2,1)S(1)} %get-tuple-element.74.refs_0_), channel_id=1, source_target_pairs={{24,8},{28,12},{25,9},{29,13},{26,10},{30,14},{27,11},{31,15}} | collective-permute-start | bytes 1572872 | tf_op jit(solution)/shard_map/far_down_c3/ppermute | solution.py:695
  114.6 24.9 %collective-permute-start.25 = (bf16[1,1056,256]{2,1,0:T(8,128)(2,1)S(1)}, bf16[1,1056,256]{2,1,0:T(8,128)(2,1)S(1)}, u32[]{:S(2)}, u32[]{:S(2)}) collective-permute-start(bf16[1,1056,256]{2,1,0:T(8,128)(2,1)S(1)} %get-tuple-element.76.refs_0_), channel_id=1, source_target_pairs={{8,16},{12,20},{16,24},{20,28},{9,17},{13,21},{17,25},{21,29},{10,... | collective-permute-start | bytes 1622024 | tf_op jit(solution)/shard_map/near_up_c2/ppermute | solution.py:695
  120.7 18.8 %collective-permute-start.26 = (bf16[1,1056,256]{2,1,0:T(8,128)(2,1)S(1)}, bf16[1,1056,256]{2,1,0:T(8,128)(2,1)S(1)}, u32[]{:S(2)}, u32[]{:S(2)}) collective-permute-start(bf16[1,1056,256]{2,1,0:T(8,128)(2,1)S(1)} %get-tuple-element.88), channel_id=1, source_target_pairs={{8,24},{12,28},{9,25},{13,29},{10,26},{14,30},{11,27},{15,31}} | collective-permute-start | bytes 1622024 | tf_op jit(solution)/shard_map/far_up_c2/ppermute | solution.py:695
  126.7 19.0 %collective-permute-start.28 = (bf16[1,528,256]{2,1,0:T(8,128)(2,1)S(1)}, bf16[1,528,256]{2,1,0:T(8,128)(2,1)S(1)}, u32[]{:S(2)}, u32[]{:S(2)}) collective-permute-start(bf16[1,528,256]{2,1,0:T(8,128)(2,1)S(1)} %get-tuple-element.92), channel_id=1, source_target_pairs={{0,4},{4,0},{8,12},{12,8},{16,20},{20,16},{24,28},{28,24},{1,5},{5... | collective-permute-start | bytes 811016 | tf_op jit(solution)/shard_map/back_own_c3/ppermute | solution.py:695
  128.9 19.0 %collective-permute-start.29 = (bf16[1,528,256]{2,1,0:T(8,128)(2,1)S(1)}, bf16[1,528,256]{2,1,0:T(8,128)(2,1)S(1)}, u32[]{:S(2)}, u32[]{:S(2)}) collective-permute-start(bf16[1,528,256]{2,1,0:T(8,128)(2,1)S(1)} %get-tuple-element.84.refs_0_), channel_id=1, source_target_pairs={{8,16},{12,20},{16,24},{20,28},{9,17},{13,21},{17,25},{21,29},{10,... | collective-permute-start | bytes 811016 | tf_op jit(solution)/shard_map/near_up_same_c3/ppermute | solution.py:695
  140.5 24.2 %copy-start.10 = (bf16[1024]{0:T(1024)(128)(2,1)S(1)}, bf16[1024]{0:T(1024)(128)(2,1)}, u32[]{:S(2)}) copy-start(bf16[1024]{0:T(1024)(128)(2,1)} %param.9) | copy-start | bytes 6148
  140.5 4.0 %collective-permute-start.27 = (f32[4,256]{1,0:T(4,128)S(1)}, f32[4,256]{1,0:T(4,128)S(1)}, u32[]{:S(2)}, u32[]{:S(2)}) collective-permute-start(f32[4,256]{1,0:T(4,128)S(1)} %slice.23), channel_id=1, source_target_pairs={{0,4},{4,0},{8,12},{12,8},{16,20},{20,16},{24,28},{28,24},{1,5},{5... | collective-permute-start | bytes 12296 | tf_op jit(solution)/shard_map/squares_swap/ppermute | solution.py:695
  141.9 19.0 %collective-permute-start.30 = (bf16[1,528,256]{2,1,0:T(8,128)(2,1)S(1)}, bf16[1,528,256]{2,1,0:T(8,128)(2,1)S(1)}, u32[]{:S(2)}, u32[]{:S(2)}) collective-permute-start(bf16[1,528,256]{2,1,0:T(8,128)(2,1)S(1)} %get-tuple-element.93), channel_id=1, source_target_pairs={{8,20},{12,16},{16,28},{20,24},{9,21},{13,17},{17,29},{21,25},{10,... | collective-permute-start | bytes 811016 | tf_op jit(solution)/shard_map/near_up_cross_c3/ppermute | solution.py:695
  143.2 17.7 %collective-permute-start.31 = (bf16[1,528,256]{2,1,0:T(8,128)(2,1)S(1)}, bf16[1,528,256]{2,1,0:T(8,128)(2,1)S(1)}, u32[]{:S(2)}, u32[]{:S(2)}) collective-permute-start(bf16[1,528,256]{2,1,0:T(8,128)(2,1)S(1)} %get-tuple-element.94), channel_id=1, source_target_pairs={{8,24},{12,28},{9,25},{13,29},{10,26},{14,30},{11,27},{15,31}} | collective-permute-start | bytes 811016 | tf_op jit(solution)/shard_map/far_up_same_c3/ppermute | solution.py:695
  144.5 16.4 %collective-permute-start.32 = (bf16[1,528,256]{2,1,0:T(8,128)(2,1)S(1)}, bf16[1,528,256]{2,1,0:T(8,128)(2,1)S(1)}, u32[]{:S(2)}, u32[]{:S(2)}) collective-permute-start(bf16[1,528,256]{2,1,0:T(8,128)(2,1)S(1)} %get-tuple-element.95), channel_id=1, source_target_pairs={{8,28},{12,24},{9,29},{13,25},{10,30},{14,26},{11,31},{15,27}} | collective-permute-start | bytes 811016 | tf_op jit(solution)/shard_map/far_up_cross_c3/ppermute | solution.py:695
  145.8 20.9 %collective-permute-start.33 = (bf16[1,1024,128]{2,1,0:T(8,128)(2,1)S(1)}, bf16[1,1024,128]{2,1,0:T(8,128)(2,1)S(1)}, u32[]{:S(2)}, u32[]{:S(2)}) collective-permute-start(bf16[1,1024,128]{2,1,0:T(8,128)(2,1)S(1)} %get-tuple-element.97), channel_id=1, source_target_pairs={{0,4},{4,0},{8,12},{12,8},{16,20},{20,16},{24,28},{28,24},{1,5},{5... | collective-permute-start | bytes 786440 | tf_op jit(solution)/shard_map/back_c1/ppermute | solution.py:695
  147.9 18.8 %collective-permute-start.34 = (bf16[1,1024,128]{2,1,0:T(8,128)(2,1)S(1)}, bf16[1,1024,128]{2,1,0:T(8,128)(2,1)S(1)}, u32[]{:S(2)}, u32[]{:S(2)}) collective-permute-start(bf16[1,1024,128]{2,1,0:T(8,128)(2,1)S(1)} %get-tuple-element.98), channel_id=1, source_target_pairs={{0,4},{4,0},{8,12},{12,8},{16,20},{20,16},{24,28},{28,24},{1,5},{5... | collective-permute-start | bytes 786440 | tf_op jit(solution)/shard_map/back_c2/ppermute | solution.py:695
  161.9 1.2 collective-permute-start.35
  163.1 3.6 %collective-permute-start.36 = (f32[4,256]{1,0:T(4,128)S(1)}, f32[4,256]{1,0:T(4,128)S(1)}, u32[]{:S(2)}, u32[]{:S(2)}) collective-permute-start(f32[4,256]{1,0:T(4,128)S(1)} %add.296), channel_id=1, source_target_pairs={{0,2},{1,3},{2,0},{3,1},{4,6},{5,7},{6,4},{7,5},{8,10},{9,11},{10,... | collective-permute-start | bytes 12296 | tf_op jit(solution)/shard_map/ppermute | solution.py:877

commit v8 on v7

--- a/solution.py
+++ b/solution.py
@@ -133,10 +133,11 @@
 ORDER = (
     ("p", 0),
     ("w", "plan"),
+    ("p", 1),
     ("w", "near_down_keep_c0"),
     ("w", "far_down_keep_c0"),
     ("w", "lift_keep_c0"),
-    ("p", 1),
+    ("w", "served"),
     ("j", 0),
     ("p", 2),
     ("j", 1),
@@ -161,7 +162,7 @@
 DIRECT = True
 NOTE_ROWS = 16
 UNROLL = 2
-VMEM_LIMIT = 16 * 1024 * 1024
+VMEM_LIMIT = 10 * 1024 * 1024
 
 
 def unit_fields(code):
@@ -174,7 +175,6 @@
 
 PIECES = {
     "head": lambda ref, h, rows: ref.at[h],
-    "next head": lambda ref, h, rows: ref.at[h + 1],
     "top rows": lambda ref, h, rows: ref.at[h, pl.ds(0, rows)],
     "queries": lambda ref, h, rows: ref.at[h, 0],
     "keys_values": lambda ref, h, rows: ref.at[h, pl.ds(1, 2)],
@@ -373,96 +373,81 @@
 
 
 def pack_kernel(shape, place, q_ref, k_ref, v_ref, *refs):
-    heads, first, half, rows, split, scatter = shape
-    outs, (scr, t_scr, sems) = refs[:-3], refs[-3:]
+    sides, head, half, rows, noted = shape
+    n_out = len(sides) + noted
+    note_ref, refs = (refs[0], refs[1:]) if noted else (None, refs)
+    outs, (scr, t_scr, note_scr, sems) = refs[:n_out], refs[n_out:]
     loads, stores = {}, []
-    places = [(side, h) for h in range(heads) for side in (1, 0)]
-    for side, h in places:
-        start = pl.multiple_of((place[side] * half + first + h) * HD, HD)
+    for side in sides:
+        start = pl.multiple_of((place[side] * half + head) * HD, HD)
         for i, ref in enumerate((q_ref, k_ref, v_ref)):
-            loads[side, h, i] = pltpu.make_async_copy(
-                ref.at[:, pl.ds(start, HD)], scr.at[side, h, i], sems.at[0, side, h, i]
+            loads[side, i] = pltpu.make_async_copy(
+                ref.at[:, pl.ds(start, HD)], scr.at[side, i], sems.at[0, side, i]
             )
-            loads[side, h, i].start()
-
-    if scatter:
-        for h in range(heads):
-            t_scr[0, h] = jnp.zeros_like(t_scr[0, h])
-            for i in range(3):
-                blank = pltpu.make_async_copy(
-                    t_scr.at[0, h], outs[-heads + h].at[place[0], i], sems.at[2, 0, h, i]
-                )
-                blank.start()
-                blank.wait()
-
-    def store(side, h, i, source):
-        if side:
-            target = outs[-heads + h].at[place[1] if scatter else 0, i]
-        elif split:
-            target = outs[1].at[h, i - 1] if i else outs[0].at[h]
-        else:
-            target = outs[0].at[h, i]
-        copy = pltpu.make_async_copy(source, target, sems.at[1, side, h, i])
+            loads[side, i].start()
+
+    def store(source, target, side, i):
+        copy = pltpu.make_async_copy(source, target, sems.at[1, side, i])
         copy.start()
         stores.append(copy)
 
-    for side, h in places:
+    if noted:
+        load = pltpu.make_async_copy(note_ref, note_scr, sems.at[0, 0, 3])
+        load.start()
+        load.wait()
+        store(note_scr, outs[0].at[0, pl.ds(rows, NOTE_ROWS)], 0, 3)
+    for side, out in zip(sides, outs[noted:]):
+        targets = [out.at[0, i] for i in range(3)]
+        if noted:
+            targets = [outs[0].at[0, pl.ds(0, rows)], out.at[0, 0], out.at[0, 1]]
         for i in range(2):
-            loads[side, h, i].wait()
-            store(side, h, i, scr.at[side, h, i])
-        loads[side, h, 2].wait()
+            loads[side, i].wait()
+            store(scr.at[side, i], targets[i], side, i)
+        loads[side, 2].wait()
         for tile in range(rows // HD):
             at = slice(tile * HD, (tile + 1) * HD)
-            t_scr[side, h, at, :] = scr[side, h, 2, at, :].T
-        store(side, h, 2, t_scr.at[side, h])
+            t_scr[side, at, :] = scr[side, 2, at, :].T
+        store(t_scr.at[side], targets[2], side, 2)
     for copy in stores:
         copy.wait()
 
 
-def pack_call(place, queries, keys, values, heads, first, half, split, scatter, after=()):
+def pack_call(place, queries, keys, values, head, half, sides=(1, 0), note=None, after=()):
     rows = queries.shape[0]
     hbm = pl.BlockSpec(memory_space=pltpu.HBM)
     bf16 = jnp.bfloat16
     queries, keys, values = (
         pltpu.with_memory_space_constraint(array, pltpu.HBM) for array in (queries, keys, values)
     )
-    if split:
-        outs = [
-            jax.ShapeDtypeStruct((heads, rows, HD), bf16),
-            jax.ShapeDtypeStruct((heads, 2, rows, HD), bf16),
-        ]
+    noted = note is not None
+    if noted:
+        shapes, notes = [(1, rows + NOTE_ROWS, HD), (1, 2, rows, HD)], [note]
     else:
-        outs = [jax.ShapeDtypeStruct((heads, 3, rows, HD), bf16)]
-    outs += [jax.ShapeDtypeStruct((2 if scatter else 1, 3, rows, HD), bf16)] * heads
+        shapes, notes = [(1, 3, rows, HD)] * len(sides), []
     return pl.pallas_call(
-        ordered(partial(pack_kernel, (heads, first, half, rows, split, scatter)), len(after)),
-        out_shape=outs,
-        in_specs=[hbm] * len(after) + [pl.BlockSpec(memory_space=pltpu.SMEM)] + [hbm] * 3,
-        out_specs=[hbm] * len(outs),
+        ordered(partial(pack_kernel, (sides, head, half, rows, noted)), len(after)),
+        out_shape=[jax.ShapeDtypeStruct(shape, bf16) for shape in shapes],
+        in_specs=[hbm] * len(after) + [pl.BlockSpec(memory_space=pltpu.SMEM)] + [hbm] * (3 + noted),
+        out_specs=[hbm] * len(shapes),
         scratch_shapes=[
-            pltpu.VMEM((2, heads, 3, rows, HD), bf16),
-            pltpu.VMEM((2, heads, rows, HD), bf16),
-            pltpu.SemaphoreType.DMA((3, 2, heads, 3)),
+            pltpu.VMEM((2, 3, rows, HD), bf16),
+            pltpu.VMEM((2, rows, HD), bf16),
+            pltpu.VMEM((NOTE_ROWS, HD), bf16),
+            pltpu.SemaphoreType.DMA((2, 2, 4)),
         ],
         compiler_params=pltpu.CompilerParams(vmem_limit_bytes=VMEM_LIMIT),
         cost_estimate=cost("pack"),
         name="pack",
-    )(*after, place, queries, keys, values)
-
-
-def cut_kernel(rows, note_ref, ref, q_ref, kv_ref, scr, note_scr, sems):
-    loads = [
-        pltpu.make_async_copy(ref, scr, sems.at[0]),
-        pltpu.make_async_copy(note_ref, note_scr, sems.at[1]),
-    ]
-    for load in loads:
-        load.start()
-    for load in loads:
-        load.wait()
+    )(*after, place, queries, keys, values, *notes)
+
+
+def cut_kernel(ref, q_ref, kv_ref, scr, sems):
+    load = pltpu.make_async_copy(ref, scr, sems.at[0])
+    load.start()
+    load.wait()
     stores = [
-        pltpu.make_async_copy(scr.at[0, 0], q_ref.at[0, pl.ds(0, rows)], sems.at[2]),
-        pltpu.make_async_copy(note_scr, q_ref.at[0, pl.ds(rows, NOTE_ROWS)], sems.at[3]),
-        pltpu.make_async_copy(scr.at[0, pl.ds(1, 2)], kv_ref.at[0], sems.at[4]),
+        pltpu.make_async_copy(scr.at[0, 0], q_ref.at[0], sems.at[1]),
+        pltpu.make_async_copy(scr.at[0, pl.ds(1, 2)], kv_ref.at[0], sems.at[2]),
     ]
     for store in stores:
         store.start()
@@ -470,26 +455,25 @@
         store.wait()
 
 
-def cut_call(packed, note, after=()):
+def cut_call(packed, after=()):
     _, _, rows, _ = packed.shape
     hbm = pl.BlockSpec(memory_space=pltpu.HBM)
     return pl.pallas_call(
-        ordered(partial(cut_kernel, rows), len(after)),
+        ordered(cut_kernel, len(after)),
         out_shape=(
-            jax.ShapeDtypeStruct((1, rows + NOTE_ROWS, HD), jnp.bfloat16),
+            jax.ShapeDtypeStruct((1, rows, HD), jnp.bfloat16),
             jax.ShapeDtypeStruct((1, 2, rows, HD), jnp.bfloat16),
         ),
-        in_specs=[hbm] * (len(after) + 2),
+        in_specs=[hbm] * (len(after) + 1),
         out_specs=(hbm, hbm),
         scratch_shapes=[
             pltpu.VMEM(packed.shape, jnp.bfloat16),
-            pltpu.VMEM((NOTE_ROWS, HD), jnp.bfloat16),
-            pltpu.SemaphoreType.DMA((5,)),
+            pltpu.SemaphoreType.DMA((3,)),
         ],
         compiler_params=pltpu.CompilerParams(vmem_limit_bytes=VMEM_LIMIT),
         cost_estimate=cost("join"),
         name="join",
-    )(*after, note, packed)
+    )(*after, packed)
 
 
 def join_kernel(heads, keep_ref, swap_ref, q_ref, kv_ref, scr, sems):
@@ -759,27 +743,25 @@
         far = to(q, far_down, f"far_down_{name}")
         return to(q, near_down, f"near_down_{name}"), far, low
 
-    def pack(*chunks):
-        c = chunks[0]
-        packed = pack_call(
-            place, queries, keys, values, len(chunks), c, half, split[c], SCATTER[c], last
-        )
-        last[:] = [packed[0]]
-        if SCATTER[c]:
-            swapped = [exchange(p, f"swap_c{d}") for d, p in zip(chunks, packed[-len(chunks) :])]
+    def pack(c):
+        if split[c]:
+            (send,) = pack_call(place, queries, keys, values, c, half, (1,), None, last)
+            swapped = to(send, swap, f"swap_c{c}")
+            q_keep, kv_keep = pack_call(
+                place, queries, keys, values, c, half, (0,), note, (*last, send)
+            )
+            last[:] = [q_keep]
+            downs_of[c] = downs(q_keep, kv_keep, f"keep_c{c}")
+            served_plan.append(served_lists(*downs_of[c][:2]))
+            z_arrays[c] = (swapped,)
+            own_pieces[c] = (
+                [(q_keep, "top rows"), (swapped, "queries")],
+                [(kv_keep, "head"), (swapped, "keys_values")],
+            )
         else:
-            swapped = [to(p, swap, f"swap_c{d}") for d, p in zip(chunks, packed[-len(chunks) :])]
-        if split[c]:
-            keeps = downs(packed[0], packed[1], f"keep_c{c}")
-            for d, kind, swap_d in zip(chunks, ("head", "next head"), swapped):
-                downs_of[d] = [(array, kind) for array in keeps]
-                z_arrays[d] = (swap_d,)
-                own_pieces[d] = (
-                    [(packed[0], kind), (swap_d, "queries")],
-                    [(packed[1], kind), (swap_d, "keys_values")],
-                )
-        else:
-            z_arrays[c] = (packed[0], swapped[0])
+            send, keep = pack_call(place, queries, keys, values, c, half, (1, 0), None, last)
+            last[:] = [keep]
+            z_arrays[c] = (keep, to(send, swap, f"swap_c{c}"))
             own_pieces[c] = (
                 [(array, "queries") for array in z_arrays[c]],
                 [(array, "keys_values") for array in z_arrays[c]],
@@ -787,13 +769,11 @@
 
     def join(c):
         if split[c]:
-            q_swap, kv_swap = cut_call(*z_arrays[c], note, last)
+            q_swap, kv_swap = cut_call(*z_arrays[c], last)
             last[:] = [q_swap]
             swaps = downs(q_swap, kv_swap, f"recv_c{c}")
-            if not served_plan:
-                served_plan.append(served_lists(*swaps[:2]))
             near, far, low = [
-                [k, (r, kind)]
+                [(k, kind), (r, "head")]
                 for k, r, kind in zip(downs_of[c], swaps, ("top rows", "top rows", "head"))
             ]
         else:
@@ -865,7 +845,8 @@
     steps = {"p": pack, "j": join, "s": serve, "a": attend, "m": merge}
     for what, *args in order:
         if what == "w":
-            last.append(own_plan if args[0] == "plan" else sent[args[0]])
+            tokens = {"plan": own_plan, "served": served_plan and served_plan[0], **sent}
+            last.append(tokens[args[0]])
         else:
             steps[what](*args)
     square = squares[0]

time: 171 us -> 167 us (0.977)
  waiting for transfers between devices: 56.7 us -> 41.8 us
  starting transfers between devices: 60.2 us -> 69.2 us
  local copies, waits for them, and re-layouts: 4.24 us -> 6.26 us
    ppermute x35, waiting for transfers between devices: 53.5 us -> 38.6 us  [to(): sent[name] = lax.ppermute(array, 'ctx', pairs)]
    ppermute x35, starting transfers between devices: 58.6 us -> 67.7 us  [to(): sent[name] = lax.ppermute(array, 'ctx', pairs)]
    pallas_call x5 -> x6, Pallas kernels: 10.8 us -> 12.8 us  [the longest x5 11.8 us: pack_call(): pl.pallas_call(ordered(partial(pack_kernel, (sides, head, half, rows, not...]
    unnamed x22 -> x20, local copies, waits for them, and re-layouts: 3.18 us -> 5.2 us
  transfers between devices with their start and end apart: 37 -> 37, of which waited for: 13 -> 11; matrix products, arithmetic and copies ran while one was open for 3% -> 3% of each run, Pallas kernels for 21% -> 23%
where the time goes in v8:
time: 167 us; the launch traced here: 165 us
  starting transfers between devices  69.2 us (41%)
  waiting for transfers between devices  41.8 us (25%)
  Pallas kernels  41.4 us (25%)
  local copies, waits for them, and re-layouts  6.26 us (4%)
  other arithmetic  3.45 us (2%)
  between operations  3.32 us (2%)
    ppermute x35, starting transfers between devices, to(): sent[name] = lax.ppermute(array, 'ctx', pairs)  67.7 us
    ppermute x35, waiting for transfers between devices, to(): sent[name] = lax.ppermute(array, 'ctx', pairs)  38.6 us
    pallas_call x8, Pallas kernels, attention_call(): pl.pallas_call(ordered(partial(attention_kernel, (heads, per_dev, block_r...  20.8 us
    pallas_call x5, Pallas kernels, pack_call(): pl.pallas_call(ordered(partial(pack_kernel, (sides, head, half, rows, not...  11.8 us
    unnamed x20, local copies, waits for them, and re-layouts  5.2 us
  transfers between devices with their start and end apart: 37, of which 11 were waited for; matrix products, arithmetic and copies ran while one was open for 3% of the time, Pallas kernels for 23%

profile of v8, /device:TPU:24, one launch (start us, length us, event | category | flops | bytes accessed | tf_op | source)
XLA Modules:
  0.0 165.4 jit_solution(15827965564852321287)
XLA Ops:
  0.0 1.5 collective-permute-start
  1.6 2.0 %pack.5.refs_0_ = bf16[1,3,1024,128]{3,2,1,0:T(8,128)(2,1)S(1)} custom-call(s32[2]{0:T(128)S(1)} %pad_add_fusion.2.refs_0_.refs_1_.refs_2_.place, bf16[1024,1024]{1,0:T(8,128)(2,1)} %refs_2_.7, bf16[1024,1024]{1,0:T(8,128)(2,1)} %refs_3_.9, bf16[1024,1024]{1,0:T(8,128)(2,1)} %refs_4_.7), custom_call_target="tpu_custom_call" | custom-call | flops 2000000000 | bytes 6800001 | tf_op jit(solution)/shard_map/pack/pallas_call | solution.py:427
  5.0 2.4 %pack.6 = (bf16[1,1040,128]{2,1,0:T(8,128)(2,1)}, bf16[1,2,1024,128]{3,2,1,0:T(8,128)(2,1)S(1)}) custom-call(bf16[1,3,1024,128]{3,2,1,0:T(8,128)(2,1)S(1)} %pack.5.refs_0_, s32[2]{0:T(128)S(1)} %pad_add_fusion.2.refs_0_.refs_1_.refs_2_.place, bf16[1024,1024]{1,0:T(8,128)(2,1)} %refs_2_.7, bf16[1024,1024]{1,0:T(8,128)(2,1)} %refs_3_.9, ...), custom_call_target="tpu_custom_call" | custom-call | flops 2000000000 | bytes 6800001 | tf_op jit(solution)/shard_map/pack/pallas_call | solution.py:427
  7.4 2.4 %collective-permute-start.1 = (bf16[1,1040,128]{2,1,0:T(8,128)(2,1)}, bf16[1,1040,128]{2,1,0:T(8,128)(2,1)S(1)}, u32[]{:S(2)}, u32[]{:S(2)}) collective-permute-start(bf16[1,1040,128]{2,1,0:T(8,128)(2,1)} %get-tuple-element.52.refs_0_.refs_2_), channel_id=1, source_target_pairs={{16,8},{20,12},{24,16},{28,20},{17,9},{21,13},{25,17},{29,21},{18,... | collective-permute-start | bytes 798728 | tf_op jit(solution)/shard_map/near_down_keep_c0/ppermute | solution.py:679
  9.7 1.3 collective-permute-start.2
  14.2 2.6 %pack.7 = (bf16[1,3,1024,128]{3,2,1,0:T(8,128)(2,1)}, bf16[1,3,1024,128]{3,2,1,0:T(8,128)(2,1)S(1)}) custom-call(bf16[1,1040,128]{2,1,0:T(8,128)(2,1)} %get-tuple-element.52.refs_0_.refs_2_, s32[81]{0:T(128)S(1)} %pad_add_fusion.4.refs_1_, s32[2]{0:T(128)S(1)} %pad_add_fusion.2.refs_0_.refs_1_.refs_2_.place, bf16[1024,1024]{1,0:T(8,128)(2,1)} %refs_2_.7, ...), custom_call_target="tpu_custom_call" | custom-call | flops 2000000000 | bytes 6800001 | tf_op jit(solution)/shard_map/pack/pallas_call | solution.py:427
  17.7 1.4 collective-permute-start.3
  19.2 1.5 collective-permute-start.5
  24.1 1.1 copy-done.1
  26.2 1.5 collective-permute-start.8
  27.7 3.1 %collective-permute-start.6 = (bf16[1,1024,128]{2,1,0:T(8,128)(2,1)}, bf16[1,1024,128]{2,1,0:T(8,128)(2,1)}, u32[]{:S(2)}, u32[]{:S(2)}) collective-permute-start(bf16[1,1024,128]{2,1,0:T(8,128)(2,1)} %get-tuple-element.55.refs_0_), channel_id=1, source_target_pairs={{16,8},{20,12},{24,16},{28,20},{17,9},{21,13},{25,17},{29,21},{18,... | collective-permute-start | bytes 786440 | tf_op jit(solution)/shard_map/near_down_recv_c0/ppermute | solution.py:679
  30.7 8.7 %collective-permute-start.7 = (bf16[1,1024,128]{2,1,0:T(8,128)(2,1)}, bf16[1,1024,128]{2,1,0:T(8,128)(2,1)}, u32[]{:S(2)}, u32[]{:S(2)}) collective-permute-start(bf16[1,1024,128]{2,1,0:T(8,128)(2,1)} %get-tuple-element.55.refs_0_), channel_id=1, source_target_pairs={{24,8},{28,12},{25,9},{29,13},{26,10},{30,14},{27,11},{31,15}} | collective-permute-start | bytes 786440 | tf_op jit(solution)/shard_map/far_down_recv_c0/ppermute | solution.py:679
  39.4 2.7 %pack.8 = (bf16[1,3,1024,128]{3,2,1,0:T(8,128)(2,1)}, bf16[1,3,1024,128]{3,2,1,0:T(8,128)(2,1)S(1)}) custom-call(bf16[1,1024,128]{2,1,0:T(8,128)(2,1)} %get-tuple-element.55.refs_0_, s32[2]{0:T(128)S(1)} %pad_add_fusion.2.refs_0_.refs_1_.refs_2_.place, bf16[1024,1024]{1,0:T(8,128)(2,1)} %refs_2_.7, bf16[1024,1024]{1,0:T(8,128)(2,1)} %refs_3_.9, ...), custom_call_target="tpu_custom_call" | custom-call | flops 2000000000 | bytes 6800001 | tf_op jit(solution)/shard_map/pack/pallas_call | solution.py:427
  43.0 1.5 collective-permute-start.9
  44.6 1.1 copy-done.2
  47.1 1.9 %collective-permute-start.10 = (bf16[2,1,1024,128]{3,2,1,0:T(8,128)(2,1)S(1)}, bf16[2,1,1024,128]{3,2,1,0:T(8,128)(2,1)S(1)}, u32[]{:S(2)}, u32[]{:S(2)}) collective-permute-start(bf16[2,1,1024,128]{3,2,1,0:T(8,128)(2,1)S(1)} %get-tuple-element.58.refs_0_), channel_id=1, source_target_pairs={{16,8},{20,12},{24,16},{28,20},{17,9},{21,13},{25,17},{29,21},{18,... | collective-permute-start | bytes 1572872 | tf_op jit(solution)/shard_map/near_down_c1/ppermute | solution.py:679
  49.0 3.4 %collective-permute-start.11 = (bf16[2,1,1024,128]{3,2,1,0:T(8,128)(2,1)S(1)}, bf16[2,1,1024,128]{3,2,1,0:T(8,128)(2,1)S(1)}, u32[]{:S(2)}, u32[]{:S(2)}) collective-permute-start(bf16[2,1,1024,128]{3,2,1,0:T(8,128)(2,1)S(1)} %get-tuple-element.58.refs_0_), channel_id=1, source_target_pairs={{24,8},{28,12},{25,9},{29,13},{26,10},{30,14},{27,11},{31,15}} | collective-permute-start | bytes 1572872 | tf_op jit(solution)/shard_map/far_down_c1/ppermute | solution.py:679
  53.3 2.2 %served_attention.4 = (bf16[1,1056,256]{2,1,0:T(8,128)(2,1)S(1)}, bf16[1,1056,256]{2,1,0:T(8,128)(2,1)S(1)}) custom-call(bf16[2,1,1024,128]{3,2,1,0:T(8,128)(2,1)S(1)} %get-tuple-element.58.refs_0_, s32[129]{0:T(256)S(1)} %pad_add_fusion.1.refs_4_.refs_1_.refs_2_, bf16[1,1040,128]{2,1,0:T(8,128)(2,1)S(1)} %collective-permute-done.1.refs_1_.refs_2_, ...), custom_call_target="tpu_custom_call" | custom-call | flops 6000000000 | bytes 20400000 | tf_op jit(solution)/shard_map/served_attention/pallas_call | solution.py:352
  55.5 1.3 collective-permute-start.13
  56.8 3.9 %collective-permute-done.9.refs_2_.refs_5_.refs_3_ = bf16[1,3,1024,128]{3,2,1,0:T(8,128)(2,1)S(1)} collective-permute-done((bf16[1,3,1024,128]{3,2,1,0:T(8,128)(2,1)}, bf16[1,3,1024,128]{3,2,1,0:T(8,128)(2,1)S(1)}, u32[]{:S(2)}, u32[]{:S(2)}) %collective-permute-start.9) | collective-permute-done | bytes 786464 | tf_op jit(solution)/shard_map/swap_c2/ppermute | solution.py:679
  60.7 1.3 collective-permute-start.14
  62.3 4.6 %own_attention.4 = (f32[1,8,128,256]{3,2,1,0:T(8,128)S(1)}, f32[1,8,256]{2,1,0:T(8,128)S(1)}) custom-call(bf16[2,1,1024,128]{3,2,1,0:T(8,128)(2,1)S(1)} %get-tuple-element.62.refs_0_, s32[81]{0:T(128)S(1)} %pad_add_fusion.4.refs_1_, bf16[1,1040,128]{2,1,0:T(8,128)(2,1)} %get-tuple-element.52.refs_0_.refs_2_, ...), custom_call_target="tpu_custom_call" | custom-call | flops 5000000000 | bytes 17000000 | tf_op jit(solution)/shard_map/own_attention/pallas_call | solution.py:352
  66.9 2.2 %pack.9 = (bf16[1,3,1024,128]{3,2,1,0:T(8,128)(2,1)S(1)}, bf16[1,3,1024,128]{3,2,1,0:T(8,128)(2,1)S(1)}) custom-call(f32[1,8,256]{2,1,0:T(8,128)S(1)} %get-tuple-element.63.refs_0_.refs_4_, s32[2]{0:T(128)S(1)} %pad_add_fusion.2.refs_0_.refs_1_.refs_2_.place, bf16[1024,1024]{1,0:T(8,128)(2,1)} %refs_2_.7, bf16[1024,1024]{1,0:T(8,128)(2,1)} %refs_3_.9, ...), custom_call_target="tpu_custom_call" | custom-call | flops 2000000000 | bytes 6800001 | tf_op jit(solution)/shard_map/pack/pallas_call | solution.py:427
  69.2 1.3 collective-permute-start.16
  70.6 3.2 %collective-permute-start.15 = (bf16[1,3,1024,128]{3,2,1,0:T(8,128)(2,1)S(1)}, bf16[1,3,1024,128]{3,2,1,0:T(8,128)(2,1)S(1)}, u32[]{:S(2)}, u32[]{:S(2)}) collective-permute-start(bf16[1,3,1024,128]{3,2,1,0:T(8,128)(2,1)S(1)} %get-tuple-element.71), channel_id=1, source_target_pairs={{0,4},{4,0},{8,12},{12,8},{16,20},{20,16},{24,28},{28,24},{1,5},{5... | collective-permute-start | bytes 2359304 | tf_op jit(solution)/shard_map/swap_c3/ppermute | solution.py:679
  75.6 9.6 %collective-permute-start.17 = (bf16[2,1,1024,128]{3,2,1,0:T(8,128)(2,1)S(1)}, bf16[2,1,1024,128]{3,2,1,0:T(8,128)(2,1)S(1)}, u32[]{:S(2)}, u32[]{:S(2)}) collective-permute-start(bf16[2,1,1024,128]{3,2,1,0:T(8,128)(2,1)S(1)} %get-tuple-element.62.refs_0_), channel_id=1, source_target_pairs={{24,8},{28,12},{25,9},{29,13},{26,10},{30,14},{27,11},{31,15}} | collective-permute-start | bytes 1572872 | tf_op jit(solution)/shard_map/far_down_c2/ppermute | solution.py:679
  85.2 1.3 collective-permute-start.19
  87.5 3.6 %own_attention.5 = (f32[1,8,128,256]{3,2,1,0:T(8,128)S(1)}, f32[1,8,256]{2,1,0:T(8,128)S(1)}) custom-call(bf16[1,1024,128]{2,1,0:T(8,128)(2,1)S(1)} %get-tuple-element.69.refs_0_, s32[81]{0:T(128)S(1)} %pad_add_fusion.4.refs_1_, bf16[1,3,1024,128]{3,2,1,0:T(8,128)(2,1)S(1)} %copy-done.3, ...), custom_call_target="tpu_custom_call" | custom-call | flops 5000000000 | bytes 17000000 | tf_op jit(solution)/shard_map/own_attention/pallas_call | solution.py:352
  91.1 1.3 collective-permute-start.20
  94.4 5.4 %collective-permute-start.22 = (bf16[2,1,1024,128]{3,2,1,0:T(8,128)(2,1)S(1)}, bf16[2,1,1024,128]{3,2,1,0:T(8,128)(2,1)S(1)}, u32[]{:S(2)}, u32[]{:S(2)}) collective-permute-start(bf16[2,1,1024,128]{3,2,1,0:T(8,128)(2,1)S(1)} %get-tuple-element.72.refs_0_), channel_id=1, source_target_pairs={{16,8},{20,12},{24,16},{28,20},{17,9},{21,13},{25,17},{29,21},{18,... | collective-permute-start | bytes 1572872 | tf_op jit(solution)/shard_map/near_down_c3/ppermute | solution.py:679
  100.9 8.8 %collective-permute-done.19.refs_5_ = bf16[1,1056,256]{2,1,0:T(8,128)(2,1)S(1)} collective-permute-done((bf16[1,1056,256]{2,1,0:T(8,128)(2,1)S(1)}, bf16[1,1056,256]{2,1,0:T(8,128)(2,1)S(1)}, u32[]{:S(2)}, u32[]{:S(2)}) %collective-permute-start.19) | collective-permute-done | bytes 540704 | tf_op jit(solution)/shard_map/near_up_c1/ppermute | solution.py:679
  109.7 2.0 %collective-permute-start.23 = (bf16[2,1,1024,128]{3,2,1,0:T(8,128)(2,1)S(1)}, bf16[2,1,1024,128]{3,2,1,0:T(8,128)(2,1)S(1)}, u32[]{:S(2)}, u32[]{:S(2)}) collective-permute-start(bf16[2,1,1024,128]{3,2,1,0:T(8,128)(2,1)S(1)} %get-tuple-element.72.refs_0_), channel_id=1, source_target_pairs={{24,8},{28,12},{25,9},{29,13},{26,10},{30,14},{27,11},{31,15}} | collective-permute-start | bytes 1572872 | tf_op jit(solution)/shard_map/far_down_c3/ppermute | solution.py:679
  111.7 1.3 collective-permute-start.25
  114.0 3.7 %own_attention.6 = (f32[1,8,128,256]{3,2,1,0:T(8,128)S(1)}, f32[1,8,256]{2,1,0:T(8,128)S(1)}) custom-call(bf16[1,1024,128]{2,1,0:T(8,128)(2,1)S(1)} %get-tuple-element.78.refs_0_.refs_1_, s32[81]{0:T(128)S(1)} %pad_add_fusion.4.refs_1_, bf16[1,3,1024,128]{3,2,1,0:T(8,128)(2,1)S(1)} %copy-done.6, ...), custom_call_target="tpu_custom_call" | custom-call | flops 5000000000 | bytes 17000000 | tf_op jit(solution)/shard_map/own_attention/pallas_call | solution.py:352
  117.8 1.3 collective-permute-start.26
  120.2 3.6 %own_attention.7 = (f32[1,4,128,256]{3,2,1,0:T(8,128)S(1)}, f32[1,4,256]{2,1,0:T(4,128)S(1)}, bf16[1,528,256]{2,1,0:T(8,128)(2,1)S(1)}) custom-call(bf16[1,528,256]{2,1,0:T(8,128)(2,1)S(1)} %get-tuple-element.82.refs_0_, s32[81]{0:T(128)S(1)} %pad_add_fusion.4.refs_1_, bf16[1,3,1024,128]{3,2,1,0:T(8,128)(2,1)S(1)} %get-tuple-element.64.refs_0_.refs_1_.refs_5_.refs_2_, ...), custom_call_target="tpu_custom_call" | custom-call | flops 5000000000 | bytes 17000000 | tf_op jit(solution)/shard_map/own_attention/pallas_call | solution.py:352
  124.0 1.3 collective-permute-start.29
  125.3 11.6 %collective-permute-done.25.refs_5_ = bf16[1,1056,256]{2,1,0:T(8,128)(2,1)S(1)} collective-permute-done((bf16[1,1056,256]{2,1,0:T(8,128)(2,1)S(1)}, bf16[1,1056,256]{2,1,0:T(8,128)(2,1)S(1)}, u32[]{:S(2)}, u32[]{:S(2)}) %collective-permute-start.25) | collective-permute-done | bytes 540704 | tf_op jit(solution)/shard_map/near_up_c2/ppermute | solution.py:679
  138.1 1.3 collective-permute-start.30
  139.4 1.3 collective-permute-start.31
  140.7 1.1 collective-permute-done.27.refs_3_
  141.8 1.3 collective-permute-start.32
  144.1 2.8 %collective-permute-done.29.refs_7_ = bf16[1,528,256]{2,1,0:T(8,128)(2,1)S(1)} collective-permute-done((bf16[1,528,256]{2,1,0:T(8,128)(2,1)S(1)}, bf16[1,528,256]{2,1,0:T(8,128)(2,1)S(1)}, u32[]{:S(2)}, u32[]{:S(2)}) %collective-permute-start.29) | collective-permute-done | bytes 270368 | tf_op jit(solution)/shard_map/near_up_same_c3/ppermute | solution.py:679
  146.9 9.8 %collective-permute-done.30.refs_8_ = bf16[1,528,256]{2,1,0:T(8,128)(2,1)S(1)} collective-permute-done((bf16[1,528,256]{2,1,0:T(8,128)(2,1)S(1)}, bf16[1,528,256]{2,1,0:T(8,128)(2,1)S(1)}, u32[]{:S(2)}, u32[]{:S(2)}) %collective-permute-start.30) | collective-permute-done | bytes 270368 | tf_op jit(solution)/shard_map/near_up_cross_c3/ppermute | solution.py:679
  157.8 1.2 collective-permute-done.35
  159.0 1.5 collective-permute-start.36
  160.5 2.1 %collective-permute-done.36 = f32[4,256]{1,0:T(4,128)S(1)} collective-permute-done((f32[4,256]{1,0:T(4,128)S(1)}, f32[4,256]{1,0:T(4,128)S(1)}, u32[]{:S(2)}, u32[]{:S(2)}) %collective-permute-start.36) | collective-permute-done | bytes 4128 | tf_op jit(solution)/shard_map/ppermute | solution.py:858
  162.6 2.8 %finish.1 = bf16[1024,1024]{1,0:T(8,128)(2,1)} custom-call(s32[2]{0:T(128)S(1)} %pad_add_fusion.2.refs_0_.refs_1_.refs_2_.place, bf16[1,1024,128]{2,1,0:T(8,128)(2,1)S(1)} %get-tuple-element.69.refs_0_, bf16[1,1024,128]{2,1,0:T(8,128)(2,1)S(1)} %get-tuple-element.78.refs_0_.refs_1_, bf16[1,1024,128]{2,1,0:T(8,128)(2,1)S(1)} %get-tuple-element.87.refs_0_.refs_2_, ...), custom_call_target="tpu_custom_call" | custom-call | flops 3000000000 | bytes 10200001 | tf_op jit(solution)/shard_map/finish/pallas_call | solution.py:636
  (123 shorter events, 22.1 us)
Async XLA Ops:
  0.0 5.0 %collective-permute-start = (s32[4,8]{1,0:T(4,128)}, s32[4,8]{1,0:T(4,128)S(1)}, u32[]{:S(2)}, u32[]{:S(2)}) collective-permute-start(s32[4,8]{1,0:T(4,128)} %param.8), channel_id=1, source_target_pairs={{0,4},{4,0},{8,12},{12,8},{16,20},{20,16},{24,28},{28,24},{1,5},{5... | collective-permute-start | bytes 392 | tf_op jit(solution)/shard_map/selection_swap/ppermute | solution.py:679
  1.6 3.4 %copy-start.8 = (s32[4,8]{1,0:T(4,128)S(1)}, s32[4,8]{1,0:T(4,128)}, u32[]{:S(2)}) copy-start(s32[4,8]{1,0:T(4,128)} %param.8) | copy-start | bytes 388
  3.5 20.5 %collective-permute-start.4 = (bf16[1,3,1024,128]{3,2,1,0:T(8,128)(2,1)S(1)}, bf16[1,3,1024,128]{3,2,1,0:T(8,128)(2,1)S(1)}, u32[]{:S(2)}, u32[]{:S(2)}) collective-permute-start(bf16[1,3,1024,128]{3,2,1,0:T(8,128)(2,1)S(1)} %pack.5.refs_0_), channel_id=1, source_target_pairs={{0,4},{4,0},{8,12},{12,8},{16,20},{20,16},{24,28},{28,24},{1,5},{5... | collective-permute-start | bytes 2359304 | tf_op jit(solution)/shard_map/swap_c0/ppermute | solution.py:679
  5.0 8.7 %copy-start.7 = (s32[8,8]{1,0:T(8,128)S(1)}, s32[8,8]{1,0:T(8,128)}, u32[]{:S(2)}) copy-start(s32[8,8]{1,0:T(8,128)} %constant.159.clone.1) | copy-start | bytes 772
  7.4 13.3 %collective-permute-start.1 = (bf16[1,1040,128]{2,1,0:T(8,128)(2,1)}, bf16[1,1040,128]{2,1,0:T(8,128)(2,1)S(1)}, u32[]{:S(2)}, u32[]{:S(2)}) collective-permute-start(bf16[1,1040,128]{2,1,0:T(8,128)(2,1)} %get-tuple-element.52.refs_0_.refs_2_), channel_id=1, source_target_pairs={{16,8},{20,12},{24,16},{28,20},{17,9},{21,13},{25,17},{29,21},{18,... | collective-permute-start | bytes 798728 | tf_op jit(solution)/shard_map/near_down_keep_c0/ppermute | solution.py:679
  9.7 11.1 %collective-permute-start.2 = (bf16[1,1040,128]{2,1,0:T(8,128)(2,1)}, bf16[1,1040,128]{2,1,0:T(8,128)(2,1)S(1)}, u32[]{:S(2)}, u32[]{:S(2)}) collective-permute-start(bf16[1,1040,128]{2,1,0:T(8,128)(2,1)} %get-tuple-element.52.refs_0_.refs_2_), channel_id=1, source_target_pairs={{24,8},{28,12},{25,9},{29,13},{26,10},{30,14},{27,11},{31,15}} | collective-permute-start | bytes 798728 | tf_op jit(solution)/shard_map/far_down_keep_c0/ppermute | solution.py:679
  16.8 0.9 copy-start
  17.7 6.1 %collective-permute-start.3 = (bf16[1,2,1024,128]{3,2,1,0:T(8,128)(2,1)S(1)}, bf16[1,2,1024,128]{3,2,1,0:T(8,128)(2,1)}, u32[]{:S(2)}, u32[]{:S(2)}) collective-permute-start(bf16[1,2,1024,128]{3,2,1,0:T(8,128)(2,1)S(1)} %get-tuple-element.54.refs_6_.refs_4_), channel_id=1, source_target_pairs={{0,8},{4,12},{1,9},{5,13},{2,10},{6,14},{3,11},{7,15}} | collective-permute-start | bytes 1572872 | tf_op jit(solution)/shard_map/lift_keep_c0/ppermute | solution.py:679
  19.2 25.4 %collective-permute-start.5 = (bf16[1,3,1024,128]{3,2,1,0:T(8,128)(2,1)}, bf16[1,3,1024,128]{3,2,1,0:T(8,128)(2,1)S(1)}, u32[]{:S(2)}, u32[]{:S(2)}) collective-permute-start(bf16[1,3,1024,128]{3,2,1,0:T(8,128)(2,1)} %get-tuple-element.57), channel_id=1, source_target_pairs={{0,4},{4,0},{8,12},{12,8},{16,20},{20,16},{24,28},{28,24},{1,5},{5... | collective-permute-start | bytes 2359304 | tf_op jit(solution)/shard_map/swap_c1/ppermute | solution.py:679
  24.1 1.1 copy-start.1
  26.2 27.1 %collective-permute-start.8 = (bf16[1,2,1024,128]{3,2,1,0:T(8,128)(2,1)}, bf16[1,2,1024,128]{3,2,1,0:T(8,128)(2,1)}, u32[]{:S(2)}, u32[]{:S(2)}) collective-permute-start(bf16[1,2,1024,128]{3,2,1,0:T(8,128)(2,1)} %get-tuple-element.59), channel_id=1, source_target_pairs={{0,8},{4,12},{1,9},{5,13},{2,10},{6,14},{3,11},{7,15}} | collective-permute-start | bytes 1572872 | tf_op jit(solution)/shard_map/lift_recv_c0/ppermute | solution.py:679
  27.7 21.3 %collective-permute-start.6 = (bf16[1,1024,128]{2,1,0:T(8,128)(2,1)}, bf16[1,1024,128]{2,1,0:T(8,128)(2,1)}, u32[]{:S(2)}, u32[]{:S(2)}) collective-permute-start(bf16[1,1024,128]{2,1,0:T(8,128)(2,1)} %get-tuple-element.55.refs_0_), channel_id=1, source_target_pairs={{16,8},{20,12},{24,16},{28,20},{17,9},{21,13},{25,17},{29,21},{18,... | collective-permute-start | bytes 786440 | tf_op jit(solution)/shard_map/near_down_recv_c0/ppermute | solution.py:679
  30.7 21.7 %collective-permute-start.7 = (bf16[1,1024,128]{2,1,0:T(8,128)(2,1)}, bf16[1,1024,128]{2,1,0:T(8,128)(2,1)}, u32[]{:S(2)}, u32[]{:S(2)}) collective-permute-start(bf16[1,1024,128]{2,1,0:T(8,128)(2,1)} %get-tuple-element.55.refs_0_), channel_id=1, source_target_pairs={{24,8},{28,12},{25,9},{29,13},{26,10},{30,14},{27,11},{31,15}} | collective-permute-start | bytes 786440 | tf_op jit(solution)/shard_map/far_down_recv_c0/ppermute | solution.py:679
  42.1 0.9 copy-start.4
  43.0 17.7 %collective-permute-start.9 = (bf16[1,3,1024,128]{3,2,1,0:T(8,128)(2,1)}, bf16[1,3,1024,128]{3,2,1,0:T(8,128)(2,1)S(1)}, u32[]{:S(2)}, u32[]{:S(2)}) collective-permute-start(bf16[1,3,1024,128]{3,2,1,0:T(8,128)(2,1)} %get-tuple-element.61), channel_id=1, source_target_pairs={{0,4},{4,0},{8,12},{12,8},{16,20},{20,16},{24,28},{28,24},{1,5},{5... | collective-permute-start | bytes 2359304 | tf_op jit(solution)/shard_map/swap_c2/ppermute | solution.py:679
  44.6 1.1 copy-start.2
  45.7 1.1 copy-start.5
  47.1 22.0 %collective-permute-start.10 = (bf16[2,1,1024,128]{3,2,1,0:T(8,128)(2,1)S(1)}, bf16[2,1,1024,128]{3,2,1,0:T(8,128)(2,1)S(1)}, u32[]{:S(2)}, u32[]{:S(2)}) collective-permute-start(bf16[2,1,1024,128]{3,2,1,0:T(8,128)(2,1)S(1)} %get-tuple-element.58.refs_0_), channel_id=1, source_target_pairs={{16,8},{20,12},{24,16},{28,20},{17,9},{21,13},{25,17},{29,21},{18,... | collective-permute-start | bytes 1572872 | tf_op jit(solution)/shard_map/near_down_c1/ppermute | solution.py:679
  49.0 21.6 %collective-permute-start.11 = (bf16[2,1,1024,128]{3,2,1,0:T(8,128)(2,1)S(1)}, bf16[2,1,1024,128]{3,2,1,0:T(8,128)(2,1)S(1)}, u32[]{:S(2)}, u32[]{:S(2)}) collective-permute-start(bf16[2,1,1024,128]{3,2,1,0:T(8,128)(2,1)S(1)} %get-tuple-element.58.refs_0_), channel_id=1, source_target_pairs={{24,8},{28,12},{25,9},{29,13},{26,10},{30,14},{27,11},{31,15}} | collective-permute-start | bytes 1572872 | tf_op jit(solution)/shard_map/far_down_c1/ppermute | solution.py:679
  52.5 9.6 %copy-start.6 = (bf16[1,3,1024,128]{3,2,1,0:T(8,128)(2,1)S(1)}, bf16[1,3,1024,128]{3,2,1,0:T(8,128)(2,1)}, u32[]{:S(2)}) copy-start(bf16[1,3,1024,128]{3,2,1,0:T(8,128)(2,1)} %copy-done.4) | copy-start | bytes 2359300
  52.5 21.3 %collective-permute-start.12 = (bf16[2,1,2,1024,128]{4,3,2,1,0:T(8,128)(2,1)S(1)}, bf16[2,1,2,1024,128]{4,3,2,1,0:T(8,128)(2,1)S(1)}, u32[]{:S(2)}, u32[]{:S(2)}) collective-permute-start(bf16[2,1,2,1024,128]{4,3,2,1,0:T(8,128)(2,1)S(1)} %get-tuple-element.65), channel_id=1, source_target_pairs={{0,8},{4,12},{1,9},{5,13},{2,10},{6,14},{3,11},{7,15}} | collective-permute-start | bytes 3145736 | tf_op jit(solution)/shard_map/lift_c1/ppermute | solution.py:679
  55.5 20.0 %collective-permute-start.13 = (bf16[1,1056,256]{2,1,0:T(8,128)(2,1)S(1)}, bf16[1,1056,256]{2,1,0:T(8,128)(2,1)S(1)}, u32[]{:S(2)}, u32[]{:S(2)}) collective-permute-start(bf16[1,1056,256]{2,1,0:T(8,128)(2,1)S(1)} %get-tuple-element.60.refs_0_), channel_id=1, source_target_pairs={{8,16},{12,20},{16,24},{20,28},{9,17},{13,21},{17,25},{21,29},{10,... | collective-permute-start | bytes 1622024 | tf_op jit(solution)/shard_map/near_up_c0/ppermute | solution.py:679
  60.7 24.5 %collective-permute-start.14 = (bf16[1,1056,256]{2,1,0:T(8,128)(2,1)S(1)}, bf16[1,1056,256]{2,1,0:T(8,128)(2,1)S(1)}, u32[]{:S(2)}, u32[]{:S(2)}) collective-permute-start(bf16[1,1056,256]{2,1,0:T(8,128)(2,1)S(1)} %get-tuple-element.68), channel_id=1, source_target_pairs={{8,24},{12,28},{9,25},{13,29},{10,26},{14,30},{11,27},{15,31}} | collective-permute-start | bytes 1622024 | tf_op jit(solution)/shard_map/far_up_c0/ppermute | solution.py:679
  66.9 7.6 %copy-start.3 = (bf16[1,3,1024,128]{3,2,1,0:T(8,128)(2,1)S(1)}, bf16[1,3,1024,128]{3,2,1,0:T(8,128)(2,1)}, u32[]{:S(2)}) copy-start(bf16[1,3,1024,128]{3,2,1,0:T(8,128)(2,1)} %copy-done) | copy-start | bytes 2359300
  69.2 23.6 %collective-permute-start.16 = (bf16[2,1,1024,128]{3,2,1,0:T(8,128)(2,1)S(1)}, bf16[2,1,1024,128]{3,2,1,0:T(8,128)(2,1)S(1)}, u32[]{:S(2)}, u32[]{:S(2)}) collective-permute-start(bf16[2,1,1024,128]{3,2,1,0:T(8,128)(2,1)S(1)} %get-tuple-element.62.refs_0_), channel_id=1, source_target_pairs={{16,8},{20,12},{24,16},{28,20},{17,9},{21,13},{25,17},{29,21},{18,... | collective-permute-start | bytes 1572872 | tf_op jit(solution)/shard_map/near_down_c2/ppermute | solution.py:679
  70.6 20.5 %collective-permute-start.15 = (bf16[1,3,1024,128]{3,2,1,0:T(8,128)(2,1)S(1)}, bf16[1,3,1024,128]{3,2,1,0:T(8,128)(2,1)S(1)}, u32[]{:S(2)}, u32[]{:S(2)}) collective-permute-start(bf16[1,3,1024,128]{3,2,1,0:T(8,128)(2,1)S(1)} %get-tuple-element.71), channel_id=1, source_target_pairs={{0,4},{4,0},{8,12},{12,8},{16,20},{20,16},{24,28},{28,24},{1,5},{5... | collective-permute-start | bytes 2359304 | tf_op jit(solution)/shard_map/swap_c3/ppermute | solution.py:679
  73.8 20.7 %collective-permute-start.18 = (bf16[2,1,2,1024,128]{4,3,2,1,0:T(8,128)(2,1)S(1)}, bf16[2,1,2,1024,128]{4,3,2,1,0:T(8,128)(2,1)S(1)}, u32[]{:S(2)}, u32[]{:S(2)}) collective-permute-start(bf16[2,1,2,1024,128]{4,3,2,1,0:T(8,128)(2,1)S(1)} %get-tuple-element.73), channel_id=1, source_target_pairs={{0,8},{4,12},{1,9},{5,13},{2,10},{6,14},{3,11},{7,15}} | collective-permute-start | bytes 3145736 | tf_op jit(solution)/shard_map/lift_c2/ppermute | solution.py:679
  75.6 18.1 %collective-permute-start.17 = (bf16[2,1,1024,128]{3,2,1,0:T(8,128)(2,1)S(1)}, bf16[2,1,1024,128]{3,2,1,0:T(8,128)(2,1)S(1)}, u32[]{:S(2)}, u32[]{:S(2)}) collective-permute-start(bf16[2,1,1024,128]{3,2,1,0:T(8,128)(2,1)S(1)} %get-tuple-element.62.refs_0_), channel_id=1, source_target_pairs={{24,8},{28,12},{25,9},{29,13},{26,10},{30,14},{27,11},{31,15}} | collective-permute-start | bytes 1572872 | tf_op jit(solution)/shard_map/far_down_c2/ppermute | solution.py:679
  85.2 24.5 %collective-permute-start.19 = (bf16[1,1056,256]{2,1,0:T(8,128)(2,1)S(1)}, bf16[1,1056,256]{2,1,0:T(8,128)(2,1)S(1)}, u32[]{:S(2)}, u32[]{:S(2)}) collective-permute-start(bf16[1,1056,256]{2,1,0:T(8,128)(2,1)S(1)} %get-tuple-element.66.refs_0_), channel_id=1, source_target_pairs={{8,16},{12,20},{16,24},{20,28},{9,17},{13,21},{17,25},{21,29},{10,... | collective-permute-start | bytes 1622024 | tf_op jit(solution)/shard_map/near_up_c1/ppermute | solution.py:679
  91.1 20.6 %collective-permute-start.20 = (bf16[1,1056,256]{2,1,0:T(8,128)(2,1)S(1)}, bf16[1,1056,256]{2,1,0:T(8,128)(2,1)S(1)}, u32[]{:S(2)}, u32[]{:S(2)}) collective-permute-start(bf16[1,1056,256]{2,1,0:T(8,128)(2,1)S(1)} %get-tuple-element.77), channel_id=1, source_target_pairs={{8,24},{12,28},{9,25},{13,29},{10,26},{14,30},{11,27},{15,31}} | collective-permute-start | bytes 1622024 | tf_op jit(solution)/shard_map/far_up_c1/ppermute | solution.py:679
  92.7 25.0 %collective-permute-start.21 = (bf16[1,1024,128]{2,1,0:T(8,128)(2,1)S(1)}, bf16[1,1024,128]{2,1,0:T(8,128)(2,1)S(1)}, u32[]{:S(2)}, u32[]{:S(2)}) collective-permute-start(bf16[1,1024,128]{2,1,0:T(8,128)(2,1)S(1)} %get-tuple-element.80), channel_id=1, source_target_pairs={{0,4},{4,0},{8,12},{12,8},{16,20},{20,16},{24,28},{28,24},{1,5},{5... | collective-permute-start | bytes 786440 | tf_op jit(solution)/shard_map/back_c0/ppermute | solution.py:679
  93.7 25.4 %collective-permute-start.24 = (bf16[2,1,2,1024,128]{4,3,2,1,0:T(8,128)(2,1)S(1)}, bf16[2,1,2,1024,128]{4,3,2,1,0:T(8,128)(2,1)S(1)}, u32[]{:S(2)}, u32[]{:S(2)}) collective-permute-start(bf16[2,1,2,1024,128]{4,3,2,1,0:T(8,128)(2,1)S(1)} %get-tuple-element.81), channel_id=1, source_target_pairs={{0,8},{4,12},{1,9},{5,13},{2,10},{6,14},{3,11},{7,15}} | collective-permute-start | bytes 3145736 | tf_op jit(solution)/shard_map/lift_c3/ppermute | solution.py:679
  94.4 24.7 %collective-permute-start.22 = (bf16[2,1,1024,128]{3,2,1,0:T(8,128)(2,1)S(1)}, bf16[2,1,1024,128]{3,2,1,0:T(8,128)(2,1)S(1)}, u32[]{:S(2)}, u32[]{:S(2)}) collective-permute-start(bf16[2,1,1024,128]{3,2,1,0:T(8,128)(2,1)S(1)} %get-tuple-element.72.refs_0_), channel_id=1, source_target_pairs={{16,8},{20,12},{24,16},{28,20},{17,9},{21,13},{25,17},{29,21},{18,... | collective-permute-start | bytes 1572872 | tf_op jit(solution)/shard_map/near_down_c3/ppermute | solution.py:679
  109.7 9.4 %collective-permute-start.23 = (bf16[2,1,1024,128]{3,2,1,0:T(8,128)(2,1)S(1)}, bf16[2,1,1024,128]{3,2,1,0:T(8,128)(2,1)S(1)}, u32[]{:S(2)}, u32[]{:S(2)}) collective-permute-start(bf16[2,1,1024,128]{3,2,1,0:T(8,128)(2,1)S(1)} %get-tuple-element.72.refs_0_), channel_id=1, source_target_pairs={{24,8},{28,12},{25,9},{29,13},{26,10},{30,14},{27,11},{31,15}} | collective-permute-start | bytes 1572872 | tf_op jit(solution)/shard_map/far_down_c3/ppermute | solution.py:679
  111.7 25.2 %collective-permute-start.25 = (bf16[1,1056,256]{2,1,0:T(8,128)(2,1)S(1)}, bf16[1,1056,256]{2,1,0:T(8,128)(2,1)S(1)}, u32[]{:S(2)}, u32[]{:S(2)}) collective-permute-start(bf16[1,1056,256]{2,1,0:T(8,128)(2,1)S(1)} %get-tuple-element.74.refs_0_), channel_id=1, source_target_pairs={{8,16},{12,20},{16,24},{20,28},{9,17},{13,21},{17,25},{21,29},{10,... | collective-permute-start | bytes 1622024 | tf_op jit(solution)/shard_map/near_up_c2/ppermute | solution.py:679
  117.8 19.2 %collective-permute-start.26 = (bf16[1,1056,256]{2,1,0:T(8,128)(2,1)S(1)}, bf16[1,1056,256]{2,1,0:T(8,128)(2,1)S(1)}, u32[]{:S(2)}, u32[]{:S(2)}) collective-permute-start(bf16[1,1056,256]{2,1,0:T(8,128)(2,1)S(1)} %get-tuple-element.86), channel_id=1, source_target_pairs={{8,24},{12,28},{9,25},{13,29},{10,26},{14,30},{11,27},{15,31}} | collective-permute-start | bytes 1622024 | tf_op jit(solution)/shard_map/far_up_c2/ppermute | solution.py:679
  123.8 19.3 %collective-permute-start.28 = (bf16[1,528,256]{2,1,0:T(8,128)(2,1)S(1)}, bf16[1,528,256]{2,1,0:T(8,128)(2,1)S(1)}, u32[]{:S(2)}, u32[]{:S(2)}) collective-permute-start(bf16[1,528,256]{2,1,0:T(8,128)(2,1)S(1)} %get-tuple-element.90), channel_id=1, source_target_pairs={{0,4},{4,0},{8,12},{12,8},{16,20},{20,16},{24,28},{28,24},{1,5},{5... | collective-permute-start | bytes 811016 | tf_op jit(solution)/shard_map/back_own_c3/ppermute | solution.py:679
  124.0 22.9 %collective-permute-start.29 = (bf16[1,528,256]{2,1,0:T(8,128)(2,1)S(1)}, bf16[1,528,256]{2,1,0:T(8,128)(2,1)S(1)}, u32[]{:S(2)}, u32[]{:S(2)}) collective-permute-start(bf16[1,528,256]{2,1,0:T(8,128)(2,1)S(1)} %get-tuple-element.82.refs_0_), channel_id=1, source_target_pairs={{8,16},{12,20},{16,24},{20,28},{9,17},{13,21},{17,25},{21,29},{10,... | collective-permute-start | bytes 811016 | tf_op jit(solution)/shard_map/near_up_same_c3/ppermute | solution.py:679
  138.0 22.6 %copy-start.9 = (bf16[1024]{0:T(1024)(128)(2,1)S(1)}, bf16[1024]{0:T(1024)(128)(2,1)}, u32[]{:S(2)}) copy-start(bf16[1024]{0:T(1024)(128)(2,1)} %param.9) | copy-start | bytes 6148
  138.0 3.8 %collective-permute-start.27 = (f32[4,256]{1,0:T(4,128)S(1)}, f32[4,256]{1,0:T(4,128)S(1)}, u32[]{:S(2)}, u32[]{:S(2)}) collective-permute-start(f32[4,256]{1,0:T(4,128)S(1)} %slice.23), channel_id=1, source_target_pairs={{0,4},{4,0},{8,12},{12,8},{16,20},{20,16},{24,28},{28,24},{1,5},{5... | collective-permute-start | bytes 12296 | tf_op jit(solution)/shard_map/squares_swap/ppermute | solution.py:679
  138.1 18.6 %collective-permute-start.30 = (bf16[1,528,256]{2,1,0:T(8,128)(2,1)S(1)}, bf16[1,528,256]{2,1,0:T(8,128)(2,1)S(1)}, u32[]{:S(2)}, u32[]{:S(2)}) collective-permute-start(bf16[1,528,256]{2,1,0:T(8,128)(2,1)S(1)} %get-tuple-element.91), channel_id=1, source_target_pairs={{8,20},{12,16},{16,28},{20,24},{9,21},{13,17},{17,29},{21,25},{10,... | collective-permute-start | bytes 811016 | tf_op jit(solution)/shard_map/near_up_cross_c3/ppermute | solution.py:679
  139.4 17.3 %collective-permute-start.31 = (bf16[1,528,256]{2,1,0:T(8,128)(2,1)S(1)}, bf16[1,528,256]{2,1,0:T(8,128)(2,1)S(1)}, u32[]{:S(2)}, u32[]{:S(2)}) collective-permute-start(bf16[1,528,256]{2,1,0:T(8,128)(2,1)S(1)} %get-tuple-element.92), channel_id=1, source_target_pairs={{8,24},{12,28},{9,25},{13,29},{10,26},{14,30},{11,27},{15,31}} | collective-permute-start | bytes 811016 | tf_op jit(solution)/shard_map/far_up_same_c3/ppermute | solution.py:679
  141.8 14.9 %collective-permute-start.32 = (bf16[1,528,256]{2,1,0:T(8,128)(2,1)S(1)}, bf16[1,528,256]{2,1,0:T(8,128)(2,1)S(1)}, u32[]{:S(2)}, u32[]{:S(2)}) collective-permute-start(bf16[1,528,256]{2,1,0:T(8,128)(2,1)S(1)} %get-tuple-element.93), channel_id=1, source_target_pairs={{8,28},{12,24},{9,29},{13,25},{10,30},{14,26},{11,31},{15,27}} | collective-permute-start | bytes 811016 | tf_op jit(solution)/shard_map/far_up_cross_c3/ppermute | solution.py:679
  143.1 19.5 %collective-permute-start.33 = (bf16[1,1024,128]{2,1,0:T(8,128)(2,1)S(1)}, bf16[1,1024,128]{2,1,0:T(8,128)(2,1)S(1)}, u32[]{:S(2)}, u32[]{:S(2)}) collective-permute-start(bf16[1,1024,128]{2,1,0:T(8,128)(2,1)S(1)} %get-tuple-element.95), channel_id=1, source_target_pairs={{0,4},{4,0},{8,12},{12,8},{16,20},{20,16},{24,28},{28,24},{1,5},{5... | collective-permute-start | bytes 786440 | tf_op jit(solution)/shard_map/back_c1/ppermute | solution.py:679
  146.9 15.7 %collective-permute-start.34 = (bf16[1,1024,128]{2,1,0:T(8,128)(2,1)S(1)}, bf16[1,1024,128]{2,1,0:T(8,128)(2,1)S(1)}, u32[]{:S(2)}, u32[]{:S(2)}) collective-permute-start(bf16[1,1024,128]{2,1,0:T(8,128)(2,1)S(1)} %get-tuple-element.96), channel_id=1, source_target_pairs={{0,4},{4,0},{8,12},{12,8},{16,20},{20,16},{24,28},{28,24},{1,5},{5... | collective-permute-start | bytes 786440 | tf_op jit(solution)/shard_map/back_c2/ppermute | solution.py:679
  157.8 1.2 collective-permute-start.35
  159.0 3.6 %collective-permute-start.36 = (f32[4,256]{1,0:T(4,128)S(1)}, f32[4,256]{1,0:T(4,128)S(1)}, u32[]{:S(2)}, u32[]{:S(2)}) collective-permute-start(f32[4,256]{1,0:T(4,128)S(1)} %add.296), channel_id=1, source_target_pairs={{0,2},{1,3},{2,0},{3,1},{4,6},{5,7},{6,4},{7,5},{8,10},{9,11},{10,... | collective-permute-start | bytes 12296 | tf_op jit(solution)/shard_map/ppermute | solution.py:858

commit v9 on v8

--- a/solution.py
+++ b/solution.py
@@ -129,16 +129,15 @@
 
 
 SPLIT = (True, False, False, False)
-SCATTER = (False, False, False, False)
 ORDER = (
     ("p", 0),
     ("w", "plan"),
     ("p", 1),
     ("w", "near_down_keep_c0"),
     ("w", "far_down_keep_c0"),
+    ("j", 0),
     ("w", "lift_keep_c0"),
     ("w", "served"),
-    ("j", 0),
     ("p", 2),
     ("j", 1),
     ("s", 0),
@@ -679,14 +678,6 @@
             sent[name] = lax.ppermute(array, "ctx", pairs)
         return sent[name]
 
-    def exchange(array, name):
-        pairs = [[d, d + 1] for d in range(0, 8, 2)]
-        with jax.named_scope(name):
-            sent[name] = lax.psum_scatter(
-                array, "ctx", scatter_dimension=0, axis_index_groups=pairs, tiled=True
-            )
-        return sent[name]
-
     swap = [(d, d ^ 1) for d in range(8)]
     lift = [(0, 2), (1, 3)]
     near_down, far_down = [(4, 2), (5, 3), (6, 4), (7, 5)], [(6, 2), (7, 3)]

time: 167 us -> 163 us (0.976)
  waiting for transfers between devices: 41.8 us -> 35.8 us
  starting transfers between devices: 69.2 us -> 71.8 us
    ppermute x35, waiting for transfers between devices: 38.6 us -> 32.6 us  [to(): sent[name] = lax.ppermute(array, 'ctx', pairs)]
    ppermute x35, starting transfers between devices: 67.7 us -> 70.3 us  [to(): sent[name] = lax.ppermute(array, 'ctx', pairs)]
  transfers between devices with their start and end apart: 37 -> 37, of which waited for: 11 -> 10; matrix products, arithmetic and copies ran while one was open for 3% -> 3% of each run, Pallas kernels for 23% -> 24%
where the time goes in v9:
time: 163 us; the launch traced here: 162 us
  starting transfers between devices  71.8 us (44%)
  Pallas kernels  41.4 us (25%)
  waiting for transfers between devices  35.8 us (22%)
  local copies, waits for them, and re-layouts  6.26 us (4%)
  other arithmetic  3.46 us (2%)
  between operations  3.31 us (2%)
    ppermute x35, starting transfers between devices, to(): sent[name] = lax.ppermute(array, 'ctx', pairs)  70.3 us
    ppermute x35, waiting for transfers between devices, to(): sent[name] = lax.ppermute(array, 'ctx', pairs)  32.6 us
    pallas_call x8, Pallas kernels, attention_call(): pl.pallas_call(ordered(partial(attention_kernel, (heads, per_dev, block_r...  20.8 us
    pallas_call x5, Pallas kernels, pack_call(): pl.pallas_call(ordered(partial(pack_kernel, (sides, head, half, rows, not...  11.8 us
    unnamed x20, local copies, waits for them, and re-layouts  5.2 us
  transfers between devices with their start and end apart: 37, of which 10 were waited for; matrix products, arithmetic and copies ran while one was open for 3% of the time, Pallas kernels for 24%

profile of v9, /device:TPU:24, one launch (start us, length us, event | category | flops | bytes accessed | tf_op | source)
XLA Modules:
  0.0 162.1 jit_solution(2379956879314576388)
XLA Ops:
  0.0 1.5 collective-permute-start
  1.6 2.0 %pack.5.refs_0_ = bf16[1,3,1024,128]{3,2,1,0:T(8,128)(2,1)S(1)} custom-call(s32[2]{0:T(128)S(1)} %pad_add_fusion.2.refs_0_.refs_1_.refs_2_.refs_3_.place, bf16[1024,1024]{1,0:T(8,128)(2,1)} %refs_2_.5, bf16[1024,1024]{1,0:T(8,128)(2,1)} %refs_3_.7, bf16[1024,1024]{1,0:T(8,128)(2,1)} %refs_4_.7), custom_call_target="tpu_custom_call" | custom-call | flops 2000000000 | bytes 6800001 | tf_op jit(solution)/shard_map/pack/pallas_call | solution.py:426
  5.0 2.4 %pack.6 = (bf16[1,1040,128]{2,1,0:T(8,128)(2,1)}, bf16[1,2,1024,128]{3,2,1,0:T(8,128)(2,1)S(1)}) custom-call(bf16[1,3,1024,128]{3,2,1,0:T(8,128)(2,1)S(1)} %pack.5.refs_0_, s32[2]{0:T(128)S(1)} %pad_add_fusion.2.refs_0_.refs_1_.refs_2_.refs_3_.place, bf16[1024,1024]{1,0:T(8,128)(2,1)} %refs_2_.5, bf16[1024,1024]{1,0:T(8,128)(2,1)} %refs_3_.7, ...), custom_call_target="tpu_custom_call" | custom-call | flops 2000000000 | bytes 6800001 | tf_op jit(solution)/shard_map/pack/pallas_call | solution.py:426
  7.4 2.4 %collective-permute-start.1 = (bf16[1,1040,128]{2,1,0:T(8,128)(2,1)}, bf16[1,1040,128]{2,1,0:T(8,128)(2,1)S(1)}, u32[]{:S(2)}, u32[]{:S(2)}) collective-permute-start(bf16[1,1040,128]{2,1,0:T(8,128)(2,1)} %get-tuple-element.52.refs_0_.refs_2_), channel_id=1, source_target_pairs={{16,8},{20,12},{24,16},{28,20},{17,9},{21,13},{25,17},{29,21},{18,... | collective-permute-start | bytes 798728 | tf_op jit(solution)/shard_map/near_down_keep_c0/ppermute | solution.py:678
  9.7 1.3 collective-permute-start.2
  14.2 2.6 %pack.7 = (bf16[1,3,1024,128]{3,2,1,0:T(8,128)(2,1)}, bf16[1,3,1024,128]{3,2,1,0:T(8,128)(2,1)S(1)}) custom-call(bf16[1,1040,128]{2,1,0:T(8,128)(2,1)} %get-tuple-element.52.refs_0_.refs_2_, s32[81]{0:T(128)S(1)} %pad_add_fusion.4.refs_1_, s32[2]{0:T(128)S(1)} %pad_add_fusion.2.refs_0_.refs_1_.refs_2_.refs_3_.place, bf16[1024,1024]{1,0:T(8,128)(2,1)} %refs_2_.5, ...), custom_call_target="tpu_custom_call" | custom-call | flops 2000000000 | bytes 6800001 | tf_op jit(solution)/shard_map/pack/pallas_call | solution.py:426
  17.7 1.4 collective-permute-start.4
  19.2 1.5 collective-permute-start.5
  26.2 1.5 collective-permute-start.8
  27.7 3.1 %collective-permute-start.6 = (bf16[1,1024,128]{2,1,0:T(8,128)(2,1)}, bf16[1,1024,128]{2,1,0:T(8,128)(2,1)}, u32[]{:S(2)}, u32[]{:S(2)}) collective-permute-start(bf16[1,1024,128]{2,1,0:T(8,128)(2,1)} %get-tuple-element.54.refs_0_), channel_id=1, source_target_pairs={{16,8},{20,12},{24,16},{28,20},{17,9},{21,13},{25,17},{29,21},{18,... | collective-permute-start | bytes 786440 | tf_op jit(solution)/shard_map/near_down_recv_c0/ppermute | solution.py:678
  30.8 3.7 %collective-permute-start.7 = (bf16[1,1024,128]{2,1,0:T(8,128)(2,1)}, bf16[1,1024,128]{2,1,0:T(8,128)(2,1)}, u32[]{:S(2)}, u32[]{:S(2)}) collective-permute-start(bf16[1,1024,128]{2,1,0:T(8,128)(2,1)} %get-tuple-element.54.refs_0_), channel_id=1, source_target_pairs={{24,8},{28,12},{25,9},{29,13},{26,10},{30,14},{27,11},{31,15}} | collective-permute-start | bytes 786440 | tf_op jit(solution)/shard_map/far_down_recv_c0/ppermute | solution.py:678
  34.5 2.7 %pack.8 = (bf16[1,3,1024,128]{3,2,1,0:T(8,128)(2,1)}, bf16[1,3,1024,128]{3,2,1,0:T(8,128)(2,1)S(1)}) custom-call(bf16[1,1024,128]{2,1,0:T(8,128)(2,1)} %get-tuple-element.54.refs_0_, bf16[1,2,1024,128]{3,2,1,0:T(8,128)(2,1)} %collective-permute-done.4.refs_1_.refs_8_.refs_5_, s32[129]{0:T(256)S(1)} %pad_add_fusion.1.refs_2_.refs_1_, ...), custom_call_target="tpu_custom_call" | custom-call | flops 2000000000 | bytes 6800001 | tf_op jit(solution)/shard_map/pack/pallas_call | solution.py:426
  38.1 1.5 collective-permute-start.9
  42.4 2.9 %collective-permute-start.10 = (bf16[2,1,1024,128]{3,2,1,0:T(8,128)(2,1)S(1)}, bf16[2,1,1024,128]{3,2,1,0:T(8,128)(2,1)S(1)}, u32[]{:S(2)}, u32[]{:S(2)}) collective-permute-start(bf16[2,1,1024,128]{3,2,1,0:T(8,128)(2,1)S(1)} %get-tuple-element.58.refs_0_), channel_id=1, source_target_pairs={{16,8},{20,12},{24,16},{28,20},{17,9},{21,13},{25,17},{29,21},{18,... | collective-permute-start | bytes 1572872 | tf_op jit(solution)/shard_map/near_down_c1/ppermute | solution.py:678
  45.3 1.7 %collective-permute-start.11 = (bf16[2,1,1024,128]{3,2,1,0:T(8,128)(2,1)S(1)}, bf16[2,1,1024,128]{3,2,1,0:T(8,128)(2,1)S(1)}, u32[]{:S(2)}, u32[]{:S(2)}) collective-permute-start(bf16[2,1,1024,128]{3,2,1,0:T(8,128)(2,1)S(1)} %get-tuple-element.58.refs_0_), channel_id=1, source_target_pairs={{24,8},{28,12},{25,9},{29,13},{26,10},{30,14},{27,11},{31,15}} | collective-permute-start | bytes 1572872 | tf_op jit(solution)/shard_map/far_down_c1/ppermute | solution.py:678
  48.0 2.2 %served_attention.4 = (bf16[1,1056,256]{2,1,0:T(8,128)(2,1)S(1)}, bf16[1,1056,256]{2,1,0:T(8,128)(2,1)S(1)}) custom-call(bf16[2,1,1024,128]{3,2,1,0:T(8,128)(2,1)S(1)} %get-tuple-element.58.refs_0_, s32[129]{0:T(256)S(1)} %pad_add_fusion.1.refs_2_.refs_1_, bf16[1,1040,128]{2,1,0:T(8,128)(2,1)S(1)} %collective-permute-done.1.refs_1_.refs_2_, ...), custom_call_target="tpu_custom_call" | custom-call | flops 6000000000 | bytes 20400000 | tf_op jit(solution)/shard_map/served_attention/pallas_call | solution.py:351
  50.1 1.3 collective-permute-start.13
  51.4 4.9 %collective-permute-done.9.refs_2_.refs_5_.refs_3_ = bf16[1,3,1024,128]{3,2,1,0:T(8,128)(2,1)S(1)} collective-permute-done((bf16[1,3,1024,128]{3,2,1,0:T(8,128)(2,1)}, bf16[1,3,1024,128]{3,2,1,0:T(8,128)(2,1)S(1)}, u32[]{:S(2)}, u32[]{:S(2)}) %collective-permute-start.9) | collective-permute-done | bytes 786464 | tf_op jit(solution)/shard_map/swap_c2/ppermute | solution.py:678
  56.3 1.3 collective-permute-start.14
  57.9 4.6 %own_attention.4 = (f32[1,8,128,256]{3,2,1,0:T(8,128)S(1)}, f32[1,8,256]{2,1,0:T(8,128)S(1)}) custom-call(bf16[2,1,1024,128]{3,2,1,0:T(8,128)(2,1)S(1)} %get-tuple-element.62.refs_0_, s32[81]{0:T(128)S(1)} %pad_add_fusion.4.refs_1_, bf16[1,1040,128]{2,1,0:T(8,128)(2,1)} %get-tuple-element.52.refs_0_.refs_2_, ...), custom_call_target="tpu_custom_call" | custom-call | flops 5000000000 | bytes 17000000 | tf_op jit(solution)/shard_map/own_attention/pallas_call | solution.py:351
  62.5 2.2 %pack.9 = (bf16[1,3,1024,128]{3,2,1,0:T(8,128)(2,1)S(1)}, bf16[1,3,1024,128]{3,2,1,0:T(8,128)(2,1)S(1)}) custom-call(f32[1,8,256]{2,1,0:T(8,128)S(1)} %get-tuple-element.63.refs_0_.refs_4_, s32[2]{0:T(128)S(1)} %pad_add_fusion.2.refs_0_.refs_1_.refs_2_.refs_3_.place, bf16[1024,1024]{1,0:T(8,128)(2,1)} %refs_2_.5, bf16[1024,1024]{1,0:T(8,128)(2,1)} %refs_3_.7, ...), custom_call_target="tpu_custom_call" | custom-call | flops 2000000000 | bytes 6800001 | tf_op jit(solution)/shard_map/pack/pallas_call | solution.py:426
  64.7 1.8 %collective-permute-start.16 = (bf16[2,1,1024,128]{3,2,1,0:T(8,128)(2,1)S(1)}, bf16[2,1,1024,128]{3,2,1,0:T(8,128)(2,1)S(1)}, u32[]{:S(2)}, u32[]{:S(2)}) collective-permute-start(bf16[2,1,1024,128]{3,2,1,0:T(8,128)(2,1)S(1)} %get-tuple-element.62.refs_0_), channel_id=1, source_target_pairs={{16,8},{20,12},{24,16},{28,20},{17,9},{21,13},{25,17},{29,21},{18,... | collective-permute-start | bytes 1572872 | tf_op jit(solution)/shard_map/near_down_c2/ppermute | solution.py:678
  66.5 1.5 collective-permute-start.15
  69.8 10.5 %collective-permute-start.17 = (bf16[2,1,1024,128]{3,2,1,0:T(8,128)(2,1)S(1)}, bf16[2,1,1024,128]{3,2,1,0:T(8,128)(2,1)S(1)}, u32[]{:S(2)}, u32[]{:S(2)}) collective-permute-start(bf16[2,1,1024,128]{3,2,1,0:T(8,128)(2,1)S(1)} %get-tuple-element.62.refs_0_), channel_id=1, source_target_pairs={{24,8},{28,12},{25,9},{29,13},{26,10},{30,14},{27,11},{31,15}} | collective-permute-start | bytes 1572872 | tf_op jit(solution)/shard_map/far_down_c2/ppermute | solution.py:678
  80.3 1.3 collective-permute-start.19
  82.7 3.6 %own_attention.5 = (f32[1,8,128,256]{3,2,1,0:T(8,128)S(1)}, f32[1,8,256]{2,1,0:T(8,128)S(1)}) custom-call(bf16[1,1024,128]{2,1,0:T(8,128)(2,1)S(1)} %get-tuple-element.69.refs_0_, s32[81]{0:T(128)S(1)} %pad_add_fusion.4.refs_1_, bf16[1,3,1024,128]{3,2,1,0:T(8,128)(2,1)S(1)} %copy-done.6, ...), custom_call_target="tpu_custom_call" | custom-call | flops 5000000000 | bytes 17000000 | tf_op jit(solution)/shard_map/own_attention/pallas_call | solution.py:351
  86.2 1.3 collective-permute-start.20
  89.7 5.3 %collective-permute-start.22 = (bf16[2,1,1024,128]{3,2,1,0:T(8,128)(2,1)S(1)}, bf16[2,1,1024,128]{3,2,1,0:T(8,128)(2,1)S(1)}, u32[]{:S(2)}, u32[]{:S(2)}) collective-permute-start(bf16[2,1,1024,128]{3,2,1,0:T(8,128)(2,1)S(1)} %get-tuple-element.72.refs_0_), channel_id=1, source_target_pairs={{16,8},{20,12},{24,16},{28,20},{17,9},{21,13},{25,17},{29,21},{18,... | collective-permute-start | bytes 1572872 | tf_op jit(solution)/shard_map/near_down_c3/ppermute | solution.py:678
  96.0 8.8 %collective-permute-done.19.refs_5_ = bf16[1,1056,256]{2,1,0:T(8,128)(2,1)S(1)} collective-permute-done((bf16[1,1056,256]{2,1,0:T(8,128)(2,1)S(1)}, bf16[1,1056,256]{2,1,0:T(8,128)(2,1)S(1)}, u32[]{:S(2)}, u32[]{:S(2)}) %collective-permute-start.19) | collective-permute-done | bytes 540704 | tf_op jit(solution)/shard_map/near_up_c1/ppermute | solution.py:678
  104.8 1.3 collective-permute-start.23
  106.1 1.3 collective-permute-start.25
  108.4 3.7 %own_attention.6 = (f32[1,8,128,256]{3,2,1,0:T(8,128)S(1)}, f32[1,8,256]{2,1,0:T(8,128)S(1)}) custom-call(bf16[1,1024,128]{2,1,0:T(8,128)(2,1)S(1)} %get-tuple-element.78.refs_0_.refs_1_, s32[81]{0:T(128)S(1)} %pad_add_fusion.4.refs_1_, bf16[1,3,1024,128]{3,2,1,0:T(8,128)(2,1)S(1)} %copy-done.2, ...), custom_call_target="tpu_custom_call" | custom-call | flops 5000000000 | bytes 17000000 | tf_op jit(solution)/shard_map/own_attention/pallas_call | solution.py:351
  112.2 1.3 collective-permute-start.26
  114.6 3.6 %own_attention.7 = (f32[1,4,128,256]{3,2,1,0:T(8,128)S(1)}, f32[1,4,256]{2,1,0:T(4,128)S(1)}, bf16[1,528,256]{2,1,0:T(8,128)(2,1)S(1)}) custom-call(bf16[1,528,256]{2,1,0:T(8,128)(2,1)S(1)} %get-tuple-element.82.refs_0_, s32[81]{0:T(128)S(1)} %pad_add_fusion.4.refs_1_, bf16[1,3,1024,128]{3,2,1,0:T(8,128)(2,1)S(1)} %get-tuple-element.64.refs_0_.refs_1_.refs_5_.refs_2_, ...), custom_call_target="tpu_custom_call" | custom-call | flops 5000000000 | bytes 17000000 | tf_op jit(solution)/shard_map/own_attention/pallas_call | solution.py:351
  118.2 2.2 %collective-permute-start.28 = (bf16[1,528,256]{2,1,0:T(8,128)(2,1)S(1)}, bf16[1,528,256]{2,1,0:T(8,128)(2,1)S(1)}, u32[]{:S(2)}, u32[]{:S(2)}) collective-permute-start(bf16[1,528,256]{2,1,0:T(8,128)(2,1)S(1)} %get-tuple-element.90), channel_id=1, source_target_pairs={{0,4},{4,0},{8,12},{12,8},{16,20},{20,16},{24,28},{28,24},{1,5},{5... | collective-permute-start | bytes 811016 | tf_op jit(solution)/shard_map/back_own_c3/ppermute | solution.py:678
  120.4 1.3 collective-permute-start.29
  121.6 8.9 %collective-permute-done.25.refs_5_ = bf16[1,1056,256]{2,1,0:T(8,128)(2,1)S(1)} collective-permute-done((bf16[1,1056,256]{2,1,0:T(8,128)(2,1)S(1)}, bf16[1,1056,256]{2,1,0:T(8,128)(2,1)S(1)}, u32[]{:S(2)}, u32[]{:S(2)}) %collective-permute-start.25) | collective-permute-done | bytes 540704 | tf_op jit(solution)/shard_map/near_up_c2/ppermute | solution.py:678
  131.6 3.1 %collective-permute-start.27 = (f32[4,256]{1,0:T(4,128)S(1)}, f32[4,256]{1,0:T(4,128)S(1)}, u32[]{:S(2)}, u32[]{:S(2)}) collective-permute-start(f32[4,256]{1,0:T(4,128)S(1)} %slice.23), channel_id=1, source_target_pairs={{0,4},{4,0},{8,12},{12,8},{16,20},{20,16},{24,28},{28,24},{1,5},{5... | collective-permute-start | bytes 12296 | tf_op jit(solution)/shard_map/squares_swap/ppermute | solution.py:678
  134.6 1.3 collective-permute-start.30
  135.9 1.3 collective-permute-start.31
  137.2 1.3 collective-permute-start.32
  138.5 1.2 collective-permute-start.33
  139.8 1.2 collective-permute-done.29.refs_7_
  140.9 4.2 %collective-permute-start.34 = (bf16[1,1024,128]{2,1,0:T(8,128)(2,1)S(1)}, bf16[1,1024,128]{2,1,0:T(8,128)(2,1)S(1)}, u32[]{:S(2)}, u32[]{:S(2)}) collective-permute-start(bf16[1,1024,128]{2,1,0:T(8,128)(2,1)S(1)} %get-tuple-element.96), channel_id=1, source_target_pairs={{0,4},{4,0},{8,12},{12,8},{16,20},{20,16},{24,28},{28,24},{1,5},{5... | collective-permute-start | bytes 786440 | tf_op jit(solution)/shard_map/back_c2/ppermute | solution.py:678
  145.1 8.2 %collective-permute-done.30.refs_8_ = bf16[1,528,256]{2,1,0:T(8,128)(2,1)S(1)} collective-permute-done((bf16[1,528,256]{2,1,0:T(8,128)(2,1)S(1)}, bf16[1,528,256]{2,1,0:T(8,128)(2,1)S(1)}, u32[]{:S(2)}, u32[]{:S(2)}) %collective-permute-start.30) | collective-permute-done | bytes 270368 | tf_op jit(solution)/shard_map/near_up_cross_c3/ppermute | solution.py:678
  155.6 1.5 collective-permute-start.36
  157.1 2.1 %collective-permute-done.36 = f32[4,256]{1,0:T(4,128)S(1)} collective-permute-done((f32[4,256]{1,0:T(4,128)S(1)}, f32[4,256]{1,0:T(4,128)S(1)}, u32[]{:S(2)}, u32[]{:S(2)}) %collective-permute-start.36) | collective-permute-done | bytes 4128 | tf_op jit(solution)/shard_map/ppermute | solution.py:849
  159.2 2.8 %finish.1 = bf16[1024,1024]{1,0:T(8,128)(2,1)} custom-call(s32[2]{0:T(128)S(1)} %pad_add_fusion.2.refs_0_.refs_1_.refs_2_.refs_3_.place, bf16[1,1024,128]{2,1,0:T(8,128)(2,1)S(1)} %get-tuple-element.69.refs_0_, bf16[1,1024,128]{2,1,0:T(8,128)(2,1)S(1)} %get-tuple-element.78.refs_0_.refs_1_, bf16[1,1024,128]{2,1,0:T(8,128)(2,1)S(1)} %get-tuple-element.87.refs_0_.refs_2_, ...), custom_call_target="tpu_custom_call" | custom-call | flops 3000000000 | bytes 10200001 | tf_op jit(solution)/shard_map/finish/pallas_call | solution.py:635
  (123 shorter events, 24.6 us)
Async XLA Ops:
  0.0 5.0 %collective-permute-start = (s32[4,8]{1,0:T(4,128)}, s32[4,8]{1,0:T(4,128)S(1)}, u32[]{:S(2)}, u32[]{:S(2)}) collective-permute-start(s32[4,8]{1,0:T(4,128)} %param.8), channel_id=1, source_target_pairs={{0,4},{4,0},{8,12},{12,8},{16,20},{20,16},{24,28},{28,24},{1,5},{5... | collective-permute-start | bytes 392 | tf_op jit(solution)/shard_map/selection_swap/ppermute | solution.py:678
  1.6 3.4 %copy-start.8 = (s32[4,8]{1,0:T(4,128)S(1)}, s32[4,8]{1,0:T(4,128)}, u32[]{:S(2)}) copy-start(s32[4,8]{1,0:T(4,128)} %param.8) | copy-start | bytes 388
  3.5 20.5 %collective-permute-start.3 = (bf16[1,3,1024,128]{3,2,1,0:T(8,128)(2,1)S(1)}, bf16[1,3,1024,128]{3,2,1,0:T(8,128)(2,1)S(1)}, u32[]{:S(2)}, u32[]{:S(2)}) collective-permute-start(bf16[1,3,1024,128]{3,2,1,0:T(8,128)(2,1)S(1)} %pack.5.refs_0_), channel_id=1, source_target_pairs={{0,4},{4,0},{8,12},{12,8},{16,20},{20,16},{24,28},{28,24},{1,5},{5... | collective-permute-start | bytes 2359304 | tf_op jit(solution)/shard_map/swap_c0/ppermute | solution.py:678
  5.0 8.7 %copy-start.7 = (s32[8,8]{1,0:T(8,128)S(1)}, s32[8,8]{1,0:T(8,128)}, u32[]{:S(2)}) copy-start(s32[8,8]{1,0:T(8,128)} %constant.159.clone.1) | copy-start | bytes 772
  7.4 13.3 %collective-permute-start.1 = (bf16[1,1040,128]{2,1,0:T(8,128)(2,1)}, bf16[1,1040,128]{2,1,0:T(8,128)(2,1)S(1)}, u32[]{:S(2)}, u32[]{:S(2)}) collective-permute-start(bf16[1,1040,128]{2,1,0:T(8,128)(2,1)} %get-tuple-element.52.refs_0_.refs_2_), channel_id=1, source_target_pairs={{16,8},{20,12},{24,16},{28,20},{17,9},{21,13},{25,17},{29,21},{18,... | collective-permute-start | bytes 798728 | tf_op jit(solution)/shard_map/near_down_keep_c0/ppermute | solution.py:678
  9.7 11.1 %collective-permute-start.2 = (bf16[1,1040,128]{2,1,0:T(8,128)(2,1)}, bf16[1,1040,128]{2,1,0:T(8,128)(2,1)S(1)}, u32[]{:S(2)}, u32[]{:S(2)}) collective-permute-start(bf16[1,1040,128]{2,1,0:T(8,128)(2,1)} %get-tuple-element.52.refs_0_.refs_2_), channel_id=1, source_target_pairs={{24,8},{28,12},{25,9},{29,13},{26,10},{30,14},{27,11},{31,15}} | collective-permute-start | bytes 798728 | tf_op jit(solution)/shard_map/far_down_keep_c0/ppermute | solution.py:678
  16.8 0.9 copy-start.3
  17.7 16.8 %collective-permute-start.4 = (bf16[1,2,1024,128]{3,2,1,0:T(8,128)(2,1)S(1)}, bf16[1,2,1024,128]{3,2,1,0:T(8,128)(2,1)}, u32[]{:S(2)}, u32[]{:S(2)}) collective-permute-start(bf16[1,2,1024,128]{3,2,1,0:T(8,128)(2,1)S(1)} %get-tuple-element.55.refs_6_.refs_4_), channel_id=1, source_target_pairs={{0,8},{4,12},{1,9},{5,13},{2,10},{6,14},{3,11},{7,15}} | collective-permute-start | bytes 1572872 | tf_op jit(solution)/shard_map/lift_keep_c0/ppermute | solution.py:678
  19.2 20.7 %collective-permute-start.5 = (bf16[1,3,1024,128]{3,2,1,0:T(8,128)(2,1)}, bf16[1,3,1024,128]{3,2,1,0:T(8,128)(2,1)S(1)}, u32[]{:S(2)}, u32[]{:S(2)}) collective-permute-start(bf16[1,3,1024,128]{3,2,1,0:T(8,128)(2,1)} %get-tuple-element.57), channel_id=1, source_target_pairs={{0,4},{4,0},{8,12},{12,8},{16,20},{20,16},{24,28},{28,24},{1,5},{5... | collective-permute-start | bytes 2359304 | tf_op jit(solution)/shard_map/swap_c1/ppermute | solution.py:678
  24.1 1.1 copy-start.4
  26.2 21.8 %collective-permute-start.8 = (bf16[1,2,1024,128]{3,2,1,0:T(8,128)(2,1)}, bf16[1,2,1024,128]{3,2,1,0:T(8,128)(2,1)}, u32[]{:S(2)}, u32[]{:S(2)}) collective-permute-start(bf16[1,2,1024,128]{3,2,1,0:T(8,128)(2,1)} %get-tuple-element.59), channel_id=1, source_target_pairs={{0,8},{4,12},{1,9},{5,13},{2,10},{6,14},{3,11},{7,15}} | collective-permute-start | bytes 1572872 | tf_op jit(solution)/shard_map/lift_recv_c0/ppermute | solution.py:678
  27.7 17.6 %collective-permute-start.6 = (bf16[1,1024,128]{2,1,0:T(8,128)(2,1)}, bf16[1,1024,128]{2,1,0:T(8,128)(2,1)}, u32[]{:S(2)}, u32[]{:S(2)}) collective-permute-start(bf16[1,1024,128]{2,1,0:T(8,128)(2,1)} %get-tuple-element.54.refs_0_), channel_id=1, source_target_pairs={{16,8},{20,12},{24,16},{28,20},{17,9},{21,13},{25,17},{29,21},{18,... | collective-permute-start | bytes 786440 | tf_op jit(solution)/shard_map/near_down_recv_c0/ppermute | solution.py:678
  30.8 16.3 %collective-permute-start.7 = (bf16[1,1024,128]{2,1,0:T(8,128)(2,1)}, bf16[1,1024,128]{2,1,0:T(8,128)(2,1)}, u32[]{:S(2)}, u32[]{:S(2)}) collective-permute-start(bf16[1,1024,128]{2,1,0:T(8,128)(2,1)} %get-tuple-element.54.refs_0_), channel_id=1, source_target_pairs={{24,8},{28,12},{25,9},{29,13},{26,10},{30,14},{27,11},{31,15}} | collective-permute-start | bytes 786440 | tf_op jit(solution)/shard_map/far_down_recv_c0/ppermute | solution.py:678
  37.2 0.9 copy-start
  38.1 18.2 %collective-permute-start.9 = (bf16[1,3,1024,128]{3,2,1,0:T(8,128)(2,1)}, bf16[1,3,1024,128]{3,2,1,0:T(8,128)(2,1)S(1)}, u32[]{:S(2)}, u32[]{:S(2)}) collective-permute-start(bf16[1,3,1024,128]{3,2,1,0:T(8,128)(2,1)} %get-tuple-element.61), channel_id=1, source_target_pairs={{0,4},{4,0},{8,12},{12,8},{16,20},{20,16},{24,28},{28,24},{1,5},{5... | collective-permute-start | bytes 2359304 | tf_op jit(solution)/shard_map/swap_c2/ppermute | solution.py:678
  39.9 1.1 copy-start.1
  41.0 1.1 copy-start.5
  42.4 22.3 %collective-permute-start.10 = (bf16[2,1,1024,128]{3,2,1,0:T(8,128)(2,1)S(1)}, bf16[2,1,1024,128]{3,2,1,0:T(8,128)(2,1)S(1)}, u32[]{:S(2)}, u32[]{:S(2)}) collective-permute-start(bf16[2,1,1024,128]{3,2,1,0:T(8,128)(2,1)S(1)} %get-tuple-element.58.refs_0_), channel_id=1, source_target_pairs={{16,8},{20,12},{24,16},{28,20},{17,9},{21,13},{25,17},{29,21},{18,... | collective-permute-start | bytes 1572872 | tf_op jit(solution)/shard_map/near_down_c1/ppermute | solution.py:678
  45.3 21.2 %collective-permute-start.11 = (bf16[2,1,1024,128]{3,2,1,0:T(8,128)(2,1)S(1)}, bf16[2,1,1024,128]{3,2,1,0:T(8,128)(2,1)S(1)}, u32[]{:S(2)}, u32[]{:S(2)}) collective-permute-start(bf16[2,1,1024,128]{3,2,1,0:T(8,128)(2,1)S(1)} %get-tuple-element.58.refs_0_), channel_id=1, source_target_pairs={{24,8},{28,12},{25,9},{29,13},{26,10},{30,14},{27,11},{31,15}} | collective-permute-start | bytes 1572872 | tf_op jit(solution)/shard_map/far_down_c1/ppermute | solution.py:678
  47.1 10.5 %copy-start.2 = (bf16[1,3,1024,128]{3,2,1,0:T(8,128)(2,1)S(1)}, bf16[1,3,1024,128]{3,2,1,0:T(8,128)(2,1)}, u32[]{:S(2)}) copy-start(bf16[1,3,1024,128]{3,2,1,0:T(8,128)(2,1)} %copy-done) | copy-start | bytes 2359300
  47.1 20.9 %collective-permute-start.12 = (bf16[2,1,2,1024,128]{4,3,2,1,0:T(8,128)(2,1)S(1)}, bf16[2,1,2,1024,128]{4,3,2,1,0:T(8,128)(2,1)S(1)}, u32[]{:S(2)}, u32[]{:S(2)}) collective-permute-start(bf16[2,1,2,1024,128]{4,3,2,1,0:T(8,128)(2,1)S(1)} %get-tuple-element.65), channel_id=1, source_target_pairs={{0,8},{4,12},{1,9},{5,13},{2,10},{6,14},{3,11},{7,15}} | collective-permute-start | bytes 3145736 | tf_op jit(solution)/shard_map/lift_c1/ppermute | solution.py:678
  50.1 19.7 %collective-permute-start.13 = (bf16[1,1056,256]{2,1,0:T(8,128)(2,1)S(1)}, bf16[1,1056,256]{2,1,0:T(8,128)(2,1)S(1)}, u32[]{:S(2)}, u32[]{:S(2)}) collective-permute-start(bf16[1,1056,256]{2,1,0:T(8,128)(2,1)S(1)} %get-tuple-element.60.refs_0_), channel_id=1, source_target_pairs={{8,16},{12,20},{16,24},{20,28},{9,17},{13,21},{17,25},{21,29},{10,... | collective-permute-start | bytes 1622024 | tf_op jit(solution)/shard_map/near_up_c0/ppermute | solution.py:678
  56.3 24.0 %collective-permute-start.14 = (bf16[1,1056,256]{2,1,0:T(8,128)(2,1)S(1)}, bf16[1,1056,256]{2,1,0:T(8,128)(2,1)S(1)}, u32[]{:S(2)}, u32[]{:S(2)}) collective-permute-start(bf16[1,1056,256]{2,1,0:T(8,128)(2,1)S(1)} %get-tuple-element.68), channel_id=1, source_target_pairs={{8,24},{12,28},{9,25},{13,29},{10,26},{14,30},{11,27},{15,31}} | collective-permute-start | bytes 1622024 | tf_op jit(solution)/shard_map/far_up_c0/ppermute | solution.py:678
  62.5 6.3 %copy-start.6 = (bf16[1,3,1024,128]{3,2,1,0:T(8,128)(2,1)S(1)}, bf16[1,3,1024,128]{3,2,1,0:T(8,128)(2,1)}, u32[]{:S(2)}) copy-start(bf16[1,3,1024,128]{3,2,1,0:T(8,128)(2,1)} %copy-done.3) | copy-start | bytes 2359300
  64.7 23.1 %collective-permute-start.16 = (bf16[2,1,1024,128]{3,2,1,0:T(8,128)(2,1)S(1)}, bf16[2,1,1024,128]{3,2,1,0:T(8,128)(2,1)S(1)}, u32[]{:S(2)}, u32[]{:S(2)}) collective-permute-start(bf16[2,1,1024,128]{3,2,1,0:T(8,128)(2,1)S(1)} %get-tuple-element.62.refs_0_), channel_id=1, source_target_pairs={{16,8},{20,12},{24,16},{28,20},{17,9},{21,13},{25,17},{29,21},{18,... | collective-permute-start | bytes 1572872 | tf_op jit(solution)/shard_map/near_down_c2/ppermute | solution.py:678
  66.5 19.7 %collective-permute-start.15 = (bf16[1,3,1024,128]{3,2,1,0:T(8,128)(2,1)S(1)}, bf16[1,3,1024,128]{3,2,1,0:T(8,128)(2,1)S(1)}, u32[]{:S(2)}, u32[]{:S(2)}) collective-permute-start(bf16[1,3,1024,128]{3,2,1,0:T(8,128)(2,1)S(1)} %get-tuple-element.71), channel_id=1, source_target_pairs={{0,4},{4,0},{8,12},{12,8},{16,20},{20,16},{24,28},{28,24},{1,5},{5... | collective-permute-start | bytes 2359304 | tf_op jit(solution)/shard_map/swap_c3/ppermute | solution.py:678
  68.0 21.6 %collective-permute-start.18 = (bf16[2,1,2,1024,128]{4,3,2,1,0:T(8,128)(2,1)S(1)}, bf16[2,1,2,1024,128]{4,3,2,1,0:T(8,128)(2,1)S(1)}, u32[]{:S(2)}, u32[]{:S(2)}) collective-permute-start(bf16[2,1,2,1024,128]{4,3,2,1,0:T(8,128)(2,1)S(1)} %get-tuple-element.73), channel_id=1, source_target_pairs={{0,8},{4,12},{1,9},{5,13},{2,10},{6,14},{3,11},{7,15}} | collective-permute-start | bytes 3145736 | tf_op jit(solution)/shard_map/lift_c2/ppermute | solution.py:678
  69.8 19.1 %collective-permute-start.17 = (bf16[2,1,1024,128]{3,2,1,0:T(8,128)(2,1)S(1)}, bf16[2,1,1024,128]{3,2,1,0:T(8,128)(2,1)S(1)}, u32[]{:S(2)}, u32[]{:S(2)}) collective-permute-start(bf16[2,1,1024,128]{3,2,1,0:T(8,128)(2,1)S(1)} %get-tuple-element.62.refs_0_), channel_id=1, source_target_pairs={{24,8},{28,12},{25,9},{29,13},{26,10},{30,14},{27,11},{31,15}} | collective-permute-start | bytes 1572872 | tf_op jit(solution)/shard_map/far_down_c2/ppermute | solution.py:678
  80.3 24.5 %collective-permute-start.19 = (bf16[1,1056,256]{2,1,0:T(8,128)(2,1)S(1)}, bf16[1,1056,256]{2,1,0:T(8,128)(2,1)S(1)}, u32[]{:S(2)}, u32[]{:S(2)}) collective-permute-start(bf16[1,1056,256]{2,1,0:T(8,128)(2,1)S(1)} %get-tuple-element.66.refs_0_), channel_id=1, source_target_pairs={{8,16},{12,20},{16,24},{20,28},{9,17},{13,21},{17,25},{21,29},{10,... | collective-permute-start | bytes 1622024 | tf_op jit(solution)/shard_map/near_up_c1/ppermute | solution.py:678
  86.2 19.9 %collective-permute-start.20 = (bf16[1,1056,256]{2,1,0:T(8,128)(2,1)S(1)}, bf16[1,1056,256]{2,1,0:T(8,128)(2,1)S(1)}, u32[]{:S(2)}, u32[]{:S(2)}) collective-permute-start(bf16[1,1056,256]{2,1,0:T(8,128)(2,1)S(1)} %get-tuple-element.77), channel_id=1, source_target_pairs={{8,24},{12,28},{9,25},{13,29},{10,26},{14,30},{11,27},{15,31}} | collective-permute-start | bytes 1622024 | tf_op jit(solution)/shard_map/far_up_c1/ppermute | solution.py:678
  87.8 24.4 %collective-permute-start.21 = (bf16[1,1024,128]{2,1,0:T(8,128)(2,1)S(1)}, bf16[1,1024,128]{2,1,0:T(8,128)(2,1)S(1)}, u32[]{:S(2)}, u32[]{:S(2)}) collective-permute-start(bf16[1,1024,128]{2,1,0:T(8,128)(2,1)S(1)} %get-tuple-element.80), channel_id=1, source_target_pairs={{0,4},{4,0},{8,12},{12,8},{16,20},{20,16},{24,28},{28,24},{1,5},{5... | collective-permute-start | bytes 786440 | tf_op jit(solution)/shard_map/back_c0/ppermute | solution.py:678
  88.9 24.6 %collective-permute-start.24 = (bf16[2,1,2,1024,128]{4,3,2,1,0:T(8,128)(2,1)S(1)}, bf16[2,1,2,1024,128]{4,3,2,1,0:T(8,128)(2,1)S(1)}, u32[]{:S(2)}, u32[]{:S(2)}) collective-permute-start(bf16[2,1,2,1024,128]{4,3,2,1,0:T(8,128)(2,1)S(1)} %get-tuple-element.81), channel_id=1, source_target_pairs={{0,8},{4,12},{1,9},{5,13},{2,10},{6,14},{3,11},{7,15}} | collective-permute-start | bytes 3145736 | tf_op jit(solution)/shard_map/lift_c3/ppermute | solution.py:678
  89.7 23.9 %collective-permute-start.22 = (bf16[2,1,1024,128]{3,2,1,0:T(8,128)(2,1)S(1)}, bf16[2,1,1024,128]{3,2,1,0:T(8,128)(2,1)S(1)}, u32[]{:S(2)}, u32[]{:S(2)}) collective-permute-start(bf16[2,1,1024,128]{3,2,1,0:T(8,128)(2,1)S(1)} %get-tuple-element.72.refs_0_), channel_id=1, source_target_pairs={{16,8},{20,12},{24,16},{28,20},{17,9},{21,13},{25,17},{29,21},{18,... | collective-permute-start | bytes 1572872 | tf_op jit(solution)/shard_map/near_down_c3/ppermute | solution.py:678
  104.8 8.7 %collective-permute-start.23 = (bf16[2,1,1024,128]{3,2,1,0:T(8,128)(2,1)S(1)}, bf16[2,1,1024,128]{3,2,1,0:T(8,128)(2,1)S(1)}, u32[]{:S(2)}, u32[]{:S(2)}) collective-permute-start(bf16[2,1,1024,128]{3,2,1,0:T(8,128)(2,1)S(1)} %get-tuple-element.72.refs_0_), channel_id=1, source_target_pairs={{24,8},{28,12},{25,9},{29,13},{26,10},{30,14},{27,11},{31,15}} | collective-permute-start | bytes 1572872 | tf_op jit(solution)/shard_map/far_down_c3/ppermute | solution.py:678
  106.1 24.4 %collective-permute-start.25 = (bf16[1,1056,256]{2,1,0:T(8,128)(2,1)S(1)}, bf16[1,1056,256]{2,1,0:T(8,128)(2,1)S(1)}, u32[]{:S(2)}, u32[]{:S(2)}) collective-permute-start(bf16[1,1056,256]{2,1,0:T(8,128)(2,1)S(1)} %get-tuple-element.74.refs_0_), channel_id=1, source_target_pairs={{8,16},{12,20},{16,24},{20,28},{9,17},{13,21},{17,25},{21,29},{10,... | collective-permute-start | bytes 1622024 | tf_op jit(solution)/shard_map/near_up_c2/ppermute | solution.py:678
  112.2 18.3 %collective-permute-start.26 = (bf16[1,1056,256]{2,1,0:T(8,128)(2,1)S(1)}, bf16[1,1056,256]{2,1,0:T(8,128)(2,1)S(1)}, u32[]{:S(2)}, u32[]{:S(2)}) collective-permute-start(bf16[1,1056,256]{2,1,0:T(8,128)(2,1)S(1)} %get-tuple-element.86), channel_id=1, source_target_pairs={{8,24},{12,28},{9,25},{13,29},{10,26},{14,30},{11,27},{15,31}} | collective-permute-start | bytes 1622024 | tf_op jit(solution)/shard_map/far_up_c2/ppermute | solution.py:678
  118.2 20.4 %collective-permute-start.28 = (bf16[1,528,256]{2,1,0:T(8,128)(2,1)S(1)}, bf16[1,528,256]{2,1,0:T(8,128)(2,1)S(1)}, u32[]{:S(2)}, u32[]{:S(2)}) collective-permute-start(bf16[1,528,256]{2,1,0:T(8,128)(2,1)S(1)} %get-tuple-element.90), channel_id=1, source_target_pairs={{0,4},{4,0},{8,12},{12,8},{16,20},{20,16},{24,28},{28,24},{1,5},{5... | collective-permute-start | bytes 811016 | tf_op jit(solution)/shard_map/back_own_c3/ppermute | solution.py:678
  120.4 20.6 %collective-permute-start.29 = (bf16[1,528,256]{2,1,0:T(8,128)(2,1)S(1)}, bf16[1,528,256]{2,1,0:T(8,128)(2,1)S(1)}, u32[]{:S(2)}, u32[]{:S(2)}) collective-permute-start(bf16[1,528,256]{2,1,0:T(8,128)(2,1)S(1)} %get-tuple-element.82.refs_0_), channel_id=1, source_target_pairs={{8,16},{12,20},{16,24},{20,28},{9,17},{13,21},{17,25},{21,29},{10,... | collective-permute-start | bytes 811016 | tf_op jit(solution)/shard_map/near_up_same_c3/ppermute | solution.py:678
  131.5 25.6 %copy-start.9 = (bf16[1024]{0:T(1024)(128)(2,1)S(1)}, bf16[1024]{0:T(1024)(128)(2,1)}, u32[]{:S(2)}) copy-start(bf16[1024]{0:T(1024)(128)(2,1)} %param.9) | copy-start | bytes 6148
  131.6 5.7 %collective-permute-start.27 = (f32[4,256]{1,0:T(4,128)S(1)}, f32[4,256]{1,0:T(4,128)S(1)}, u32[]{:S(2)}, u32[]{:S(2)}) collective-permute-start(f32[4,256]{1,0:T(4,128)S(1)} %slice.23), channel_id=1, source_target_pairs={{0,4},{4,0},{8,12},{12,8},{16,20},{20,16},{24,28},{28,24},{1,5},{5... | collective-permute-start | bytes 12296 | tf_op jit(solution)/shard_map/squares_swap/ppermute | solution.py:678
  134.6 18.7 %collective-permute-start.30 = (bf16[1,528,256]{2,1,0:T(8,128)(2,1)S(1)}, bf16[1,528,256]{2,1,0:T(8,128)(2,1)S(1)}, u32[]{:S(2)}, u32[]{:S(2)}) collective-permute-start(bf16[1,528,256]{2,1,0:T(8,128)(2,1)S(1)} %get-tuple-element.91), channel_id=1, source_target_pairs={{8,20},{12,16},{16,28},{20,24},{9,21},{13,17},{17,29},{21,25},{10,... | collective-permute-start | bytes 811016 | tf_op jit(solution)/shard_map/near_up_cross_c3/ppermute | solution.py:678
  135.9 17.4 %collective-permute-start.31 = (bf16[1,528,256]{2,1,0:T(8,128)(2,1)S(1)}, bf16[1,528,256]{2,1,0:T(8,128)(2,1)S(1)}, u32[]{:S(2)}, u32[]{:S(2)}) collective-permute-start(bf16[1,528,256]{2,1,0:T(8,128)(2,1)S(1)} %get-tuple-element.92), channel_id=1, source_target_pairs={{8,24},{12,28},{9,25},{13,29},{10,26},{14,30},{11,27},{15,31}} | collective-permute-start | bytes 811016 | tf_op jit(solution)/shard_map/far_up_same_c3/ppermute | solution.py:678
  137.2 16.1 %collective-permute-start.32 = (bf16[1,528,256]{2,1,0:T(8,128)(2,1)S(1)}, bf16[1,528,256]{2,1,0:T(8,128)(2,1)S(1)}, u32[]{:S(2)}, u32[]{:S(2)}) collective-permute-start(bf16[1,528,256]{2,1,0:T(8,128)(2,1)S(1)} %get-tuple-element.93), channel_id=1, source_target_pairs={{8,28},{12,24},{9,29},{13,25},{10,30},{14,26},{11,31},{15,27}} | collective-permute-start | bytes 811016 | tf_op jit(solution)/shard_map/far_up_cross_c3/ppermute | solution.py:678
  138.5 20.7 %collective-permute-start.33 = (bf16[1,1024,128]{2,1,0:T(8,128)(2,1)S(1)}, bf16[1,1024,128]{2,1,0:T(8,128)(2,1)S(1)}, u32[]{:S(2)}, u32[]{:S(2)}) collective-permute-start(bf16[1,1024,128]{2,1,0:T(8,128)(2,1)S(1)} %get-tuple-element.95), channel_id=1, source_target_pairs={{0,4},{4,0},{8,12},{12,8},{16,20},{20,16},{24,28},{28,24},{1,5},{5... | collective-permute-start | bytes 786440 | tf_op jit(solution)/shard_map/back_c1/ppermute | solution.py:678
  140.9 18.3 %collective-permute-start.34 = (bf16[1,1024,128]{2,1,0:T(8,128)(2,1)S(1)}, bf16[1,1024,128]{2,1,0:T(8,128)(2,1)S(1)}, u32[]{:S(2)}, u32[]{:S(2)}) collective-permute-start(bf16[1,1024,128]{2,1,0:T(8,128)(2,1)S(1)} %get-tuple-element.96), channel_id=1, source_target_pairs={{0,4},{4,0},{8,12},{12,8},{16,20},{20,16},{24,28},{28,24},{1,5},{5... | collective-permute-start | bytes 786440 | tf_op jit(solution)/shard_map/back_c2/ppermute | solution.py:678
  154.4 1.2 collective-permute-start.35
  155.6 3.6 %collective-permute-start.36 = (f32[4,256]{1,0:T(4,128)S(1)}, f32[4,256]{1,0:T(4,128)S(1)}, u32[]{:S(2)}, u32[]{:S(2)}) collective-permute-start(f32[4,256]{1,0:T(4,128)S(1)} %add.296), channel_id=1, source_target_pairs={{0,2},{1,3},{2,0},{3,1},{4,6},{5,7},{6,4},{7,5},{8,10},{9,11},{10,... | collective-permute-start | bytes 12296 | tf_op jit(solution)/shard_map/ppermute | solution.py:849

commit v10 on v9

--- a/solution.py
+++ b/solution.py
@@ -131,8 +131,8 @@
 SPLIT = (True, False, False, False)
 ORDER = (
     ("p", 0),
+    ("p", 1),
     ("w", "plan"),
-    ("p", 1),
     ("w", "near_down_keep_c0"),
     ("w", "far_down_keep_c0"),
     ("j", 0),
@@ -151,7 +151,6 @@
     ("s", 2),
     ("m", 1),
     ("a", 2),
-    ("w", "back_c0"),
     ("s", 3),
     ("a", 3),
     ("m", 2),
@@ -611,7 +610,8 @@
 def finish_kernel(per_dev, sizes, place, *refs):
     n = len(sizes)
     kept, returned = refs[:n], refs[n : 2 * n]
-    squares_ref, gain_ref, out_ref = refs[2 * n :]
+    squares_ref, gain_ref, out_ref, scr, sems = refs[2 * n :]
+    copies = []
     block_rows = squares_ref.shape[1]
     half = sum(sizes)
     factor = lax.rsqrt(squares_ref[...] / (HEADS * HD) + 1e-06)
@@ -625,8 +625,13 @@
                     start = pl.multiple_of((place[side] * half + head) * HD, HD)
                     gain = gain_ref[:, pl.ds(start, HD)].astype(jnp.float32)
                     value = piece[h, rows, :].astype(jnp.float32) * column * gain
-                    out_ref[rows, pl.ds(start, HD)] = value.astype(out_ref.dtype)
+                    scr[rows, pl.ds(start, HD)] = value.astype(out_ref.dtype)
                     head += 1
+        copy = pltpu.make_async_copy(scr.at[rows], out_ref.at[rows], sems.at[b])
+        copy.start()
+        copies.append(copy)
+    for copy in copies:
+        copy.wait()
 
 
 def finish_call(place, kept, returned, squares, gain, per_dev):
@@ -636,7 +641,11 @@
         partial(finish_kernel, per_dev, [k.shape[0] for k in kept]),
         out_shape=jax.ShapeDtypeStruct((rows, width), jnp.bfloat16),
         in_specs=[pl.BlockSpec(memory_space=pltpu.SMEM)] + [vmem] * (2 * len(kept) + 2),
-        out_specs=vmem,
+        out_specs=pl.BlockSpec(memory_space=pltpu.HBM),
+        scratch_shapes=[
+            pltpu.VMEM((rows, width), jnp.bfloat16),
+            pltpu.SemaphoreType.DMA((per_dev,)),
+        ],
         compiler_params=pltpu.CompilerParams(vmem_limit_bytes=VMEM_LIMIT),
         cost_estimate=cost("finish"),
         name="finish",

time: 163 us -> 162 us (level)
  waiting for transfers between devices: 35.8 us -> 34.1 us
    ppermute x35, waiting for transfers between devices: 32.6 us -> 30.9 us  [to(): sent[name] = lax.ppermute(array, 'ctx', pairs)]
    unnamed x20 -> x22, local copies, waits for them, and re-layouts: 5.2 us -> 6.07 us
where the time goes in v10:
time: 162 us
  starting transfers between devices  73.2 us (45%)
  Pallas kernels  40.4 us (25%)
  waiting for transfers between devices  34.1 us (21%)
  local copies, waits for them, and re-layouts  7.13 us (4%)
  between operations  3.42 us (2%)
  other arithmetic  3.39 us (2%)
    ppermute x35, starting transfers between devices, to(): sent[name] = lax.ppermute(array, 'ctx', pairs)  71.6 us
    ppermute x35, waiting for transfers between devices, to(): sent[name] = lax.ppermute(array, 'ctx', pairs)  30.9 us
    pallas_call x8, Pallas kernels, attention_call(): pl.pallas_call(ordered(partial(attention_kernel, (heads, per_dev, block_r...  20.8 us
    pallas_call x5, Pallas kernels, pack_call(): pl.pallas_call(ordered(partial(pack_kernel, (sides, head, half, rows, not...  11.4 us
    unnamed x22, local copies, waits for them, and re-layouts  6.07 us
  transfers between devices with their start and end apart: 37, of which 10 were waited for; matrix products, arithmetic and copies ran while one was open for 3% of the time, Pallas kernels for 24%

profile of v10, /device:TPU:24, one launch (start us, length us, event | category | flops | bytes accessed | tf_op | source)
XLA Modules:
  0.0 161.6 jit_solution(769195004827145047)
XLA Ops:
  0.0 1.5 collective-permute-start
  1.6 2.0 %pack.5.refs_0_ = bf16[1,3,1024,128]{3,2,1,0:T(8,128)(2,1)S(1)} custom-call(s32[2]{0:T(128)S(1)} %pad_add_fusion.2.refs_0_.refs_1_.refs_3_.place, bf16[1024,1024]{1,0:T(8,128)(2,1)} %refs_2_.7, bf16[1024,1024]{1,0:T(8,128)(2,1)} %refs_3_.7, bf16[1024,1024]{1,0:T(8,128)(2,1)} %refs_4_.7), custom_call_target="tpu_custom_call" | custom-call | flops 2000000000 | bytes 6800001 | tf_op jit(solution)/shard_map/pack/pallas_call | solution.py:425
  5.0 2.3 %pack.6 = (bf16[1,1040,128]{2,1,0:T(8,128)(2,1)}, bf16[1,2,1024,128]{3,2,1,0:T(8,128)(2,1)S(1)}) custom-call(bf16[1,3,1024,128]{3,2,1,0:T(8,128)(2,1)S(1)} %pack.5.refs_0_, s32[2]{0:T(128)S(1)} %pad_add_fusion.2.refs_0_.refs_1_.refs_3_.place, bf16[1024,1024]{1,0:T(8,128)(2,1)} %refs_2_.7, bf16[1024,1024]{1,0:T(8,128)(2,1)} %refs_3_.7, ...), custom_call_target="tpu_custom_call" | custom-call | flops 2000000000 | bytes 6800001 | tf_op jit(solution)/shard_map/pack/pallas_call | solution.py:425
  7.4 2.4 %collective-permute-start.1 = (bf16[1,1040,128]{2,1,0:T(8,128)(2,1)}, bf16[1,1040,128]{2,1,0:T(8,128)(2,1)S(1)}, u32[]{:S(2)}, u32[]{:S(2)}) collective-permute-start(bf16[1,1040,128]{2,1,0:T(8,128)(2,1)} %get-tuple-element.52.refs_0_.refs_2_), channel_id=1, source_target_pairs={{16,8},{20,12},{24,16},{28,20},{17,9},{21,13},{25,17},{29,21},{18,... | collective-permute-start | bytes 798728 | tf_op jit(solution)/shard_map/near_down_keep_c0/ppermute | solution.py:687
  9.7 1.3 collective-permute-start.2
  13.2 2.2 %pack.7 = (bf16[1,3,1024,128]{3,2,1,0:T(8,128)(2,1)S(1)}, bf16[1,3,1024,128]{3,2,1,0:T(8,128)(2,1)S(1)}) custom-call(bf16[1,1040,128]{2,1,0:T(8,128)(2,1)} %get-tuple-element.52.refs_0_.refs_2_, s32[2]{0:T(128)S(1)} %pad_add_fusion.2.refs_0_.refs_1_.refs_3_.place, bf16[1024,1024]{1,0:T(8,128)(2,1)} %refs_2_.7, bf16[1024,1024]{1,0:T(8,128)(2,1)} %refs_3_.7, ...), custom_call_target="tpu_custom_call" | custom-call | flops 2000000000 | bytes 6800001 | tf_op jit(solution)/shard_map/pack/pallas_call | solution.py:425
  18.0 1.5 collective-permute-start.4
  19.4 1.5 collective-permute-start.5
  26.2 1.5 collective-permute-start.8
  27.7 3.1 %collective-permute-start.6 = (bf16[1,1024,128]{2,1,0:T(8,128)(2,1)}, bf16[1,1024,128]{2,1,0:T(8,128)(2,1)}, u32[]{:S(2)}, u32[]{:S(2)}) collective-permute-start(bf16[1,1024,128]{2,1,0:T(8,128)(2,1)} %get-tuple-element.54.refs_0_), channel_id=1, source_target_pairs={{16,8},{20,12},{24,16},{28,20},{17,9},{21,13},{25,17},{29,21},{18,... | collective-permute-start | bytes 786440 | tf_op jit(solution)/shard_map/near_down_recv_c0/ppermute | solution.py:687
  30.8 3.6 %collective-permute-start.7 = (bf16[1,1024,128]{2,1,0:T(8,128)(2,1)}, bf16[1,1024,128]{2,1,0:T(8,128)(2,1)}, u32[]{:S(2)}, u32[]{:S(2)}) collective-permute-start(bf16[1,1024,128]{2,1,0:T(8,128)(2,1)} %get-tuple-element.54.refs_0_), channel_id=1, source_target_pairs={{24,8},{28,12},{25,9},{29,13},{26,10},{30,14},{27,11},{31,15}} | collective-permute-start | bytes 786440 | tf_op jit(solution)/shard_map/far_down_recv_c0/ppermute | solution.py:687
  34.4 2.7 %pack.8 = (bf16[1,3,1024,128]{3,2,1,0:T(8,128)(2,1)}, bf16[1,3,1024,128]{3,2,1,0:T(8,128)(2,1)S(1)}) custom-call(bf16[1,1024,128]{2,1,0:T(8,128)(2,1)} %get-tuple-element.54.refs_0_, bf16[1,2,1024,128]{3,2,1,0:T(8,128)(2,1)} %collective-permute-done.4.refs_1_.refs_8_.refs_5_, s32[129]{0:T(256)S(1)} %pad_add_fusion.1.refs_2_.refs_1_, ...), custom_call_target="tpu_custom_call" | custom-call | flops 2000000000 | bytes 6800001 | tf_op jit(solution)/shard_map/pack/pallas_call | solution.py:425
  38.0 1.5 collective-permute-start.9
  42.6 2.9 %collective-permute-start.10 = (bf16[2,1,1024,128]{3,2,1,0:T(8,128)(2,1)S(1)}, bf16[2,1,1024,128]{3,2,1,0:T(8,128)(2,1)S(1)}, u32[]{:S(2)}, u32[]{:S(2)}) collective-permute-start(bf16[2,1,1024,128]{3,2,1,0:T(8,128)(2,1)S(1)} %get-tuple-element.58.refs_0_), channel_id=1, source_target_pairs={{16,8},{20,12},{24,16},{28,20},{17,9},{21,13},{25,17},{29,21},{18,... | collective-permute-start | bytes 1572872 | tf_op jit(solution)/shard_map/near_down_c1/ppermute | solution.py:687
  45.5 1.6 collective-permute-start.11
  48.0 2.2 %served_attention.4 = (bf16[1,1056,256]{2,1,0:T(8,128)(2,1)S(1)}, bf16[1,1056,256]{2,1,0:T(8,128)(2,1)S(1)}) custom-call(bf16[2,1,1024,128]{3,2,1,0:T(8,128)(2,1)S(1)} %get-tuple-element.58.refs_0_, s32[129]{0:T(256)S(1)} %pad_add_fusion.1.refs_2_.refs_1_, bf16[1,1040,128]{2,1,0:T(8,128)(2,1)S(1)} %collective-permute-done.1.refs_2_, ...), custom_call_target="tpu_custom_call" | custom-call | flops 6000000000 | bytes 20400000 | tf_op jit(solution)/shard_map/served_attention/pallas_call | solution.py:350
  50.1 1.3 collective-permute-start.13
  51.4 4.9 %collective-permute-done.9.refs_2_.refs_5_.refs_3_ = bf16[1,3,1024,128]{3,2,1,0:T(8,128)(2,1)S(1)} collective-permute-done((bf16[1,3,1024,128]{3,2,1,0:T(8,128)(2,1)}, bf16[1,3,1024,128]{3,2,1,0:T(8,128)(2,1)S(1)}, u32[]{:S(2)}, u32[]{:S(2)}) %collective-permute-start.9) | collective-permute-done | bytes 786464 | tf_op jit(solution)/shard_map/swap_c2/ppermute | solution.py:687
  56.3 1.3 collective-permute-start.14
  57.9 4.6 %own_attention.4 = (f32[1,8,128,256]{3,2,1,0:T(8,128)S(1)}, f32[1,8,256]{2,1,0:T(8,128)S(1)}) custom-call(bf16[2,1,1024,128]{3,2,1,0:T(8,128)(2,1)S(1)} %get-tuple-element.62.refs_0_, s32[81]{0:T(128)S(1)} %pad_add_fusion.4.refs_1_, bf16[1,1040,128]{2,1,0:T(8,128)(2,1)} %get-tuple-element.52.refs_0_.refs_2_, ...), custom_call_target="tpu_custom_call" | custom-call | flops 5000000000 | bytes 17000000 | tf_op jit(solution)/shard_map/own_attention/pallas_call | solution.py:350
  62.5 2.2 %pack.9 = (bf16[1,3,1024,128]{3,2,1,0:T(8,128)(2,1)S(1)}, bf16[1,3,1024,128]{3,2,1,0:T(8,128)(2,1)S(1)}) custom-call(f32[1,8,256]{2,1,0:T(8,128)S(1)} %get-tuple-element.63.refs_0_.refs_4_, s32[2]{0:T(128)S(1)} %pad_add_fusion.2.refs_0_.refs_1_.refs_3_.place, bf16[1024,1024]{1,0:T(8,128)(2,1)} %refs_2_.7, bf16[1024,1024]{1,0:T(8,128)(2,1)} %refs_3_.7, ...), custom_call_target="tpu_custom_call" | custom-call | flops 2000000000 | bytes 6800001 | tf_op jit(solution)/shard_map/pack/pallas_call | solution.py:425
  64.7 1.8 %collective-permute-start.16 = (bf16[2,1,1024,128]{3,2,1,0:T(8,128)(2,1)S(1)}, bf16[2,1,1024,128]{3,2,1,0:T(8,128)(2,1)S(1)}, u32[]{:S(2)}, u32[]{:S(2)}) collective-permute-start(bf16[2,1,1024,128]{3,2,1,0:T(8,128)(2,1)S(1)} %get-tuple-element.62.refs_0_), channel_id=1, source_target_pairs={{16,8},{20,12},{24,16},{28,20},{17,9},{21,13},{25,17},{29,21},{18,... | collective-permute-start | bytes 1572872 | tf_op jit(solution)/shard_map/near_down_c2/ppermute | solution.py:687
  66.6 2.0 %collective-permute-start.15 = (bf16[1,3,1024,128]{3,2,1,0:T(8,128)(2,1)S(1)}, bf16[1,3,1024,128]{3,2,1,0:T(8,128)(2,1)S(1)}, u32[]{:S(2)}, u32[]{:S(2)}) collective-permute-start(bf16[1,3,1024,128]{3,2,1,0:T(8,128)(2,1)S(1)} %get-tuple-element.71), channel_id=1, source_target_pairs={{0,4},{4,0},{8,12},{12,8},{16,20},{20,16},{24,28},{28,24},{1,5},{5... | collective-permute-start | bytes 2359304 | tf_op jit(solution)/shard_map/swap_c3/ppermute | solution.py:687
  70.4 10.2 %collective-permute-start.17 = (bf16[2,1,1024,128]{3,2,1,0:T(8,128)(2,1)S(1)}, bf16[2,1,1024,128]{3,2,1,0:T(8,128)(2,1)S(1)}, u32[]{:S(2)}, u32[]{:S(2)}) collective-permute-start(bf16[2,1,1024,128]{3,2,1,0:T(8,128)(2,1)S(1)} %get-tuple-element.62.refs_0_), channel_id=1, source_target_pairs={{24,8},{28,12},{25,9},{29,13},{26,10},{30,14},{27,11},{31,15}} | collective-permute-start | bytes 1572872 | tf_op jit(solution)/shard_map/far_down_c2/ppermute | solution.py:687
  80.5 1.3 collective-permute-start.19
  82.9 3.6 %own_attention.5 = (f32[1,8,128,256]{3,2,1,0:T(8,128)S(1)}, f32[1,8,256]{2,1,0:T(8,128)S(1)}) custom-call(bf16[1,1024,128]{2,1,0:T(8,128)(2,1)S(1)} %get-tuple-element.69.refs_0_, s32[81]{0:T(128)S(1)} %pad_add_fusion.4.refs_1_, bf16[1,3,1024,128]{3,2,1,0:T(8,128)(2,1)S(1)} %copy-done.7, ...), custom_call_target="tpu_custom_call" | custom-call | flops 5000000000 | bytes 17000000 | tf_op jit(solution)/shard_map/own_attention/pallas_call | solution.py:350
  86.5 1.3 collective-permute-start.20
  88.1 7.6 %collective-permute-start.21 = (bf16[2,1,1024,128]{3,2,1,0:T(8,128)(2,1)S(1)}, bf16[2,1,1024,128]{3,2,1,0:T(8,128)(2,1)S(1)}, u32[]{:S(2)}, u32[]{:S(2)}) collective-permute-start(bf16[2,1,1024,128]{3,2,1,0:T(8,128)(2,1)S(1)} %get-tuple-element.72.refs_0_), channel_id=1, source_target_pairs={{16,8},{20,12},{24,16},{28,20},{17,9},{21,13},{25,17},{29,21},{18,... | collective-permute-start | bytes 1572872 | tf_op jit(solution)/shard_map/near_down_c3/ppermute | solution.py:687
  95.7 3.2 %collective-permute-start.22 = (bf16[2,1,1024,128]{3,2,1,0:T(8,128)(2,1)S(1)}, bf16[2,1,1024,128]{3,2,1,0:T(8,128)(2,1)S(1)}, u32[]{:S(2)}, u32[]{:S(2)}) collective-permute-start(bf16[2,1,1024,128]{3,2,1,0:T(8,128)(2,1)S(1)} %get-tuple-element.72.refs_0_), channel_id=1, source_target_pairs={{24,8},{28,12},{25,9},{29,13},{26,10},{30,14},{27,11},{31,15}} | collective-permute-start | bytes 1572872 | tf_op jit(solution)/shard_map/far_down_c3/ppermute | solution.py:687
  100.7 6.1 %collective-permute-done.19.refs_5_ = bf16[1,1056,256]{2,1,0:T(8,128)(2,1)S(1)} collective-permute-done((bf16[1,1056,256]{2,1,0:T(8,128)(2,1)S(1)}, bf16[1,1056,256]{2,1,0:T(8,128)(2,1)S(1)}, u32[]{:S(2)}, u32[]{:S(2)}) %collective-permute-start.19) | collective-permute-done | bytes 540704 | tf_op jit(solution)/shard_map/near_up_c1/ppermute | solution.py:687
  106.8 1.3 collective-permute-start.24
  108.1 1.3 collective-permute-start.25
  110.4 3.7 %own_attention.6 = (f32[1,8,128,256]{3,2,1,0:T(8,128)S(1)}, f32[1,8,256]{2,1,0:T(8,128)S(1)}) custom-call(bf16[1,1024,128]{2,1,0:T(8,128)(2,1)S(1)} %get-tuple-element.78.refs_0_.refs_1_, s32[81]{0:T(128)S(1)} %pad_add_fusion.4.refs_1_, bf16[1,3,1024,128]{3,2,1,0:T(8,128)(2,1)S(1)} %copy-done.3, ...), custom_call_target="tpu_custom_call" | custom-call | flops 5000000000 | bytes 17000000 | tf_op jit(solution)/shard_map/own_attention/pallas_call | solution.py:350
  115.2 3.6 %own_attention.7 = (f32[1,4,128,256]{3,2,1,0:T(8,128)S(1)}, f32[1,4,256]{2,1,0:T(4,128)S(1)}, bf16[1,528,256]{2,1,0:T(8,128)(2,1)S(1)}) custom-call(bf16[1,528,256]{2,1,0:T(8,128)(2,1)S(1)} %get-tuple-element.81.refs_0_, s32[81]{0:T(128)S(1)} %pad_add_fusion.4.refs_1_, bf16[1,3,1024,128]{3,2,1,0:T(8,128)(2,1)S(1)} %get-tuple-element.64.refs_0_.refs_1_.refs_4_.refs_2_, ...), custom_call_target="tpu_custom_call" | custom-call | flops 5000000000 | bytes 17000000 | tf_op jit(solution)/shard_map/own_attention/pallas_call | solution.py:350
  118.8 1.8 %collective-permute-start.27 = (bf16[1,528,256]{2,1,0:T(8,128)(2,1)S(1)}, bf16[1,528,256]{2,1,0:T(8,128)(2,1)S(1)}, u32[]{:S(2)}, u32[]{:S(2)}) collective-permute-start(bf16[1,528,256]{2,1,0:T(8,128)(2,1)S(1)} %get-tuple-element.89), channel_id=1, source_target_pairs={{0,4},{4,0},{8,12},{12,8},{16,20},{20,16},{24,28},{28,24},{1,5},{5... | collective-permute-start | bytes 811016 | tf_op jit(solution)/shard_map/back_own_c3/ppermute | solution.py:687
  120.6 1.3 collective-permute-start.28
  121.9 1.3 collective-permute-start.29
  123.2 7.9 %collective-permute-done.24.refs_5_ = bf16[1,1056,256]{2,1,0:T(8,128)(2,1)S(1)} collective-permute-done((bf16[1,1056,256]{2,1,0:T(8,128)(2,1)S(1)}, bf16[1,1056,256]{2,1,0:T(8,128)(2,1)S(1)}, u32[]{:S(2)}, u32[]{:S(2)}) %collective-permute-start.24) | collective-permute-done | bytes 540704 | tf_op jit(solution)/shard_map/near_up_c2/ppermute | solution.py:687
  132.1 1.8 %collective-permute-start.26 = (f32[4,256]{1,0:T(4,128)S(1)}, f32[4,256]{1,0:T(4,128)S(1)}, u32[]{:S(2)}, u32[]{:S(2)}) collective-permute-start(f32[4,256]{1,0:T(4,128)S(1)} %slice.23), channel_id=1, source_target_pairs={{0,4},{4,0},{8,12},{12,8},{16,20},{20,16},{24,28},{28,24},{1,5},{5... | collective-permute-start | bytes 12296 | tf_op jit(solution)/shard_map/squares_swap/ppermute | solution.py:687
  133.9 1.3 collective-permute-start.30
  135.8 1.3 collective-permute-start.31
  137.1 1.8 %collective-permute-start.32 = (bf16[1,1024,128]{2,1,0:T(8,128)(2,1)S(1)}, bf16[1,1024,128]{2,1,0:T(8,128)(2,1)S(1)}, u32[]{:S(2)}, u32[]{:S(2)}) collective-permute-start(bf16[1,1024,128]{2,1,0:T(8,128)(2,1)S(1)} %get-tuple-element.94), channel_id=1, source_target_pairs={{0,4},{4,0},{8,12},{12,8},{16,20},{20,16},{24,28},{28,24},{1,5},{5... | collective-permute-start | bytes 786440 | tf_op jit(solution)/shard_map/back_c0/ppermute | solution.py:687
  138.9 1.4 collective-permute-done.28.refs_7_
  140.3 3.1 %collective-permute-start.33 = (bf16[1,1024,128]{2,1,0:T(8,128)(2,1)S(1)}, bf16[1,1024,128]{2,1,0:T(8,128)(2,1)S(1)}, u32[]{:S(2)}, u32[]{:S(2)}) collective-permute-start(bf16[1,1024,128]{2,1,0:T(8,128)(2,1)S(1)} %get-tuple-element.95), channel_id=1, source_target_pairs={{0,4},{4,0},{8,12},{12,8},{16,20},{20,16},{24,28},{28,24},{1,5},{5... | collective-permute-start | bytes 786440 | tf_op jit(solution)/shard_map/back_c1/ppermute | solution.py:687
  143.4 8.4 %collective-permute-done.29.refs_8_ = bf16[1,528,256]{2,1,0:T(8,128)(2,1)S(1)} collective-permute-done((bf16[1,528,256]{2,1,0:T(8,128)(2,1)S(1)}, bf16[1,528,256]{2,1,0:T(8,128)(2,1)S(1)}, u32[]{:S(2)}, u32[]{:S(2)}) %collective-permute-start.29) | collective-permute-done | bytes 270368 | tf_op jit(solution)/shard_map/near_up_cross_c3/ppermute | solution.py:687
  154.5 1.5 collective-permute-start.36
  156.0 2.1 %collective-permute-done.36 = f32[4,256]{1,0:T(4,128)S(1)} collective-permute-done((f32[4,256]{1,0:T(4,128)S(1)}, f32[4,256]{1,0:T(4,128)S(1)}, u32[]{:S(2)}, u32[]{:S(2)}) %collective-permute-start.36) | collective-permute-done | bytes 4128 | tf_op jit(solution)/shard_map/ppermute | solution.py:858
  159.1 2.3 %finish.1 = bf16[1024,1024]{1,0:T(8,128)(2,1)} custom-call(s32[2]{0:T(128)S(1)} %pad_add_fusion.2.refs_0_.refs_1_.refs_3_.place, bf16[1,1024,128]{2,1,0:T(8,128)(2,1)S(1)} %get-tuple-element.69.refs_0_, bf16[1,1024,128]{2,1,0:T(8,128)(2,1)S(1)} %get-tuple-element.78.refs_0_.refs_1_, bf16[1,1024,128]{2,1,0:T(8,128)(2,1)S(1)} %get-tuple-element.86.refs_0_.refs_2_, ...), custom_call_target="tpu_custom_call" | custom-call | flops 3000000000 | bytes 10200001 | tf_op jit(solution)/shard_map/finish/pallas_call | solution.py:640
  (125 shorter events, 26.3 us)
Async XLA Ops:
  0.0 5.0 %collective-permute-start = (s32[4,8]{1,0:T(4,128)}, s32[4,8]{1,0:T(4,128)S(1)}, u32[]{:S(2)}, u32[]{:S(2)}) collective-permute-start(s32[4,8]{1,0:T(4,128)} %param.8), channel_id=1, source_target_pairs={{0,4},{4,0},{8,12},{12,8},{16,20},{20,16},{24,28},{28,24},{1,5},{5... | collective-permute-start | bytes 392 | tf_op jit(solution)/shard_map/selection_swap/ppermute | solution.py:687
  1.6 3.4 %copy-start.9 = (s32[4,8]{1,0:T(4,128)S(1)}, s32[4,8]{1,0:T(4,128)}, u32[]{:S(2)}) copy-start(s32[4,8]{1,0:T(4,128)} %param.8) | copy-start | bytes 388
  3.5 20.5 %collective-permute-start.3 = (bf16[1,3,1024,128]{3,2,1,0:T(8,128)(2,1)S(1)}, bf16[1,3,1024,128]{3,2,1,0:T(8,128)(2,1)S(1)}, u32[]{:S(2)}, u32[]{:S(2)}) collective-permute-start(bf16[1,3,1024,128]{3,2,1,0:T(8,128)(2,1)S(1)} %pack.5.refs_0_), channel_id=1, source_target_pairs={{0,4},{4,0},{8,12},{12,8},{16,20},{20,16},{24,28},{28,24},{1,5},{5... | collective-permute-start | bytes 2359304 | tf_op jit(solution)/shard_map/swap_c0/ppermute | solution.py:687
  7.4 13.7 %collective-permute-start.1 = (bf16[1,1040,128]{2,1,0:T(8,128)(2,1)}, bf16[1,1040,128]{2,1,0:T(8,128)(2,1)S(1)}, u32[]{:S(2)}, u32[]{:S(2)}) collective-permute-start(bf16[1,1040,128]{2,1,0:T(8,128)(2,1)} %get-tuple-element.52.refs_0_.refs_2_), channel_id=1, source_target_pairs={{16,8},{20,12},{24,16},{28,20},{17,9},{21,13},{25,17},{29,21},{18,... | collective-permute-start | bytes 798728 | tf_op jit(solution)/shard_map/near_down_keep_c0/ppermute | solution.py:687
  9.7 11.5 %collective-permute-start.2 = (bf16[1,1040,128]{2,1,0:T(8,128)(2,1)}, bf16[1,1040,128]{2,1,0:T(8,128)(2,1)S(1)}, u32[]{:S(2)}, u32[]{:S(2)}) collective-permute-start(bf16[1,1040,128]{2,1,0:T(8,128)(2,1)} %get-tuple-element.52.refs_0_.refs_2_), channel_id=1, source_target_pairs={{24,8},{28,12},{25,9},{29,13},{26,10},{30,14},{27,11},{31,15}} | collective-permute-start | bytes 798728 | tf_op jit(solution)/shard_map/far_down_keep_c0/ppermute | solution.py:687
  13.1 4.5 %copy-start.8 = (s32[8,8]{1,0:T(8,128)S(1)}, s32[8,8]{1,0:T(8,128)}, u32[]{:S(2)}) copy-start(s32[8,8]{1,0:T(8,128)} %constant.159.clone.1) | copy-start | bytes 772
  15.4 0.9 copy-start
  16.3 0.9 copy-start.4
  18.0 16.4 %collective-permute-start.4 = (bf16[1,2,1024,128]{3,2,1,0:T(8,128)(2,1)S(1)}, bf16[1,2,1024,128]{3,2,1,0:T(8,128)(2,1)}, u32[]{:S(2)}, u32[]{:S(2)}) collective-permute-start(bf16[1,2,1024,128]{3,2,1,0:T(8,128)(2,1)S(1)} %get-tuple-element.55.refs_6_.refs_4_), channel_id=1, source_target_pairs={{0,8},{4,12},{1,9},{5,13},{2,10},{6,14},{3,11},{7,15}} | collective-permute-start | bytes 1572872 | tf_op jit(solution)/shard_map/lift_keep_c0/ppermute | solution.py:687
  19.4 20.6 %collective-permute-start.5 = (bf16[1,3,1024,128]{3,2,1,0:T(8,128)(2,1)}, bf16[1,3,1024,128]{3,2,1,0:T(8,128)(2,1)S(1)}, u32[]{:S(2)}, u32[]{:S(2)}) collective-permute-start(bf16[1,3,1024,128]{3,2,1,0:T(8,128)(2,1)} %copy-done), channel_id=1, source_target_pairs={{0,4},{4,0},{8,12},{12,8},{16,20},{20,16},{24,28},{28,24},{1,5},{5... | collective-permute-start | bytes 2359304 | tf_op jit(solution)/shard_map/swap_c1/ppermute | solution.py:687
  24.1 1.1 copy-start.5
  26.2 21.8 %collective-permute-start.8 = (bf16[1,2,1024,128]{3,2,1,0:T(8,128)(2,1)}, bf16[1,2,1024,128]{3,2,1,0:T(8,128)(2,1)}, u32[]{:S(2)}, u32[]{:S(2)}) collective-permute-start(bf16[1,2,1024,128]{3,2,1,0:T(8,128)(2,1)} %get-tuple-element.59), channel_id=1, source_target_pairs={{0,8},{4,12},{1,9},{5,13},{2,10},{6,14},{3,11},{7,15}} | collective-permute-start | bytes 1572872 | tf_op jit(solution)/shard_map/lift_recv_c0/ppermute | solution.py:687
  27.7 17.8 %collective-permute-start.6 = (bf16[1,1024,128]{2,1,0:T(8,128)(2,1)}, bf16[1,1024,128]{2,1,0:T(8,128)(2,1)}, u32[]{:S(2)}, u32[]{:S(2)}) collective-permute-start(bf16[1,1024,128]{2,1,0:T(8,128)(2,1)} %get-tuple-element.54.refs_0_), channel_id=1, source_target_pairs={{16,8},{20,12},{24,16},{28,20},{17,9},{21,13},{25,17},{29,21},{18,... | collective-permute-start | bytes 786440 | tf_op jit(solution)/shard_map/near_down_recv_c0/ppermute | solution.py:687
  30.8 16.3 %collective-permute-start.7 = (bf16[1,1024,128]{2,1,0:T(8,128)(2,1)}, bf16[1,1024,128]{2,1,0:T(8,128)(2,1)}, u32[]{:S(2)}, u32[]{:S(2)}) collective-permute-start(bf16[1,1024,128]{2,1,0:T(8,128)(2,1)} %get-tuple-element.54.refs_0_), channel_id=1, source_target_pairs={{24,8},{28,12},{25,9},{29,13},{26,10},{30,14},{27,11},{31,15}} | collective-permute-start | bytes 786440 | tf_op jit(solution)/shard_map/far_down_recv_c0/ppermute | solution.py:687
  37.1 0.9 copy-start.1
  38.0 18.3 %collective-permute-start.9 = (bf16[1,3,1024,128]{3,2,1,0:T(8,128)(2,1)}, bf16[1,3,1024,128]{3,2,1,0:T(8,128)(2,1)S(1)}, u32[]{:S(2)}, u32[]{:S(2)}) collective-permute-start(bf16[1,3,1024,128]{3,2,1,0:T(8,128)(2,1)} %get-tuple-element.61), channel_id=1, source_target_pairs={{0,4},{4,0},{8,12},{12,8},{16,20},{20,16},{24,28},{28,24},{1,5},{5... | collective-permute-start | bytes 2359304 | tf_op jit(solution)/shard_map/swap_c2/ppermute | solution.py:687
  40.0 1.1 copy-start.2
  41.1 1.1 copy-start.6
  42.6 22.2 %collective-permute-start.10 = (bf16[2,1,1024,128]{3,2,1,0:T(8,128)(2,1)S(1)}, bf16[2,1,1024,128]{3,2,1,0:T(8,128)(2,1)S(1)}, u32[]{:S(2)}, u32[]{:S(2)}) collective-permute-start(bf16[2,1,1024,128]{3,2,1,0:T(8,128)(2,1)S(1)} %get-tuple-element.58.refs_0_), channel_id=1, source_target_pairs={{16,8},{20,12},{24,16},{28,20},{17,9},{21,13},{25,17},{29,21},{18,... | collective-permute-start | bytes 1572872 | tf_op jit(solution)/shard_map/near_down_c1/ppermute | solution.py:687
  45.5 21.1 %collective-permute-start.11 = (bf16[2,1,1024,128]{3,2,1,0:T(8,128)(2,1)S(1)}, bf16[2,1,1024,128]{3,2,1,0:T(8,128)(2,1)S(1)}, u32[]{:S(2)}, u32[]{:S(2)}) collective-permute-start(bf16[2,1,1024,128]{3,2,1,0:T(8,128)(2,1)S(1)} %get-tuple-element.58.refs_0_), channel_id=1, source_target_pairs={{24,8},{28,12},{25,9},{29,13},{26,10},{30,14},{27,11},{31,15}} | collective-permute-start | bytes 1572872 | tf_op jit(solution)/shard_map/far_down_c1/ppermute | solution.py:687
  47.1 10.5 %copy-start.3 = (bf16[1,3,1024,128]{3,2,1,0:T(8,128)(2,1)S(1)}, bf16[1,3,1024,128]{3,2,1,0:T(8,128)(2,1)}, u32[]{:S(2)}) copy-start(bf16[1,3,1024,128]{3,2,1,0:T(8,128)(2,1)} %copy-done.1) | copy-start | bytes 2359300
  47.1 21.5 %collective-permute-start.12 = (bf16[2,1,2,1024,128]{4,3,2,1,0:T(8,128)(2,1)S(1)}, bf16[2,1,2,1024,128]{4,3,2,1,0:T(8,128)(2,1)S(1)}, u32[]{:S(2)}, u32[]{:S(2)}) collective-permute-start(bf16[2,1,2,1024,128]{4,3,2,1,0:T(8,128)(2,1)S(1)} %get-tuple-element.65), channel_id=1, source_target_pairs={{0,8},{4,12},{1,9},{5,13},{2,10},{6,14},{3,11},{7,15}} | collective-permute-start | bytes 3145736 | tf_op jit(solution)/shard_map/lift_c1/ppermute | solution.py:687
  50.1 20.2 %collective-permute-start.13 = (bf16[1,1056,256]{2,1,0:T(8,128)(2,1)S(1)}, bf16[1,1056,256]{2,1,0:T(8,128)(2,1)S(1)}, u32[]{:S(2)}, u32[]{:S(2)}) collective-permute-start(bf16[1,1056,256]{2,1,0:T(8,128)(2,1)S(1)} %get-tuple-element.60.refs_0_), channel_id=1, source_target_pairs={{8,16},{12,20},{16,24},{20,28},{9,17},{13,21},{17,25},{21,29},{10,... | collective-permute-start | bytes 1622024 | tf_op jit(solution)/shard_map/near_up_c0/ppermute | solution.py:687
  56.3 24.2 %collective-permute-start.14 = (bf16[1,1056,256]{2,1,0:T(8,128)(2,1)S(1)}, bf16[1,1056,256]{2,1,0:T(8,128)(2,1)S(1)}, u32[]{:S(2)}, u32[]{:S(2)}) collective-permute-start(bf16[1,1056,256]{2,1,0:T(8,128)(2,1)S(1)} %get-tuple-element.68), channel_id=1, source_target_pairs={{8,24},{12,28},{9,25},{13,29},{10,26},{14,30},{11,27},{15,31}} | collective-permute-start | bytes 1622024 | tf_op jit(solution)/shard_map/far_up_c0/ppermute | solution.py:687
  62.5 6.8 %copy-start.7 = (bf16[1,3,1024,128]{3,2,1,0:T(8,128)(2,1)S(1)}, bf16[1,3,1024,128]{3,2,1,0:T(8,128)(2,1)}, u32[]{:S(2)}) copy-start(bf16[1,3,1024,128]{3,2,1,0:T(8,128)(2,1)} %copy-done.4) | copy-start | bytes 2359300
  64.7 23.3 %collective-permute-start.16 = (bf16[2,1,1024,128]{3,2,1,0:T(8,128)(2,1)S(1)}, bf16[2,1,1024,128]{3,2,1,0:T(8,128)(2,1)S(1)}, u32[]{:S(2)}, u32[]{:S(2)}) collective-permute-start(bf16[2,1,1024,128]{3,2,1,0:T(8,128)(2,1)S(1)} %get-tuple-element.62.refs_0_), channel_id=1, source_target_pairs={{16,8},{20,12},{24,16},{28,20},{17,9},{21,13},{25,17},{29,21},{18,... | collective-permute-start | bytes 1572872 | tf_op jit(solution)/shard_map/near_down_c2/ppermute | solution.py:687
  66.6 19.9 %collective-permute-start.15 = (bf16[1,3,1024,128]{3,2,1,0:T(8,128)(2,1)S(1)}, bf16[1,3,1024,128]{3,2,1,0:T(8,128)(2,1)S(1)}, u32[]{:S(2)}, u32[]{:S(2)}) collective-permute-start(bf16[1,3,1024,128]{3,2,1,0:T(8,128)(2,1)S(1)} %get-tuple-element.71), channel_id=1, source_target_pairs={{0,4},{4,0},{8,12},{12,8},{16,20},{20,16},{24,28},{28,24},{1,5},{5... | collective-permute-start | bytes 2359304 | tf_op jit(solution)/shard_map/swap_c3/ppermute | solution.py:687
  68.6 30.3 %collective-permute-start.18 = (bf16[2,1,2,1024,128]{4,3,2,1,0:T(8,128)(2,1)S(1)}, bf16[2,1,2,1024,128]{4,3,2,1,0:T(8,128)(2,1)S(1)}, u32[]{:S(2)}, u32[]{:S(2)}) collective-permute-start(bf16[2,1,2,1024,128]{4,3,2,1,0:T(8,128)(2,1)S(1)} %get-tuple-element.73), channel_id=1, source_target_pairs={{0,8},{4,12},{1,9},{5,13},{2,10},{6,14},{3,11},{7,15}} | collective-permute-start | bytes 3145736 | tf_op jit(solution)/shard_map/lift_c2/ppermute | solution.py:687
  70.4 25.3 %collective-permute-start.17 = (bf16[2,1,1024,128]{3,2,1,0:T(8,128)(2,1)S(1)}, bf16[2,1,1024,128]{3,2,1,0:T(8,128)(2,1)S(1)}, u32[]{:S(2)}, u32[]{:S(2)}) collective-permute-start(bf16[2,1,1024,128]{3,2,1,0:T(8,128)(2,1)S(1)} %get-tuple-element.62.refs_0_), channel_id=1, source_target_pairs={{24,8},{28,12},{25,9},{29,13},{26,10},{30,14},{27,11},{31,15}} | collective-permute-start | bytes 1572872 | tf_op jit(solution)/shard_map/far_down_c2/ppermute | solution.py:687
  80.5 26.2 %collective-permute-start.19 = (bf16[1,1056,256]{2,1,0:T(8,128)(2,1)S(1)}, bf16[1,1056,256]{2,1,0:T(8,128)(2,1)S(1)}, u32[]{:S(2)}, u32[]{:S(2)}) collective-permute-start(bf16[1,1056,256]{2,1,0:T(8,128)(2,1)S(1)} %get-tuple-element.66.refs_0_), channel_id=1, source_target_pairs={{8,16},{12,20},{16,24},{20,28},{9,17},{13,21},{17,25},{21,29},{10,... | collective-permute-start | bytes 1622024 | tf_op jit(solution)/shard_map/near_up_c1/ppermute | solution.py:687
  86.5 21.6 %collective-permute-start.20 = (bf16[1,1056,256]{2,1,0:T(8,128)(2,1)S(1)}, bf16[1,1056,256]{2,1,0:T(8,128)(2,1)S(1)}, u32[]{:S(2)}, u32[]{:S(2)}) collective-permute-start(bf16[1,1056,256]{2,1,0:T(8,128)(2,1)S(1)} %get-tuple-element.77), channel_id=1, source_target_pairs={{8,24},{12,28},{9,25},{13,29},{10,26},{14,30},{11,27},{15,31}} | collective-permute-start | bytes 1622024 | tf_op jit(solution)/shard_map/far_up_c1/ppermute | solution.py:687
  88.1 26.1 %collective-permute-start.21 = (bf16[2,1,1024,128]{3,2,1,0:T(8,128)(2,1)S(1)}, bf16[2,1,1024,128]{3,2,1,0:T(8,128)(2,1)S(1)}, u32[]{:S(2)}, u32[]{:S(2)}) collective-permute-start(bf16[2,1,1024,128]{3,2,1,0:T(8,128)(2,1)S(1)} %get-tuple-element.72.refs_0_), channel_id=1, source_target_pairs={{16,8},{20,12},{24,16},{28,20},{17,9},{21,13},{25,17},{29,21},{18,... | collective-permute-start | bytes 1572872 | tf_op jit(solution)/shard_map/near_down_c3/ppermute | solution.py:687
  95.7 18.5 %collective-permute-start.22 = (bf16[2,1,1024,128]{3,2,1,0:T(8,128)(2,1)S(1)}, bf16[2,1,1024,128]{3,2,1,0:T(8,128)(2,1)S(1)}, u32[]{:S(2)}, u32[]{:S(2)}) collective-permute-start(bf16[2,1,1024,128]{3,2,1,0:T(8,128)(2,1)S(1)} %get-tuple-element.72.refs_0_), channel_id=1, source_target_pairs={{24,8},{28,12},{25,9},{29,13},{26,10},{30,14},{27,11},{31,15}} | collective-permute-start | bytes 1572872 | tf_op jit(solution)/shard_map/far_down_c3/ppermute | solution.py:687
  98.9 15.3 %collective-permute-start.23 = (bf16[2,1,2,1024,128]{4,3,2,1,0:T(8,128)(2,1)S(1)}, bf16[2,1,2,1024,128]{4,3,2,1,0:T(8,128)(2,1)S(1)}, u32[]{:S(2)}, u32[]{:S(2)}) collective-permute-start(bf16[2,1,2,1024,128]{4,3,2,1,0:T(8,128)(2,1)S(1)} %get-tuple-element.80), channel_id=1, source_target_pairs={{0,8},{4,12},{1,9},{5,13},{2,10},{6,14},{3,11},{7,15}} | collective-permute-start | bytes 3145736 | tf_op jit(solution)/shard_map/lift_c3/ppermute | solution.py:687
  106.8 24.3 %collective-permute-start.24 = (bf16[1,1056,256]{2,1,0:T(8,128)(2,1)S(1)}, bf16[1,1056,256]{2,1,0:T(8,128)(2,1)S(1)}, u32[]{:S(2)}, u32[]{:S(2)}) collective-permute-start(bf16[1,1056,256]{2,1,0:T(8,128)(2,1)S(1)} %get-tuple-element.74.refs_0_), channel_id=1, source_target_pairs={{8,16},{12,20},{16,24},{20,28},{9,17},{13,21},{17,25},{21,29},{10,... | collective-permute-start | bytes 1622024 | tf_op jit(solution)/shard_map/near_up_c2/ppermute | solution.py:687
  108.1 23.0 %collective-permute-start.25 = (bf16[1,1056,256]{2,1,0:T(8,128)(2,1)S(1)}, bf16[1,1056,256]{2,1,0:T(8,128)(2,1)S(1)}, u32[]{:S(2)}, u32[]{:S(2)}) collective-permute-start(bf16[1,1056,256]{2,1,0:T(8,128)(2,1)S(1)} %get-tuple-element.85), channel_id=1, source_target_pairs={{8,24},{12,28},{9,25},{13,29},{10,26},{14,30},{11,27},{15,31}} | collective-permute-start | bytes 1622024 | tf_op jit(solution)/shard_map/far_up_c2/ppermute | solution.py:687
  118.8 18.3 %collective-permute-start.27 = (bf16[1,528,256]{2,1,0:T(8,128)(2,1)S(1)}, bf16[1,528,256]{2,1,0:T(8,128)(2,1)S(1)}, u32[]{:S(2)}, u32[]{:S(2)}) collective-permute-start(bf16[1,528,256]{2,1,0:T(8,128)(2,1)S(1)} %get-tuple-element.89), channel_id=1, source_target_pairs={{0,4},{4,0},{8,12},{12,8},{16,20},{20,16},{24,28},{28,24},{1,5},{5... | collective-permute-start | bytes 811016 | tf_op jit(solution)/shard_map/back_own_c3/ppermute | solution.py:687
  120.6 19.7 %collective-permute-start.28 = (bf16[1,528,256]{2,1,0:T(8,128)(2,1)S(1)}, bf16[1,528,256]{2,1,0:T(8,128)(2,1)S(1)}, u32[]{:S(2)}, u32[]{:S(2)}) collective-permute-start(bf16[1,528,256]{2,1,0:T(8,128)(2,1)S(1)} %get-tuple-element.81.refs_0_), channel_id=1, source_target_pairs={{8,16},{12,20},{16,24},{20,28},{9,17},{13,21},{17,25},{21,29},{10,... | collective-permute-start | bytes 811016 | tf_op jit(solution)/shard_map/near_up_same_c3/ppermute | solution.py:687
  121.9 29.9 %collective-permute-start.29 = (bf16[1,528,256]{2,1,0:T(8,128)(2,1)S(1)}, bf16[1,528,256]{2,1,0:T(8,128)(2,1)S(1)}, u32[]{:S(2)}, u32[]{:S(2)}) collective-permute-start(bf16[1,528,256]{2,1,0:T(8,128)(2,1)S(1)} %get-tuple-element.90), channel_id=1, source_target_pairs={{8,20},{12,16},{16,28},{20,24},{9,21},{13,17},{17,29},{21,25},{10,... | collective-permute-start | bytes 811016 | tf_op jit(solution)/shard_map/near_up_cross_c3/ppermute | solution.py:687
  132.1 23.9 %copy-start.10 = (bf16[1024]{0:T(1024)(128)(2,1)S(1)}, bf16[1024]{0:T(1024)(128)(2,1)}, u32[]{:S(2)}) copy-start(bf16[1024]{0:T(1024)(128)(2,1)} %param.9) | copy-start | bytes 6148
  132.1 3.7 %collective-permute-start.26 = (f32[4,256]{1,0:T(4,128)S(1)}, f32[4,256]{1,0:T(4,128)S(1)}, u32[]{:S(2)}, u32[]{:S(2)}) collective-permute-start(f32[4,256]{1,0:T(4,128)S(1)} %slice.23), channel_id=1, source_target_pairs={{0,4},{4,0},{8,12},{12,8},{16,20},{20,16},{24,28},{28,24},{1,5},{5... | collective-permute-start | bytes 12296 | tf_op jit(solution)/shard_map/squares_swap/ppermute | solution.py:687
  133.9 18.3 %collective-permute-start.30 = (bf16[1,528,256]{2,1,0:T(8,128)(2,1)S(1)}, bf16[1,528,256]{2,1,0:T(8,128)(2,1)S(1)}, u32[]{:S(2)}, u32[]{:S(2)}) collective-permute-start(bf16[1,528,256]{2,1,0:T(8,128)(2,1)S(1)} %get-tuple-element.91), channel_id=1, source_target_pairs={{8,24},{12,28},{9,25},{13,29},{10,26},{14,30},{11,27},{15,31}} | collective-permute-start | bytes 811016 | tf_op jit(solution)/shard_map/far_up_same_c3/ppermute | solution.py:687
  135.8 16.4 %collective-permute-start.31 = (bf16[1,528,256]{2,1,0:T(8,128)(2,1)S(1)}, bf16[1,528,256]{2,1,0:T(8,128)(2,1)S(1)}, u32[]{:S(2)}, u32[]{:S(2)}) collective-permute-start(bf16[1,528,256]{2,1,0:T(8,128)(2,1)S(1)} %get-tuple-element.92), channel_id=1, source_target_pairs={{8,28},{12,24},{9,29},{13,25},{10,30},{14,26},{11,31},{15,27}} | collective-permute-start | bytes 811016 | tf_op jit(solution)/shard_map/far_up_cross_c3/ppermute | solution.py:687
  137.1 21.0 %collective-permute-start.32 = (bf16[1,1024,128]{2,1,0:T(8,128)(2,1)S(1)}, bf16[1,1024,128]{2,1,0:T(8,128)(2,1)S(1)}, u32[]{:S(2)}, u32[]{:S(2)}) collective-permute-start(bf16[1,1024,128]{2,1,0:T(8,128)(2,1)S(1)} %get-tuple-element.94), channel_id=1, source_target_pairs={{0,4},{4,0},{8,12},{12,8},{16,20},{20,16},{24,28},{28,24},{1,5},{5... | collective-permute-start | bytes 786440 | tf_op jit(solution)/shard_map/back_c0/ppermute | solution.py:687
  140.3 17.8 %collective-permute-start.33 = (bf16[1,1024,128]{2,1,0:T(8,128)(2,1)S(1)}, bf16[1,1024,128]{2,1,0:T(8,128)(2,1)S(1)}, u32[]{:S(2)}, u32[]{:S(2)}) collective-permute-start(bf16[1,1024,128]{2,1,0:T(8,128)(2,1)S(1)} %get-tuple-element.95), channel_id=1, source_target_pairs={{0,4},{4,0},{8,12},{12,8},{16,20},{20,16},{24,28},{28,24},{1,5},{5... | collective-permute-start | bytes 786440 | tf_op jit(solution)/shard_map/back_c1/ppermute | solution.py:687
  151.8 7.3 %collective-permute-start.34 = (bf16[1,1024,128]{2,1,0:T(8,128)(2,1)S(1)}, bf16[1,1024,128]{2,1,0:T(8,128)(2,1)S(1)}, u32[]{:S(2)}, u32[]{:S(2)}) collective-permute-start(bf16[1,1024,128]{2,1,0:T(8,128)(2,1)S(1)} %get-tuple-element.96), channel_id=1, source_target_pairs={{0,4},{4,0},{8,12},{12,8},{16,20},{20,16},{24,28},{28,24},{1,5},{5... | collective-permute-start | bytes 786440 | tf_op jit(solution)/shard_map/back_c2/ppermute | solution.py:687
  153.2 1.2 collective-permute-start.35
  154.5 3.6 %collective-permute-start.36 = (f32[4,256]{1,0:T(4,128)S(1)}, f32[4,256]{1,0:T(4,128)S(1)}, u32[]{:S(2)}, u32[]{:S(2)}) collective-permute-start(f32[4,256]{1,0:T(4,128)S(1)} %add.296), channel_id=1, source_target_pairs={{0,2},{1,3},{2,0},{3,1},{4,6},{5,7},{6,4},{7,5},{8,10},{9,11},{10,... | collective-permute-start | bytes 12296 | tf_op jit(solution)/shard_map/ppermute | solution.py:858

commit v11 on v10

--- a/solution.py
+++ b/solution.py
@@ -212,6 +212,12 @@
         query_pos = lax.broadcasted_iota(jnp.int32, (block_rows, block_rows), 1)
         bias_scr[0] = jnp.zeros((block_rows, block_rows), jnp.float32)
         bias_scr[1] = jnp.where(key_pos <= query_pos, 0.0, -1e30)
+    def clear():
+        if not own:
+            o_scr[...] = jnp.zeros_like(o_scr)
+            lse_scr[...] = jnp.full_like(lse_scr, -1e30)
+
+    clear()
     for copy in copies:
         copy.wait()
 
@@ -251,8 +257,8 @@
         return acc, top, total
 
     for h in range(heads):
-        o_scr[...] = jnp.zeros_like(o_scr)
-        lse_scr[...] = jnp.full_like(lse_scr, -1e30)
+        if h:
+            clear()
 
         def two_steps(i, carry):
             state = (acc_scr[...], top_scr[...], sum_scr[...])

time: 162 us -> 163 us (level)
  transfers between devices with their start and end apart: 37 -> 37, of which waited for: 10 -> 10; matrix products, arithmetic and copies ran while one was open for 3% -> 3% of each run, Pallas kernels for 24% -> 23%
where the time goes in v11:
time: 163 us; the launch traced here: 162 us
  starting transfers between devices  74.2 us (46%)
  Pallas kernels  40.1 us (25%)
  waiting for transfers between devices  33.3 us (20%)
  local copies, waits for them, and re-layouts  7.13 us (4%)
  between operations  3.42 us (2%)
  other arithmetic  3.39 us (2%)
    ppermute x35, starting transfers between devices, to(): sent[name] = lax.ppermute(array, 'ctx', pairs)  72.6 us
    ppermute x35, waiting for transfers between devices, to(): sent[name] = lax.ppermute(array, 'ctx', pairs)  30.1 us
    pallas_call x8, Pallas kernels, attention_call(): pl.pallas_call(ordered(partial(attention_kernel, (heads, per_dev, block_r...  20.5 us
    pallas_call x5, Pallas kernels, pack_call(): pl.pallas_call(ordered(partial(pack_kernel, (sides, head, half, rows, not...  11.4 us
    unnamed x22, local copies, waits for them, and re-layouts  6.07 us
  transfers between devices with their start and end apart: 37, of which 10 were waited for; matrix products, arithmetic and copies ran while one was open for 3% of the time, Pallas kernels for 23%

profile of v11, /device:TPU:24, one launch (start us, length us, event | category | flops | bytes accessed | tf_op | source)
XLA Modules:
  0.0 161.6 jit_solution(2578435021884769038)
XLA Ops:
  0.0 1.5 collective-permute-start
  1.6 2.0 %pack.5.refs_0_ = bf16[1,3,1024,128]{3,2,1,0:T(8,128)(2,1)S(1)} custom-call(s32[2]{0:T(128)S(1)} %pad_add_fusion.2.refs_0_.refs_1_.refs_3_.place, bf16[1024,1024]{1,0:T(8,128)(2,1)} %refs_2_.7, bf16[1024,1024]{1,0:T(8,128)(2,1)} %refs_3_.7, bf16[1024,1024]{1,0:T(8,128)(2,1)} %refs_4_.7), custom_call_target="tpu_custom_call" | custom-call | flops 2000000000 | bytes 6800001 | tf_op jit(solution)/shard_map/pack/pallas_call | solution.py:431
  5.0 2.3 %pack.6 = (bf16[1,1040,128]{2,1,0:T(8,128)(2,1)}, bf16[1,2,1024,128]{3,2,1,0:T(8,128)(2,1)S(1)}) custom-call(bf16[1,3,1024,128]{3,2,1,0:T(8,128)(2,1)S(1)} %pack.5.refs_0_, s32[2]{0:T(128)S(1)} %pad_add_fusion.2.refs_0_.refs_1_.refs_3_.place, bf16[1024,1024]{1,0:T(8,128)(2,1)} %refs_2_.7, bf16[1024,1024]{1,0:T(8,128)(2,1)} %refs_3_.7, ...), custom_call_target="tpu_custom_call" | custom-call | flops 2000000000 | bytes 6800001 | tf_op jit(solution)/shard_map/pack/pallas_call | solution.py:431
  7.4 2.4 %collective-permute-start.1 = (bf16[1,1040,128]{2,1,0:T(8,128)(2,1)}, bf16[1,1040,128]{2,1,0:T(8,128)(2,1)S(1)}, u32[]{:S(2)}, u32[]{:S(2)}) collective-permute-start(bf16[1,1040,128]{2,1,0:T(8,128)(2,1)} %get-tuple-element.52.refs_0_.refs_2_), channel_id=1, source_target_pairs={{16,8},{20,12},{24,16},{28,20},{17,9},{21,13},{25,17},{29,21},{18,... | collective-permute-start | bytes 798728 | tf_op jit(solution)/shard_map/near_down_keep_c0/ppermute | solution.py:693
  9.7 1.3 collective-permute-start.2
  13.2 2.2 %pack.7 = (bf16[1,3,1024,128]{3,2,1,0:T(8,128)(2,1)S(1)}, bf16[1,3,1024,128]{3,2,1,0:T(8,128)(2,1)S(1)}) custom-call(bf16[1,1040,128]{2,1,0:T(8,128)(2,1)} %get-tuple-element.52.refs_0_.refs_2_, s32[2]{0:T(128)S(1)} %pad_add_fusion.2.refs_0_.refs_1_.refs_3_.place, bf16[1024,1024]{1,0:T(8,128)(2,1)} %refs_2_.7, bf16[1024,1024]{1,0:T(8,128)(2,1)} %refs_3_.7, ...), custom_call_target="tpu_custom_call" | custom-call | flops 2000000000 | bytes 6800001 | tf_op jit(solution)/shard_map/pack/pallas_call | solution.py:431
  18.0 1.5 collective-permute-start.4
  19.4 1.5 collective-permute-start.5
  26.2 1.5 collective-permute-start.8
  27.7 3.1 %collective-permute-start.6 = (bf16[1,1024,128]{2,1,0:T(8,128)(2,1)}, bf16[1,1024,128]{2,1,0:T(8,128)(2,1)}, u32[]{:S(2)}, u32[]{:S(2)}) collective-permute-start(bf16[1,1024,128]{2,1,0:T(8,128)(2,1)} %get-tuple-element.54.refs_0_), channel_id=1, source_target_pairs={{16,8},{20,12},{24,16},{28,20},{17,9},{21,13},{25,17},{29,21},{18,... | collective-permute-start | bytes 786440 | tf_op jit(solution)/shard_map/near_down_recv_c0/ppermute | solution.py:693
  30.8 3.6 %collective-permute-start.7 = (bf16[1,1024,128]{2,1,0:T(8,128)(2,1)}, bf16[1,1024,128]{2,1,0:T(8,128)(2,1)}, u32[]{:S(2)}, u32[]{:S(2)}) collective-permute-start(bf16[1,1024,128]{2,1,0:T(8,128)(2,1)} %get-tuple-element.54.refs_0_), channel_id=1, source_target_pairs={{24,8},{28,12},{25,9},{29,13},{26,10},{30,14},{27,11},{31,15}} | collective-permute-start | bytes 786440 | tf_op jit(solution)/shard_map/far_down_recv_c0/ppermute | solution.py:693
  34.4 2.7 %pack.8 = (bf16[1,3,1024,128]{3,2,1,0:T(8,128)(2,1)}, bf16[1,3,1024,128]{3,2,1,0:T(8,128)(2,1)S(1)}) custom-call(bf16[1,1024,128]{2,1,0:T(8,128)(2,1)} %get-tuple-element.54.refs_0_, bf16[1,2,1024,128]{3,2,1,0:T(8,128)(2,1)} %collective-permute-done.4.refs_1_.refs_8_.refs_5_, s32[129]{0:T(256)S(1)} %pad_add_fusion.1.refs_2_.refs_1_, ...), custom_call_target="tpu_custom_call" | custom-call | flops 2000000000 | bytes 6800001 | tf_op jit(solution)/shard_map/pack/pallas_call | solution.py:431
  38.0 1.5 collective-permute-start.9
  42.6 2.9 %collective-permute-start.10 = (bf16[2,1,1024,128]{3,2,1,0:T(8,128)(2,1)S(1)}, bf16[2,1,1024,128]{3,2,1,0:T(8,128)(2,1)S(1)}, u32[]{:S(2)}, u32[]{:S(2)}) collective-permute-start(bf16[2,1,1024,128]{3,2,1,0:T(8,128)(2,1)S(1)} %get-tuple-element.58.refs_0_), channel_id=1, source_target_pairs={{16,8},{20,12},{24,16},{28,20},{17,9},{21,13},{25,17},{29,21},{18,... | collective-permute-start | bytes 1572872 | tf_op jit(solution)/shard_map/near_down_c1/ppermute | solution.py:693
  45.5 1.6 collective-permute-start.11
  48.0 2.1 %served_attention.4 = (bf16[1,1056,256]{2,1,0:T(8,128)(2,1)S(1)}, bf16[1,1056,256]{2,1,0:T(8,128)(2,1)S(1)}) custom-call(bf16[2,1,1024,128]{3,2,1,0:T(8,128)(2,1)S(1)} %get-tuple-element.58.refs_0_, s32[129]{0:T(256)S(1)} %pad_add_fusion.1.refs_2_.refs_1_, bf16[1,1040,128]{2,1,0:T(8,128)(2,1)S(1)} %collective-permute-done.1.refs_2_, ...), custom_call_target="tpu_custom_call" | custom-call | flops 6000000000 | bytes 20400000 | tf_op jit(solution)/shard_map/served_attention/pallas_call | solution.py:356
  50.1 1.3 collective-permute-start.13
  51.4 4.9 %collective-permute-done.9.refs_2_.refs_5_.refs_3_ = bf16[1,3,1024,128]{3,2,1,0:T(8,128)(2,1)S(1)} collective-permute-done((bf16[1,3,1024,128]{3,2,1,0:T(8,128)(2,1)}, bf16[1,3,1024,128]{3,2,1,0:T(8,128)(2,1)S(1)}, u32[]{:S(2)}, u32[]{:S(2)}) %collective-permute-start.9) | collective-permute-done | bytes 786464 | tf_op jit(solution)/shard_map/swap_c2/ppermute | solution.py:693
  56.3 1.3 collective-permute-start.14
  57.9 4.5 %own_attention.4 = (f32[1,8,128,256]{3,2,1,0:T(8,128)S(1)}, f32[1,8,256]{2,1,0:T(8,128)S(1)}) custom-call(bf16[2,1,1024,128]{3,2,1,0:T(8,128)(2,1)S(1)} %get-tuple-element.62.refs_0_, s32[81]{0:T(128)S(1)} %pad_add_fusion.4.refs_1_, bf16[1,1040,128]{2,1,0:T(8,128)(2,1)} %get-tuple-element.52.refs_0_.refs_2_, ...), custom_call_target="tpu_custom_call" | custom-call | flops 5000000000 | bytes 17000000 | tf_op jit(solution)/shard_map/own_attention/pallas_call | solution.py:356
  62.4 2.2 %pack.9 = (bf16[1,3,1024,128]{3,2,1,0:T(8,128)(2,1)S(1)}, bf16[1,3,1024,128]{3,2,1,0:T(8,128)(2,1)S(1)}) custom-call(f32[1,8,256]{2,1,0:T(8,128)S(1)} %get-tuple-element.63.refs_0_.refs_4_, s32[2]{0:T(128)S(1)} %pad_add_fusion.2.refs_0_.refs_1_.refs_3_.place, bf16[1024,1024]{1,0:T(8,128)(2,1)} %refs_2_.7, bf16[1024,1024]{1,0:T(8,128)(2,1)} %refs_3_.7, ...), custom_call_target="tpu_custom_call" | custom-call | flops 2000000000 | bytes 6800001 | tf_op jit(solution)/shard_map/pack/pallas_call | solution.py:431
  64.7 1.8 %collective-permute-start.16 = (bf16[2,1,1024,128]{3,2,1,0:T(8,128)(2,1)S(1)}, bf16[2,1,1024,128]{3,2,1,0:T(8,128)(2,1)S(1)}, u32[]{:S(2)}, u32[]{:S(2)}) collective-permute-start(bf16[2,1,1024,128]{3,2,1,0:T(8,128)(2,1)S(1)} %get-tuple-element.62.refs_0_), channel_id=1, source_target_pairs={{16,8},{20,12},{24,16},{28,20},{17,9},{21,13},{25,17},{29,21},{18,... | collective-permute-start | bytes 1572872 | tf_op jit(solution)/shard_map/near_down_c2/ppermute | solution.py:693
  66.5 2.2 %collective-permute-start.15 = (bf16[1,3,1024,128]{3,2,1,0:T(8,128)(2,1)S(1)}, bf16[1,3,1024,128]{3,2,1,0:T(8,128)(2,1)S(1)}, u32[]{:S(2)}, u32[]{:S(2)}) collective-permute-start(bf16[1,3,1024,128]{3,2,1,0:T(8,128)(2,1)S(1)} %get-tuple-element.71), channel_id=1, source_target_pairs={{0,4},{4,0},{8,12},{12,8},{16,20},{20,16},{24,28},{28,24},{1,5},{5... | collective-permute-start | bytes 2359304 | tf_op jit(solution)/shard_map/swap_c3/ppermute | solution.py:693
  70.5 10.2 %collective-permute-start.17 = (bf16[2,1,1024,128]{3,2,1,0:T(8,128)(2,1)S(1)}, bf16[2,1,1024,128]{3,2,1,0:T(8,128)(2,1)S(1)}, u32[]{:S(2)}, u32[]{:S(2)}) collective-permute-start(bf16[2,1,1024,128]{3,2,1,0:T(8,128)(2,1)S(1)} %get-tuple-element.62.refs_0_), channel_id=1, source_target_pairs={{24,8},{28,12},{25,9},{29,13},{26,10},{30,14},{27,11},{31,15}} | collective-permute-start | bytes 1572872 | tf_op jit(solution)/shard_map/far_down_c2/ppermute | solution.py:693
  80.7 1.3 collective-permute-start.19
  83.0 3.5 %own_attention.5 = (f32[1,8,128,256]{3,2,1,0:T(8,128)S(1)}, f32[1,8,256]{2,1,0:T(8,128)S(1)}) custom-call(bf16[1,1024,128]{2,1,0:T(8,128)(2,1)S(1)} %get-tuple-element.69.refs_0_, s32[81]{0:T(128)S(1)} %pad_add_fusion.4.refs_1_, bf16[1,3,1024,128]{3,2,1,0:T(8,128)(2,1)S(1)} %copy-done.7, ...), custom_call_target="tpu_custom_call" | custom-call | flops 5000000000 | bytes 17000000 | tf_op jit(solution)/shard_map/own_attention/pallas_call | solution.py:356
  86.5 1.3 collective-permute-start.20
  88.1 7.4 %collective-permute-start.21 = (bf16[2,1,1024,128]{3,2,1,0:T(8,128)(2,1)S(1)}, bf16[2,1,1024,128]{3,2,1,0:T(8,128)(2,1)S(1)}, u32[]{:S(2)}, u32[]{:S(2)}) collective-permute-start(bf16[2,1,1024,128]{3,2,1,0:T(8,128)(2,1)S(1)} %get-tuple-element.72.refs_0_), channel_id=1, source_target_pairs={{16,8},{20,12},{24,16},{28,20},{17,9},{21,13},{25,17},{29,21},{18,... | collective-permute-start | bytes 1572872 | tf_op jit(solution)/shard_map/near_down_c3/ppermute | solution.py:693
  95.5 3.2 %collective-permute-start.22 = (bf16[2,1,1024,128]{3,2,1,0:T(8,128)(2,1)S(1)}, bf16[2,1,1024,128]{3,2,1,0:T(8,128)(2,1)S(1)}, u32[]{:S(2)}, u32[]{:S(2)}) collective-permute-start(bf16[2,1,1024,128]{3,2,1,0:T(8,128)(2,1)S(1)} %get-tuple-element.72.refs_0_), channel_id=1, source_target_pairs={{24,8},{28,12},{25,9},{29,13},{26,10},{30,14},{27,11},{31,15}} | collective-permute-start | bytes 1572872 | tf_op jit(solution)/shard_map/far_down_c3/ppermute | solution.py:693
  100.6 6.1 %collective-permute-done.19.refs_5_ = bf16[1,1056,256]{2,1,0:T(8,128)(2,1)S(1)} collective-permute-done((bf16[1,1056,256]{2,1,0:T(8,128)(2,1)S(1)}, bf16[1,1056,256]{2,1,0:T(8,128)(2,1)S(1)}, u32[]{:S(2)}, u32[]{:S(2)}) %collective-permute-start.19) | collective-permute-done | bytes 540704 | tf_op jit(solution)/shard_map/near_up_c1/ppermute | solution.py:693
  106.7 1.3 collective-permute-start.24
  108.0 1.3 collective-permute-start.25
  110.3 3.7 %own_attention.6 = (f32[1,8,128,256]{3,2,1,0:T(8,128)S(1)}, f32[1,8,256]{2,1,0:T(8,128)S(1)}) custom-call(bf16[1,1024,128]{2,1,0:T(8,128)(2,1)S(1)} %get-tuple-element.78.refs_0_.refs_1_, s32[81]{0:T(128)S(1)} %pad_add_fusion.4.refs_1_, bf16[1,3,1024,128]{3,2,1,0:T(8,128)(2,1)S(1)} %copy-done.3, ...), custom_call_target="tpu_custom_call" | custom-call | flops 5000000000 | bytes 17000000 | tf_op jit(solution)/shard_map/own_attention/pallas_call | solution.py:356
  115.1 3.5 %own_attention.7 = (f32[1,4,128,256]{3,2,1,0:T(8,128)S(1)}, f32[1,4,256]{2,1,0:T(4,128)S(1)}, bf16[1,528,256]{2,1,0:T(8,128)(2,1)S(1)}) custom-call(bf16[1,528,256]{2,1,0:T(8,128)(2,1)S(1)} %get-tuple-element.81.refs_0_, s32[81]{0:T(128)S(1)} %pad_add_fusion.4.refs_1_, bf16[1,3,1024,128]{3,2,1,0:T(8,128)(2,1)S(1)} %get-tuple-element.64.refs_0_.refs_1_.refs_4_.refs_2_, ...), custom_call_target="tpu_custom_call" | custom-call | flops 5000000000 | bytes 17000000 | tf_op jit(solution)/shard_map/own_attention/pallas_call | solution.py:356
  118.6 1.8 %collective-permute-start.27 = (bf16[1,528,256]{2,1,0:T(8,128)(2,1)S(1)}, bf16[1,528,256]{2,1,0:T(8,128)(2,1)S(1)}, u32[]{:S(2)}, u32[]{:S(2)}) collective-permute-start(bf16[1,528,256]{2,1,0:T(8,128)(2,1)S(1)} %get-tuple-element.89), channel_id=1, source_target_pairs={{0,4},{4,0},{8,12},{12,8},{16,20},{20,16},{24,28},{28,24},{1,5},{5... | collective-permute-start | bytes 811016 | tf_op jit(solution)/shard_map/back_own_c3/ppermute | solution.py:693
  120.4 1.3 collective-permute-start.28
  121.7 1.3 collective-permute-start.29
  123.0 8.0 %collective-permute-done.24.refs_5_ = bf16[1,1056,256]{2,1,0:T(8,128)(2,1)S(1)} collective-permute-done((bf16[1,1056,256]{2,1,0:T(8,128)(2,1)S(1)}, bf16[1,1056,256]{2,1,0:T(8,128)(2,1)S(1)}, u32[]{:S(2)}, u32[]{:S(2)}) %collective-permute-start.24) | collective-permute-done | bytes 540704 | tf_op jit(solution)/shard_map/near_up_c2/ppermute | solution.py:693
  132.1 2.8 %collective-permute-start.26 = (f32[4,256]{1,0:T(4,128)S(1)}, f32[4,256]{1,0:T(4,128)S(1)}, u32[]{:S(2)}, u32[]{:S(2)}) collective-permute-start(f32[4,256]{1,0:T(4,128)S(1)} %slice.23), channel_id=1, source_target_pairs={{0,4},{4,0},{8,12},{12,8},{16,20},{20,16},{24,28},{28,24},{1,5},{5... | collective-permute-start | bytes 12296 | tf_op jit(solution)/shard_map/squares_swap/ppermute | solution.py:693
  134.9 1.3 collective-permute-start.30
  136.5 1.3 collective-permute-start.31
  137.8 2.1 %collective-permute-start.32 = (bf16[1,1024,128]{2,1,0:T(8,128)(2,1)S(1)}, bf16[1,1024,128]{2,1,0:T(8,128)(2,1)S(1)}, u32[]{:S(2)}, u32[]{:S(2)}) collective-permute-start(bf16[1,1024,128]{2,1,0:T(8,128)(2,1)S(1)} %get-tuple-element.94), channel_id=1, source_target_pairs={{0,4},{4,0},{8,12},{12,8},{16,20},{20,16},{24,28},{28,24},{1,5},{5... | collective-permute-start | bytes 786440 | tf_op jit(solution)/shard_map/back_c0/ppermute | solution.py:693
  140.7 2.9 %collective-permute-start.33 = (bf16[1,1024,128]{2,1,0:T(8,128)(2,1)S(1)}, bf16[1,1024,128]{2,1,0:T(8,128)(2,1)S(1)}, u32[]{:S(2)}, u32[]{:S(2)}) collective-permute-start(bf16[1,1024,128]{2,1,0:T(8,128)(2,1)S(1)} %get-tuple-element.95), channel_id=1, source_target_pairs={{0,4},{4,0},{8,12},{12,8},{16,20},{20,16},{24,28},{28,24},{1,5},{5... | collective-permute-start | bytes 786440 | tf_op jit(solution)/shard_map/back_c1/ppermute | solution.py:693
  143.5 8.2 %collective-permute-done.29.refs_8_ = bf16[1,528,256]{2,1,0:T(8,128)(2,1)S(1)} collective-permute-done((bf16[1,528,256]{2,1,0:T(8,128)(2,1)S(1)}, bf16[1,528,256]{2,1,0:T(8,128)(2,1)S(1)}, u32[]{:S(2)}, u32[]{:S(2)}) %collective-permute-start.29) | collective-permute-done | bytes 270368 | tf_op jit(solution)/shard_map/near_up_cross_c3/ppermute | solution.py:693
  153.2 1.2 collective-permute-done.35
  154.4 1.5 collective-permute-start.36
  155.9 2.1 %collective-permute-done.36 = f32[4,256]{1,0:T(4,128)S(1)} collective-permute-done((f32[4,256]{1,0:T(4,128)S(1)}, f32[4,256]{1,0:T(4,128)S(1)}, u32[]{:S(2)}, u32[]{:S(2)}) %collective-permute-start.36) | collective-permute-done | bytes 4128 | tf_op jit(solution)/shard_map/ppermute | solution.py:864
  159.1 2.3 %finish.1 = bf16[1024,1024]{1,0:T(8,128)(2,1)} custom-call(s32[2]{0:T(128)S(1)} %pad_add_fusion.2.refs_0_.refs_1_.refs_3_.place, bf16[1,1024,128]{2,1,0:T(8,128)(2,1)S(1)} %get-tuple-element.69.refs_0_, bf16[1,1024,128]{2,1,0:T(8,128)(2,1)S(1)} %get-tuple-element.78.refs_0_.refs_1_, bf16[1,1024,128]{2,1,0:T(8,128)(2,1)S(1)} %get-tuple-element.86.refs_0_.refs_2_, ...), custom_call_target="tpu_custom_call" | custom-call | flops 3000000000 | bytes 10200001 | tf_op jit(solution)/shard_map/finish/pallas_call | solution.py:646
  (125 shorter events, 25.7 us)
Async XLA Ops:
  0.0 5.0 %collective-permute-start = (s32[4,8]{1,0:T(4,128)}, s32[4,8]{1,0:T(4,128)S(1)}, u32[]{:S(2)}, u32[]{:S(2)}) collective-permute-start(s32[4,8]{1,0:T(4,128)} %param.8), channel_id=1, source_target_pairs={{0,4},{4,0},{8,12},{12,8},{16,20},{20,16},{24,28},{28,24},{1,5},{5... | collective-permute-start | bytes 392 | tf_op jit(solution)/shard_map/selection_swap/ppermute | solution.py:693
  1.6 3.4 %copy-start.9 = (s32[4,8]{1,0:T(4,128)S(1)}, s32[4,8]{1,0:T(4,128)}, u32[]{:S(2)}) copy-start(s32[4,8]{1,0:T(4,128)} %param.8) | copy-start | bytes 388
  3.5 20.5 %collective-permute-start.3 = (bf16[1,3,1024,128]{3,2,1,0:T(8,128)(2,1)S(1)}, bf16[1,3,1024,128]{3,2,1,0:T(8,128)(2,1)S(1)}, u32[]{:S(2)}, u32[]{:S(2)}) collective-permute-start(bf16[1,3,1024,128]{3,2,1,0:T(8,128)(2,1)S(1)} %pack.5.refs_0_), channel_id=1, source_target_pairs={{0,4},{4,0},{8,12},{12,8},{16,20},{20,16},{24,28},{28,24},{1,5},{5... | collective-permute-start | bytes 2359304 | tf_op jit(solution)/shard_map/swap_c0/ppermute | solution.py:693
  7.4 13.7 %collective-permute-start.1 = (bf16[1,1040,128]{2,1,0:T(8,128)(2,1)}, bf16[1,1040,128]{2,1,0:T(8,128)(2,1)S(1)}, u32[]{:S(2)}, u32[]{:S(2)}) collective-permute-start(bf16[1,1040,128]{2,1,0:T(8,128)(2,1)} %get-tuple-element.52.refs_0_.refs_2_), channel_id=1, source_target_pairs={{16,8},{20,12},{24,16},{28,20},{17,9},{21,13},{25,17},{29,21},{18,... | collective-permute-start | bytes 798728 | tf_op jit(solution)/shard_map/near_down_keep_c0/ppermute | solution.py:693
  9.7 11.5 %collective-permute-start.2 = (bf16[1,1040,128]{2,1,0:T(8,128)(2,1)}, bf16[1,1040,128]{2,1,0:T(8,128)(2,1)S(1)}, u32[]{:S(2)}, u32[]{:S(2)}) collective-permute-start(bf16[1,1040,128]{2,1,0:T(8,128)(2,1)} %get-tuple-element.52.refs_0_.refs_2_), channel_id=1, source_target_pairs={{24,8},{28,12},{25,9},{29,13},{26,10},{30,14},{27,11},{31,15}} | collective-permute-start | bytes 798728 | tf_op jit(solution)/shard_map/far_down_keep_c0/ppermute | solution.py:693
  13.1 4.5 %copy-start.8 = (s32[8,8]{1,0:T(8,128)S(1)}, s32[8,8]{1,0:T(8,128)}, u32[]{:S(2)}) copy-start(s32[8,8]{1,0:T(8,128)} %constant.159.clone.1) | copy-start | bytes 772
  15.4 0.9 copy-start
  16.3 0.9 copy-start.4
  18.0 16.4 %collective-permute-start.4 = (bf16[1,2,1024,128]{3,2,1,0:T(8,128)(2,1)S(1)}, bf16[1,2,1024,128]{3,2,1,0:T(8,128)(2,1)}, u32[]{:S(2)}, u32[]{:S(2)}) collective-permute-start(bf16[1,2,1024,128]{3,2,1,0:T(8,128)(2,1)S(1)} %get-tuple-element.55.refs_6_.refs_4_), channel_id=1, source_target_pairs={{0,8},{4,12},{1,9},{5,13},{2,10},{6,14},{3,11},{7,15}} | collective-permute-start | bytes 1572872 | tf_op jit(solution)/shard_map/lift_keep_c0/ppermute | solution.py:693
  19.4 20.6 %collective-permute-start.5 = (bf16[1,3,1024,128]{3,2,1,0:T(8,128)(2,1)}, bf16[1,3,1024,128]{3,2,1,0:T(8,128)(2,1)S(1)}, u32[]{:S(2)}, u32[]{:S(2)}) collective-permute-start(bf16[1,3,1024,128]{3,2,1,0:T(8,128)(2,1)} %copy-done), channel_id=1, source_target_pairs={{0,4},{4,0},{8,12},{12,8},{16,20},{20,16},{24,28},{28,24},{1,5},{5... | collective-permute-start | bytes 2359304 | tf_op jit(solution)/shard_map/swap_c1/ppermute | solution.py:693
  24.1 1.1 copy-start.5
  26.2 21.8 %collective-permute-start.8 = (bf16[1,2,1024,128]{3,2,1,0:T(8,128)(2,1)}, bf16[1,2,1024,128]{3,2,1,0:T(8,128)(2,1)}, u32[]{:S(2)}, u32[]{:S(2)}) collective-permute-start(bf16[1,2,1024,128]{3,2,1,0:T(8,128)(2,1)} %get-tuple-element.59), channel_id=1, source_target_pairs={{0,8},{4,12},{1,9},{5,13},{2,10},{6,14},{3,11},{7,15}} | collective-permute-start | bytes 1572872 | tf_op jit(solution)/shard_map/lift_recv_c0/ppermute | solution.py:693
  27.7 17.8 %collective-permute-start.6 = (bf16[1,1024,128]{2,1,0:T(8,128)(2,1)}, bf16[1,1024,128]{2,1,0:T(8,128)(2,1)}, u32[]{:S(2)}, u32[]{:S(2)}) collective-permute-start(bf16[1,1024,128]{2,1,0:T(8,128)(2,1)} %get-tuple-element.54.refs_0_), channel_id=1, source_target_pairs={{16,8},{20,12},{24,16},{28,20},{17,9},{21,13},{25,17},{29,21},{18,... | collective-permute-start | bytes 786440 | tf_op jit(solution)/shard_map/near_down_recv_c0/ppermute | solution.py:693
  30.8 16.3 %collective-permute-start.7 = (bf16[1,1024,128]{2,1,0:T(8,128)(2,1)}, bf16[1,1024,128]{2,1,0:T(8,128)(2,1)}, u32[]{:S(2)}, u32[]{:S(2)}) collective-permute-start(bf16[1,1024,128]{2,1,0:T(8,128)(2,1)} %get-tuple-element.54.refs_0_), channel_id=1, source_target_pairs={{24,8},{28,12},{25,9},{29,13},{26,10},{30,14},{27,11},{31,15}} | collective-permute-start | bytes 786440 | tf_op jit(solution)/shard_map/far_down_recv_c0/ppermute | solution.py:693
  37.1 0.9 copy-start.1
  38.0 18.3 %collective-permute-start.9 = (bf16[1,3,1024,128]{3,2,1,0:T(8,128)(2,1)}, bf16[1,3,1024,128]{3,2,1,0:T(8,128)(2,1)S(1)}, u32[]{:S(2)}, u32[]{:S(2)}) collective-permute-start(bf16[1,3,1024,128]{3,2,1,0:T(8,128)(2,1)} %get-tuple-element.61), channel_id=1, source_target_pairs={{0,4},{4,0},{8,12},{12,8},{16,20},{20,16},{24,28},{28,24},{1,5},{5... | collective-permute-start | bytes 2359304 | tf_op jit(solution)/shard_map/swap_c2/ppermute | solution.py:693
  40.0 1.1 copy-start.2
  41.1 1.1 copy-start.6
  42.6 22.1 %collective-permute-start.10 = (bf16[2,1,1024,128]{3,2,1,0:T(8,128)(2,1)S(1)}, bf16[2,1,1024,128]{3,2,1,0:T(8,128)(2,1)S(1)}, u32[]{:S(2)}, u32[]{:S(2)}) collective-permute-start(bf16[2,1,1024,128]{3,2,1,0:T(8,128)(2,1)S(1)} %get-tuple-element.58.refs_0_), channel_id=1, source_target_pairs={{16,8},{20,12},{24,16},{28,20},{17,9},{21,13},{25,17},{29,21},{18,... | collective-permute-start | bytes 1572872 | tf_op jit(solution)/shard_map/near_down_c1/ppermute | solution.py:693
  45.5 21.0 %collective-permute-start.11 = (bf16[2,1,1024,128]{3,2,1,0:T(8,128)(2,1)S(1)}, bf16[2,1,1024,128]{3,2,1,0:T(8,128)(2,1)S(1)}, u32[]{:S(2)}, u32[]{:S(2)}) collective-permute-start(bf16[2,1,1024,128]{3,2,1,0:T(8,128)(2,1)S(1)} %get-tuple-element.58.refs_0_), channel_id=1, source_target_pairs={{24,8},{28,12},{25,9},{29,13},{26,10},{30,14},{27,11},{31,15}} | collective-permute-start | bytes 1572872 | tf_op jit(solution)/shard_map/far_down_c1/ppermute | solution.py:693
  47.1 10.5 %copy-start.3 = (bf16[1,3,1024,128]{3,2,1,0:T(8,128)(2,1)S(1)}, bf16[1,3,1024,128]{3,2,1,0:T(8,128)(2,1)}, u32[]{:S(2)}) copy-start(bf16[1,3,1024,128]{3,2,1,0:T(8,128)(2,1)} %copy-done.1) | copy-start | bytes 2359300
  47.1 21.6 %collective-permute-start.12 = (bf16[2,1,2,1024,128]{4,3,2,1,0:T(8,128)(2,1)S(1)}, bf16[2,1,2,1024,128]{4,3,2,1,0:T(8,128)(2,1)S(1)}, u32[]{:S(2)}, u32[]{:S(2)}) collective-permute-start(bf16[2,1,2,1024,128]{4,3,2,1,0:T(8,128)(2,1)S(1)} %get-tuple-element.65), channel_id=1, source_target_pairs={{0,8},{4,12},{1,9},{5,13},{2,10},{6,14},{3,11},{7,15}} | collective-permute-start | bytes 3145736 | tf_op jit(solution)/shard_map/lift_c1/ppermute | solution.py:693
  50.1 20.4 %collective-permute-start.13 = (bf16[1,1056,256]{2,1,0:T(8,128)(2,1)S(1)}, bf16[1,1056,256]{2,1,0:T(8,128)(2,1)S(1)}, u32[]{:S(2)}, u32[]{:S(2)}) collective-permute-start(bf16[1,1056,256]{2,1,0:T(8,128)(2,1)S(1)} %get-tuple-element.60.refs_0_), channel_id=1, source_target_pairs={{8,16},{12,20},{16,24},{20,28},{9,17},{13,21},{17,25},{21,29},{10,... | collective-permute-start | bytes 1622024 | tf_op jit(solution)/shard_map/near_up_c0/ppermute | solution.py:693
  56.3 24.4 %collective-permute-start.14 = (bf16[1,1056,256]{2,1,0:T(8,128)(2,1)S(1)}, bf16[1,1056,256]{2,1,0:T(8,128)(2,1)S(1)}, u32[]{:S(2)}, u32[]{:S(2)}) collective-permute-start(bf16[1,1056,256]{2,1,0:T(8,128)(2,1)S(1)} %get-tuple-element.68), channel_id=1, source_target_pairs={{8,24},{12,28},{9,25},{13,29},{10,26},{14,30},{11,27},{15,31}} | collective-permute-start | bytes 1622024 | tf_op jit(solution)/shard_map/far_up_c0/ppermute | solution.py:693
  62.4 7.0 %copy-start.7 = (bf16[1,3,1024,128]{3,2,1,0:T(8,128)(2,1)S(1)}, bf16[1,3,1024,128]{3,2,1,0:T(8,128)(2,1)}, u32[]{:S(2)}) copy-start(bf16[1,3,1024,128]{3,2,1,0:T(8,128)(2,1)} %copy-done.4) | copy-start | bytes 2359300
  64.7 23.4 %collective-permute-start.16 = (bf16[2,1,1024,128]{3,2,1,0:T(8,128)(2,1)S(1)}, bf16[2,1,1024,128]{3,2,1,0:T(8,128)(2,1)S(1)}, u32[]{:S(2)}, u32[]{:S(2)}) collective-permute-start(bf16[2,1,1024,128]{3,2,1,0:T(8,128)(2,1)S(1)} %get-tuple-element.62.refs_0_), channel_id=1, source_target_pairs={{16,8},{20,12},{24,16},{28,20},{17,9},{21,13},{25,17},{29,21},{18,... | collective-permute-start | bytes 1572872 | tf_op jit(solution)/shard_map/near_down_c2/ppermute | solution.py:693
  66.5 20.0 %collective-permute-start.15 = (bf16[1,3,1024,128]{3,2,1,0:T(8,128)(2,1)S(1)}, bf16[1,3,1024,128]{3,2,1,0:T(8,128)(2,1)S(1)}, u32[]{:S(2)}, u32[]{:S(2)}) collective-permute-start(bf16[1,3,1024,128]{3,2,1,0:T(8,128)(2,1)S(1)} %get-tuple-element.71), channel_id=1, source_target_pairs={{0,4},{4,0},{8,12},{12,8},{16,20},{20,16},{24,28},{28,24},{1,5},{5... | collective-permute-start | bytes 2359304 | tf_op jit(solution)/shard_map/swap_c3/ppermute | solution.py:693
  68.7 30.1 %collective-permute-start.18 = (bf16[2,1,2,1024,128]{4,3,2,1,0:T(8,128)(2,1)S(1)}, bf16[2,1,2,1024,128]{4,3,2,1,0:T(8,128)(2,1)S(1)}, u32[]{:S(2)}, u32[]{:S(2)}) collective-permute-start(bf16[2,1,2,1024,128]{4,3,2,1,0:T(8,128)(2,1)S(1)} %get-tuple-element.73), channel_id=1, source_target_pairs={{0,8},{4,12},{1,9},{5,13},{2,10},{6,14},{3,11},{7,15}} | collective-permute-start | bytes 3145736 | tf_op jit(solution)/shard_map/lift_c2/ppermute | solution.py:693
  70.5 25.0 %collective-permute-start.17 = (bf16[2,1,1024,128]{3,2,1,0:T(8,128)(2,1)S(1)}, bf16[2,1,1024,128]{3,2,1,0:T(8,128)(2,1)S(1)}, u32[]{:S(2)}, u32[]{:S(2)}) collective-permute-start(bf16[2,1,1024,128]{3,2,1,0:T(8,128)(2,1)S(1)} %get-tuple-element.62.refs_0_), channel_id=1, source_target_pairs={{24,8},{28,12},{25,9},{29,13},{26,10},{30,14},{27,11},{31,15}} | collective-permute-start | bytes 1572872 | tf_op jit(solution)/shard_map/far_down_c2/ppermute | solution.py:693
  80.7 26.0 %collective-permute-start.19 = (bf16[1,1056,256]{2,1,0:T(8,128)(2,1)S(1)}, bf16[1,1056,256]{2,1,0:T(8,128)(2,1)S(1)}, u32[]{:S(2)}, u32[]{:S(2)}) collective-permute-start(bf16[1,1056,256]{2,1,0:T(8,128)(2,1)S(1)} %get-tuple-element.66.refs_0_), channel_id=1, source_target_pairs={{8,16},{12,20},{16,24},{20,28},{9,17},{13,21},{17,25},{21,29},{10,... | collective-permute-start | bytes 1622024 | tf_op jit(solution)/shard_map/near_up_c1/ppermute | solution.py:693
  86.5 21.5 %collective-permute-start.20 = (bf16[1,1056,256]{2,1,0:T(8,128)(2,1)S(1)}, bf16[1,1056,256]{2,1,0:T(8,128)(2,1)S(1)}, u32[]{:S(2)}, u32[]{:S(2)}) collective-permute-start(bf16[1,1056,256]{2,1,0:T(8,128)(2,1)S(1)} %get-tuple-element.77), channel_id=1, source_target_pairs={{8,24},{12,28},{9,25},{13,29},{10,26},{14,30},{11,27},{15,31}} | collective-permute-start | bytes 1622024 | tf_op jit(solution)/shard_map/far_up_c1/ppermute | solution.py:693
  88.1 25.9 %collective-permute-start.21 = (bf16[2,1,1024,128]{3,2,1,0:T(8,128)(2,1)S(1)}, bf16[2,1,1024,128]{3,2,1,0:T(8,128)(2,1)S(1)}, u32[]{:S(2)}, u32[]{:S(2)}) collective-permute-start(bf16[2,1,1024,128]{3,2,1,0:T(8,128)(2,1)S(1)} %get-tuple-element.72.refs_0_), channel_id=1, source_target_pairs={{16,8},{20,12},{24,16},{28,20},{17,9},{21,13},{25,17},{29,21},{18,... | collective-permute-start | bytes 1572872 | tf_op jit(solution)/shard_map/near_down_c3/ppermute | solution.py:693
  95.5 18.5 %collective-permute-start.22 = (bf16[2,1,1024,128]{3,2,1,0:T(8,128)(2,1)S(1)}, bf16[2,1,1024,128]{3,2,1,0:T(8,128)(2,1)S(1)}, u32[]{:S(2)}, u32[]{:S(2)}) collective-permute-start(bf16[2,1,1024,128]{3,2,1,0:T(8,128)(2,1)S(1)} %get-tuple-element.72.refs_0_), channel_id=1, source_target_pairs={{24,8},{28,12},{25,9},{29,13},{26,10},{30,14},{27,11},{31,15}} | collective-permute-start | bytes 1572872 | tf_op jit(solution)/shard_map/far_down_c3/ppermute | solution.py:693
  98.8 15.3 %collective-permute-start.23 = (bf16[2,1,2,1024,128]{4,3,2,1,0:T(8,128)(2,1)S(1)}, bf16[2,1,2,1024,128]{4,3,2,1,0:T(8,128)(2,1)S(1)}, u32[]{:S(2)}, u32[]{:S(2)}) collective-permute-start(bf16[2,1,2,1024,128]{4,3,2,1,0:T(8,128)(2,1)S(1)} %get-tuple-element.80), channel_id=1, source_target_pairs={{0,8},{4,12},{1,9},{5,13},{2,10},{6,14},{3,11},{7,15}} | collective-permute-start | bytes 3145736 | tf_op jit(solution)/shard_map/lift_c3/ppermute | solution.py:693
  106.7 24.3 %collective-permute-start.24 = (bf16[1,1056,256]{2,1,0:T(8,128)(2,1)S(1)}, bf16[1,1056,256]{2,1,0:T(8,128)(2,1)S(1)}, u32[]{:S(2)}, u32[]{:S(2)}) collective-permute-start(bf16[1,1056,256]{2,1,0:T(8,128)(2,1)S(1)} %get-tuple-element.74.refs_0_), channel_id=1, source_target_pairs={{8,16},{12,20},{16,24},{20,28},{9,17},{13,21},{17,25},{21,29},{10,... | collective-permute-start | bytes 1622024 | tf_op jit(solution)/shard_map/near_up_c2/ppermute | solution.py:693
  108.0 23.0 %collective-permute-start.25 = (bf16[1,1056,256]{2,1,0:T(8,128)(2,1)S(1)}, bf16[1,1056,256]{2,1,0:T(8,128)(2,1)S(1)}, u32[]{:S(2)}, u32[]{:S(2)}) collective-permute-start(bf16[1,1056,256]{2,1,0:T(8,128)(2,1)S(1)} %get-tuple-element.85), channel_id=1, source_target_pairs={{8,24},{12,28},{9,25},{13,29},{10,26},{14,30},{11,27},{15,31}} | collective-permute-start | bytes 1622024 | tf_op jit(solution)/shard_map/far_up_c2/ppermute | solution.py:693
  118.6 19.2 %collective-permute-start.27 = (bf16[1,528,256]{2,1,0:T(8,128)(2,1)S(1)}, bf16[1,528,256]{2,1,0:T(8,128)(2,1)S(1)}, u32[]{:S(2)}, u32[]{:S(2)}) collective-permute-start(bf16[1,528,256]{2,1,0:T(8,128)(2,1)S(1)} %get-tuple-element.89), channel_id=1, source_target_pairs={{0,4},{4,0},{8,12},{12,8},{16,20},{20,16},{24,28},{28,24},{1,5},{5... | collective-permute-start | bytes 811016 | tf_op jit(solution)/shard_map/back_own_c3/ppermute | solution.py:693
  120.4 20.2 %collective-permute-start.28 = (bf16[1,528,256]{2,1,0:T(8,128)(2,1)S(1)}, bf16[1,528,256]{2,1,0:T(8,128)(2,1)S(1)}, u32[]{:S(2)}, u32[]{:S(2)}) collective-permute-start(bf16[1,528,256]{2,1,0:T(8,128)(2,1)S(1)} %get-tuple-element.81.refs_0_), channel_id=1, source_target_pairs={{8,16},{12,20},{16,24},{20,28},{9,17},{13,21},{17,25},{21,29},{10,... | collective-permute-start | bytes 811016 | tf_op jit(solution)/shard_map/near_up_same_c3/ppermute | solution.py:693
  121.7 30.0 %collective-permute-start.29 = (bf16[1,528,256]{2,1,0:T(8,128)(2,1)S(1)}, bf16[1,528,256]{2,1,0:T(8,128)(2,1)S(1)}, u32[]{:S(2)}, u32[]{:S(2)}) collective-permute-start(bf16[1,528,256]{2,1,0:T(8,128)(2,1)S(1)} %get-tuple-element.90), channel_id=1, source_target_pairs={{8,20},{12,16},{16,28},{20,24},{9,21},{13,17},{17,29},{21,25},{10,... | collective-permute-start | bytes 811016 | tf_op jit(solution)/shard_map/near_up_cross_c3/ppermute | solution.py:693
  132.0 23.9 %copy-start.10 = (bf16[1024]{0:T(1024)(128)(2,1)S(1)}, bf16[1024]{0:T(1024)(128)(2,1)}, u32[]{:S(2)}) copy-start(bf16[1024]{0:T(1024)(128)(2,1)} %param.9) | copy-start | bytes 6148
  132.1 4.5 %collective-permute-start.26 = (f32[4,256]{1,0:T(4,128)S(1)}, f32[4,256]{1,0:T(4,128)S(1)}, u32[]{:S(2)}, u32[]{:S(2)}) collective-permute-start(f32[4,256]{1,0:T(4,128)S(1)} %slice.23), channel_id=1, source_target_pairs={{0,4},{4,0},{8,12},{12,8},{16,20},{20,16},{24,28},{28,24},{1,5},{5... | collective-permute-start | bytes 12296 | tf_op jit(solution)/shard_map/squares_swap/ppermute | solution.py:693
  134.9 17.2 %collective-permute-start.30 = (bf16[1,528,256]{2,1,0:T(8,128)(2,1)S(1)}, bf16[1,528,256]{2,1,0:T(8,128)(2,1)S(1)}, u32[]{:S(2)}, u32[]{:S(2)}) collective-permute-start(bf16[1,528,256]{2,1,0:T(8,128)(2,1)S(1)} %get-tuple-element.91), channel_id=1, source_target_pairs={{8,24},{12,28},{9,25},{13,29},{10,26},{14,30},{11,27},{15,31}} | collective-permute-start | bytes 811016 | tf_op jit(solution)/shard_map/far_up_same_c3/ppermute | solution.py:693
  136.5 15.6 %collective-permute-start.31 = (bf16[1,528,256]{2,1,0:T(8,128)(2,1)S(1)}, bf16[1,528,256]{2,1,0:T(8,128)(2,1)S(1)}, u32[]{:S(2)}, u32[]{:S(2)}) collective-permute-start(bf16[1,528,256]{2,1,0:T(8,128)(2,1)S(1)} %get-tuple-element.92), channel_id=1, source_target_pairs={{8,28},{12,24},{9,29},{13,25},{10,30},{14,26},{11,31},{15,27}} | collective-permute-start | bytes 811016 | tf_op jit(solution)/shard_map/far_up_cross_c3/ppermute | solution.py:693
  137.8 20.2 %collective-permute-start.32 = (bf16[1,1024,128]{2,1,0:T(8,128)(2,1)S(1)}, bf16[1,1024,128]{2,1,0:T(8,128)(2,1)S(1)}, u32[]{:S(2)}, u32[]{:S(2)}) collective-permute-start(bf16[1,1024,128]{2,1,0:T(8,128)(2,1)S(1)} %get-tuple-element.94), channel_id=1, source_target_pairs={{0,4},{4,0},{8,12},{12,8},{16,20},{20,16},{24,28},{28,24},{1,5},{5... | collective-permute-start | bytes 786440 | tf_op jit(solution)/shard_map/back_c0/ppermute | solution.py:693
  140.7 17.3 %collective-permute-start.33 = (bf16[1,1024,128]{2,1,0:T(8,128)(2,1)S(1)}, bf16[1,1024,128]{2,1,0:T(8,128)(2,1)S(1)}, u32[]{:S(2)}, u32[]{:S(2)}) collective-permute-start(bf16[1,1024,128]{2,1,0:T(8,128)(2,1)S(1)} %get-tuple-element.95), channel_id=1, source_target_pairs={{0,4},{4,0},{8,12},{12,8},{16,20},{20,16},{24,28},{28,24},{1,5},{5... | collective-permute-start | bytes 786440 | tf_op jit(solution)/shard_map/back_c1/ppermute | solution.py:693
  151.8 7.4 %collective-permute-start.34 = (bf16[1,1024,128]{2,1,0:T(8,128)(2,1)S(1)}, bf16[1,1024,128]{2,1,0:T(8,128)(2,1)S(1)}, u32[]{:S(2)}, u32[]{:S(2)}) collective-permute-start(bf16[1,1024,128]{2,1,0:T(8,128)(2,1)S(1)} %get-tuple-element.96), channel_id=1, source_target_pairs={{0,4},{4,0},{8,12},{12,8},{16,20},{20,16},{24,28},{28,24},{1,5},{5... | collective-permute-start | bytes 786440 | tf_op jit(solution)/shard_map/back_c2/ppermute | solution.py:693
  153.2 1.2 collective-permute-start.35
  154.4 3.6 %collective-permute-start.36 = (f32[4,256]{1,0:T(4,128)S(1)}, f32[4,256]{1,0:T(4,128)S(1)}, u32[]{:S(2)}, u32[]{:S(2)}) collective-permute-start(f32[4,256]{1,0:T(4,128)S(1)} %add.296), channel_id=1, source_target_pairs={{0,2},{1,3},{2,0},{3,1},{4,6},{5,7},{6,4},{7,5},{8,10},{9,11},{10,... | collective-permute-start | bytes 12296 | tf_op jit(solution)/shard_map/ppermute | solution.py:864
